TPU v7x, 32 devices: a whole 2x2x4 slice. The times are simulated.
32 devices in a mesh: grp: 4 (over y, x), dev: 8 (over z, core).
Axes of the slice: x: 2, y: 2, z: 4, core: 2. Of those that a mesh axis runs over, the one named last changes fastest.
Arguments:
- counts: bfloat16 [768, 64, 4096], P(('grp', 'dev')), may hold values from 0.099609375 to 10
- src_factor: bfloat16 [8192, 256], P(('grp', 'dev')), may hold values from -0.5 to 0.5
- dst_factor: bfloat16 [2048, 256], P('dev'), may hold values from -0.5 to 0.5
- hour_factor: bfloat16 [4096, 256], replicated, may hold values from -0.5 to 0.5
- src_owner: int32 [768, 1], P(('grp', 'dev')), may hold values from 0 to 7; in each aligned block of 24 rows (0 to 23, 24 to 47, ...) at most 4 rows name the same one
- src_slot: int32 [768], P(('grp', 'dev')), may hold values from 0 to 3
- dst_owner: int32 [768, 1], P(('grp', 'dev')), may hold values from 0 to 7; in each aligned block of 24 rows (0 to 23, 24 to 47, ...) at most 4 rows name the same one
- dst_slot: int32 [768], P(('grp', 'dev')), may hold values from 0 to 3
- hour_block: int32 [768], P(('grp', 'dev')), may hold values from 0 to 63
Outputs:
- grad_src: float32 [8192, 256], P(('grp', 'dev'))
- grad_dst: float32 [2048, 256], P('dev')
- grad_hour: float32 [4096, 256], replicated
Inputs may be any that keep to these rules, and one draw needn't show every extreme that they name: `src_owner`: among the 24 rows of one device no owner is named more than 4 times; in every draw some device names some owner exactly 4 times. `dst_owner`: among the 24 rows of one device no owner is named more than 4 times; in every draw some device names some owner exactly 4 times.
All inputs are finite; a program needn't handle non-finite values.
Results may differ from a plain program's by a relative error of at most 0.003.
Values may be sent and summed in bfloat16 or wider, within the bound.
No kernel may reach another device: no remote copies, remote signals or barrier semaphores. Data moves between devices by JAX's collectives and lax.ppermute only.
A program may use at most 128 MiB of HBM per device.

v0:
```python
import jax
import jax.numpy as jnp
from jax import lax
from jax.sharding import PartitionSpec as P


def slot_layout(owner_list, owner_count, capacity):
    onehot = (owner_list[:, None] == jnp.arange(owner_count, dtype=jnp.int32)[None, :]).astype(
        jnp.int32
    )
    earlier = jnp.cumsum(onehot, axis=0) - onehot
    within = jnp.sum(earlier * onehot, axis=1)
    return owner_list * capacity + within


def block_terms(block, src_rows, dst_rows, hour_rows):
    block_side = block.shape[0]
    factor_rank = src_rows.shape[1]
    scale = 1.0 / block_side
    wide_a = src_rows.astype(jnp.float32)
    wide_b = dst_rows.astype(jnp.float32)
    wide_c = hour_rows.astype(jnp.float32)
    pair_bc = (wide_b[:, None, :] * wide_c[None, :, :]).astype(jnp.bfloat16)
    pair_ac = (wide_a[:, None, :] * wide_c[None, :, :]).astype(jnp.bfloat16)
    pair_ab = (wide_a[:, None, :] * wide_b[None, :, :]).astype(jnp.bfloat16)
    flat_bc = pair_bc.reshape(block_side * block_side, factor_rank)
    theta = lax.dot_general(
        src_rows, flat_bc, (((1,), (1,)), ((), ())), preferred_element_type=jnp.float32
    )
    resid = (jnp.exp(theta) - block.astype(jnp.float32)).astype(jnp.bfloat16)
    grad_a = jnp.dot(resid, flat_bc, preferred_element_type=jnp.float32) * scale
    cube = resid.reshape(block_side, block_side, block_side)
    grad_b = jnp.einsum("ijk,ikr->jr", cube, pair_ac, preferred_element_type=jnp.float32) * scale
    grad_c = jnp.einsum("ijk,ijr->kr", cube, pair_ab, preferred_element_type=jnp.float32) * scale
    return (grad_a, grad_b, grad_c)


def per_device(
    counts,
    src_factor,
    dst_factor,
    hour_factor,
    src_owner,
    src_slot,
    dst_owner,
    dst_slot,
    hour_block,
):
    blocks = counts.shape[0]
    block_side = counts.shape[1]
    factor_rank = src_factor.shape[1]
    owner_count = lax.axis_size("dev")
    src_table = src_factor.reshape(-1, block_side, factor_rank)
    dst_table = dst_factor.reshape(-1, block_side, factor_rank)
    src_local = src_table.shape[0]
    dst_local = dst_table.shape[0]
    src_own = src_owner[:, 0]
    dst_own = dst_owner[:, 0]
    capacity = max(2, (blocks + owner_count - 1) // owner_count + 1)
    src_pos = slot_layout(src_own, owner_count, capacity)
    dst_pos = slot_layout(dst_own, owner_count, capacity)
    unused_slots = jnp.full((owner_count * capacity,), -1, jnp.int32)
    src_wanted = unused_slots.at[src_pos].set(src_slot).reshape(owner_count, capacity)
    dst_wanted = unused_slots.at[dst_pos].set(dst_slot).reshape(owner_count, capacity)
    asked_src = lax.all_to_all(src_wanted, "dev", split_axis=0, concat_axis=0, tiled=True)
    asked_dst = lax.all_to_all(dst_wanted, "dev", split_axis=0, concat_axis=0, tiled=True)
    found_src = src_table[jnp.clip(asked_src, 0, src_local - 1)]
    found_dst = dst_table[jnp.clip(asked_dst, 0, dst_local - 1)]
    back_src = lax.all_to_all(found_src, "dev", split_axis=0, concat_axis=0, tiled=True)
    back_dst = lax.all_to_all(found_dst, "dev", split_axis=0, concat_axis=0, tiled=True)
    back_src, back_dst, asked_src, asked_dst = (back_src, back_dst, asked_src, asked_dst)
    src_rows = back_src.reshape(-1, block_side, factor_rank)[src_pos]
    dst_rows = back_dst.reshape(-1, block_side, factor_rank)[dst_pos]

    def visit(hour_acc, inputs):
        block, a_rows, b_rows, hour_pick = inputs
        start = hour_pick * block_side
        c_rows = lax.dynamic_slice_in_dim(hour_factor, start, block_side, 0)
        grad_a, grad_b, grad_c = block_terms(block, a_rows, b_rows, c_rows)
        current = lax.dynamic_slice_in_dim(hour_acc, start, block_side, 0)
        hour_acc = lax.dynamic_update_slice_in_dim(hour_acc, current + grad_c, start, 0)
        return (hour_acc, (grad_a, grad_b))

    start_hours = jnp.zeros(hour_factor.shape, jnp.float32)
    hour_acc, grads = lax.scan(visit, start_hours, (counts, src_rows, dst_rows, hour_block))
    grads_src, grads_dst = grads
    send_src = (
        jnp.zeros((owner_count * capacity, block_side, factor_rank), jnp.float32)
        .at[src_pos]
        .set(grads_src)
    )
    send_dst = (
        jnp.zeros((owner_count * capacity, block_side, factor_rank), jnp.float32)
        .at[dst_pos]
        .set(grads_dst)
    )
    send_src = send_src.reshape(owner_count, capacity, block_side, factor_rank)
    send_dst = send_dst.reshape(owner_count, capacity, block_side, factor_rank)
    got_src, got_dst = (
        lax.all_to_all(send_src, "dev", split_axis=0, concat_axis=0, tiled=True),
        lax.all_to_all(send_dst, "dev", split_axis=0, concat_axis=0, tiled=True),
    )
    keep_src = (asked_src >= 0).astype(jnp.float32)[:, :, None, None]
    keep_dst = (asked_dst >= 0).astype(jnp.float32)[:, :, None, None]
    part_src = (
        jnp.zeros((src_local, block_side, factor_rank), jnp.float32)
        .at[jnp.clip(asked_src, 0, src_local - 1)]
        .add(got_src * keep_src)
    )
    part_dst = (
        jnp.zeros((dst_local, block_side, factor_rank), jnp.float32)
        .at[jnp.clip(asked_dst, 0, dst_local - 1)]
        .add(got_dst * keep_dst)
    )
    part_src = part_src.reshape(-1, factor_rank)
    part_dst = part_dst.reshape(-1, factor_rank)
    dst_total = lax.psum(part_dst, "grp")
    hour_total = lax.psum(hour_acc, ("grp", "dev"))
    return (part_src, dst_total, hour_total)


def solution(mesh):
    in_specs = (
        P(("grp", "dev"), None, None),
        P(("grp", "dev"), None),
        P("dev", None),
        P(),
        P(("grp", "dev"), None),
        P(("grp", "dev")),
        P(("grp", "dev"), None),
        P(("grp", "dev")),
        P(("grp", "dev")),
    )
    out_specs = (P(("grp", "dev"), None), P("dev", None), P())
    return jax.shard_map(
        per_device, mesh=mesh, in_specs=in_specs, out_specs=out_specs, check_vma=False
    )
```

profile of v0, /device:TPU:0, one launch (start us, length us, event | category | flops | bytes accessed | tf_op | source)
XLA Modules:
  0.0 687.4 jit_solution(2938416612306715198)
XLA Ops:
  10.9 6.3 all-to-all-start
  22.8 3.4 all-to-all-start.2
  28.0 3.6 all-to-all-done.2
  31.6 3.6 all-to-all-start.1
  37.0 24.6 %all-to-all-done.1 = bf16[8,4,64,256]{3,2,1,0:T(8,128)(2,1)S(1)} async-done(((bf16[8,4,64,256]{3,2,1,0:T(8,128)(2,1)}), bf16[8,4,64,256]{3,2,1,0:T(8,128)(2,1)S(1)}, u32[]{:S(2)}, u32[]{:S(2)}) %all-to-all-start.1) | async-done | bytes 1048608 | tf_op jit(solution)/shard_map/all_to_all | solution.py:69
  61.7 3.6 all-to-all-start.3
  66.8 24.9 %all-to-all-done.3 = bf16[8,4,64,256]{3,2,1,0:T(8,128)(2,1)S(1)} async-done(((bf16[8,4,64,256]{3,2,1,0:T(8,128)(2,1)}), bf16[8,4,64,256]{3,2,1,0:T(8,128)(2,1)S(1)}, u32[]{:S(2)}, u32[]{:S(2)}) %all-to-all-start.3) | async-done | bytes 1048608 | tf_op jit(solution)/shard_map/all_to_all | solution.py:70
  94.7 291.9 %while.14 = (s32[]{:T(128)}, f32[4096,256]{1,0:T(8,128)}, f32[24,64,256]{2,1,0:T(8,128)}, f32[24,64,256]{2,1,0:T(8,128)}, s32[24]{0:T(128)S(1)}, /*index=5*/bf16...) while((s32[]{:T(128)}, f32[4096,256]{1,0:T(8,128)}, ...), condition=%wide.region_7.8_spmd, body=%wide.region_6.7_spmd.sunk | while | flops 544063488 | bytes 19859736 | solution.py:85
  102.2 2.4 fusion.51
  114.3 2.4 fusion.51
  163.0 2.4 fusion.51
  175.1 2.4 fusion.51
  187.3 2.4 fusion.51
  199.4 2.4 fusion.51
  211.6 2.4 fusion.51
  235.9 2.4 fusion.51
  248.1 2.4 fusion.51
  260.3 2.4 fusion.51
  272.4 2.4 fusion.51
  284.6 2.4 fusion.51
  388.1 5.9 scatter_fusion.2
  394.0 3.6 all-to-all-start.5
  399.2 6.1 scatter_fusion
  405.3 41.3 %all-to-all-done.5 = f32[8,4,64,256]{3,2,1,0:T(8,128)S(1)} async-done(((f32[8,4,64,256]{3,2,1,0:T(8,128)}), f32[8,4,64,256]{3,2,1,0:T(8,128)S(1)}, u32[]{:S(2)}, u32[]{:S(2)}) %all-to-all-start.5) | async-done | bytes 2097184 | tf_op jit(solution)/shard_map/all_to_all | solution.py:101
  448.0 3.6 all-to-all-start.4
  452.6 3.2 broadcast_multiply_fusion
  455.8 4.7 scatter_fusion.3
  461.2 55.6 %all-to-all-done.4 = f32[8,4,64,256]{3,2,1,0:T(8,128)S(1)} async-done(((f32[8,4,64,256]{3,2,1,0:T(8,128)}), f32[8,4,64,256]{3,2,1,0:T(8,128)S(1)}, u32[]{:S(2)}, u32[]{:S(2)}) %all-to-all-start.4) | async-done | bytes 2097184 | tf_op jit(solution)/shard_map/all_to_all | solution.py:100
  518.3 4.7 scatter_fusion.1
  523.0 106.1 %all-reduce.5.cloned.1.call-done = f32[4096,256]{1,0:T(8,128)} async-done(((f32[4096,256]{1,0:T(8,128)}), f32[4096,256]{1,0:T(8,128)}) %all-reduce.5.cloned.1.call-update) | async-done | bytes 4194320 | tf_op jit(solution)/shard_map/psum | solution.py:118
  629.1 45.4 %all-reduce.3.cloned.1.call-done = f32[256,256]{1,0:T(8,128)} async-done(((f32[256,256]{1,0:T(8,128)}), f32[256,256]{1,0:T(8,128)}) %all-reduce.3.cloned.1.call-update) | async-done | bytes 262160 | tf_op jit(solution)/shard_map/psum | solution.py:117
  676.1 4.5 copy.75
  (406 shorter events, 273.5 us)
Async XLA Ops:
  7.2 19.2 %copy-start = (bf16[256,256]{1,0:T(8,128)(2,1)S(1)}, bf16[256,256]{1,0:T(8,128)(2,1)}, u32[]{:S(2)}) copy-start(bf16[256,256]{1,0:T(8,128)(2,1)} %param.12) | copy-start | bytes 393220
  10.9 11.8 %all-to-all-start = ((s32[8,1,4]{2,1,0:T(1,128)}), s32[8,1,4]{2,1,0:T(1,128)S(1)}, u32[]{:S(2)}, u32[]{:S(2)}) async-start(s32[8,1,4]{2,1,0:T(1,128)} %bitcast.13), calls=%async_computation | async-start | bytes 8192 | tf_op jit(solution)/shard_map/all_to_all | solution.py:65
  22.8 8.8 %all-to-all-start.2 = ((s32[8,1,4]{2,1,0:T(1,128)}), s32[8,1,4]{2,1,0:T(1,128)S(1)}, u32[]{:S(2)}, u32[]{:S(2)}) async-start(s32[8,1,4]{2,1,0:T(1,128)} %bitcast.22), calls=%async_computation.2 | async-start | bytes 8192 | tf_op jit(solution)/shard_map/all_to_all | solution.py:66
  26.4 9.0 %copy-start.5 = (bf16[256,256]{1,0:T(8,128)(2,1)S(1)}, bf16[256,256]{1,0:T(8,128)(2,1)}, u32[]{:S(2)}) copy-start(bf16[256,256]{1,0:T(8,128)(2,1)} %param.13) | copy-start | bytes 393220
  31.6 30.1 %all-to-all-start.1 = ((bf16[8,4,64,256]{3,2,1,0:T(8,128)(2,1)}), bf16[8,4,64,256]{3,2,1,0:T(8,128)(2,1)S(1)}, u32[]{:S(2)}, u32[]{:S(2)}) async-start(bf16[8,4,64,256]{3,2,1,0:T(8,128)(2,1)} %bitcast.16), calls=%async_computation.1 | async-start | bytes 2097152 | tf_op jit(solution)/shard_map/all_to_all | solution.py:69
  61.7 30.1 %all-to-all-start.3 = ((bf16[8,4,64,256]{3,2,1,0:T(8,128)(2,1)}), bf16[8,4,64,256]{3,2,1,0:T(8,128)(2,1)S(1)}, u32[]{:S(2)}, u32[]{:S(2)}) async-start(bf16[8,4,64,256]{3,2,1,0:T(8,128)(2,1)} %bitcast.24), calls=%async_computation.3 | async-start | bytes 2097152 | tf_op jit(solution)/shard_map/all_to_all | solution.py:70
  102.2 3.5 copy-start.1
  114.3 3.5 copy-start.1
  126.5 3.5 copy-start.1
  138.6 3.5 copy-start.1
  150.8 3.5 copy-start.1
  163.0 3.5 copy-start.1
  175.1 3.5 copy-start.1
  187.3 3.5 copy-start.1
  211.6 3.5 copy-start.1
  235.9 3.5 copy-start.1
  260.3 3.5 copy-start.1
  272.4 3.5 copy-start.1
  284.6 3.5 copy-start.1
  296.8 3.5 copy-start.1
  308.9 3.5 copy-start.1
  321.1 3.5 copy-start.1
  333.2 3.5 copy-start.1
  345.4 3.5 copy-start.1
  357.6 3.5 copy-start.1
  369.7 3.5 copy-start.1
  381.9 3.5 copy-start.1
  394.0 52.6 %all-to-all-start.5 = ((f32[8,4,64,256]{3,2,1,0:T(8,128)}), f32[8,4,64,256]{3,2,1,0:T(8,128)S(1)}, u32[]{:S(2)}, u32[]{:S(2)}) async-start(f32[8,4,64,256]{3,2,1,0:T(8,128)} %bitcast.30), calls=%async_computation.5 | async-start | bytes 4194304 | tf_op jit(solution)/shard_map/all_to_all | solution.py:101
  448.0 68.8 %all-to-all-start.4 = ((f32[8,4,64,256]{3,2,1,0:T(8,128)}), f32[8,4,64,256]{3,2,1,0:T(8,128)S(1)}, u32[]{:S(2)}, u32[]{:S(2)}) async-start(f32[8,4,64,256]{3,2,1,0:T(8,128)} %bitcast.26), calls=%async_computation.4 | async-start | bytes 4194304 | tf_op jit(solution)/shard_map/all_to_all | solution.py:100
  451.6 177.5 %all-reduce.5.cloned.1.call-start = ((), (), s32[]{:S(2)}) async-start(), calls=%async_computation.7 | async-start | bytes 8388608 | tf_op jit(solution)/shard_map/psum | solution.py:118
  452.3 222.1 %all-reduce.3.cloned.1.call-start = ((), (), s32[]{:S(2)}) async-start(), calls=%async_computation.6 | async-start | bytes 524288 | tf_op jit(solution)/shard_map/psum | solution.py:117
  523.0 157.6 %copy-start.3 = (f32[4,64,256]{2,1,0:T(8,128)}, f32[4,64,256]{2,1,0:T(8,128)S(1)}, u32[]{:S(2)}) copy-start(f32[4,64,256]{2,1,0:T(8,128)S(1)} %scatter_fusion.1) | copy-start | bytes 786436
  (54 other events, 112.0 us)
Sparse Core Ops, SparseCore 0:
  458.5 170.4 all-reduce.4
  632.6 41.8 all-reduce.2
where the time goes:
time: 693 us; the launch traced here: 687 us
  waiting for transfers between devices  304 us (44%)
  matrix products  155 us (22%)
  local copies, waits for them, and re-layouts  102 us (15%)
  other arithmetic  71.9 us (10%)
  starting transfers between devices  24.1 us (3%)
  loops' own time  16.5 us (2%)
  between operations  14.2 us (2%)
    psum x1, waiting for transfers between devices, per_device(): hour_total = lax.psum(hour_acc, ('grp', 'dev'))  106 us
    dot_general x24, matrix products, block_terms(): jnp.einsum('ijk,ijr->kr', cube, pair_ab, preferred_element_type=jnp.float32)  57.3 us
    all_to_all x1, waiting for transfers between devices, per_device(): lax.all_to_all(send_src, 'dev', split_axis=0, concat_axis=0, tiled=True)  55.6 us
    reshape x24, local copies, waits for them, and re-layouts, block_terms(): cube = resid.reshape(block_side, block_side, block_side)  50.5 us
    psum x1, waiting for transfers between devices, per_device(): dst_total = lax.psum(part_dst, 'grp')  45.4 us
    dot_general x24, matrix products, block_terms(): lax.dot_general(src_rows, flat_bc, (((1,), (1,)), ((), ())), preferred_el...  43.9 us
    all_to_all x1, waiting for transfers between devices, per_device(): lax.all_to_all(send_dst, 'dev', split_axis=0, concat_axis=0, tiled=True)  41.3 us
    dot_general x24, matrix products, block_terms(): jnp.einsum('ijk,ikr->jr', cube, pair_ac, preferred_element_type=jnp.float32)  28 us
  transfers between devices with their start and end apart: 8, of which 8 were waited for; matrix products, arithmetic and copies ran while one was open for 4% of the time, Pallas kernels for 0%

commit v1 on v0

v1 whole, which is shorter than its diff:
```python
import functools

import jax
import jax.numpy as jnp
from jax import lax
from jax.experimental import pallas as pl
from jax.experimental.pallas import tpu as pltpu
from jax.sharding import PartitionSpec as P

F32 = jnp.float32
BF16 = jnp.bfloat16
SIDE = 64
RING = 6
PITCH = 72

VMEM = pl.BlockSpec(memory_space=pltpu.VMEM)
SMEM = pl.BlockSpec(memory_space=pltpu.SMEM)
ANY = pl.BlockSpec(memory_space=pl.ANY)


def mesh_sizes(mesh):
    return mesh.shape["grp"], mesh.shape["dev"]


def swap(x, axis, size, mask):
    return lax.ppermute(x, axis, [(i, i ^ mask) for i in range(size)])


def block_terms(count, a, b, c, cube, even, odd):
    rank = a.shape[1]
    resids, pairs_bc, turned, pairs_ab = [], [], [], []
    for g in range(SIDE // 4):
        b4 = b[g * 4 : g * 4 + 4]
        bc = (b4[:, None, :] * c[None, :, :]).reshape(4 * SIDE, rank)
        ab = (b4[:, None, :] * a[None, :, :]).reshape(4 * SIDE, rank)
        theta = lax.dot_general(a, bc, (((1,), (1,)), ((), ())), preferred_element_type=F32)
        wide = jnp.exp(theta) - count[:, g * 256 : (g + 1) * 256].astype(F32)
        for p in range(2):
            cube[pl.ds((g * 2 + p) * PITCH, SIDE), :] = wide[:, p * 128 : (p + 1) * 128]
        resid = wide.astype(BF16)
        flip = resid.T
        turned += [flip[q * SIDE : (q + 1) * SIDE] for q in range(4)]
        resids.append(resid)
        pairs_bc.append(bc)
        pairs_ab.append(ab)
    term_a = jnp.dot(
        jnp.concatenate(resids, axis=1),
        jnp.concatenate(pairs_bc, axis=0),
        preferred_element_type=F32,
    )
    term_c = jnp.dot(
        jnp.concatenate(turned, axis=1),
        jnp.concatenate(pairs_ab, axis=0),
        preferred_element_type=F32,
    )
    low = lax.broadcasted_iota(jnp.int32, (SIDE // 2, 128), 1) < SIDE
    rows, pairs_ac = [], []
    for g in range(SIDE // 4):
        x = [cube[pl.ds(g * 4 + q, SIDE // 2, stride=PITCH), :] for q in range(4)]
        y = [pltpu.roll(v, SIDE, 1) for v in x]
        evens = [jnp.where(low, x[0], y[1]), jnp.where(low, x[2], y[3])]
        odds = [jnp.where(low, y[0], x[1]), jnp.where(low, y[2], x[3])]
        both = [jnp.concatenate(evens, axis=1), jnp.concatenate(odds, axis=1)]
        rows.append(jnp.concatenate(both, axis=0).astype(BF16))
        pairs_ac.append((a[g * 4 : g * 4 + 4][:, None, :] * c[None, :, :]).reshape(4 * SIDE, rank))
    mixed = jnp.dot(
        jnp.concatenate(rows, axis=1),
        jnp.concatenate(pairs_ac, axis=0),
        preferred_element_type=F32,
    )
    half = SIDE // 2
    for u in range(2):
        even[pl.ds(u, half, stride=2), :] = mixed[u * half : (u + 1) * half, :128]
        odd[pl.ds(u, half, stride=2), :] = mixed[u * half : (u + 1) * half, 128:]
    term_b = jnp.concatenate([even[...], odd[...]], axis=1)
    return term_a, term_b, term_c


def main_kernel(shape, ids, counts, hours, *refs):
    grps, devs, local, hour_rows = shape
    depth = devs // 2
    pieces = refs[:devs]
    hd_keep, s_keep, hd_send, s_send = refs[devs : devs + 4]
    (ring, table, hd_acc, s_acc, hd_out, s_out, cube, even, odd, ring_sem, in_sem, out_sem) = refs[
        devs + 4 :
    ]
    blocks = counts.shape[0]
    hour_part = hour_rows // (2 * grps)
    dst_part = local // grps
    part = hour_part + depth * dst_part
    hour_blocks = hour_part // SIDE

    def fetch(t):
        slot = lax.rem(t, RING)
        return pltpu.make_async_copy(counts.at[t], ring.at[slot], ring_sem.at[slot])

    for t in range(min(RING, blocks)):
        fetch(t).start()
    loads = [
        pltpu.make_async_copy(pieces[m], table.at[pl.ds(m * 2 * local, 2 * local)], in_sem.at[m])
        for m in range(devs)
    ]
    for load in loads:
        load.start()
    hd_acc[...] = jnp.zeros_like(hd_acc)
    s_acc[...] = jnp.zeros_like(s_acc)
    for load in loads:
        load.wait()
    me, grp = ids[0], ids[1]
    core = me & 1
    base = 8

    def visit(t, carry):
        src_from = ids[base + t] ^ me
        src_slot = ids[base + blocks + t]
        dst_from = ids[base + 2 * blocks + t] ^ me
        dst_slot = ids[base + 3 * blocks + t]
        hour = ids[base + 4 * blocks + t]
        fetch(t).wait()
        a_at = pl.multiple_of(src_from * (2 * local) + src_slot * SIDE, SIDE)
        b_at = pl.multiple_of(dst_from * (2 * local) + local + dst_slot * SIDE, SIDE)
        c_at = pl.multiple_of(hour * SIDE, SIDE)
        term_a, term_b, term_c = block_terms(
            ring.at[lax.rem(t, RING)],
            table[pl.ds(a_at, SIDE), :],
            table[pl.ds(b_at, SIDE), :],
            hours[pl.ds(c_at, SIDE), :],
            cube,
            even,
            odd,
        )
        s_at = (src_from & 1) * (depth * local) + (src_from >> 1) * local + src_slot * SIDE
        row = dst_slot * SIDE
        d_at = ((dst_from & 1) * grps + ((row // dst_part) ^ grp)) * part + hour_part
        d_at = d_at + (dst_from >> 1) * dst_part + row % dst_part
        home = hour // hour_blocks
        h_at = (((home // grps) ^ core) * grps + ((home % grps) ^ grp)) * part
        h_at = h_at + (hour % hour_blocks) * SIDE
        s_acc[pl.ds(pl.multiple_of(s_at, SIDE), SIDE), :] += term_a
        hd_acc[pl.ds(pl.multiple_of(d_at, SIDE), SIDE), :] += term_b
        hd_acc[pl.ds(pl.multiple_of(h_at, SIDE), SIDE), :] += term_c

        @pl.when(t + RING < blocks)
        def _():
            fetch(t + RING).start()

        return carry

    lax.fori_loop(0, blocks, visit, 0)
    hd_half, s_half = grps * part, depth * local
    stores = [
        pltpu.make_async_copy(hd_acc.at[pl.ds(0, hd_half)], hd_keep, out_sem.at[0]),
        pltpu.make_async_copy(s_acc.at[pl.ds(0, s_half)], s_keep, out_sem.at[1]),
        pltpu.make_async_copy(hd_out, hd_send, out_sem.at[2]),
        pltpu.make_async_copy(s_out, s_send, out_sem.at[3]),
    ]
    hd_out[...] = hd_acc[pl.ds(hd_half, hd_half), :].astype(BF16)
    stores[2].start()
    stores[0].start()
    s_out[...] = s_acc[pl.ds(s_half, s_half), :].astype(BF16)
    stores[3].start()
    stores[1].start()
    for store in stores:
        store.wait()


def run_main(shape, ids, counts, hours, pieces):
    grps, devs, local, hour_rows = shape
    depth = devs // 2
    rank = hours.shape[1]
    part = hour_rows // (2 * grps) + depth * (local // grps)
    hd_half, s_half = grps * part, depth * local
    scratch = [
        ((RING,) + counts.shape[1:], BF16),
        ((devs * 2 * local, rank), BF16),
        ((2 * hd_half, rank), F32),
        ((2 * s_half, rank), F32),
        ((hd_half, rank), BF16),
        ((s_half, rank), BF16),
        ((SIDE // 2 * PITCH, 128), F32),
        ((SIDE, 128), F32),
        ((SIDE, 128), F32),
    ]
    need = sum(jnp.dtype(t).itemsize * functools.reduce(lambda x, y: x * y, s) for s, t in scratch)
    need += hours.size * 2 + (10 << 20)
    blocks = counts.shape[0]
    flops = 8 * blocks * SIDE**3 * rank
    return pl.pallas_call(
        functools.partial(main_kernel, shape),
        in_specs=[SMEM, ANY, VMEM] + [ANY] * devs,
        out_specs=[ANY] * 4,
        out_shape=[
            jax.ShapeDtypeStruct((hd_half, rank), F32),
            jax.ShapeDtypeStruct((s_half, rank), F32),
            jax.ShapeDtypeStruct((hd_half, rank), BF16),
            jax.ShapeDtypeStruct((s_half, rank), BF16),
        ],
        scratch_shapes=[pltpu.VMEM(s, t) for s, t in scratch]
        + [
            pltpu.SemaphoreType.DMA((RING,)),
            pltpu.SemaphoreType.DMA((devs,)),
            pltpu.SemaphoreType.DMA((4,)),
        ],
        compiler_params=pltpu.CompilerParams(vmem_limit_bytes=need),
        cost_estimate=pl.CostEstimate(
            flops=flops, bytes_accessed=counts.size * 2, transcendentals=counts.size
        ),
        name="terms",
    )(ids, counts, hours, *pieces)


def split_kernel(ways, keep, got, mine, *sends):
    rows = mine.shape[0]
    mine[...] = keep[pl.ds(0, rows), :] + got[pl.ds(0, rows), :].astype(F32)
    for m in range(1, ways):
        at = pl.ds(m * rows, rows)
        sends[m - 1][...] = (keep[at, :] + got[at, :].astype(F32)).astype(BF16)


def run_split(ways, keep, got, name):
    rows, rank = keep.shape[0] // ways, keep.shape[1]
    return pl.pallas_call(
        functools.partial(split_kernel, ways),
        in_specs=[VMEM, VMEM],
        out_specs=[VMEM] * ways,
        out_shape=[jax.ShapeDtypeStruct((rows, rank), F32)]
        + [jax.ShapeDtypeStruct((rows, rank), BF16)] * (ways - 1),
        compiler_params=pltpu.CompilerParams(vmem_limit_bytes=40 << 20),
        name=name,
    )(keep, got)


def run_grp_sum(hour_part, depth, ids, parts):
    rows, rank = parts[0].shape
    hour_rows = hour_part // depth
    dst_rows = (rows - hour_part) // depth
    ways = len(parts)

    def kernel(ids, *refs):
        ins, outs, total = refs[:ways], refs[ways:-1], refs[-1]
        z = ids[0] >> 1
        acc = ins[0][...]
        for r in ins[1:]:
            acc = acc + r[...].astype(F32)
        total[...] = acc
        for m in range(depth):
            at = pl.multiple_of((z ^ m) * hour_rows, hour_rows)
            kind = F32 if m == 0 else BF16
            outs[m][pl.ds(0, hour_rows), :] = total[pl.ds(at, hour_rows), :].astype(kind)
            low = hour_part + m * dst_rows
            outs[m][pl.ds(hour_rows, dst_rows), :] = total[pl.ds(low, dst_rows), :].astype(kind)

    each = hour_rows + dst_rows
    return pl.pallas_call(
        kernel,
        in_specs=[SMEM] + [VMEM] * ways,
        out_specs=[VMEM] * depth,
        out_shape=[jax.ShapeDtypeStruct((each, rank), F32)]
        + [jax.ShapeDtypeStruct((each, rank), BF16)] * (depth - 1),
        scratch_shapes=[pltpu.VMEM((rows, rank), F32)],
        compiler_params=pltpu.CompilerParams(vmem_limit_bytes=32 << 20),
        name="grp_sum",
    )(ids, *parts)


def run_z_sum(hour_rows, hd_parts, s_parts):
    rank = hd_parts[0].shape[1]
    dst_rows = hd_parts[0].shape[0] - hour_rows
    src_rows = s_parts[0].shape[0]
    n = len(hd_parts)

    def kernel(*refs):
        hd, s, (h_out, d_out, s_out) = refs[:n], refs[n : 2 * n], refs[2 * n :]
        acc = hd[0][...]
        for r in hd[1:]:
            acc = acc + r[...].astype(F32)
        acc = acc * (1.0 / SIDE)
        h_out[...] = acc[:hour_rows].astype(BF16)
        d_out[...] = acc[hour_rows:]
        acc = s[0][...]
        for r in s[1:]:
            acc = acc + r[...].astype(F32)
        s_out[...] = acc * (1.0 / SIDE)

    return pl.pallas_call(
        kernel,
        in_specs=[VMEM] * (2 * n),
        out_specs=[VMEM] * 3,
        out_shape=[
            jax.ShapeDtypeStruct((hour_rows, rank), BF16),
            jax.ShapeDtypeStruct((dst_rows, rank), F32),
            jax.ShapeDtypeStruct((src_rows, rank), F32),
        ],
        compiler_params=pltpu.CompilerParams(vmem_limit_bytes=32 << 20),
        name="z_sum",
    )(*hd_parts, *s_parts)


def run_place(grps, depth, ids, hour_parts, dst_parts):
    part, rank = hour_parts[0].shape
    rows = part // depth
    dst_rows = dst_parts[0].shape[0]
    n = len(hour_parts)

    def kernel(ids, *refs):
        hours, dsts, h_out, d_out = refs[:n], refs[n : n + grps], refs[-2], refs[-1]
        core, z, grp = ids[0] & 1, ids[0] >> 1, ids[1]
        for m in range(n):
            home = ((core ^ (m // grps)) * grps + (grp ^ (m % grps))) * part
            for k in range(depth):
                at = pl.multiple_of(home + (z ^ k) * rows, rows)
                h_out[pl.ds(at, rows), :] = hours[m][pl.ds(k * rows, rows), :].astype(F32)
        for m in range(grps):
            at = pl.multiple_of((grp ^ m) * dst_rows, dst_rows)
            d_out[pl.ds(at, dst_rows), :] = dsts[m][...]

    return pl.pallas_call(
        kernel,
        in_specs=[SMEM] + [VMEM] * (n + grps),
        out_specs=[VMEM] * 2,
        out_shape=[
            jax.ShapeDtypeStruct((n * part, rank), F32),
            jax.ShapeDtypeStruct((grps * dst_rows, rank), F32),
        ],
        compiler_params=pltpu.CompilerParams(vmem_limit_bytes=32 << 20),
        name="place",
    )(ids, *hour_parts, *dst_parts)


def per_device(
    sizes,
    counts,
    src_factor,
    dst_factor,
    hour_factor,
    src_owner,
    src_slot,
    dst_owner,
    dst_slot,
    hour_block,
):
    grps, devs = sizes
    depth = devs // 2
    local = src_factor.shape[0]
    hour_rows = hour_factor.shape[0]
    me = lax.axis_index("dev").astype(jnp.int32)
    grp = lax.axis_index("grp").astype(jnp.int32)
    place = jnp.stack([me, grp] + [me * 0] * 6)
    ids = jnp.concatenate(
        [place, src_owner[:, 0], src_slot, dst_owner[:, 0], dst_slot, hour_block]
    )
    own = jnp.concatenate([src_factor, dst_factor], axis=0)
    along = [own] + [swap(own, "dev", devs, 2 * m) for m in range(1, depth)]
    across = [swap(x, "dev", devs, 1) for x in along]
    pieces = [x for pair in zip(along, across) for x in pair]
    shape = (grps, devs, local, hour_rows)
    hd_keep, s_keep, hd_send, s_send = run_main(shape, ids, counts, hour_factor, pieces)
    hd_got = swap(hd_send, "dev", devs, 1)
    s_got = swap(s_send, "dev", devs, 1)
    hd = run_split(grps, hd_keep, hd_got, "core_hd")
    s = run_split(depth, s_keep, s_got, "core_s")
    hd = [hd[0]] + [swap(x, "grp", grps, m) for m, x in enumerate(hd) if m]
    s = [s[0]] + [swap(x, "dev", devs, 2 * m) for m, x in enumerate(s) if m]
    hour_part = hour_rows // (2 * grps)
    hd = run_grp_sum(hour_part, depth, ids, hd)
    hd = [hd[0]] + [swap(x, "dev", devs, 2 * m) for m, x in enumerate(hd) if m]
    hour, dst, grad_src = run_z_sum(hour_part // depth, hd, s)
    dsts = [dst] + [swap(dst, "grp", grps, m) for m in range(1, grps)]
    hour = jnp.concatenate(
        [hour] + [swap(hour, "dev", devs, 2 * m) for m in range(1, depth)], axis=0
    )
    hours = [hour] + [swap(hour, "grp", grps, m) for m in range(1, grps)]
    hours = hours + [swap(x, "dev", devs, 1) for x in hours]
    grad_hour, grad_dst = run_place(grps, depth, ids, hours, dsts)
    return grad_src, grad_dst, grad_hour


def solution(mesh):
    in_specs = (
        P(("grp", "dev"), None, None),
        P(("grp", "dev"), None),
        P("dev", None),
        P(),
        P(("grp", "dev"), None),
        P(("grp", "dev")),
        P(("grp", "dev"), None),
        P(("grp", "dev")),
        P(("grp", "dev")),
    )
    out_specs = (P(("grp", "dev"), None), P("dev", None), P())
    return jax.shard_map(
        functools.partial(per_device, mesh_sizes(mesh)),
        mesh=mesh,
        in_specs=in_specs,
        out_specs=out_specs,
        check_vma=False,
    )
```

time: 693 us -> 161 us (0.23)
  waiting for transfers between devices: 304 us -> 63.5 us
  matrix products: 155 us -> 0 us
  local copies, waits for them, and re-layouts: 102 us -> 8.82 us
  other arithmetic: 71.9 us -> 0 us
  Pallas kernels: 0 us -> 54.4 us
  loops' own time: 16.5 us -> 0 us
  between operations: 14.2 us -> 0.74 us
  starting transfers between devices: 24.1 us -> 33.2 us
    dot_general x96 -> x0, matrix products: 155 us -> none  [the longest x24 57.3 us: block_terms(): jnp.einsum('ijk,ijr->kr', cube, pair_ab, preferred_element_type=jnp.float32)]
    all_to_all x6 -> x0, waiting for transfers between devices: 152 us -> none  [the longest x1 55.6 us: per_device(): lax.all_to_all(send_src, 'dev', split_axis=0, concat_axis=0, tiled=True)]
    psum x2 -> x0, waiting for transfers between devices: 151 us -> none  [the longest x1 106 us: per_device(): hour_total = lax.psum(hour_acc, ('grp', 'dev'))]
    ppermute x0 -> x31, waiting for transfers between devices: none -> 63.5 us  [swap(): return lax.ppermute(x, axis, [(i, i ^ mask) for i in range(size)])]
    convert_element_type x76 -> x0, other arithmetic: 54.7 us -> none  [the longest x24 18.5 us: block_terms(): wide_c = hour_rows.astype(jnp.float32)]
    pallas_call x0 -> x6, Pallas kernels: none -> 54.4 us  [the longest x1 49.5 us: run_main(): pl.pallas_call(functools.partial(main_kernel, shape), in_specs=[SMEM, ANY...]
    reshape x24 -> x0, local copies, waits for them, and re-layouts: 50.5 us -> none  [block_terms(): cube = resid.reshape(block_side, block_side, block_side)]
    ppermute x0 -> x31, starting transfers between devices: none -> 33.2 us  [swap(): return lax.ppermute(x, axis, [(i, i ^ mask) for i in range(size)])]
  transfers between devices with their start and end apart: 8 -> 31, of which waited for: 8 -> 16; matrix products, arithmetic and copies ran while one was open for 4% -> 1% of each run, Pallas kernels for 0% -> 1%
where the time goes in v1:
time: 161 us
  waiting for transfers between devices  63.5 us (39%)
  Pallas kernels  54.4 us (34%)
  starting transfers between devices  33.2 us (21%)
  local copies, waits for them, and re-layouts  8.82 us (5%)
    ppermute x31, waiting for transfers between devices, swap(): return lax.ppermute(x, axis, [(i, i ^ mask) for i in range(size)])  63.5 us
    pallas_call x1, Pallas kernels, run_main(): pl.pallas_call(functools.partial(main_kernel, shape), in_specs=[SMEM, ANY...  49.5 us
    ppermute x31, starting transfers between devices, swap(): return lax.ppermute(x, axis, [(i, i ^ mask) for i in range(size)])  33.2 us
    unnamed x8, local copies, waits for them, and re-layouts  7.1 us
  transfers between devices with their start and end apart: 31, of which 16 were waited for; matrix products, arithmetic and copies ran while one was open for 1% of the time, Pallas kernels for 1%

profile of v1, /device:TPU:0, one launch (start us, length us, event | category | flops | bytes accessed | tf_op | source)
XLA Modules:
  0.0 160.7 jit_solution(12100602592284454001)
XLA Ops:
  0.6 0.9 constant_dynamic-update-slice_fusion.1
  1.5 0.9 constant_dynamic-update-slice_fusion.refs_0_
  2.5 5.1 %collective-permute-start.5 = (bf16[512,256]{1,0:T(8,128)(2,1)S(1)}, bf16[512,256]{1,0:T(8,128)(2,1)S(1)}, u32[]{:S(2)}, u32[]{:S(2)}) collective-permute-start(bf16[512,256]{1,0:T(8,128)(2,1)S(1)} %constant_dynamic-update-slice_fusion.refs_0_), channel_id=1, source_target_pairs={{0,6},{1,7},{2,4},{3,5},{4,2},{5,3},{6,0},{7,1},{8,14},{9,15},{10,... | collective-permute-start | bytes 786440 | tf_op jit(solution)/shard_map/ppermute | solution.py:26
  8.2 6.6 %collective-permute-done.5.refs_6_ = bf16[512,256]{1,0:T(8,128)(2,1)S(1)} collective-permute-done((bf16[512,256]{1,0:T(8,128)(2,1)S(1)}, bf16[512,256]{1,0:T(8,128)(2,1)S(1)}, u32[]{:S(2)}, u32[]{:S(2)}) %collective-permute-start.5) | collective-permute-done | bytes 262176 | tf_op jit(solution)/shard_map/ppermute | solution.py:26
  14.9 15.0 %collective-permute-done.3.refs_4_ = bf16[512,256]{1,0:T(8,128)(2,1)S(1)} collective-permute-done((bf16[512,256]{1,0:T(8,128)(2,1)S(1)}, bf16[512,256]{1,0:T(8,128)(2,1)S(1)}, u32[]{:S(2)}, u32[]{:S(2)}) %collective-permute-start.3) | collective-permute-done | bytes 262176 | tf_op jit(solution)/shard_map/ppermute | solution.py:26
  31.8 4.6 %copy-done = bf16[24,64,4096]{2,1,0:T(8,128)(2,1)S(1)} copy-done((bf16[24,64,4096]{2,1,0:T(8,128)(2,1)S(1)}, bf16[24,64,4096]{2,1,0:T(8,128)(2,1)}, u32[]{:S(2)}) %copy-start) | copy-done | bytes 12582936
  36.4 1.6 copy-done.1
  38.0 49.5 %terms.1 = (f32[3072,256]{1,0:T(8,128)S(1)}, f32[1024,256]{1,0:T(8,128)S(1)}, bf16[3072,256]{1,0:T(8,128)(2,1)S(1)}, bf16[1024,256]{1,0:T(8,128)(2,1)S(1)}) custom-call(s32[128]{0:T(128)S(1)} %concatenate.9.ids, bf16[24,64,4096]{2,1,0:T(8,128)(2,1)S(1)} %copy-done, bf16[4096,256]{1,0:T(8,128)(2,1)S(1)} %copy-done.1, ...), custom_call_target="tpu_custom_call" | custom-call | flops 12884901888 | bytes 12582912 | tf_op jit(solution)/shard_map/terms/pallas_call | solution.py:188
  88.1 2.9 %collective-permute-done.7.got = bf16[3072,256]{1,0:T(8,128)(2,1)S(1)} collective-permute-done((bf16[3072,256]{1,0:T(8,128)(2,1)S(1)}, bf16[3072,256]{1,0:T(8,128)(2,1)S(1)}, u32[]{:S(2)}, u32[]{:S(2)}) %collective-permute-start.7) | collective-permute-done | bytes 1572896 | tf_op jit(solution)/shard_map/ppermute | solution.py:26
  91.3 1.6 collective-permute-start.8
  92.9 1.5 collective-permute-start.9
  95.0 3.0 %collective-permute-start.16 = (bf16[256,256]{1,0:T(8,128)(2,1)S(1)}, bf16[256,256]{1,0:T(8,128)(2,1)S(1)}, u32[]{:S(2)}, u32[]{:S(2)}) collective-permute-start(bf16[256,256]{1,0:T(8,128)(2,1)S(1)} %get-tuple-element.38), channel_id=1, source_target_pairs={{0,4},{1,5},{2,6},{3,7},{4,0},{5,1},{6,2},{7,3},{8,12},{9,13},{10,... | collective-permute-start | bytes 393224 | tf_op jit(solution)/shard_map/ppermute | solution.py:26
  98.1 5.3 %collective-permute-done.8.refs_1_ = bf16[768,256]{1,0:T(8,128)(2,1)S(1)} collective-permute-done((bf16[768,256]{1,0:T(8,128)(2,1)S(1)}, bf16[768,256]{1,0:T(8,128)(2,1)S(1)}, u32[]{:S(2)}, u32[]{:S(2)}) %collective-permute-start.8) | collective-permute-done | bytes 393248 | tf_op jit(solution)/shard_map/ppermute | solution.py:26
  103.3 2.5 %collective-permute-start.17 = (bf16[256,256]{1,0:T(8,128)(2,1)S(1)}, bf16[256,256]{1,0:T(8,128)(2,1)S(1)}, u32[]{:S(2)}, u32[]{:S(2)}) collective-permute-start(bf16[256,256]{1,0:T(8,128)(2,1)S(1)} %get-tuple-element.39), channel_id=1, source_target_pairs={{0,6},{1,7},{2,4},{3,5},{4,2},{5,3},{6,0},{7,1},{8,14},{9,15},{10,... | collective-permute-start | bytes 393224 | tf_op jit(solution)/shard_map/ppermute | solution.py:26
  105.8 6.4 %collective-permute-done.9.refs_2_ = bf16[768,256]{1,0:T(8,128)(2,1)S(1)} collective-permute-done((bf16[768,256]{1,0:T(8,128)(2,1)S(1)}, bf16[768,256]{1,0:T(8,128)(2,1)S(1)}, u32[]{:S(2)}, u32[]{:S(2)}) %collective-permute-start.9) | collective-permute-done | bytes 393248 | tf_op jit(solution)/shard_map/ppermute | solution.py:26
  113.1 3.0 %collective-permute-start.12 = (bf16[192,256]{1,0:T(8,128)(2,1)S(1)}, bf16[192,256]{1,0:T(8,128)(2,1)S(1)}, u32[]{:S(2)}, u32[]{:S(2)}) collective-permute-start(bf16[192,256]{1,0:T(8,128)(2,1)S(1)} %get-tuple-element.32), channel_id=1, source_target_pairs={{0,4},{1,5},{2,6},{3,7},{4,0},{5,1},{6,2},{7,3},{8,12},{9,13},{10,... | collective-permute-start | bytes 294920 | tf_op jit(solution)/shard_map/ppermute | solution.py:26
  116.1 1.3 collective-permute-start.13
  118.0 5.2 %collective-permute-done.12.refs_2_ = bf16[192,256]{1,0:T(8,128)(2,1)S(1)} collective-permute-done((bf16[192,256]{1,0:T(8,128)(2,1)S(1)}, bf16[192,256]{1,0:T(8,128)(2,1)S(1)}, u32[]{:S(2)}, u32[]{:S(2)}) %collective-permute-start.12) | collective-permute-done | bytes 98336 | tf_op jit(solution)/shard_map/ppermute | solution.py:26
  123.9 2.4 %collective-permute-start.20 = (bf16[128,256]{1,0:T(8,128)(2,1)S(1)}, bf16[128,256]{1,0:T(8,128)(2,1)S(1)}, u32[]{:S(2)}, u32[]{:S(2)}) collective-permute-start(bf16[128,256]{1,0:T(8,128)(2,1)S(1)} %get-tuple-element.41), channel_id=1, source_target_pairs={{0,6},{1,7},{2,4},{3,5},{4,2},{5,3},{6,0},{7,1},{8,14},{9,15},{10,... | collective-permute-start | bytes 196616 | tf_op jit(solution)/shard_map/ppermute | solution.py:26
  127.0 1.3 collective-permute-start.18
  128.3 3.2 %collective-permute-done.18 = bf16[128,256]{1,0:T(8,128)(2,1)S(1)} collective-permute-done((bf16[128,256]{1,0:T(8,128)(2,1)S(1)}, bf16[128,256]{1,0:T(8,128)(2,1)S(1)}, u32[]{:S(2)}, u32[]{:S(2)}) %collective-permute-start.18) | collective-permute-done | bytes 65568 | tf_op jit(solution)/shard_map/ppermute | solution.py:26
  132.3 1.5 collective-permute-start.23
  133.8 1.5 collective-permute-start.22
  135.8 5.0 %collective-permute-done.23.refs_3_ = bf16[512,256]{1,0:T(8,128)(2,1)S(1)} collective-permute-done((bf16[512,256]{1,0:T(8,128)(2,1)S(1)}, bf16[512,256]{1,0:T(8,128)(2,1)S(1)}, u32[]{:S(2)}, u32[]{:S(2)}) %collective-permute-start.23) | collective-permute-done | bytes 262176 | tf_op jit(solution)/shard_map/ppermute | solution.py:26
  140.9 2.7 %collective-permute-done.22.refs_2_ = bf16[512,256]{1,0:T(8,128)(2,1)S(1)} collective-permute-done((bf16[512,256]{1,0:T(8,128)(2,1)S(1)}, bf16[512,256]{1,0:T(8,128)(2,1)S(1)}, u32[]{:S(2)}, u32[]{:S(2)}) %collective-permute-start.22) | collective-permute-done | bytes 262176 | tf_op jit(solution)/shard_map/ppermute | solution.py:26
  144.1 1.4 collective-permute-start.30
  145.5 3.7 %collective-permute-done.30.refs_11_ = f32[64,256]{1,0:T(8,128)S(1)} collective-permute-done((f32[64,256]{1,0:T(8,128)S(1)}, f32[64,256]{1,0:T(8,128)S(1)}, u32[]{:S(2)}, u32[]{:S(2)}) %collective-permute-start.30) | collective-permute-done | bytes 65568 | tf_op jit(solution)/shard_map/ppermute | solution.py:26
  149.2 1.4 collective-permute-start.29
  150.6 2.9 %collective-permute-done.29.refs_10_ = f32[64,256]{1,0:T(8,128)S(1)} collective-permute-done((f32[64,256]{1,0:T(8,128)S(1)}, f32[64,256]{1,0:T(8,128)S(1)}, u32[]{:S(2)}, u32[]{:S(2)}) %collective-permute-start.29) | collective-permute-done | bytes 65568 | tf_op jit(solution)/shard_map/ppermute | solution.py:26
  153.5 1.5 collective-permute-start.28
  155.0 2.8 %collective-permute-done.28.refs_9_ = f32[64,256]{1,0:T(8,128)S(1)} collective-permute-done((f32[64,256]{1,0:T(8,128)S(1)}, f32[64,256]{1,0:T(8,128)S(1)}, u32[]{:S(2)}, u32[]{:S(2)}) %collective-permute-start.28) | collective-permute-done | bytes 65568 | tf_op jit(solution)/shard_map/ppermute | solution.py:26
  157.8 2.9 %place.1 = (f32[4096,256]{1,0:T(8,128)}, f32[256,256]{1,0:T(8,128)}) custom-call(s32[128]{0:T(128)S(1)} %concatenate.9.ids, bf16[512,256]{1,0:T(8,128)(2,1)S(1)} %constant_dynamic-update-slice_fusion.2.refs_0_, bf16[512,256]{1,0:T(8,128)(2,1)S(1)} %collective-permute-done.21.refs_1_, bf16[512,256]{1,0:T(8,128)(2,1)S(1)} %collective-permute-done.22.refs_2_, ...), custom_call_target="tpu_custom_call" | custom-call | tf_op jit(solution)/shard_map/place/pallas_call | solution.py:317
  (49 shorter events, 8.8 us)
Async XLA Ops:
  2.5 12.4 %collective-permute-start.5 = (bf16[512,256]{1,0:T(8,128)(2,1)S(1)}, bf16[512,256]{1,0:T(8,128)(2,1)S(1)}, u32[]{:S(2)}, u32[]{:S(2)}) collective-permute-start(bf16[512,256]{1,0:T(8,128)(2,1)S(1)} %constant_dynamic-update-slice_fusion.refs_0_), channel_id=1, source_target_pairs={{0,6},{1,7},{2,4},{3,5},{4,2},{5,3},{6,0},{7,1},{8,14},{9,15},{10,... | collective-permute-start | bytes 786440 | tf_op jit(solution)/shard_map/ppermute | solution.py:26
  7.6 22.3 %collective-permute-start.3 = (bf16[512,256]{1,0:T(8,128)(2,1)S(1)}, bf16[512,256]{1,0:T(8,128)(2,1)S(1)}, u32[]{:S(2)}, u32[]{:S(2)}) collective-permute-start(bf16[512,256]{1,0:T(8,128)(2,1)S(1)} %constant_dynamic-update-slice_fusion.refs_0_), channel_id=1, source_target_pairs={{0,4},{1,5},{2,6},{3,7},{4,0},{5,1},{6,2},{7,3},{8,12},{9,13},{10,... | collective-permute-start | bytes 786440 | tf_op jit(solution)/shard_map/ppermute | solution.py:26
  7.6 22.3 %collective-permute-start.1 = (bf16[512,256]{1,0:T(8,128)(2,1)S(1)}, bf16[512,256]{1,0:T(8,128)(2,1)S(1)}, u32[]{:S(2)}, u32[]{:S(2)}) collective-permute-start(bf16[512,256]{1,0:T(8,128)(2,1)S(1)} %constant_dynamic-update-slice_fusion.refs_0_), channel_id=1, source_target_pairs={{0,2},{1,3},{2,0},{3,1},{4,6},{5,7},{6,4},{7,5},{8,10},{9,11},{10,... | collective-permute-start | bytes 786440 | tf_op jit(solution)/shard_map/ppermute | solution.py:26
  8.2 23.0 %collective-permute-start = (bf16[512,256]{1,0:T(8,128)(2,1)S(1)}, bf16[512,256]{1,0:T(8,128)(2,1)S(1)}, u32[]{:S(2)}, u32[]{:S(2)}) collective-permute-start(bf16[512,256]{1,0:T(8,128)(2,1)S(1)} %constant_dynamic-update-slice_fusion.refs_0_), channel_id=1, source_target_pairs={{0,1},{1,0},{2,3},{3,2},{4,5},{5,4},{6,7},{7,6},{8,9},{9,8},{10,11... | collective-permute-start | bytes 786440 | tf_op jit(solution)/shard_map/ppermute | solution.py:26
  14.9 16.4 %collective-permute-start.6 = (bf16[512,256]{1,0:T(8,128)(2,1)S(1)}, bf16[512,256]{1,0:T(8,128)(2,1)S(1)}, u32[]{:S(2)}, u32[]{:S(2)}) collective-permute-start(bf16[512,256]{1,0:T(8,128)(2,1)S(1)} %collective-permute-done.5.refs_6_), channel_id=1, source_target_pairs={{0,1},{1,0},{2,3},{3,2},{4,5},{5,4},{6,7},{7,6},{8,9},{9,8},{10,11... | collective-permute-start | bytes 786440 | tf_op jit(solution)/shard_map/ppermute | solution.py:26
  29.9 1.5 collective-permute-start.4
  29.9 1.9 %collective-permute-start.2 = (bf16[512,256]{1,0:T(8,128)(2,1)S(1)}, bf16[512,256]{1,0:T(8,128)(2,1)S(1)}, u32[]{:S(2)}, u32[]{:S(2)}) collective-permute-start(bf16[512,256]{1,0:T(8,128)(2,1)S(1)} %collective-permute-done.1.refs_2_), channel_id=1, source_target_pairs={{0,1},{1,0},{2,3},{3,2},{4,5},{5,4},{6,7},{7,6},{8,9},{9,8},{10,11... | collective-permute-start | bytes 786440 | tf_op jit(solution)/shard_map/ppermute | solution.py:26
  31.8 4.6 %copy-start = (bf16[24,64,4096]{2,1,0:T(8,128)(2,1)S(1)}, bf16[24,64,4096]{2,1,0:T(8,128)(2,1)}, u32[]{:S(2)}) copy-start(bf16[24,64,4096]{2,1,0:T(8,128)(2,1)} %counts.1) | copy-start | bytes 37748740
  87.5 3.5 %collective-permute-start.7 = (bf16[3072,256]{1,0:T(8,128)(2,1)S(1)}, bf16[3072,256]{1,0:T(8,128)(2,1)S(1)}, u32[]{:S(2)}, u32[]{:S(2)}) collective-permute-start(bf16[3072,256]{1,0:T(8,128)(2,1)S(1)} %get-tuple-element.25), channel_id=1, source_target_pairs={{0,1},{1,0},{2,3},{3,2},{4,5},{5,4},{6,7},{7,6},{8,9},{9,8},{10,11... | collective-permute-start | bytes 4718600 | tf_op jit(solution)/shard_map/ppermute | solution.py:26
  87.7 7.2 %collective-permute-start.14 = (bf16[1024,256]{1,0:T(8,128)(2,1)S(1)}, bf16[1024,256]{1,0:T(8,128)(2,1)S(1)}, u32[]{:S(2)}, u32[]{:S(2)}) collective-permute-start(bf16[1024,256]{1,0:T(8,128)(2,1)S(1)} %get-tuple-element.35), channel_id=1, source_target_pairs={{0,1},{1,0},{2,3},{3,2},{4,5},{5,4},{6,7},{7,6},{8,9},{9,8},{10,11... | collective-permute-start | bytes 1572872 | tf_op jit(solution)/shard_map/ppermute | solution.py:26
  91.3 12.0 %collective-permute-start.8 = (bf16[768,256]{1,0:T(8,128)(2,1)S(1)}, bf16[768,256]{1,0:T(8,128)(2,1)S(1)}, u32[]{:S(2)}, u32[]{:S(2)}) collective-permute-start(bf16[768,256]{1,0:T(8,128)(2,1)S(1)} %get-tuple-element.27), channel_id=1, source_target_pairs={{0,8},{8,0},{16,24},{24,16},{1,9},{9,1},{17,25},{25,17},{2,10},{10... | collective-permute-start | bytes 1179656 | tf_op jit(solution)/shard_map/ppermute | solution.py:26
  92.9 19.3 %collective-permute-start.9 = (bf16[768,256]{1,0:T(8,128)(2,1)S(1)}, bf16[768,256]{1,0:T(8,128)(2,1)S(1)}, u32[]{:S(2)}, u32[]{:S(2)}) collective-permute-start(bf16[768,256]{1,0:T(8,128)(2,1)S(1)} %get-tuple-element.28), channel_id=1, source_target_pairs={{0,16},{8,24},{16,0},{24,8},{1,17},{9,25},{17,1},{25,9},{2,18},{10... | collective-permute-start | bytes 1179656 | tf_op jit(solution)/shard_map/ppermute | solution.py:26
  94.4 17.8 %collective-permute-start.10 = (bf16[768,256]{1,0:T(8,128)(2,1)S(1)}, bf16[768,256]{1,0:T(8,128)(2,1)S(1)}, u32[]{:S(2)}, u32[]{:S(2)}) collective-permute-start(bf16[768,256]{1,0:T(8,128)(2,1)S(1)} %get-tuple-element.29), channel_id=1, source_target_pairs={{0,24},{8,16},{16,8},{24,0},{1,25},{9,17},{17,9},{25,1},{2,26},{10... | collective-permute-start | bytes 1179656 | tf_op jit(solution)/shard_map/ppermute | solution.py:26
  95.0 21.2 %collective-permute-start.15 = (bf16[256,256]{1,0:T(8,128)(2,1)S(1)}, bf16[256,256]{1,0:T(8,128)(2,1)S(1)}, u32[]{:S(2)}, u32[]{:S(2)}) collective-permute-start(bf16[256,256]{1,0:T(8,128)(2,1)S(1)} %get-tuple-element.37), channel_id=1, source_target_pairs={{0,2},{1,3},{2,0},{3,1},{4,6},{5,7},{6,4},{7,5},{8,10},{9,11},{10,... | collective-permute-start | bytes 393224 | tf_op jit(solution)/shard_map/ppermute | solution.py:26
  95.0 22.4 %collective-permute-start.16 = (bf16[256,256]{1,0:T(8,128)(2,1)S(1)}, bf16[256,256]{1,0:T(8,128)(2,1)S(1)}, u32[]{:S(2)}, u32[]{:S(2)}) collective-permute-start(bf16[256,256]{1,0:T(8,128)(2,1)S(1)} %get-tuple-element.38), channel_id=1, source_target_pairs={{0,4},{1,5},{2,6},{3,7},{4,0},{5,1},{6,2},{7,3},{8,12},{9,13},{10,... | collective-permute-start | bytes 393224 | tf_op jit(solution)/shard_map/ppermute | solution.py:26
  103.3 14.1 %collective-permute-start.17 = (bf16[256,256]{1,0:T(8,128)(2,1)S(1)}, bf16[256,256]{1,0:T(8,128)(2,1)S(1)}, u32[]{:S(2)}, u32[]{:S(2)}) collective-permute-start(bf16[256,256]{1,0:T(8,128)(2,1)S(1)} %get-tuple-element.39), channel_id=1, source_target_pairs={{0,6},{1,7},{2,4},{3,5},{4,2},{5,3},{6,0},{7,1},{8,14},{9,15},{10,... | collective-permute-start | bytes 393224 | tf_op jit(solution)/shard_map/ppermute | solution.py:26
  113.0 5.0 %collective-permute-start.11 = (bf16[192,256]{1,0:T(8,128)(2,1)S(1)}, bf16[192,256]{1,0:T(8,128)(2,1)S(1)}, u32[]{:S(2)}, u32[]{:S(2)}) collective-permute-start(bf16[192,256]{1,0:T(8,128)(2,1)S(1)} %get-tuple-element.31), channel_id=1, source_target_pairs={{0,2},{1,3},{2,0},{3,1},{4,6},{5,7},{6,4},{7,5},{8,10},{9,11},{10,... | collective-permute-start | bytes 294920 | tf_op jit(solution)/shard_map/ppermute | solution.py:26
  113.1 10.1 %collective-permute-start.12 = (bf16[192,256]{1,0:T(8,128)(2,1)S(1)}, bf16[192,256]{1,0:T(8,128)(2,1)S(1)}, u32[]{:S(2)}, u32[]{:S(2)}) collective-permute-start(bf16[192,256]{1,0:T(8,128)(2,1)S(1)} %get-tuple-element.32), channel_id=1, source_target_pairs={{0,4},{1,5},{2,6},{3,7},{4,0},{5,1},{6,2},{7,3},{8,12},{9,13},{10,... | collective-permute-start | bytes 294920 | tf_op jit(solution)/shard_map/ppermute | solution.py:26
  116.1 7.0 %collective-permute-start.13 = (bf16[192,256]{1,0:T(8,128)(2,1)S(1)}, bf16[192,256]{1,0:T(8,128)(2,1)S(1)}, u32[]{:S(2)}, u32[]{:S(2)}) collective-permute-start(bf16[192,256]{1,0:T(8,128)(2,1)S(1)} %get-tuple-element.33), channel_id=1, source_target_pairs={{0,6},{1,7},{2,4},{3,5},{4,2},{5,3},{6,0},{7,1},{8,14},{9,15},{10,... | collective-permute-start | bytes 294920 | tf_op jit(solution)/shard_map/ppermute | solution.py:26
  123.9 8.3 %collective-permute-start.20 = (bf16[128,256]{1,0:T(8,128)(2,1)S(1)}, bf16[128,256]{1,0:T(8,128)(2,1)S(1)}, u32[]{:S(2)}, u32[]{:S(2)}) collective-permute-start(bf16[128,256]{1,0:T(8,128)(2,1)S(1)} %get-tuple-element.41), channel_id=1, source_target_pairs={{0,6},{1,7},{2,4},{3,5},{4,2},{5,3},{6,0},{7,1},{8,14},{9,15},{10,... | collective-permute-start | bytes 196616 | tf_op jit(solution)/shard_map/ppermute | solution.py:26
  126.4 5.9 %collective-permute-start.19 = (bf16[128,256]{1,0:T(8,128)(2,1)S(1)}, bf16[128,256]{1,0:T(8,128)(2,1)S(1)}, u32[]{:S(2)}, u32[]{:S(2)}) collective-permute-start(bf16[128,256]{1,0:T(8,128)(2,1)S(1)} %get-tuple-element.41), channel_id=1, source_target_pairs={{0,4},{1,5},{2,6},{3,7},{4,0},{5,1},{6,2},{7,3},{8,12},{9,13},{10,... | collective-permute-start | bytes 196616 | tf_op jit(solution)/shard_map/ppermute | solution.py:26
  127.0 4.5 %collective-permute-start.18 = (bf16[128,256]{1,0:T(8,128)(2,1)S(1)}, bf16[128,256]{1,0:T(8,128)(2,1)S(1)}, u32[]{:S(2)}, u32[]{:S(2)}) collective-permute-start(bf16[128,256]{1,0:T(8,128)(2,1)S(1)} %get-tuple-element.41), channel_id=1, source_target_pairs={{0,2},{1,3},{2,0},{3,1},{4,6},{5,7},{6,4},{7,5},{8,10},{9,11},{10,... | collective-permute-start | bytes 196616 | tf_op jit(solution)/shard_map/ppermute | solution.py:26
  132.3 8.6 %collective-permute-start.23 = (bf16[512,256]{1,0:T(8,128)(2,1)S(1)}, bf16[512,256]{1,0:T(8,128)(2,1)S(1)}, u32[]{:S(2)}, u32[]{:S(2)}) collective-permute-start(bf16[512,256]{1,0:T(8,128)(2,1)S(1)} %constant_dynamic-update-slice_fusion.2.refs_0_), channel_id=1, source_target_pairs={{0,24},{8,16},{16,8},{24,0},{1,25},{9,17},{17,9},{25,1},{2,26},{10... | collective-permute-start | bytes 786440 | tf_op jit(solution)/shard_map/ppermute | solution.py:26
  133.8 9.8 %collective-permute-start.22 = (bf16[512,256]{1,0:T(8,128)(2,1)S(1)}, bf16[512,256]{1,0:T(8,128)(2,1)S(1)}, u32[]{:S(2)}, u32[]{:S(2)}) collective-permute-start(bf16[512,256]{1,0:T(8,128)(2,1)S(1)} %constant_dynamic-update-slice_fusion.2.refs_0_), channel_id=1, source_target_pairs={{0,16},{8,24},{16,0},{24,8},{1,17},{9,25},{17,1},{25,9},{2,18},{10... | collective-permute-start | bytes 786440 | tf_op jit(solution)/shard_map/ppermute | solution.py:26
  135.3 8.3 %collective-permute-start.21 = (bf16[512,256]{1,0:T(8,128)(2,1)S(1)}, bf16[512,256]{1,0:T(8,128)(2,1)S(1)}, u32[]{:S(2)}, u32[]{:S(2)}) collective-permute-start(bf16[512,256]{1,0:T(8,128)(2,1)S(1)} %constant_dynamic-update-slice_fusion.2.refs_0_), channel_id=1, source_target_pairs={{0,8},{8,0},{16,24},{24,16},{1,9},{9,1},{17,25},{25,17},{2,10},{10... | collective-permute-start | bytes 786440 | tf_op jit(solution)/shard_map/ppermute | solution.py:26
  135.8 21.9 %collective-permute-start.24 = (bf16[512,256]{1,0:T(8,128)(2,1)S(1)}, bf16[512,256]{1,0:T(8,128)(2,1)S(1)}, u32[]{:S(2)}, u32[]{:S(2)}) collective-permute-start(bf16[512,256]{1,0:T(8,128)(2,1)S(1)} %constant_dynamic-update-slice_fusion.2.refs_0_), channel_id=1, source_target_pairs={{0,1},{1,0},{2,3},{3,2},{4,5},{5,4},{6,7},{7,6},{8,9},{9,8},{10,11... | collective-permute-start | bytes 786440 | tf_op jit(solution)/shard_map/ppermute | solution.py:26
  140.9 16.9 %collective-permute-start.27 = (bf16[512,256]{1,0:T(8,128)(2,1)S(1)}, bf16[512,256]{1,0:T(8,128)(2,1)S(1)}, u32[]{:S(2)}, u32[]{:S(2)}) collective-permute-start(bf16[512,256]{1,0:T(8,128)(2,1)S(1)} %collective-permute-done.23.refs_3_), channel_id=1, source_target_pairs={{0,1},{1,0},{2,3},{3,2},{4,5},{5,4},{6,7},{7,6},{8,9},{9,8},{10,11... | collective-permute-start | bytes 786440 | tf_op jit(solution)/shard_map/ppermute | solution.py:26
  143.5 14.2 %collective-permute-start.26 = (bf16[512,256]{1,0:T(8,128)(2,1)S(1)}, bf16[512,256]{1,0:T(8,128)(2,1)S(1)}, u32[]{:S(2)}, u32[]{:S(2)}) collective-permute-start(bf16[512,256]{1,0:T(8,128)(2,1)S(1)} %collective-permute-done.22.refs_2_), channel_id=1, source_target_pairs={{0,1},{1,0},{2,3},{3,2},{4,5},{5,4},{6,7},{7,6},{8,9},{9,8},{10,11... | collective-permute-start | bytes 786440 | tf_op jit(solution)/shard_map/ppermute | solution.py:26
  143.6 14.2 %collective-permute-start.25 = (bf16[512,256]{1,0:T(8,128)(2,1)S(1)}, bf16[512,256]{1,0:T(8,128)(2,1)S(1)}, u32[]{:S(2)}, u32[]{:S(2)}) collective-permute-start(bf16[512,256]{1,0:T(8,128)(2,1)S(1)} %collective-permute-done.21.refs_1_), channel_id=1, source_target_pairs={{0,1},{1,0},{2,3},{3,2},{4,5},{5,4},{6,7},{7,6},{8,9},{9,8},{10,11... | collective-permute-start | bytes 786440 | tf_op jit(solution)/shard_map/ppermute | solution.py:26
  144.1 5.2 %collective-permute-start.30 = (f32[64,256]{1,0:T(8,128)S(1)}, f32[64,256]{1,0:T(8,128)S(1)}, u32[]{:S(2)}, u32[]{:S(2)}) collective-permute-start(f32[64,256]{1,0:T(8,128)S(1)} %get-tuple-element.42.refs_8_), channel_id=1, source_target_pairs={{0,24},{8,16},{16,8},{24,0},{1,25},{9,17},{17,9},{25,1},{2,26},{10... | collective-permute-start | bytes 196616 | tf_op jit(solution)/shard_map/ppermute | solution.py:26
  149.2 4.3 %collective-permute-start.29 = (f32[64,256]{1,0:T(8,128)S(1)}, f32[64,256]{1,0:T(8,128)S(1)}, u32[]{:S(2)}, u32[]{:S(2)}) collective-permute-start(f32[64,256]{1,0:T(8,128)S(1)} %get-tuple-element.42.refs_8_), channel_id=1, source_target_pairs={{0,16},{8,24},{16,0},{24,8},{1,17},{9,25},{17,1},{25,9},{2,18},{10... | collective-permute-start | bytes 196616 | tf_op jit(solution)/shard_map/ppermute | solution.py:26
  153.5 4.3 %collective-permute-start.28 = (f32[64,256]{1,0:T(8,128)S(1)}, f32[64,256]{1,0:T(8,128)S(1)}, u32[]{:S(2)}, u32[]{:S(2)}) collective-permute-start(f32[64,256]{1,0:T(8,128)S(1)} %get-tuple-element.42.refs_8_), channel_id=1, source_target_pairs={{0,8},{8,0},{16,24},{24,16},{1,9},{9,1},{17,25},{25,17},{2,10},{10... | collective-permute-start | bytes 196616 | tf_op jit(solution)/shard_map/ppermute | solution.py:26
  (1 other events, 1.6 us)

commit v2 on v1

v2 whole, which is shorter than its diff:
```python
import functools

import jax
import jax.numpy as jnp
from jax import lax
from jax.experimental import pallas as pl
from jax.experimental.pallas import tpu as pltpu
from jax.sharding import PartitionSpec as P

F32 = jnp.float32
BF16 = jnp.bfloat16
SIDE = 64
RING = 8
PITCH = 72
GRANT = 36 << 20

VMEM = pl.BlockSpec(memory_space=pltpu.VMEM)
SMEM = pl.BlockSpec(memory_space=pltpu.SMEM)
ANY = pl.BlockSpec(memory_space=pl.ANY)
HBM = pl.BlockSpec(memory_space=pltpu.HBM)


def mesh_sizes(mesh):
    return mesh.shape["grp"], mesh.shape["dev"]


def swap(x, axis, size, mask):
    return lax.ppermute(x, axis, [(i, i ^ mask) for i in range(size)])


def block_terms(count, a, b, c, cube, even, odd):
    rank = a.shape[1]
    resids, pairs_bc, turned, pairs_ab = [], [], [], []
    for g in range(SIDE // 4):
        b4 = b[g * 4 : g * 4 + 4]
        bc = (b4[:, None, :] * c[None, :, :]).reshape(4 * SIDE, rank)
        ab = (b4[:, None, :] * a[None, :, :]).reshape(4 * SIDE, rank)
        theta = lax.dot_general(a, bc, (((1,), (1,)), ((), ())), preferred_element_type=F32)
        wide = jnp.exp(theta) - count[:, g * 256 : (g + 1) * 256].astype(F32)
        for p in range(2):
            cube[pl.ds((g * 2 + p) * PITCH, SIDE), :] = wide[:, p * 128 : (p + 1) * 128]
        resid = wide.astype(BF16)
        flip = resid.T
        turned += [flip[q * SIDE : (q + 1) * SIDE] for q in range(4)]
        resids.append(resid)
        pairs_bc.append(bc)
        pairs_ab.append(ab)
    term_a = jnp.dot(
        jnp.concatenate(resids, axis=1),
        jnp.concatenate(pairs_bc, axis=0),
        preferred_element_type=F32,
    )
    term_c = jnp.dot(
        jnp.concatenate(turned, axis=1),
        jnp.concatenate(pairs_ab, axis=0),
        preferred_element_type=F32,
    )
    low = lax.broadcasted_iota(jnp.int32, (SIDE // 2, 128), 1) < SIDE
    rows, pairs_ac = [], []
    for g in range(SIDE // 4):
        x = [cube[pl.ds(g * 4 + q, SIDE // 2, stride=PITCH), :] for q in range(4)]
        y = [pltpu.roll(v, SIDE, 1) for v in x]
        evens = [jnp.where(low, x[0], y[1]), jnp.where(low, x[2], y[3])]
        odds = [jnp.where(low, y[0], x[1]), jnp.where(low, y[2], x[3])]
        both = [jnp.concatenate(evens, axis=1), jnp.concatenate(odds, axis=1)]
        rows.append(jnp.concatenate(both, axis=0).astype(BF16))
        pairs_ac.append((a[g * 4 : g * 4 + 4][:, None, :] * c[None, :, :]).reshape(4 * SIDE, rank))
    mixed = jnp.dot(
        jnp.concatenate(rows, axis=1),
        jnp.concatenate(pairs_ac, axis=0),
        preferred_element_type=F32,
    )
    half = SIDE // 2
    for u in range(2):
        even[pl.ds(u, half, stride=2), :] = mixed[u * half : (u + 1) * half, :128]
        odd[pl.ds(u, half, stride=2), :] = mixed[u * half : (u + 1) * half, 128:]
    term_b = jnp.concatenate([even[...], odd[...]], axis=1)
    return term_a, term_b, term_c


def run_pick(blocks, ids, hours, own):
    rank = hours.shape[1]

    def kernel(ids, hours, own, out, same, sem):
        copies = []
        for t in range(blocks):
            at = pl.multiple_of(ids[8 + 4 * blocks + t] * SIDE, SIDE)
            copies.append(
                pltpu.make_async_copy(
                    hours.at[pl.ds(at, SIDE)], out.at[pl.ds(t * SIDE, SIDE)], sem.at[t]
                )
            )
            copies[-1].start()
        same[...] = own[...]
        for copy in copies:
            copy.wait()

    return pl.pallas_call(
        kernel,
        in_specs=[SMEM, HBM, VMEM],
        out_specs=[VMEM, VMEM],
        out_shape=[
            jax.ShapeDtypeStruct((blocks * SIDE, rank), BF16),
            jax.ShapeDtypeStruct(own.shape, BF16),
        ],
        scratch_shapes=[pltpu.SemaphoreType.DMA((blocks,))],
        name="pick_hours",
    )(ids, hours, own)


def main_kernel(shape, ids, counts, hours, *refs):
    grps, devs, local, hour_rows = shape
    depth = devs // 2
    pieces = refs[:devs]
    h_acc, sd_acc, h_send, sd_send = refs[devs : devs + 4]
    ring, table, cube, even, odd, ring_sem, in_sem = refs[devs + 4 :]
    blocks = counts.shape[0]
    hour_part = hour_rows // (2 * grps)
    hour_blocks = hour_part // SIDE
    dst_part = local // grps
    sd_half = 2 * depth * local
    base = 8

    def fetch(t):
        slot = lax.rem(t, RING)
        return pltpu.make_async_copy(counts.at[t], ring.at[slot], ring_sem.at[slot])

    for t in range(min(RING, blocks)):
        fetch(t).start()
    loads = [
        pltpu.make_async_copy(pieces[m], table.at[pl.ds(m * 2 * local, 2 * local)], in_sem.at[m])
        for m in range(devs)
    ]
    for load in loads:
        load.start()
    h_acc[...] = jnp.zeros_like(h_acc)
    sd_acc[...] = jnp.zeros_like(sd_acc)
    for load in loads:
        load.wait()
    me, grp = ids[0], ids[1]
    core = me & 1

    def visit(t, carry):
        src_from = ids[base + t] ^ me
        src_slot = ids[base + blocks + t]
        dst_from = ids[base + 2 * blocks + t] ^ me
        dst_slot = ids[base + 3 * blocks + t]
        hour = ids[base + 4 * blocks + t]
        fetch(t).wait()
        slot = lax.rem(t, RING)
        a_at = pl.multiple_of(src_from * (2 * local) + src_slot * SIDE, SIDE)
        b_at = pl.multiple_of(dst_from * (2 * local) + local + dst_slot * SIDE, SIDE)
        term_a, term_b, term_c = block_terms(
            ring.at[slot],
            table[pl.ds(a_at, SIDE), :],
            table[pl.ds(b_at, SIDE), :],
            hours[pl.ds(pl.multiple_of(t * SIDE, SIDE), SIDE), :],
            cube,
            even,
            odd,
        )
        s_at = (src_from & 1) * sd_half + depth * local
        s_at = s_at + (src_from >> 1) * local + src_slot * SIDE
        row = dst_slot * SIDE
        d_at = (dst_from & 1) * sd_half + ((row // dst_part) ^ grp) * (depth * dst_part)
        d_at = d_at + (dst_from >> 1) * dst_part + row % dst_part
        home = hour // hour_blocks
        h_at = (((home // grps) ^ core) * grps + ((home % grps) ^ grp)) * hour_part
        h_at = h_at + (hour % hour_blocks) * SIDE
        sd_acc[pl.ds(pl.multiple_of(s_at, SIDE), SIDE), :] += term_a
        sd_acc[pl.ds(pl.multiple_of(d_at, SIDE), SIDE), :] += term_b
        h_acc[pl.ds(pl.multiple_of(h_at, SIDE), SIDE), :] += term_c

        @pl.when(t + RING < blocks)
        def _():
            fetch(t + RING).start()

        return carry

    lax.fori_loop(0, blocks, visit, 0)
    h_send[...] = h_acc[pl.ds(hour_rows // 2, hour_rows // 2), :].astype(BF16)
    sd_send[...] = sd_acc[pl.ds(sd_half, sd_half), :].astype(BF16)


def size_of(shapes):
    return sum(jnp.dtype(t).itemsize * functools.reduce(lambda x, y: x * y, s) for s, t in shapes)


def run_main(shape, ids, counts, hours, pieces):
    grps, devs, local, hour_rows = shape
    rank = hours.shape[1]
    outs = [
        ((hour_rows, rank), F32),
        ((2 * devs * local, rank), F32),
        ((hour_rows // 2, rank), BF16),
        ((devs * local, rank), BF16),
    ]
    scratch = [
        ((RING,) + counts.shape[1:], BF16),
        ((devs * 2 * local, rank), BF16),
        ((SIDE // 2 * PITCH, 128), F32),
        ((SIDE, 128), F32),
        ((SIDE, 128), F32),
    ]
    need = max(size_of(outs) + size_of(scratch) + (8 << 20), GRANT)
    return pl.pallas_call(
        functools.partial(main_kernel, shape),
        in_specs=[SMEM, HBM, VMEM] + [ANY] * devs,
        out_specs=[VMEM] * 4,
        out_shape=[jax.ShapeDtypeStruct(s, t) for s, t in outs],
        scratch_shapes=[pltpu.VMEM(s, t) for s, t in scratch]
        + [
            pltpu.SemaphoreType.DMA((RING,)),
            pltpu.SemaphoreType.DMA((devs,)),
        ],
        compiler_params=pltpu.CompilerParams(vmem_limit_bytes=need),
        cost_estimate=pl.CostEstimate(
            flops=8 * counts.size * rank,
            bytes_accessed=counts.size * 2,
            transcendentals=counts.size,
        ),
        name="terms",
    )(ids, counts, hours, *pieces)


def call(kernel, name, ins, outs, specs=None, scratch=()):
    shapes = [(x.shape, x.dtype) for x in ins] + list(outs) + list(scratch)
    return pl.pallas_call(
        kernel,
        in_specs=specs or [VMEM] * len(ins),
        out_specs=[VMEM] * len(outs),
        out_shape=[jax.ShapeDtypeStruct(s, t) for s, t in outs],
        scratch_shapes=[pltpu.VMEM(s, t) for s, t in scratch],
        compiler_params=pltpu.CompilerParams(vmem_limit_bytes=size_of(shapes) + (4 << 20)),
        name=name,
    )(*ins)


def cut(acc, got, start, rows, ways, outs):
    for m in range(ways):
        at = pl.ds(start + m * rows, rows)
        outs[m][...] = (acc[at, :] + got[at, :].astype(F32)).astype(outs[m].dtype)


def shares(rows, rank, ways):
    return [((rows, rank), F32)] + [((rows, rank), BF16)] * (ways - 1)


def run_cut_hours(grps, acc, got):
    rows, rank = got.shape[0] // grps, got.shape[1]

    def kernel(acc, got, *outs):
        cut(acc, got, 0, rows, grps, outs)

    return call(kernel, "core_hours", (acc, got), shares(rows, rank, grps))


def run_cut_src(depth, local, acc, got):
    rank = got.shape[1]

    def kernel(acc, got, *outs):
        cut(acc, got, depth * local, local, depth, outs)

    return call(kernel, "core_src", (acc, got), shares(local, rank, depth))


def run_cut_dst(grps, depth, local, acc, got, after):
    rank = got.shape[1]
    rows = depth * local // grps

    def kernel(acc, got, after, *outs):
        cut(acc, got, 0, rows, grps, outs)

    return call(
        kernel,
        "core_dst",
        (acc, got, after),
        shares(rows, rank, grps),
        specs=[VMEM, VMEM, ANY],
    )


def total(refs):
    acc = refs[0][...]
    for r in refs[1:]:
        acc = acc + r[...].astype(F32)
    return acc


def run_grp_hours(depth, ids, parts):
    rows, rank = parts[0].shape
    ways, each = len(parts), rows // depth

    def kernel(ids, *refs):
        outs, acc = refs[ways:-1], refs[-1]
        z = ids[0] >> 1
        acc[...] = total(refs[:ways])
        for m in range(depth):
            at = pl.multiple_of((z ^ m) * each, each)
            outs[m][...] = acc[pl.ds(at, each), :].astype(outs[m].dtype)

    return call(
        kernel,
        "grp_hours",
        (ids, *parts),
        shares(each, rank, depth),
        specs=[SMEM] + [VMEM] * ways,
        scratch=[((rows, rank), F32)],
    )


def run_grp_dst(depth, parts):
    rows, rank = parts[0].shape
    ways, each = len(parts), rows // depth

    def kernel(*refs):
        acc = total(refs[:ways])
        for m in range(depth):
            out = refs[ways + m]
            out[...] = acc[m * each : (m + 1) * each].astype(out.dtype)

    return call(kernel, "grp_dst", parts, shares(each, rank, depth))


def run_z(parts, kind, name):
    def kernel(*refs):
        refs[-1][...] = (total(refs[:-1]) * (1.0 / SIDE)).astype(kind)

    return call(kernel, name, parts, [(parts[0].shape, kind)])[0]


def run_join(parts):
    rows = [p.shape[0] for p in parts]

    def kernel(*refs):
        at = 0
        for ref, n in zip(refs[:-1], rows):
            refs[-1][at : at + n, :] = ref[...]
            at += n

    return call(kernel, "join", parts, [((sum(rows), parts[0].shape[1]), BF16)])[0]


def run_place(sizes, hour_rows, dst_rows, far, ids, parts, so_far):
    grps, devs = sizes
    depth = devs // 2
    rank = parts[0].shape[1]
    part = hour_rows // (2 * grps)
    rows = part // depth

    def kernel(ids, *refs):
        ins = refs[:grps]
        if far:
            h_out, stage, sem = refs[grps + 1 :]
        else:
            h_out, d_out, stage, sem = refs[grps:]
        core, z, grp = (ids[0] & 1) ^ far, ids[0] >> 1, ids[1]
        copies = []
        for m in range(grps):
            for k in range(depth):
                at = pl.multiple_of((z ^ k) * rows, rows)
                stage[m, pl.ds(at, rows), :] = ins[m][pl.ds(k * rows, rows), :].astype(F32)
            home = pl.multiple_of((core * grps + (grp ^ m)) * part, part)
            copies.append(
                pltpu.make_async_copy(stage.at[m], h_out.at[pl.ds(home, part)], sem.at[m])
            )
            copies[-1].start()
        if not far:
            for m in range(grps):
                at = pl.multiple_of((grp ^ m) * dst_rows, dst_rows)
                d_out[pl.ds(at, dst_rows), :] = ins[m][pl.ds(part, dst_rows), :].astype(F32)
        for copy in copies:
            copy.wait()

    hours = jax.ShapeDtypeStruct((hour_rows, rank), F32)
    dst = jax.ShapeDtypeStruct((grps * dst_rows, rank), F32)
    scratch = [((grps, part, rank), F32)]
    need = size_of([(p.shape, p.dtype) for p in parts] + scratch) + (4 << 20)
    return pl.pallas_call(
        kernel,
        in_specs=[SMEM] + [VMEM] * grps + ([HBM] if far else []),
        out_specs=[HBM] if far else [HBM, VMEM],
        out_shape=[hours] if far else [hours, dst],
        scratch_shapes=[pltpu.VMEM(s, t) for s, t in scratch]
        + [pltpu.SemaphoreType.DMA((grps,))],
        input_output_aliases={grps + 1: 0} if far else {},
        compiler_params=pltpu.CompilerParams(vmem_limit_bytes=need),
        name="place_far" if far else "place_near",
    )(ids, *parts, *([so_far] if far else []))


def per_device(
    sizes,
    counts,
    src_factor,
    dst_factor,
    hour_factor,
    src_owner,
    src_slot,
    dst_owner,
    dst_slot,
    hour_block,
):
    grps, devs = sizes
    depth = devs // 2
    local = src_factor.shape[0]
    hour_rows = hour_factor.shape[0]
    me = lax.axis_index("dev").astype(jnp.int32)
    grp = lax.axis_index("grp").astype(jnp.int32)
    place = jnp.stack([me, grp] + [me * 0] * 6)
    ids = jnp.concatenate(
        [place, src_owner[:, 0], src_slot, dst_owner[:, 0], dst_slot, hour_block]
    )
    own = run_join([src_factor, dst_factor])
    along = [own] + [swap(own, "dev", devs, 2 * m) for m in range(1, depth)]
    picked, same = run_pick(counts.shape[0], ids, hour_factor, own)
    across = [swap(x, "dev", devs, 1) for x in [same] + along[1:]]
    pieces = [x for pair in zip(along, across) for x in pair]
    shape = (grps, devs, local, hour_rows)
    h_acc, sd_acc, h_send, sd_send = run_main(shape, ids, counts, picked, pieces)

    def exchange(parts, axis, size, step):
        return [parts[0]] + [swap(x, axis, size, step * m) for m, x in enumerate(parts) if m]

    h_got = swap(h_send, "dev", devs, 1)
    sd_got = swap(sd_send, "dev", devs, 1)
    hours = run_cut_hours(grps, h_acc, h_got)
    srcs = run_cut_src(depth, local, sd_acc, sd_got)
    hours = run_grp_hours(depth, ids, exchange(hours, "grp", grps, 1))
    grad_src = run_z(exchange(srcs, "dev", devs, 2), F32, "z_src")
    dsts = run_cut_dst(grps, depth, local, sd_acc, sd_got, grad_src)
    dsts = run_grp_dst(depth, exchange(dsts, "grp", grps, 1))
    hour = run_z(exchange(hours, "dev", devs, 2), BF16, "z_hours")
    dst = run_z(exchange(dsts, "dev", devs, 2), BF16, "z_dst")
    back = [hour] + [swap(hour, "dev", devs, 2 * m) for m in range(1, depth)]
    joined = run_join(back + [dst])
    near = [joined] + [swap(joined, "grp", grps, m) for m in range(1, grps)]
    far = [swap(x, "dev", devs, 1) for x in near]
    dst_rows = dst.shape[0]
    part_done, grad_dst = run_place(sizes, hour_rows, dst_rows, 0, ids, near, None)
    grad_hour = run_place(sizes, hour_rows, dst_rows, 1, ids, far, part_done)[0]
    return grad_src, grad_dst, grad_hour


def solution(mesh):
    in_specs = (
        P(("grp", "dev"), None, None),
        P(("grp", "dev"), None),
        P("dev", None),
        P(),
        P(("grp", "dev"), None),
        P(("grp", "dev")),
        P(("grp", "dev"), None),
        P(("grp", "dev")),
        P(("grp", "dev")),
    )
    out_specs = (P(("grp", "dev"), None), P("dev", None), P())
    return jax.shard_map(
        functools.partial(per_device, mesh_sizes(mesh)),
        mesh=mesh,
        in_specs=in_specs,
        out_specs=out_specs,
        check_vma=False,
    )
```

time: 161 us -> 147 us (0.913)
  waiting for transfers between devices: 63.5 us -> 44.6 us
  Pallas kernels: 54.4 us -> 57.7 us
  starting transfers between devices: 33.2 us -> 36.5 us
  local copies, waits for them, and re-layouts: 8.82 us -> 6.7 us
    ppermute x31 -> x34, waiting for transfers between devices: 63.5 us -> 44.6 us  [swap(): return lax.ppermute(x, axis, [(i, i ^ mask) for i in range(size)])]
    ppermute x31 -> x34, starting transfers between devices: 33.2 us -> 36.5 us  [swap(): return lax.ppermute(x, axis, [(i, i ^ mask) for i in range(size)])]
    pallas_call x6 -> x14, Pallas kernels: 54.4 us -> 57.7 us  [the longest x1 47.8 us: run_main(): pl.pallas_call(functools.partial(main_kernel, shape), in_specs=[SMEM, HBM...]
    unnamed x8 -> x14, local copies, waits for them, and re-layouts: 7.1 us -> 5.41 us
  transfers between devices with their start and end apart: 31 -> 34, of which waited for: 16 -> 13; matrix products, arithmetic and copies ran while one was open for 1% -> 1% of each run, Pallas kernels for 1% -> 5%
where the time goes in v2:
time: 147 us; the launch traced here: 146 us
  Pallas kernels  57.7 us (39%)
  waiting for transfers between devices  44.6 us (30%)
  starting transfers between devices  36.5 us (25%)
  local copies, waits for them, and re-layouts  6.7 us (5%)
    pallas_call x1, Pallas kernels, run_main(): pl.pallas_call(functools.partial(main_kernel, shape), in_specs=[SMEM, HBM...  47.8 us
    ppermute x34, waiting for transfers between devices, swap(): return lax.ppermute(x, axis, [(i, i ^ mask) for i in range(size)])  44.6 us
    ppermute x34, starting transfers between devices, swap(): return lax.ppermute(x, axis, [(i, i ^ mask) for i in range(size)])  36.5 us
    unnamed x14, local copies, waits for them, and re-layouts  5.41 us
    pallas_call x2, Pallas kernels, run_place(): pl.pallas_call(kernel, in_specs=[SMEM] + [VMEM] * grps + ([HBM] if far el...  4.55 us
    pallas_call x1, Pallas kernels, run_pick(): pl.pallas_call(kernel, in_specs=[SMEM, HBM, VMEM], out_specs=[VMEM, VMEM]...  3.22 us
  transfers between devices with their start and end apart: 34, of which 13 were waited for; matrix products, arithmetic and copies ran while one was open for 1% of the time, Pallas kernels for 5%

profile of v2, /device:TPU:0, one launch (start us, length us, event | category | flops | bytes accessed | tf_op | source)
XLA Modules:
  0.0 146.3 jit_solution(14345218738605585961)
XLA Ops:
  2.5 5.1 %collective-permute-start.5 = (bf16[512,256]{1,0:T(8,128)(2,1)S(1)}, bf16[512,256]{1,0:T(8,128)(2,1)S(1)}, u32[]{:S(2)}, u32[]{:S(2)}) collective-permute-start(bf16[512,256]{1,0:T(8,128)(2,1)S(1)} %join.2.own.refs_0_), channel_id=1, source_target_pairs={{0,6},{1,7},{2,4},{3,5},{4,2},{5,3},{6,0},{7,1},{8,14},{9,15},{10,... | collective-permute-start | bytes 786440 | tf_op jit(solution)/shard_map/ppermute | solution.py:28
  8.2 1.3 concatenate.3.ids
  9.5 3.2 %pick_hours.1 = (bf16[1536,256]{1,0:T(8,128)(2,1)}, bf16[512,256]{1,0:T(8,128)(2,1)}) custom-call(s32[128]{0:T(128)} %concatenate.3.ids, bf16[4096,256]{1,0:T(8,128)(2,1)} %hours.1, bf16[512,256]{1,0:T(8,128)(2,1)} %copy-done), custom_call_target="tpu_custom_call" | custom-call | tf_op jit(solution)/shard_map/pick_hours/pallas_call | solution.py:98
  12.8 2.0 %collective-permute-done.5.refs_6_ = bf16[512,256]{1,0:T(8,128)(2,1)S(1)} collective-permute-done((bf16[512,256]{1,0:T(8,128)(2,1)S(1)}, bf16[512,256]{1,0:T(8,128)(2,1)S(1)}, u32[]{:S(2)}, u32[]{:S(2)}) %collective-permute-start.5) | collective-permute-done | bytes 262176 | tf_op jit(solution)/shard_map/ppermute | solution.py:28
  14.9 15.0 %collective-permute-done.3.refs_4_ = bf16[512,256]{1,0:T(8,128)(2,1)S(1)} collective-permute-done((bf16[512,256]{1,0:T(8,128)(2,1)S(1)}, bf16[512,256]{1,0:T(8,128)(2,1)S(1)}, u32[]{:S(2)}, u32[]{:S(2)}) %collective-permute-start.3) | collective-permute-done | bytes 262176 | tf_op jit(solution)/shard_map/ppermute | solution.py:28
  33.3 1.1 copy-done.6
  34.5 47.8 %terms.1 = (f32[4096,256]{1,0:T(8,128)S(1)}, f32[4096,256]{1,0:T(8,128)S(1)}, bf16[2048,256]{1,0:T(8,128)(2,1)S(1)}, bf16[2048,256]{1,0:T(8,128)(2,1)S(1)}) custom-call(s32[128]{0:T(128)S(1)} %copy-done.5, bf16[24,64,4096]{2,1,0:T(8,128)(2,1)} %counts.1, bf16[1536,256]{1,0:T(8,128)(2,1)S(1)} %copy-done.6, bf16[512,256]{1,0:T(8,128)(2,1)S(1)} %copy-done.1, ...), custom_call_target="tpu_custom_call" | custom-call | flops 12884901888 | bytes 12582912 | tf_op jit(solution)/shard_map/terms/pallas_call | solution.py:206
  82.9 2.1 %collective-permute-done.7.got = bf16[2048,256]{1,0:T(8,128)(2,1)S(1)} collective-permute-done((bf16[2048,256]{1,0:T(8,128)(2,1)S(1)}, bf16[2048,256]{1,0:T(8,128)(2,1)S(1)}, u32[]{:S(2)}, u32[]{:S(2)}) %collective-permute-start.7) | collective-permute-done | bytes 1048608 | tf_op jit(solution)/shard_map/ppermute | solution.py:28
  85.2 1.3 collective-permute-done.11.got
  86.7 1.6 %collective-permute-start.12 = (bf16[512,256]{1,0:T(8,128)(2,1)S(1)}, bf16[512,256]{1,0:T(8,128)(2,1)S(1)}, u32[]{:S(2)}, u32[]{:S(2)}) collective-permute-start(bf16[512,256]{1,0:T(8,128)(2,1)S(1)} %get-tuple-element.42), channel_id=1, source_target_pairs={{0,8},{8,0},{16,24},{24,16},{1,9},{9,1},{17,25},{25,17},{2,10},{10... | collective-permute-start | bytes 786440 | tf_op jit(solution)/shard_map/ppermute | solution.py:28
  88.3 1.7 %collective-permute-start.9 = (bf16[256,256]{1,0:T(8,128)(2,1)S(1)}, bf16[256,256]{1,0:T(8,128)(2,1)S(1)}, u32[]{:S(2)}, u32[]{:S(2)}) collective-permute-start(bf16[256,256]{1,0:T(8,128)(2,1)S(1)} %get-tuple-element.37), channel_id=1, source_target_pairs={{0,4},{1,5},{2,6},{3,7},{4,0},{5,1},{6,2},{7,3},{8,12},{9,13},{10,... | collective-permute-start | bytes 393224 | tf_op jit(solution)/shard_map/ppermute | solution.py:28
  90.0 1.5 %collective-permute-start.13 = (bf16[512,256]{1,0:T(8,128)(2,1)S(1)}, bf16[512,256]{1,0:T(8,128)(2,1)S(1)}, u32[]{:S(2)}, u32[]{:S(2)}) collective-permute-start(bf16[512,256]{1,0:T(8,128)(2,1)S(1)} %get-tuple-element.43), channel_id=1, source_target_pairs={{0,16},{8,24},{16,0},{24,8},{1,17},{9,25},{17,1},{25,9},{2,18},{10... | collective-permute-start | bytes 786440 | tf_op jit(solution)/shard_map/ppermute | solution.py:28
  92.0 1.3 collective-permute-start.10
  93.4 6.7 %collective-permute-done.9.refs_2_ = bf16[256,256]{1,0:T(8,128)(2,1)S(1)} collective-permute-done((bf16[256,256]{1,0:T(8,128)(2,1)S(1)}, bf16[256,256]{1,0:T(8,128)(2,1)S(1)}, u32[]{:S(2)}, u32[]{:S(2)}) %collective-permute-start.9) | collective-permute-done | bytes 131104 | tf_op jit(solution)/shard_map/ppermute | solution.py:28
  101.9 1.4 collective-permute-start.21
  103.2 1.5 %collective-permute-start.22 = (bf16[256,256]{1,0:T(8,128)(2,1)S(1)}, bf16[256,256]{1,0:T(8,128)(2,1)S(1)}, u32[]{:S(2)}, u32[]{:S(2)}) collective-permute-start(bf16[256,256]{1,0:T(8,128)(2,1)S(1)} %get-tuple-element.51), channel_id=1, source_target_pairs={{0,16},{8,24},{16,0},{24,8},{1,17},{9,25},{17,1},{25,9},{2,18},{10... | collective-permute-start | bytes 393224 | tf_op jit(solution)/shard_map/ppermute | solution.py:28
  106.2 3.3 %collective-permute-start.15 = (bf16[128,256]{1,0:T(8,128)(2,1)S(1)}, bf16[128,256]{1,0:T(8,128)(2,1)S(1)}, u32[]{:S(2)}, u32[]{:S(2)}) collective-permute-start(bf16[128,256]{1,0:T(8,128)(2,1)S(1)} %get-tuple-element.46), channel_id=1, source_target_pairs={{0,2},{1,3},{2,0},{3,1},{4,6},{5,7},{6,4},{7,5},{8,10},{9,11},{10,... | collective-permute-start | bytes 196616 | tf_op jit(solution)/shard_map/ppermute | solution.py:28
  110.6 1.4 collective-permute-start.17
  112.1 2.5 %collective-permute-start.24 = (bf16[64,256]{1,0:T(8,128)(2,1)S(1)}, bf16[64,256]{1,0:T(8,128)(2,1)S(1)}, u32[]{:S(2)}, u32[]{:S(2)}) collective-permute-start(bf16[64,256]{1,0:T(8,128)(2,1)S(1)} %get-tuple-element.54), channel_id=1, source_target_pairs={{0,2},{1,3},{2,0},{3,1},{4,6},{5,7},{6,4},{7,5},{8,10},{9,11},{10,... | collective-permute-start | bytes 98312 | tf_op jit(solution)/shard_map/ppermute | solution.py:28
  114.5 2.3 %collective-permute-done.16.refs_2_ = bf16[128,256]{1,0:T(8,128)(2,1)S(1)} collective-permute-done((bf16[128,256]{1,0:T(8,128)(2,1)S(1)}, bf16[128,256]{1,0:T(8,128)(2,1)S(1)}, u32[]{:S(2)}, u32[]{:S(2)}) %collective-permute-start.16) | collective-permute-done | bytes 65568 | tf_op jit(solution)/shard_map/ppermute | solution.py:28
  116.9 2.3 %collective-permute-start.20 = (bf16[128,256]{1,0:T(8,128)(2,1)S(1)}, bf16[128,256]{1,0:T(8,128)(2,1)S(1)}, u32[]{:S(2)}, u32[]{:S(2)}) collective-permute-start(bf16[128,256]{1,0:T(8,128)(2,1)S(1)} %z_hours.1.refs_0_), channel_id=1, source_target_pairs={{0,6},{1,7},{2,4},{3,5},{4,2},{5,3},{6,0},{7,1},{8,14},{9,15},{10,... | collective-permute-start | bytes 196616 | tf_op jit(solution)/shard_map/ppermute | solution.py:28
  119.7 1.7 %collective-permute-start.18 = (bf16[128,256]{1,0:T(8,128)(2,1)S(1)}, bf16[128,256]{1,0:T(8,128)(2,1)S(1)}, u32[]{:S(2)}, u32[]{:S(2)}) collective-permute-start(bf16[128,256]{1,0:T(8,128)(2,1)S(1)} %z_hours.1.refs_0_), channel_id=1, source_target_pairs={{0,2},{1,3},{2,0},{3,1},{4,6},{5,7},{6,4},{7,5},{8,10},{9,11},{10,... | collective-permute-start | bytes 196616 | tf_op jit(solution)/shard_map/ppermute | solution.py:28
  121.4 1.1 collective-permute-start.25
  122.5 1.6 %collective-permute-start.26 = (bf16[64,256]{1,0:T(8,128)(2,1)S(1)}, bf16[64,256]{1,0:T(8,128)(2,1)S(1)}, u32[]{:S(2)}, u32[]{:S(2)}) collective-permute-start(bf16[64,256]{1,0:T(8,128)(2,1)S(1)} %get-tuple-element.56), channel_id=1, source_target_pairs={{0,6},{1,7},{2,4},{3,5},{4,2},{5,3},{6,0},{7,1},{8,14},{9,15},{10,... | collective-permute-start | bytes 98312 | tf_op jit(solution)/shard_map/ppermute | solution.py:28
  124.0 2.8 %collective-permute-done.25.refs_2_ = bf16[64,256]{1,0:T(8,128)(2,1)S(1)} collective-permute-done((bf16[64,256]{1,0:T(8,128)(2,1)S(1)}, bf16[64,256]{1,0:T(8,128)(2,1)S(1)}, u32[]{:S(2)}, u32[]{:S(2)}) %collective-permute-start.25) | collective-permute-done | bytes 32800 | tf_op jit(solution)/shard_map/ppermute | solution.py:28
  126.8 1.4 collective-permute-done.26.refs_3_
  128.3 1.5 %collective-permute-start.29 = (bf16[576,256]{1,0:T(8,128)(2,1)S(1)}, bf16[576,256]{1,0:T(8,128)(2,1)S(1)}, u32[]{:S(2)}, u32[]{:S(2)}) collective-permute-start(bf16[576,256]{1,0:T(8,128)(2,1)S(1)} %join.3.refs_0_), channel_id=1, source_target_pairs={{0,24},{8,16},{16,8},{24,0},{1,25},{9,17},{17,9},{25,1},{2,26},{10... | collective-permute-start | bytes 884744 | tf_op jit(solution)/shard_map/ppermute | solution.py:28
  130.3 1.5 %collective-permute-start.27 = (bf16[576,256]{1,0:T(8,128)(2,1)S(1)}, bf16[576,256]{1,0:T(8,128)(2,1)S(1)}, u32[]{:S(2)}, u32[]{:S(2)}) collective-permute-start(bf16[576,256]{1,0:T(8,128)(2,1)S(1)} %join.3.refs_0_), channel_id=1, source_target_pairs={{0,8},{8,0},{16,24},{24,16},{1,9},{9,1},{17,25},{25,17},{2,10},{10... | collective-permute-start | bytes 884744 | tf_op jit(solution)/shard_map/ppermute | solution.py:28
  131.8 6.4 %collective-permute-done.29.refs_3_ = bf16[576,256]{1,0:T(8,128)(2,1)S(1)} collective-permute-done((bf16[576,256]{1,0:T(8,128)(2,1)S(1)}, bf16[576,256]{1,0:T(8,128)(2,1)S(1)}, u32[]{:S(2)}, u32[]{:S(2)}) %collective-permute-start.29) | collective-permute-done | bytes 294944 | tf_op jit(solution)/shard_map/ppermute | solution.py:28
  138.2 3.0 %collective-permute-done.28.refs_2_ = bf16[576,256]{1,0:T(8,128)(2,1)S(1)} collective-permute-done((bf16[576,256]{1,0:T(8,128)(2,1)S(1)}, bf16[576,256]{1,0:T(8,128)(2,1)S(1)}, u32[]{:S(2)}, u32[]{:S(2)}) %collective-permute-start.28) | collective-permute-done | bytes 294944 | tf_op jit(solution)/shard_map/ppermute | solution.py:28
  141.7 2.6 %place_near.1 = (f32[4096,256]{1,0:T(8,128)}, f32[256,256]{1,0:T(8,128)}) custom-call(s32[128]{0:T(128)S(1)} %copy-done.5, bf16[576,256]{1,0:T(8,128)(2,1)S(1)} %join.3.refs_0_, bf16[576,256]{1,0:T(8,128)(2,1)S(1)} %collective-permute-done.27.refs_1_, bf16[576,256]{1,0:T(8,128)(2,1)S(1)} %collective-permute-done.28.refs_2_, ...), custom_call_target="tpu_custom_call" | custom-call | tf_op jit(solution)/shard_map/place_near/pallas_call | solution.py:379
  144.4 1.9 %place_far.1 = f32[4096,256]{1,0:T(8,128)} custom-call(s32[128]{0:T(128)S(1)} %copy-done.5, bf16[576,256]{1,0:T(8,128)(2,1)S(1)} %collective-permute-done.30.refs_0_, bf16[576,256]{1,0:T(8,128)(2,1)S(1)} %collective-permute-done.31.refs_1_, bf16[576,256]{1,0:T(8,128)(2,1)S(1)} %collective-permute-done.32.refs_2_, ...), custom_call_target="tpu_custom_call", output_to_operand_aliasing={{}: (5, {})} | custom-call | tf_op jit(solution)/shard_map/place_far/pallas_call | solution.py:379
  (67 shorter events, 13.4 us)
Async XLA Ops:
  2.5 12.4 %collective-permute-start.5 = (bf16[512,256]{1,0:T(8,128)(2,1)S(1)}, bf16[512,256]{1,0:T(8,128)(2,1)S(1)}, u32[]{:S(2)}, u32[]{:S(2)}) collective-permute-start(bf16[512,256]{1,0:T(8,128)(2,1)S(1)} %join.2.own.refs_0_), channel_id=1, source_target_pairs={{0,6},{1,7},{2,4},{3,5},{4,2},{5,3},{6,0},{7,1},{8,14},{9,15},{10,... | collective-permute-start | bytes 786440 | tf_op jit(solution)/shard_map/ppermute | solution.py:28
  7.6 22.3 %collective-permute-start.3 = (bf16[512,256]{1,0:T(8,128)(2,1)S(1)}, bf16[512,256]{1,0:T(8,128)(2,1)S(1)}, u32[]{:S(2)}, u32[]{:S(2)}) collective-permute-start(bf16[512,256]{1,0:T(8,128)(2,1)S(1)} %join.2.own.refs_0_), channel_id=1, source_target_pairs={{0,4},{1,5},{2,6},{3,7},{4,0},{5,1},{6,2},{7,3},{8,12},{9,13},{10,... | collective-permute-start | bytes 786440 | tf_op jit(solution)/shard_map/ppermute | solution.py:28
  7.6 22.3 %collective-permute-start.1 = (bf16[512,256]{1,0:T(8,128)(2,1)S(1)}, bf16[512,256]{1,0:T(8,128)(2,1)S(1)}, u32[]{:S(2)}, u32[]{:S(2)}) collective-permute-start(bf16[512,256]{1,0:T(8,128)(2,1)S(1)} %join.2.own.refs_0_), channel_id=1, source_target_pairs={{0,2},{1,3},{2,0},{3,1},{4,6},{5,7},{6,4},{7,5},{8,10},{9,11},{10,... | collective-permute-start | bytes 786440 | tf_op jit(solution)/shard_map/ppermute | solution.py:28
  12.8 17.7 %collective-permute-start = (bf16[512,256]{1,0:T(8,128)(2,1)}, bf16[512,256]{1,0:T(8,128)(2,1)S(1)}, u32[]{:S(2)}, u32[]{:S(2)}) collective-permute-start(bf16[512,256]{1,0:T(8,128)(2,1)} %get-tuple-element.32), channel_id=1, source_target_pairs={{0,1},{1,0},{2,3},{3,2},{4,5},{5,4},{6,7},{7,6},{8,9},{9,8},{10,11... | collective-permute-start | bytes 786440 | tf_op jit(solution)/shard_map/ppermute | solution.py:28
  14.9 15.6 %collective-permute-start.6 = (bf16[512,256]{1,0:T(8,128)(2,1)S(1)}, bf16[512,256]{1,0:T(8,128)(2,1)S(1)}, u32[]{:S(2)}, u32[]{:S(2)}) collective-permute-start(bf16[512,256]{1,0:T(8,128)(2,1)S(1)} %collective-permute-done.5.refs_6_), channel_id=1, source_target_pairs={{0,1},{1,0},{2,3},{3,2},{4,5},{5,4},{6,7},{7,6},{8,9},{9,8},{10,11... | collective-permute-start | bytes 786440 | tf_op jit(solution)/shard_map/ppermute | solution.py:28
  82.3 2.7 %collective-permute-start.7 = (bf16[2048,256]{1,0:T(8,128)(2,1)S(1)}, bf16[2048,256]{1,0:T(8,128)(2,1)S(1)}, u32[]{:S(2)}, u32[]{:S(2)}) collective-permute-start(bf16[2048,256]{1,0:T(8,128)(2,1)S(1)} %get-tuple-element.34), channel_id=1, source_target_pairs={{0,1},{1,0},{2,3},{3,2},{4,5},{5,4},{6,7},{7,6},{8,9},{9,8},{10,11... | collective-permute-start | bytes 3145736 | tf_op jit(solution)/shard_map/ppermute | solution.py:28
  82.5 4.0 %collective-permute-start.11 = (bf16[2048,256]{1,0:T(8,128)(2,1)S(1)}, bf16[2048,256]{1,0:T(8,128)(2,1)S(1)}, u32[]{:S(2)}, u32[]{:S(2)}) collective-permute-start(bf16[2048,256]{1,0:T(8,128)(2,1)S(1)} %get-tuple-element.40), channel_id=1, source_target_pairs={{0,1},{1,0},{2,3},{3,2},{4,5},{5,4},{6,7},{7,6},{8,9},{9,8},{10,11... | collective-permute-start | bytes 3145736 | tf_op jit(solution)/shard_map/ppermute | solution.py:28
  85.1 6.9 %collective-permute-start.8 = (bf16[256,256]{1,0:T(8,128)(2,1)S(1)}, bf16[256,256]{1,0:T(8,128)(2,1)S(1)}, u32[]{:S(2)}, u32[]{:S(2)}) collective-permute-start(bf16[256,256]{1,0:T(8,128)(2,1)S(1)} %get-tuple-element.36), channel_id=1, source_target_pairs={{0,2},{1,3},{2,0},{3,1},{4,6},{5,7},{6,4},{7,5},{8,10},{9,11},{10,... | collective-permute-start | bytes 393224 | tf_op jit(solution)/shard_map/ppermute | solution.py:28
  86.7 18.0 %collective-permute-start.12 = (bf16[512,256]{1,0:T(8,128)(2,1)S(1)}, bf16[512,256]{1,0:T(8,128)(2,1)S(1)}, u32[]{:S(2)}, u32[]{:S(2)}) collective-permute-start(bf16[512,256]{1,0:T(8,128)(2,1)S(1)} %get-tuple-element.42), channel_id=1, source_target_pairs={{0,8},{8,0},{16,24},{24,16},{1,9},{9,1},{17,25},{25,17},{2,10},{10... | collective-permute-start | bytes 786440 | tf_op jit(solution)/shard_map/ppermute | solution.py:28
  88.3 11.7 %collective-permute-start.9 = (bf16[256,256]{1,0:T(8,128)(2,1)S(1)}, bf16[256,256]{1,0:T(8,128)(2,1)S(1)}, u32[]{:S(2)}, u32[]{:S(2)}) collective-permute-start(bf16[256,256]{1,0:T(8,128)(2,1)S(1)} %get-tuple-element.37), channel_id=1, source_target_pairs={{0,4},{1,5},{2,6},{3,7},{4,0},{5,1},{6,2},{7,3},{8,12},{9,13},{10,... | collective-permute-start | bytes 393224 | tf_op jit(solution)/shard_map/ppermute | solution.py:28
  90.0 15.4 %collective-permute-start.13 = (bf16[512,256]{1,0:T(8,128)(2,1)S(1)}, bf16[512,256]{1,0:T(8,128)(2,1)S(1)}, u32[]{:S(2)}, u32[]{:S(2)}) collective-permute-start(bf16[512,256]{1,0:T(8,128)(2,1)S(1)} %get-tuple-element.43), channel_id=1, source_target_pairs={{0,16},{8,24},{16,0},{24,8},{1,17},{9,25},{17,1},{25,9},{2,18},{10... | collective-permute-start | bytes 786440 | tf_op jit(solution)/shard_map/ppermute | solution.py:28
  91.5 13.9 %collective-permute-start.14 = (bf16[512,256]{1,0:T(8,128)(2,1)S(1)}, bf16[512,256]{1,0:T(8,128)(2,1)S(1)}, u32[]{:S(2)}, u32[]{:S(2)}) collective-permute-start(bf16[512,256]{1,0:T(8,128)(2,1)S(1)} %get-tuple-element.44), channel_id=1, source_target_pairs={{0,24},{8,16},{16,8},{24,0},{1,25},{9,17},{17,9},{25,1},{2,26},{10... | collective-permute-start | bytes 786440 | tf_op jit(solution)/shard_map/ppermute | solution.py:28
  92.0 8.0 %collective-permute-start.10 = (bf16[256,256]{1,0:T(8,128)(2,1)S(1)}, bf16[256,256]{1,0:T(8,128)(2,1)S(1)}, u32[]{:S(2)}, u32[]{:S(2)}) collective-permute-start(bf16[256,256]{1,0:T(8,128)(2,1)S(1)} %get-tuple-element.38), channel_id=1, source_target_pairs={{0,6},{1,7},{2,4},{3,5},{4,2},{5,3},{6,0},{7,1},{8,14},{9,15},{10,... | collective-permute-start | bytes 393224 | tf_op jit(solution)/shard_map/ppermute | solution.py:28
  101.9 8.7 %collective-permute-start.21 = (bf16[256,256]{1,0:T(8,128)(2,1)S(1)}, bf16[256,256]{1,0:T(8,128)(2,1)S(1)}, u32[]{:S(2)}, u32[]{:S(2)}) collective-permute-start(bf16[256,256]{1,0:T(8,128)(2,1)S(1)} %get-tuple-element.50), channel_id=1, source_target_pairs={{0,8},{8,0},{16,24},{24,16},{1,9},{9,1},{17,25},{25,17},{2,10},{10... | collective-permute-start | bytes 393224 | tf_op jit(solution)/shard_map/ppermute | solution.py:28
  103.2 8.8 %collective-permute-start.22 = (bf16[256,256]{1,0:T(8,128)(2,1)S(1)}, bf16[256,256]{1,0:T(8,128)(2,1)S(1)}, u32[]{:S(2)}, u32[]{:S(2)}) collective-permute-start(bf16[256,256]{1,0:T(8,128)(2,1)S(1)} %get-tuple-element.51), channel_id=1, source_target_pairs={{0,16},{8,24},{16,0},{24,8},{1,17},{9,25},{17,1},{25,9},{2,18},{10... | collective-permute-start | bytes 393224 | tf_op jit(solution)/shard_map/ppermute | solution.py:28
  104.7 7.3 %collective-permute-start.23 = (bf16[256,256]{1,0:T(8,128)(2,1)S(1)}, bf16[256,256]{1,0:T(8,128)(2,1)S(1)}, u32[]{:S(2)}, u32[]{:S(2)}) collective-permute-start(bf16[256,256]{1,0:T(8,128)(2,1)S(1)} %get-tuple-element.52), channel_id=1, source_target_pairs={{0,24},{8,16},{16,8},{24,0},{1,25},{9,17},{17,9},{25,1},{2,26},{10... | collective-permute-start | bytes 393224 | tf_op jit(solution)/shard_map/ppermute | solution.py:28
  106.2 8.4 %collective-permute-start.15 = (bf16[128,256]{1,0:T(8,128)(2,1)S(1)}, bf16[128,256]{1,0:T(8,128)(2,1)S(1)}, u32[]{:S(2)}, u32[]{:S(2)}) collective-permute-start(bf16[128,256]{1,0:T(8,128)(2,1)S(1)} %get-tuple-element.46), channel_id=1, source_target_pairs={{0,2},{1,3},{2,0},{3,1},{4,6},{5,7},{6,4},{7,5},{8,10},{9,11},{10,... | collective-permute-start | bytes 196616 | tf_op jit(solution)/shard_map/ppermute | solution.py:28
  109.5 7.4 %collective-permute-start.16 = (bf16[128,256]{1,0:T(8,128)(2,1)S(1)}, bf16[128,256]{1,0:T(8,128)(2,1)S(1)}, u32[]{:S(2)}, u32[]{:S(2)}) collective-permute-start(bf16[128,256]{1,0:T(8,128)(2,1)S(1)} %get-tuple-element.47), channel_id=1, source_target_pairs={{0,4},{1,5},{2,6},{3,7},{4,0},{5,1},{6,2},{7,3},{8,12},{9,13},{10,... | collective-permute-start | bytes 196616 | tf_op jit(solution)/shard_map/ppermute | solution.py:28
  110.6 6.3 %collective-permute-start.17 = (bf16[128,256]{1,0:T(8,128)(2,1)S(1)}, bf16[128,256]{1,0:T(8,128)(2,1)S(1)}, u32[]{:S(2)}, u32[]{:S(2)}) collective-permute-start(bf16[128,256]{1,0:T(8,128)(2,1)S(1)} %get-tuple-element.48), channel_id=1, source_target_pairs={{0,6},{1,7},{2,4},{3,5},{4,2},{5,3},{6,0},{7,1},{8,14},{9,15},{10,... | collective-permute-start | bytes 196616 | tf_op jit(solution)/shard_map/ppermute | solution.py:28
  112.1 10.4 %collective-permute-start.24 = (bf16[64,256]{1,0:T(8,128)(2,1)S(1)}, bf16[64,256]{1,0:T(8,128)(2,1)S(1)}, u32[]{:S(2)}, u32[]{:S(2)}) collective-permute-start(bf16[64,256]{1,0:T(8,128)(2,1)S(1)} %get-tuple-element.54), channel_id=1, source_target_pairs={{0,2},{1,3},{2,0},{3,1},{4,6},{5,7},{6,4},{7,5},{8,10},{9,11},{10,... | collective-permute-start | bytes 98312 | tf_op jit(solution)/shard_map/ppermute | solution.py:28
  116.9 11.3 %collective-permute-start.20 = (bf16[128,256]{1,0:T(8,128)(2,1)S(1)}, bf16[128,256]{1,0:T(8,128)(2,1)S(1)}, u32[]{:S(2)}, u32[]{:S(2)}) collective-permute-start(bf16[128,256]{1,0:T(8,128)(2,1)S(1)} %z_hours.1.refs_0_), channel_id=1, source_target_pairs={{0,6},{1,7},{2,4},{3,5},{4,2},{5,3},{6,0},{7,1},{8,14},{9,15},{10,... | collective-permute-start | bytes 196616 | tf_op jit(solution)/shard_map/ppermute | solution.py:28
  119.2 9.0 %collective-permute-start.19 = (bf16[128,256]{1,0:T(8,128)(2,1)S(1)}, bf16[128,256]{1,0:T(8,128)(2,1)S(1)}, u32[]{:S(2)}, u32[]{:S(2)}) collective-permute-start(bf16[128,256]{1,0:T(8,128)(2,1)S(1)} %z_hours.1.refs_0_), channel_id=1, source_target_pairs={{0,4},{1,5},{2,6},{3,7},{4,0},{5,1},{6,2},{7,3},{8,12},{9,13},{10,... | collective-permute-start | bytes 196616 | tf_op jit(solution)/shard_map/ppermute | solution.py:28
  119.7 8.6 %collective-permute-start.18 = (bf16[128,256]{1,0:T(8,128)(2,1)S(1)}, bf16[128,256]{1,0:T(8,128)(2,1)S(1)}, u32[]{:S(2)}, u32[]{:S(2)}) collective-permute-start(bf16[128,256]{1,0:T(8,128)(2,1)S(1)} %z_hours.1.refs_0_), channel_id=1, source_target_pairs={{0,2},{1,3},{2,0},{3,1},{4,6},{5,7},{6,4},{7,5},{8,10},{9,11},{10,... | collective-permute-start | bytes 196616 | tf_op jit(solution)/shard_map/ppermute | solution.py:28
  121.4 5.4 %collective-permute-start.25 = (bf16[64,256]{1,0:T(8,128)(2,1)S(1)}, bf16[64,256]{1,0:T(8,128)(2,1)S(1)}, u32[]{:S(2)}, u32[]{:S(2)}) collective-permute-start(bf16[64,256]{1,0:T(8,128)(2,1)S(1)} %get-tuple-element.55), channel_id=1, source_target_pairs={{0,4},{1,5},{2,6},{3,7},{4,0},{5,1},{6,2},{7,3},{8,12},{9,13},{10,... | collective-permute-start | bytes 98312 | tf_op jit(solution)/shard_map/ppermute | solution.py:28
  122.5 5.7 %collective-permute-start.26 = (bf16[64,256]{1,0:T(8,128)(2,1)S(1)}, bf16[64,256]{1,0:T(8,128)(2,1)S(1)}, u32[]{:S(2)}, u32[]{:S(2)}) collective-permute-start(bf16[64,256]{1,0:T(8,128)(2,1)S(1)} %get-tuple-element.56), channel_id=1, source_target_pairs={{0,6},{1,7},{2,4},{3,5},{4,2},{5,3},{6,0},{7,1},{8,14},{9,15},{10,... | collective-permute-start | bytes 98312 | tf_op jit(solution)/shard_map/ppermute | solution.py:28
  128.3 9.9 %collective-permute-start.29 = (bf16[576,256]{1,0:T(8,128)(2,1)S(1)}, bf16[576,256]{1,0:T(8,128)(2,1)S(1)}, u32[]{:S(2)}, u32[]{:S(2)}) collective-permute-start(bf16[576,256]{1,0:T(8,128)(2,1)S(1)} %join.3.refs_0_), channel_id=1, source_target_pairs={{0,24},{8,16},{16,8},{24,0},{1,25},{9,17},{17,9},{25,1},{2,26},{10... | collective-permute-start | bytes 884744 | tf_op jit(solution)/shard_map/ppermute | solution.py:28
  129.8 11.4 %collective-permute-start.28 = (bf16[576,256]{1,0:T(8,128)(2,1)S(1)}, bf16[576,256]{1,0:T(8,128)(2,1)S(1)}, u32[]{:S(2)}, u32[]{:S(2)}) collective-permute-start(bf16[576,256]{1,0:T(8,128)(2,1)S(1)} %join.3.refs_0_), channel_id=1, source_target_pairs={{0,16},{8,24},{16,0},{24,8},{1,17},{9,25},{17,1},{25,9},{2,18},{10... | collective-permute-start | bytes 884744 | tf_op jit(solution)/shard_map/ppermute | solution.py:28
  130.3 11.0 %collective-permute-start.27 = (bf16[576,256]{1,0:T(8,128)(2,1)S(1)}, bf16[576,256]{1,0:T(8,128)(2,1)S(1)}, u32[]{:S(2)}, u32[]{:S(2)}) collective-permute-start(bf16[576,256]{1,0:T(8,128)(2,1)S(1)} %join.3.refs_0_), channel_id=1, source_target_pairs={{0,8},{8,0},{16,24},{24,16},{1,9},{9,1},{17,25},{25,17},{2,10},{10... | collective-permute-start | bytes 884744 | tf_op jit(solution)/shard_map/ppermute | solution.py:28
  131.8 12.5 %collective-permute-start.30 = (bf16[576,256]{1,0:T(8,128)(2,1)S(1)}, bf16[576,256]{1,0:T(8,128)(2,1)S(1)}, u32[]{:S(2)}, u32[]{:S(2)}) collective-permute-start(bf16[576,256]{1,0:T(8,128)(2,1)S(1)} %join.3.refs_0_), channel_id=1, source_target_pairs={{0,1},{1,0},{2,3},{3,2},{4,5},{5,4},{6,7},{7,6},{8,9},{9,8},{10,11... | collective-permute-start | bytes 884744 | tf_op jit(solution)/shard_map/ppermute | solution.py:28
  138.2 6.2 %collective-permute-start.33 = (bf16[576,256]{1,0:T(8,128)(2,1)S(1)}, bf16[576,256]{1,0:T(8,128)(2,1)S(1)}, u32[]{:S(2)}, u32[]{:S(2)}) collective-permute-start(bf16[576,256]{1,0:T(8,128)(2,1)S(1)} %collective-permute-done.29.refs_3_), channel_id=1, source_target_pairs={{0,1},{1,0},{2,3},{3,2},{4,5},{5,4},{6,7},{7,6},{8,9},{9,8},{10,11... | collective-permute-start | bytes 884744 | tf_op jit(solution)/shard_map/ppermute | solution.py:28
  141.2 3.2 %collective-permute-start.32 = (bf16[576,256]{1,0:T(8,128)(2,1)S(1)}, bf16[576,256]{1,0:T(8,128)(2,1)S(1)}, u32[]{:S(2)}, u32[]{:S(2)}) collective-permute-start(bf16[576,256]{1,0:T(8,128)(2,1)S(1)} %collective-permute-done.28.refs_2_), channel_id=1, source_target_pairs={{0,1},{1,0},{2,3},{3,2},{4,5},{5,4},{6,7},{7,6},{8,9},{9,8},{10,11... | collective-permute-start | bytes 884744 | tf_op jit(solution)/shard_map/ppermute | solution.py:28
  141.4 3.0 %collective-permute-start.31 = (bf16[576,256]{1,0:T(8,128)(2,1)S(1)}, bf16[576,256]{1,0:T(8,128)(2,1)S(1)}, u32[]{:S(2)}, u32[]{:S(2)}) collective-permute-start(bf16[576,256]{1,0:T(8,128)(2,1)S(1)} %collective-permute-done.27.refs_1_), channel_id=1, source_target_pairs={{0,1},{1,0},{2,3},{3,2},{4,5},{5,4},{6,7},{7,6},{8,9},{9,8},{10,11... | collective-permute-start | bytes 884744 | tf_op jit(solution)/shard_map/ppermute | solution.py:28
  (9 other events, 15.9 us)

commit v3 on v2

v3 whole, which is shorter than its diff:
```python
import functools

import jax
import jax.numpy as jnp
from jax import lax
from jax.experimental import pallas as pl
from jax.experimental.pallas import tpu as pltpu
from jax.sharding import PartitionSpec as P

F32 = jnp.float32
BF16 = jnp.bfloat16
SIDE = 64
RING = 8
PITCH = 72
GRANT = 36 << 20

VMEM = pl.BlockSpec(memory_space=pltpu.VMEM)
SMEM = pl.BlockSpec(memory_space=pltpu.SMEM)
ANY = pl.BlockSpec(memory_space=pl.ANY)
HBM = pl.BlockSpec(memory_space=pltpu.HBM)


def mesh_sizes(mesh):
    return mesh.shape["grp"], mesh.shape["dev"]


def swap(x, axis, size, mask):
    return lax.ppermute(x, axis, [(i, i ^ mask) for i in range(size)])


def block_terms(count, a, b, c, cube, even, odd):
    rank = a.shape[1]
    resids, pairs_bc, turned, pairs_ab = [], [], [], []
    for g in range(SIDE // 4):
        b4 = b[g * 4 : g * 4 + 4]
        bc = (b4[:, None, :] * c[None, :, :]).reshape(4 * SIDE, rank)
        ab = (b4[:, None, :] * a[None, :, :]).reshape(4 * SIDE, rank)
        theta = lax.dot_general(a, bc, (((1,), (1,)), ((), ())), preferred_element_type=F32)
        wide = jnp.exp(theta) - count[:, g * 256 : (g + 1) * 256].astype(F32)
        for p in range(2):
            cube[pl.ds((g * 2 + p) * PITCH, SIDE), :] = wide[:, p * 128 : (p + 1) * 128]
        resid = wide.astype(BF16)
        flip = resid.T
        turned += [flip[q * SIDE : (q + 1) * SIDE] for q in range(4)]
        resids.append(resid)
        pairs_bc.append(bc)
        pairs_ab.append(ab)
    term_a = jnp.dot(
        jnp.concatenate(resids, axis=1),
        jnp.concatenate(pairs_bc, axis=0),
        preferred_element_type=F32,
    )
    term_c = jnp.dot(
        jnp.concatenate(turned, axis=1),
        jnp.concatenate(pairs_ab, axis=0),
        preferred_element_type=F32,
    )
    low = lax.broadcasted_iota(jnp.int32, (SIDE // 2, 128), 1) < SIDE
    rows, pairs_ac = [], []
    for g in range(SIDE // 4):
        x = [cube[pl.ds(g * 4 + q, SIDE // 2, stride=PITCH), :] for q in range(4)]
        y = [pltpu.roll(v, SIDE, 1) for v in x]
        evens = [jnp.where(low, x[0], y[1]), jnp.where(low, x[2], y[3])]
        odds = [jnp.where(low, y[0], x[1]), jnp.where(low, y[2], x[3])]
        both = [jnp.concatenate(evens, axis=1), jnp.concatenate(odds, axis=1)]
        rows.append(jnp.concatenate(both, axis=0).astype(BF16))
        pairs_ac.append((a[g * 4 : g * 4 + 4][:, None, :] * c[None, :, :]).reshape(4 * SIDE, rank))
    mixed = jnp.dot(
        jnp.concatenate(rows, axis=1),
        jnp.concatenate(pairs_ac, axis=0),
        preferred_element_type=F32,
    )
    half = SIDE // 2
    for u in range(2):
        even[pl.ds(u, half, stride=2), :] = mixed[u * half : (u + 1) * half, :128]
        odd[pl.ds(u, half, stride=2), :] = mixed[u * half : (u + 1) * half, 128:]
    term_b = jnp.concatenate([even[...], odd[...]], axis=1)
    return term_a, term_b, term_c


def run_pick(blocks, ids, hours, own):
    grant = 4 * blocks * SIDE * hours.shape[1] + 4 * own.size + (2 << 20)
    rank = hours.shape[1]

    def kernel(ids, hours, own, out, same, sem):
        copies = []
        for t in range(blocks):
            at = pl.multiple_of(ids[8 + 4 * blocks + t] * SIDE, SIDE)
            copies.append(
                pltpu.make_async_copy(
                    hours.at[pl.ds(at, SIDE)], out.at[pl.ds(t * SIDE, SIDE)], sem.at[t]
                )
            )
            copies[-1].start()
        same[...] = own[...]
        for copy in copies:
            copy.wait()

    return pl.pallas_call(
        kernel,
        in_specs=[SMEM, HBM, VMEM],
        out_specs=[VMEM, VMEM],
        out_shape=[
            jax.ShapeDtypeStruct((blocks * SIDE, rank), BF16),
            jax.ShapeDtypeStruct(own.shape, BF16),
        ],
        scratch_shapes=[pltpu.SemaphoreType.DMA((blocks,))],
        compiler_params=pltpu.CompilerParams(vmem_limit_bytes=grant),
        name="pick_hours",
    )(ids, hours, own)


def main_kernel(shape, ids, counts, hours, *refs):
    grps, devs, local, hour_rows = shape
    depth = devs // 2
    pieces, refs = refs[:-11], refs[-11:]
    hd_acc, s_acc, hd_send, s_send, ring, table, cube, even, odd, ring_sem, in_sem = refs
    blocks = counts.shape[0]
    hour_part = hour_rows // (2 * grps)
    hour_blocks = hour_part // SIDE
    dst_part = local // grps
    part = hour_part + depth * dst_part
    base = 8

    def fetch(t):
        slot = lax.rem(t, RING)
        return pltpu.make_async_copy(counts.at[t], ring.at[slot], ring_sem.at[slot])

    for t in range(min(RING, blocks)):
        fetch(t).start()
    loads, at = [], 0
    for m, piece in enumerate(pieces):
        rows = piece.shape[0]
        loads.append(pltpu.make_async_copy(piece, table.at[pl.ds(at, rows)], in_sem.at[m]))
        loads[-1].start()
        at += rows
    hd_acc[...] = jnp.zeros_like(hd_acc)
    s_acc[...] = jnp.zeros_like(s_acc)
    for load in loads:
        load.wait()
    me, grp = ids[0], ids[1]
    core = me & 1

    def visit(t, carry):
        src_from = ids[base + t] ^ me
        src_slot = ids[base + blocks + t]
        dst_from = ids[base + 2 * blocks + t] ^ me
        dst_slot = ids[base + 3 * blocks + t]
        hour = ids[base + 4 * blocks + t]
        fetch(t).wait()
        slot = lax.rem(t, RING)
        row = dst_slot * SIDE
        turn = (row // dst_part) ^ grp
        inner = (dst_from >> 1) * dst_part + row % dst_part
        outer = (src_from >> 1) * local + src_slot * SIDE
        half = depth * local
        a_at = pl.multiple_of((src_from & 1) * (2 * half) + outer, SIDE)
        b_at = (dst_from & 1) * (2 * half) + half + turn * (depth * dst_part) + inner
        b_at = pl.multiple_of(b_at, SIDE)
        term_a, term_b, term_c = block_terms(
            ring.at[slot],
            table[pl.ds(a_at, SIDE), :],
            table[pl.ds(b_at, SIDE), :],
            hours[pl.ds(pl.multiple_of(t * SIDE, SIDE), SIDE), :],
            cube,
            even,
            odd,
        )
        s_at = pl.multiple_of((src_from & 1) * half + outer, SIDE)
        d_at = ((dst_from & 1) * grps + turn) * part + hour_part + inner
        home = hour // hour_blocks
        h_at = (((home // grps) ^ core) * grps + ((home % grps) ^ grp)) * part
        h_at = h_at + (hour % hour_blocks) * SIDE
        s_acc[pl.ds(s_at, SIDE), :] += term_a
        hd_acc[pl.ds(pl.multiple_of(d_at, SIDE), SIDE), :] += term_b
        hd_acc[pl.ds(pl.multiple_of(h_at, SIDE), SIDE), :] += term_c

        @pl.when(t + RING < blocks)
        def _():
            fetch(t + RING).start()

        return carry

    lax.fori_loop(0, blocks, visit, 0)
    hd_half, s_half = grps * part, depth * local
    hd_send[...] = hd_acc[pl.ds(hd_half, hd_half), :].astype(BF16)
    s_send[...] = s_acc[pl.ds(s_half, s_half), :].astype(BF16)


def size_of(shapes):
    return sum(jnp.dtype(t).itemsize * functools.reduce(lambda x, y: x * y, s) for s, t in shapes)


def run_main(shape, ids, counts, hours, pieces):
    grps, devs, local, hour_rows = shape
    rank = hours.shape[1]
    hd_rows = hour_rows + devs * local
    outs = [
        ((hd_rows, rank), F32),
        ((devs * local, rank), F32),
        ((hd_rows // 2, rank), BF16),
        ((devs * local // 2, rank), BF16),
    ]
    scratch = [
        ((RING,) + counts.shape[1:], BF16),
        ((devs * 2 * local, rank), BF16),
        ((SIDE // 2 * PITCH, 128), F32),
        ((SIDE, 128), F32),
        ((SIDE, 128), F32),
    ]
    need = max(size_of(outs) + size_of(scratch) + (8 << 20), GRANT)
    return pl.pallas_call(
        functools.partial(main_kernel, shape),
        in_specs=[SMEM, HBM, VMEM] + [ANY] * len(pieces),
        out_specs=[VMEM] * 4,
        out_shape=[jax.ShapeDtypeStruct(s, t) for s, t in outs],
        scratch_shapes=[pltpu.VMEM(s, t) for s, t in scratch]
        + [pltpu.SemaphoreType.DMA((RING,)), pltpu.SemaphoreType.DMA((len(pieces),))],
        compiler_params=pltpu.CompilerParams(vmem_limit_bytes=need),
        cost_estimate=pl.CostEstimate(
            flops=8 * counts.size * rank,
            bytes_accessed=counts.size * 2,
            transcendentals=counts.size,
        ),
        name="terms",
    )(ids, counts, hours, *pieces)


def call(kernel, name, ins, outs, specs=None, scratch=()):
    shapes = [(x.shape, x.dtype) for x in ins] + list(outs) + list(scratch)
    return pl.pallas_call(
        kernel,
        in_specs=specs or [VMEM] * len(ins),
        out_specs=[VMEM] * len(outs),
        out_shape=[jax.ShapeDtypeStruct(s, t) for s, t in outs],
        scratch_shapes=[pltpu.VMEM(s, t) for s, t in scratch],
        compiler_params=pltpu.CompilerParams(vmem_limit_bytes=size_of(shapes) + (4 << 20)),
        name=name,
    )(*ins)


def shares(rows, rank, ways):
    return [((rows, rank), F32)] + [((rows, rank), BF16)] * (ways - 1)


def run_cut(ways, acc, got, name):
    rows, rank = got.shape[0] // ways, got.shape[1]

    def kernel(acc, got, *outs):
        for m in range(ways):
            at = pl.ds(m * rows, rows)
            outs[m][...] = (acc[at, :] + got[at, :].astype(F32)).astype(outs[m].dtype)

    return call(kernel, name, (acc, got), shares(rows, rank, ways))


def total(refs):
    acc = refs[0][...]
    for r in refs[1:]:
        acc = acc + r[...].astype(F32)
    return acc


def run_grp(hour_part, depth, ids, parts):
    rows, rank = parts[0].shape
    ways = len(parts)
    each, dst_rows = hour_part // depth, (rows - hour_part) // depth

    def kernel(ids, *refs):
        outs, acc = refs[ways:-1], refs[-1]
        z = ids[0] >> 1
        acc[...] = total(refs[:ways])
        for m in range(depth):
            kind = outs[m].dtype
            at = pl.multiple_of((z ^ m) * each, each)
            outs[m][pl.ds(0, each), :] = acc[pl.ds(at, each), :].astype(kind)
            at = hour_part + m * dst_rows
            outs[m][pl.ds(each, dst_rows), :] = acc[pl.ds(at, dst_rows), :].astype(kind)

    return call(
        kernel,
        "grp_sum",
        (ids, *parts),
        shares(each + dst_rows, rank, depth),
        specs=[SMEM] + [VMEM] * ways,
        scratch=[((rows, rank), F32)],
    )


def run_z(hd_parts, s_parts, hour_rows):
    n = len(hd_parts)
    rows, rank = hd_parts[0].shape

    def kernel(*refs):
        hour, dst, src = refs[2 * n :]
        acc = total(refs[:n]) * (1.0 / SIDE)
        hour[...] = acc[:hour_rows].astype(BF16)
        dst[...] = acc[hour_rows:].astype(BF16)
        src[...] = total(refs[n : 2 * n]) * (1.0 / SIDE)

    outs = [((hour_rows, rank), BF16), ((rows - hour_rows, rank), BF16), (s_parts[0].shape, F32)]
    return call(kernel, "z_sum", (*hd_parts, *s_parts), outs)


def run_join(parts):
    rows = [p.shape[0] for p in parts]

    def kernel(*refs):
        at = 0
        for ref, n in zip(refs[:-1], rows):
            refs[-1][at : at + n, :] = ref[...]
            at += n

    return call(kernel, "join", parts, [((sum(rows), parts[0].shape[1]), BF16)])[0]


def run_place(sizes, hour_rows, ids, parts, so_far, dst_rows=0, passed=()):
    grps, devs = sizes
    depth = devs // 2
    arrays = [p for p, _, _ in parts]
    rank = arrays[0].shape[1]
    part = hour_rows // (2 * grps)
    rows = part // depth
    n = len(parts)
    more = [] if so_far is None else [so_far]

    def kernel(ids, *refs):
        outs = refs[n + len(more) : -2]
        for i in passed:
            outs[-1][...] = refs[i][...]
        stage, sem = refs[-2:]
        core, z, grp = ids[0] & 1, ids[0] >> 1, ids[1]
        copies = []
        for i, (_, far, m) in enumerate(parts):
            if dst_rows and not far:
                at = pl.multiple_of((grp ^ m) * dst_rows, dst_rows)
                outs[1][pl.ds(at, dst_rows), :] = refs[i][pl.ds(part, dst_rows), :].astype(F32)
            if far is None:
                continue
            for k in range(depth):
                at = pl.multiple_of((z ^ k) * rows, rows)
                stage[i, pl.ds(at, rows), :] = refs[i][pl.ds(k * rows, rows), :].astype(F32)
            home = pl.multiple_of(((core ^ far) * grps + (grp ^ m)) * part, part)
            copies.append(
                pltpu.make_async_copy(stage.at[i], outs[0].at[pl.ds(home, part)], sem.at[i])
            )
            copies[-1].start()
        for copy in copies:
            copy.wait()

    outs = [jax.ShapeDtypeStruct((hour_rows, rank), F32)]
    if dst_rows:
        outs.append(jax.ShapeDtypeStruct((grps * dst_rows, rank), F32))
    outs += [jax.ShapeDtypeStruct(arrays[i].shape, BF16) for i in passed]
    scratch = [((n, part, rank), F32)]
    need = size_of([(p.shape, p.dtype) for p in arrays + outs[1:]] + scratch) + (4 << 20)
    return pl.pallas_call(
        kernel,
        in_specs=[SMEM] + [VMEM] * n + [HBM] * len(more),
        out_specs=[HBM] + [VMEM] * (len(outs) - 1),
        out_shape=outs,
        scratch_shapes=[pltpu.VMEM(s, t) for s, t in scratch] + [pltpu.SemaphoreType.DMA((n,))],
        input_output_aliases={n + 1: 0} if more else {},
        compiler_params=pltpu.CompilerParams(vmem_limit_bytes=need),
        name="place",
    )(ids, *arrays, *more)


def per_device(
    sizes,
    counts,
    src_factor,
    dst_factor,
    hour_factor,
    src_owner,
    src_slot,
    dst_owner,
    dst_slot,
    hour_block,
):
    grps, devs = sizes
    depth = devs // 2
    local = src_factor.shape[0]
    hour_rows = hour_factor.shape[0]
    me = lax.axis_index("dev").astype(jnp.int32)
    grp = lax.axis_index("grp").astype(jnp.int32)
    place = jnp.stack([me, grp] + [me * 0] * 6)
    ids = jnp.concatenate(
        [place, src_owner[:, 0], src_slot, dst_owner[:, 0], dst_slot, hour_block]
    )
    dst_part = local // grps
    dst_own = lax.dynamic_slice_in_dim(dst_factor, grp * dst_part, dst_part, 0)
    dst_z = [dst_own] + [swap(dst_own, "dev", devs, 2 * m) for m in range(1, depth)]
    src_z = [swap(src_factor, "dev", devs, 2 * m) for m in range(2, depth)]
    picked, src_same = run_pick(counts.shape[0], ids, hour_factor, src_factor)
    src_z = [src_factor, swap(src_same, "dev", devs, 2)] + src_z
    dst_here = run_join(dst_z)
    dsts = [dst_here] + [swap(dst_here, "grp", grps, m) for m in range(1, grps)]
    near = run_join(src_z + dsts)
    far = swap(near, "dev", devs, 1)
    shape = (grps, devs, local, hour_rows)
    hd_acc, s_acc, hd_send, s_send = run_main(shape, ids, counts, picked, [near, far])

    def exchange(parts, axis, size, step):
        return [parts[0]] + [swap(x, axis, size, step * m) for m, x in enumerate(parts) if m]

    hd_got = swap(hd_send, "dev", devs, 1)
    s_got = swap(s_send, "dev", devs, 1)
    hd = run_cut(grps, hd_acc, hd_got, "core_hours_dst")
    srcs = run_cut(depth, s_acc, s_got, "core_src")
    hour_part = hour_rows // (2 * grps)
    hd = run_grp(hour_part, depth, ids, exchange(hd, "grp", grps, 1))
    srcs = exchange(srcs, "dev", devs, 2)
    hour_each = hour_part // depth
    hour, dst, grad_src = run_z(exchange(hd, "dev", devs, 2), srcs, hour_each)
    back = [hour] + [swap(hour, "dev", devs, 2 * m) for m in range(1, depth)]
    joined = run_join(back + [dst])
    near = [joined] + [swap(joined, "grp", grps, m) for m in range(1, grps)]
    parts = [(x, 0, m) for m, x in enumerate(near)]
    parts += [(swap(x, "dev", devs, 1), 1, m) for m, x in enumerate(near)]
    grad_hour, grad_dst = run_place(sizes, hour_rows, ids, parts, None, dst_part)
    return grad_src, grad_dst, grad_hour


def solution(mesh):
    in_specs = (
        P(("grp", "dev"), None, None),
        P(("grp", "dev"), None),
        P("dev", None),
        P(),
        P(("grp", "dev"), None),
        P(("grp", "dev")),
        P(("grp", "dev"), None),
        P(("grp", "dev")),
        P(("grp", "dev")),
    )
    out_specs = (P(("grp", "dev"), None), P("dev", None), P())
    return jax.shard_map(
        functools.partial(per_device, mesh_sizes(mesh)),
        mesh=mesh,
        in_specs=in_specs,
        out_specs=out_specs,
        check_vma=False,
    )
```

time: 147 us -> 141 us (0.959)
  starting transfers between devices: 36.5 us -> 40.2 us
  waiting for transfers between devices: 44.6 us -> 40.9 us
  local copies, waits for them, and re-layouts: 6.7 us -> 3.31 us
  Pallas kernels: 57.7 us -> 55.5 us
    ppermute x34 -> x31, waiting for transfers between devices: 44.6 us -> 40.9 us  [swap(): return lax.ppermute(x, axis, [(i, i ^ mask) for i in range(size)])]
    ppermute x34 -> x31, starting transfers between devices: 36.5 us -> 40.2 us  [swap(): return lax.ppermute(x, axis, [(i, i ^ mask) for i in range(size)])]
    unnamed x14 -> x8, local copies, waits for them, and re-layouts: 5.41 us -> 2.51 us
    pallas_call x2 -> x1, Pallas kernels: 4.55 us -> 3.35 us  [run_place(): pl.pallas_call(kernel, in_specs=[SMEM] + [VMEM] * n + [HBM] * len(more),...]
  transfers between devices with their start and end apart: 34 -> 31, of which waited for: 13 -> 17; matrix products, arithmetic and copies ran while one was open for 1% -> 1% of each run, Pallas kernels for 5% -> 2%
where the time goes in v3:
time: 141 us
  Pallas kernels  55.5 us (39%)
  waiting for transfers between devices  40.9 us (29%)
  starting transfers between devices  40.2 us (29%)
  local copies, waits for them, and re-layouts  3.31 us (2%)
    pallas_call x1, Pallas kernels, run_main(): pl.pallas_call(functools.partial(main_kernel, shape), in_specs=[SMEM, HBM...  48.1 us
    ppermute x31, waiting for transfers between devices, swap(): return lax.ppermute(x, axis, [(i, i ^ mask) for i in range(size)])  40.9 us
    ppermute x31, starting transfers between devices, swap(): return lax.ppermute(x, axis, [(i, i ^ mask) for i in range(size)])  40.2 us
    pallas_call x1, Pallas kernels, run_place(): pl.pallas_call(kernel, in_specs=[SMEM] + [VMEM] * n + [HBM] * len(more),...  3.35 us
  transfers between devices with their start and end apart: 31, of which 17 were waited for; matrix products, arithmetic and copies ran while one was open for 1% of the time, Pallas kernels for 2%

profile of v3, /device:TPU:0, one launch (start us, length us, event | category | flops | bytes accessed | tf_op | source)
XLA Modules:
  0.0 140.7 jit_solution(13500254976575533263)
XLA Ops:
  0.6 4.1 %collective-permute-start.1 = (bf16[256,256]{1,0:T(8,128)(2,1)}, bf16[256,256]{1,0:T(8,128)(2,1)S(1)}, u32[]{:S(2)}, u32[]{:S(2)}) collective-permute-start(bf16[256,256]{1,0:T(8,128)(2,1)} %refs_0_.1), channel_id=1, source_target_pairs={{0,4},{1,5},{2,6},{3,7},{4,0},{5,1},{6,2},{7,3},{8,12},{9,13},{10,... | collective-permute-start | bytes 393224 | tf_op jit(solution)/shard_map/ppermute | solution.py:28
  4.8 1.8 %collective-permute-start.5 = (bf16[64,256]{1,0:T(8,128)(2,1)S(1)}, bf16[64,256]{1,0:T(8,128)(2,1)S(1)}, u32[]{:S(2)}, u32[]{:S(2)}) collective-permute-start(bf16[64,256]{1,0:T(8,128)(2,1)S(1)} %constant_dynamic-slice_fusion.refs_0_), channel_id=1, source_target_pairs={{0,6},{1,7},{2,4},{3,5},{4,2},{5,3},{6,0},{7,1},{8,14},{9,15},{10,... | collective-permute-start | bytes 98312 | tf_op jit(solution)/shard_map/ppermute | solution.py:28
  6.6 1.2 collective-permute-start.4
  7.8 1.3 collective-permute-start.3
  9.1 1.8 %collective-permute-start.2 = (bf16[256,256]{1,0:T(8,128)(2,1)}, bf16[256,256]{1,0:T(8,128)(2,1)S(1)}, u32[]{:S(2)}, u32[]{:S(2)}) collective-permute-start(bf16[256,256]{1,0:T(8,128)(2,1)} %refs_0_.1), channel_id=1, source_target_pairs={{0,6},{1,7},{2,4},{3,5},{4,2},{5,3},{6,0},{7,1},{8,14},{9,15},{10,... | collective-permute-start | bytes 393224 | tf_op jit(solution)/shard_map/ppermute | solution.py:28
  11.8 1.6 %copy-done.1 = bf16[4096,256]{1,0:T(8,128)(2,1)S(1)} copy-done((bf16[4096,256]{1,0:T(8,128)(2,1)S(1)}, bf16[4096,256]{1,0:T(8,128)(2,1)}, u32[]{:S(2)}) %copy-start.1) | copy-done | bytes 2097176
  14.3 1.9 %pick_hours.1 = (bf16[1536,256]{1,0:T(8,128)(2,1)S(1)}, bf16[256,256]{1,0:T(8,128)(2,1)S(1)}) custom-call(s32[128]{0:T(128)S(1)} %concatenate.3.ids, bf16[4096,256]{1,0:T(8,128)(2,1)S(1)} %copy-done.1, bf16[256,256]{1,0:T(8,128)(2,1)S(1)} %copy-done.2), custom_call_target="tpu_custom_call" | custom-call | tf_op jit(solution)/shard_map/pick_hours/pallas_call | solution.py:99
  16.2 1.4 collective-permute-start
  17.7 2.9 %collective-permute-start.8 = (bf16[256,256]{1,0:T(8,128)(2,1)S(1)}, bf16[256,256]{1,0:T(8,128)(2,1)S(1)}, u32[]{:S(2)}, u32[]{:S(2)}) collective-permute-start(bf16[256,256]{1,0:T(8,128)(2,1)S(1)} %join.3.refs_4_), channel_id=1, source_target_pairs={{0,24},{8,16},{16,8},{24,0},{1,25},{9,17},{17,9},{25,1},{2,26},{10... | collective-permute-start | bytes 393224 | tf_op jit(solution)/shard_map/ppermute | solution.py:28
  21.3 3.4 %collective-permute-done.8.refs_7_ = bf16[256,256]{1,0:T(8,128)(2,1)S(1)} collective-permute-done((bf16[256,256]{1,0:T(8,128)(2,1)S(1)}, bf16[256,256]{1,0:T(8,128)(2,1)S(1)}, u32[]{:S(2)}, u32[]{:S(2)}) %collective-permute-start.8) | collective-permute-done | bytes 131104 | tf_op jit(solution)/shard_map/ppermute | solution.py:28
  24.7 1.1 collective-permute-done.7.refs_6_
  26.2 2.6 %collective-permute-done.9.refs_1_ = bf16[2048,256]{1,0:T(8,128)(2,1)S(1)} collective-permute-done((bf16[2048,256]{1,0:T(8,128)(2,1)S(1)}, bf16[2048,256]{1,0:T(8,128)(2,1)S(1)}, u32[]{:S(2)}, u32[]{:S(2)}) %collective-permute-start.9) | collective-permute-done | bytes 1048608 | tf_op jit(solution)/shard_map/ppermute | solution.py:28
  28.9 48.1 %terms.1 = (f32[6144,256]{1,0:T(8,128)S(1)}, f32[2048,256]{1,0:T(8,128)S(1)}, bf16[3072,256]{1,0:T(8,128)(2,1)S(1)}, bf16[1024,256]{1,0:T(8,128)(2,1)S(1)}) custom-call(s32[128]{0:T(128)S(1)} %concatenate.3.ids, bf16[24,64,4096]{2,1,0:T(8,128)(2,1)} %counts.1, bf16[1536,256]{1,0:T(8,128)(2,1)S(1)} %get-tuple-element.26.hours, ...), custom_call_target="tpu_custom_call" | custom-call | flops 12884901888 | bytes 12582912 | tf_op jit(solution)/shard_map/terms/pallas_call | solution.py:212
  77.6 2.9 %collective-permute-done.10.got = bf16[3072,256]{1,0:T(8,128)(2,1)S(1)} collective-permute-done((bf16[3072,256]{1,0:T(8,128)(2,1)S(1)}, bf16[3072,256]{1,0:T(8,128)(2,1)S(1)}, u32[]{:S(2)}, u32[]{:S(2)}) %collective-permute-start.10) | collective-permute-done | bytes 1572896 | tf_op jit(solution)/shard_map/ppermute | solution.py:28
  80.8 1.5 %collective-permute-start.11 = (bf16[768,256]{1,0:T(8,128)(2,1)S(1)}, bf16[768,256]{1,0:T(8,128)(2,1)S(1)}, u32[]{:S(2)}, u32[]{:S(2)}) collective-permute-start(bf16[768,256]{1,0:T(8,128)(2,1)S(1)} %get-tuple-element.31), channel_id=1, source_target_pairs={{0,8},{8,0},{16,24},{24,16},{1,9},{9,1},{17,25},{25,17},{2,10},{10... | collective-permute-start | bytes 1179656 | tf_op jit(solution)/shard_map/ppermute | solution.py:28
  83.0 1.4 %collective-permute-start.13 = (bf16[768,256]{1,0:T(8,128)(2,1)S(1)}, bf16[768,256]{1,0:T(8,128)(2,1)S(1)}, u32[]{:S(2)}, u32[]{:S(2)}) collective-permute-start(bf16[768,256]{1,0:T(8,128)(2,1)S(1)} %get-tuple-element.33), channel_id=1, source_target_pairs={{0,24},{8,16},{16,8},{24,0},{1,25},{9,17},{17,9},{25,1},{2,26},{10... | collective-permute-start | bytes 1179656 | tf_op jit(solution)/shard_map/ppermute | solution.py:28
  85.4 3.3 %collective-permute-start.19 = (bf16[256,256]{1,0:T(8,128)(2,1)S(1)}, bf16[256,256]{1,0:T(8,128)(2,1)S(1)}, u32[]{:S(2)}, u32[]{:S(2)}) collective-permute-start(bf16[256,256]{1,0:T(8,128)(2,1)S(1)} %get-tuple-element.42), channel_id=1, source_target_pairs={{0,4},{1,5},{2,6},{3,7},{4,0},{5,1},{6,2},{7,3},{8,12},{9,13},{10,... | collective-permute-start | bytes 393224 | tf_op jit(solution)/shard_map/ppermute | solution.py:28
  88.8 4.1 %collective-permute-done.11.refs_1_ = bf16[768,256]{1,0:T(8,128)(2,1)S(1)} collective-permute-done((bf16[768,256]{1,0:T(8,128)(2,1)S(1)}, bf16[768,256]{1,0:T(8,128)(2,1)S(1)}, u32[]{:S(2)}, u32[]{:S(2)}) %collective-permute-start.11) | collective-permute-done | bytes 393248 | tf_op jit(solution)/shard_map/ppermute | solution.py:28
  92.8 3.6 %collective-permute-start.20 = (bf16[256,256]{1,0:T(8,128)(2,1)S(1)}, bf16[256,256]{1,0:T(8,128)(2,1)S(1)}, u32[]{:S(2)}, u32[]{:S(2)}) collective-permute-start(bf16[256,256]{1,0:T(8,128)(2,1)S(1)} %get-tuple-element.43), channel_id=1, source_target_pairs={{0,6},{1,7},{2,4},{3,5},{4,2},{5,3},{6,0},{7,1},{8,14},{9,15},{10,... | collective-permute-start | bytes 393224 | tf_op jit(solution)/shard_map/ppermute | solution.py:28
  96.5 5.1 %collective-permute-done.12.refs_2_ = bf16[768,256]{1,0:T(8,128)(2,1)S(1)} collective-permute-done((bf16[768,256]{1,0:T(8,128)(2,1)S(1)}, bf16[768,256]{1,0:T(8,128)(2,1)S(1)}, u32[]{:S(2)}, u32[]{:S(2)}) %collective-permute-start.12) | collective-permute-done | bytes 393248 | tf_op jit(solution)/shard_map/ppermute | solution.py:28
  103.4 3.4 %collective-permute-start.15 = (bf16[192,256]{1,0:T(8,128)(2,1)S(1)}, bf16[192,256]{1,0:T(8,128)(2,1)S(1)}, u32[]{:S(2)}, u32[]{:S(2)}) collective-permute-start(bf16[192,256]{1,0:T(8,128)(2,1)S(1)} %get-tuple-element.36), channel_id=1, source_target_pairs={{0,4},{1,5},{2,6},{3,7},{4,0},{5,1},{6,2},{7,3},{8,12},{9,13},{10,... | collective-permute-start | bytes 294920 | tf_op jit(solution)/shard_map/ppermute | solution.py:28
  106.9 1.1 collective-permute-done.14.refs_1_
  108.0 5.8 %collective-permute-done.15.refs_2_ = bf16[192,256]{1,0:T(8,128)(2,1)S(1)} collective-permute-done((bf16[192,256]{1,0:T(8,128)(2,1)S(1)}, bf16[192,256]{1,0:T(8,128)(2,1)S(1)}, u32[]{:S(2)}, u32[]{:S(2)}) %collective-permute-start.15) | collective-permute-done | bytes 98336 | tf_op jit(solution)/shard_map/ppermute | solution.py:28
  114.6 2.5 %collective-permute-start.23 = (bf16[128,256]{1,0:T(8,128)(2,1)S(1)}, bf16[128,256]{1,0:T(8,128)(2,1)S(1)}, u32[]{:S(2)}, u32[]{:S(2)}) collective-permute-start(bf16[128,256]{1,0:T(8,128)(2,1)S(1)} %get-tuple-element.45.refs_0_), channel_id=1, source_target_pairs={{0,6},{1,7},{2,4},{3,5},{4,2},{5,3},{6,0},{7,1},{8,14},{9,15},{10,... | collective-permute-start | bytes 196616 | tf_op jit(solution)/shard_map/ppermute | solution.py:28
  117.9 1.1 collective-permute-start.21
  118.9 2.1 %collective-permute-done.23.refs_3_ = bf16[128,256]{1,0:T(8,128)(2,1)S(1)} collective-permute-done((bf16[128,256]{1,0:T(8,128)(2,1)S(1)}, bf16[128,256]{1,0:T(8,128)(2,1)S(1)}, u32[]{:S(2)}, u32[]{:S(2)}) %collective-permute-start.23) | collective-permute-done | bytes 65568 | tf_op jit(solution)/shard_map/ppermute | solution.py:28
  121.1 1.2 collective-permute-done.22.refs_2_
  122.9 1.6 %collective-permute-start.26 = (bf16[576,256]{1,0:T(8,128)(2,1)S(1)}, bf16[576,256]{1,0:T(8,128)(2,1)S(1)}, u32[]{:S(2)}, u32[]{:S(2)}) collective-permute-start(bf16[576,256]{1,0:T(8,128)(2,1)S(1)} %join.5.refs_0_), channel_id=1, source_target_pairs={{0,24},{8,16},{16,8},{24,0},{1,25},{9,17},{17,9},{25,1},{2,26},{10... | collective-permute-start | bytes 884744 | tf_op jit(solution)/shard_map/ppermute | solution.py:28
  125.2 1.2 collective-permute-start.24
  126.4 5.9 %collective-permute-done.26.refs_3_ = bf16[576,256]{1,0:T(8,128)(2,1)S(1)} collective-permute-done((bf16[576,256]{1,0:T(8,128)(2,1)S(1)}, bf16[576,256]{1,0:T(8,128)(2,1)S(1)}, u32[]{:S(2)}, u32[]{:S(2)}) %collective-permute-start.26) | collective-permute-done | bytes 294944 | tf_op jit(solution)/shard_map/ppermute | solution.py:28
  132.3 3.0 %collective-permute-done.25.refs_2_ = bf16[576,256]{1,0:T(8,128)(2,1)S(1)} collective-permute-done((bf16[576,256]{1,0:T(8,128)(2,1)S(1)}, bf16[576,256]{1,0:T(8,128)(2,1)S(1)}, u32[]{:S(2)}, u32[]{:S(2)}) %collective-permute-start.25) | collective-permute-done | bytes 294944 | tf_op jit(solution)/shard_map/ppermute | solution.py:28
  137.3 3.3 %place.1 = (f32[4096,256]{1,0:T(8,128)}, f32[256,256]{1,0:T(8,128)}) custom-call(s32[128]{0:T(128)S(1)} %concatenate.3.ids, bf16[576,256]{1,0:T(8,128)(2,1)S(1)} %join.5.refs_0_, bf16[576,256]{1,0:T(8,128)(2,1)S(1)} %collective-permute-done.24.refs_1_, bf16[576,256]{1,0:T(8,128)(2,1)S(1)} %collective-permute-done.25.refs_2_, ...), custom_call_target="tpu_custom_call" | custom-call | tf_op jit(solution)/shard_map/place/pallas_call | solution.py:357
  (52 shorter events, 12.4 us)
Async XLA Ops:
  0.6 20.5 %collective-permute-start.1 = (bf16[256,256]{1,0:T(8,128)(2,1)}, bf16[256,256]{1,0:T(8,128)(2,1)S(1)}, u32[]{:S(2)}, u32[]{:S(2)}) collective-permute-start(bf16[256,256]{1,0:T(8,128)(2,1)} %refs_0_.1), channel_id=1, source_target_pairs={{0,4},{1,5},{2,6},{3,7},{4,0},{5,1},{6,2},{7,3},{8,12},{9,13},{10,... | collective-permute-start | bytes 393224 | tf_op jit(solution)/shard_map/ppermute | solution.py:28
  4.8 11.4 %collective-permute-start.5 = (bf16[64,256]{1,0:T(8,128)(2,1)S(1)}, bf16[64,256]{1,0:T(8,128)(2,1)S(1)}, u32[]{:S(2)}, u32[]{:S(2)}) collective-permute-start(bf16[64,256]{1,0:T(8,128)(2,1)S(1)} %constant_dynamic-slice_fusion.refs_0_), channel_id=1, source_target_pairs={{0,6},{1,7},{2,4},{3,5},{4,2},{5,3},{6,0},{7,1},{8,14},{9,15},{10,... | collective-permute-start | bytes 98312 | tf_op jit(solution)/shard_map/ppermute | solution.py:28
  6.6 11.1 %collective-permute-start.4 = (bf16[64,256]{1,0:T(8,128)(2,1)S(1)}, bf16[64,256]{1,0:T(8,128)(2,1)S(1)}, u32[]{:S(2)}, u32[]{:S(2)}) collective-permute-start(bf16[64,256]{1,0:T(8,128)(2,1)S(1)} %constant_dynamic-slice_fusion.refs_0_), channel_id=1, source_target_pairs={{0,4},{1,5},{2,6},{3,7},{4,0},{5,1},{6,2},{7,3},{8,12},{9,13},{10,... | collective-permute-start | bytes 98312 | tf_op jit(solution)/shard_map/ppermute | solution.py:28
  7.8 9.9 %collective-permute-start.3 = (bf16[64,256]{1,0:T(8,128)(2,1)S(1)}, bf16[64,256]{1,0:T(8,128)(2,1)S(1)}, u32[]{:S(2)}, u32[]{:S(2)}) collective-permute-start(bf16[64,256]{1,0:T(8,128)(2,1)S(1)} %constant_dynamic-slice_fusion.refs_0_), channel_id=1, source_target_pairs={{0,2},{1,3},{2,0},{3,1},{4,6},{5,7},{6,4},{7,5},{8,10},{9,11},{10,... | collective-permute-start | bytes 98312 | tf_op jit(solution)/shard_map/ppermute | solution.py:28
  9.1 12.1 %collective-permute-start.2 = (bf16[256,256]{1,0:T(8,128)(2,1)}, bf16[256,256]{1,0:T(8,128)(2,1)S(1)}, u32[]{:S(2)}, u32[]{:S(2)}) collective-permute-start(bf16[256,256]{1,0:T(8,128)(2,1)} %refs_0_.1), channel_id=1, source_target_pairs={{0,6},{1,7},{2,4},{3,5},{4,2},{5,3},{6,0},{7,1},{8,14},{9,15},{10,... | collective-permute-start | bytes 393224 | tf_op jit(solution)/shard_map/ppermute | solution.py:28
  14.3 11.8 %copy-start.3 = (bf16[256,256]{1,0:T(8,128)(2,1)S(1)}, bf16[256,256]{1,0:T(8,128)(2,1)}, u32[]{:S(2)}) copy-start(bf16[256,256]{1,0:T(8,128)(2,1)} %refs_0_.1) | copy-start | bytes 393220
  16.2 5.1 %collective-permute-start = (bf16[256,256]{1,0:T(8,128)(2,1)S(1)}, bf16[256,256]{1,0:T(8,128)(2,1)S(1)}, u32[]{:S(2)}, u32[]{:S(2)}) collective-permute-start(bf16[256,256]{1,0:T(8,128)(2,1)S(1)} %get-tuple-element.27), channel_id=1, source_target_pairs={{0,2},{1,3},{2,0},{3,1},{4,6},{5,7},{6,4},{7,5},{8,10},{9,11},{10,... | collective-permute-start | bytes 393224 | tf_op jit(solution)/shard_map/ppermute | solution.py:28
  17.7 7.0 %collective-permute-start.8 = (bf16[256,256]{1,0:T(8,128)(2,1)S(1)}, bf16[256,256]{1,0:T(8,128)(2,1)S(1)}, u32[]{:S(2)}, u32[]{:S(2)}) collective-permute-start(bf16[256,256]{1,0:T(8,128)(2,1)S(1)} %join.3.refs_4_), channel_id=1, source_target_pairs={{0,24},{8,16},{16,8},{24,0},{1,25},{9,17},{17,9},{25,1},{2,26},{10... | collective-permute-start | bytes 393224 | tf_op jit(solution)/shard_map/ppermute | solution.py:28
  20.6 5.3 %collective-permute-start.7 = (bf16[256,256]{1,0:T(8,128)(2,1)S(1)}, bf16[256,256]{1,0:T(8,128)(2,1)S(1)}, u32[]{:S(2)}, u32[]{:S(2)}) collective-permute-start(bf16[256,256]{1,0:T(8,128)(2,1)S(1)} %join.3.refs_4_), channel_id=1, source_target_pairs={{0,16},{8,24},{16,0},{24,8},{1,17},{9,25},{17,1},{25,9},{2,18},{10... | collective-permute-start | bytes 393224 | tf_op jit(solution)/shard_map/ppermute | solution.py:28
  21.1 5.0 %collective-permute-start.6 = (bf16[256,256]{1,0:T(8,128)(2,1)S(1)}, bf16[256,256]{1,0:T(8,128)(2,1)S(1)}, u32[]{:S(2)}, u32[]{:S(2)}) collective-permute-start(bf16[256,256]{1,0:T(8,128)(2,1)S(1)} %join.3.refs_4_), channel_id=1, source_target_pairs={{0,8},{8,0},{16,24},{24,16},{1,9},{9,1},{17,25},{25,17},{2,10},{10... | collective-permute-start | bytes 393224 | tf_op jit(solution)/shard_map/ppermute | solution.py:28
  26.1 2.7 %collective-permute-start.9 = (bf16[2048,256]{1,0:T(8,128)(2,1)S(1)}, bf16[2048,256]{1,0:T(8,128)(2,1)S(1)}, u32[]{:S(2)}, u32[]{:S(2)}) collective-permute-start(bf16[2048,256]{1,0:T(8,128)(2,1)S(1)} %join.4.refs_0_), channel_id=1, source_target_pairs={{0,1},{1,0},{2,3},{3,2},{4,5},{5,4},{6,7},{7,6},{8,9},{9,8},{10,11... | collective-permute-start | bytes 3145736 | tf_op jit(solution)/shard_map/ppermute | solution.py:28
  77.0 3.5 %collective-permute-start.10 = (bf16[3072,256]{1,0:T(8,128)(2,1)S(1)}, bf16[3072,256]{1,0:T(8,128)(2,1)S(1)}, u32[]{:S(2)}, u32[]{:S(2)}) collective-permute-start(bf16[3072,256]{1,0:T(8,128)(2,1)S(1)} %get-tuple-element.29), channel_id=1, source_target_pairs={{0,1},{1,0},{2,3},{3,2},{4,5},{5,4},{6,7},{7,6},{8,9},{9,8},{10,11... | collective-permute-start | bytes 4718600 | tf_op jit(solution)/shard_map/ppermute | solution.py:28
  77.2 7.2 %collective-permute-start.17 = (bf16[1024,256]{1,0:T(8,128)(2,1)S(1)}, bf16[1024,256]{1,0:T(8,128)(2,1)S(1)}, u32[]{:S(2)}, u32[]{:S(2)}) collective-permute-start(bf16[1024,256]{1,0:T(8,128)(2,1)S(1)} %get-tuple-element.39), channel_id=1, source_target_pairs={{0,1},{1,0},{2,3},{3,2},{4,5},{5,4},{6,7},{7,6},{8,9},{9,8},{10,11... | collective-permute-start | bytes 1572872 | tf_op jit(solution)/shard_map/ppermute | solution.py:28
  80.8 12.0 %collective-permute-start.11 = (bf16[768,256]{1,0:T(8,128)(2,1)S(1)}, bf16[768,256]{1,0:T(8,128)(2,1)S(1)}, u32[]{:S(2)}, u32[]{:S(2)}) collective-permute-start(bf16[768,256]{1,0:T(8,128)(2,1)S(1)} %get-tuple-element.31), channel_id=1, source_target_pairs={{0,8},{8,0},{16,24},{24,16},{1,9},{9,1},{17,25},{25,17},{2,10},{10... | collective-permute-start | bytes 1179656 | tf_op jit(solution)/shard_map/ppermute | solution.py:28
  82.3 19.3 %collective-permute-start.12 = (bf16[768,256]{1,0:T(8,128)(2,1)S(1)}, bf16[768,256]{1,0:T(8,128)(2,1)S(1)}, u32[]{:S(2)}, u32[]{:S(2)}) collective-permute-start(bf16[768,256]{1,0:T(8,128)(2,1)S(1)} %get-tuple-element.32), channel_id=1, source_target_pairs={{0,16},{8,24},{16,0},{24,8},{1,17},{9,25},{17,1},{25,9},{2,18},{10... | collective-permute-start | bytes 1179656 | tf_op jit(solution)/shard_map/ppermute | solution.py:28
  83.0 18.6 %collective-permute-start.13 = (bf16[768,256]{1,0:T(8,128)(2,1)S(1)}, bf16[768,256]{1,0:T(8,128)(2,1)S(1)}, u32[]{:S(2)}, u32[]{:S(2)}) collective-permute-start(bf16[768,256]{1,0:T(8,128)(2,1)S(1)} %get-tuple-element.33), channel_id=1, source_target_pairs={{0,24},{8,16},{16,8},{24,0},{1,25},{9,17},{17,9},{25,1},{2,26},{10... | collective-permute-start | bytes 1179656 | tf_op jit(solution)/shard_map/ppermute | solution.py:28
  84.5 22.3 %collective-permute-start.18 = (bf16[256,256]{1,0:T(8,128)(2,1)S(1)}, bf16[256,256]{1,0:T(8,128)(2,1)S(1)}, u32[]{:S(2)}, u32[]{:S(2)}) collective-permute-start(bf16[256,256]{1,0:T(8,128)(2,1)S(1)} %get-tuple-element.41), channel_id=1, source_target_pairs={{0,2},{1,3},{2,0},{3,1},{4,6},{5,7},{6,4},{7,5},{8,10},{9,11},{10,... | collective-permute-start | bytes 393224 | tf_op jit(solution)/shard_map/ppermute | solution.py:28
  85.4 21.5 %collective-permute-start.19 = (bf16[256,256]{1,0:T(8,128)(2,1)S(1)}, bf16[256,256]{1,0:T(8,128)(2,1)S(1)}, u32[]{:S(2)}, u32[]{:S(2)}) collective-permute-start(bf16[256,256]{1,0:T(8,128)(2,1)S(1)} %get-tuple-element.42), channel_id=1, source_target_pairs={{0,4},{1,5},{2,6},{3,7},{4,0},{5,1},{6,2},{7,3},{8,12},{9,13},{10,... | collective-permute-start | bytes 393224 | tf_op jit(solution)/shard_map/ppermute | solution.py:28
  92.8 14.1 %collective-permute-start.20 = (bf16[256,256]{1,0:T(8,128)(2,1)S(1)}, bf16[256,256]{1,0:T(8,128)(2,1)S(1)}, u32[]{:S(2)}, u32[]{:S(2)}) collective-permute-start(bf16[256,256]{1,0:T(8,128)(2,1)S(1)} %get-tuple-element.43), channel_id=1, source_target_pairs={{0,6},{1,7},{2,4},{3,5},{4,2},{5,3},{6,0},{7,1},{8,14},{9,15},{10,... | collective-permute-start | bytes 393224 | tf_op jit(solution)/shard_map/ppermute | solution.py:28
  102.4 5.6 %collective-permute-start.14 = (bf16[192,256]{1,0:T(8,128)(2,1)S(1)}, bf16[192,256]{1,0:T(8,128)(2,1)S(1)}, u32[]{:S(2)}, u32[]{:S(2)}) collective-permute-start(bf16[192,256]{1,0:T(8,128)(2,1)S(1)} %get-tuple-element.35), channel_id=1, source_target_pairs={{0,2},{1,3},{2,0},{3,1},{4,6},{5,7},{6,4},{7,5},{8,10},{9,11},{10,... | collective-permute-start | bytes 294920 | tf_op jit(solution)/shard_map/ppermute | solution.py:28
  103.4 10.3 %collective-permute-start.15 = (bf16[192,256]{1,0:T(8,128)(2,1)S(1)}, bf16[192,256]{1,0:T(8,128)(2,1)S(1)}, u32[]{:S(2)}, u32[]{:S(2)}) collective-permute-start(bf16[192,256]{1,0:T(8,128)(2,1)S(1)} %get-tuple-element.36), channel_id=1, source_target_pairs={{0,4},{1,5},{2,6},{3,7},{4,0},{5,1},{6,2},{7,3},{8,12},{9,13},{10,... | collective-permute-start | bytes 294920 | tf_op jit(solution)/shard_map/ppermute | solution.py:28
  106.8 6.9 %collective-permute-start.16 = (bf16[192,256]{1,0:T(8,128)(2,1)S(1)}, bf16[192,256]{1,0:T(8,128)(2,1)S(1)}, u32[]{:S(2)}, u32[]{:S(2)}) collective-permute-start(bf16[192,256]{1,0:T(8,128)(2,1)S(1)} %get-tuple-element.37), channel_id=1, source_target_pairs={{0,6},{1,7},{2,4},{3,5},{4,2},{5,3},{6,0},{7,1},{8,14},{9,15},{10,... | collective-permute-start | bytes 294920 | tf_op jit(solution)/shard_map/ppermute | solution.py:28
  114.6 6.5 %collective-permute-start.23 = (bf16[128,256]{1,0:T(8,128)(2,1)S(1)}, bf16[128,256]{1,0:T(8,128)(2,1)S(1)}, u32[]{:S(2)}, u32[]{:S(2)}) collective-permute-start(bf16[128,256]{1,0:T(8,128)(2,1)S(1)} %get-tuple-element.45.refs_0_), channel_id=1, source_target_pairs={{0,6},{1,7},{2,4},{3,5},{4,2},{5,3},{6,0},{7,1},{8,14},{9,15},{10,... | collective-permute-start | bytes 196616 | tf_op jit(solution)/shard_map/ppermute | solution.py:28
  117.0 5.3 %collective-permute-start.22 = (bf16[128,256]{1,0:T(8,128)(2,1)S(1)}, bf16[128,256]{1,0:T(8,128)(2,1)S(1)}, u32[]{:S(2)}, u32[]{:S(2)}) collective-permute-start(bf16[128,256]{1,0:T(8,128)(2,1)S(1)} %get-tuple-element.45.refs_0_), channel_id=1, source_target_pairs={{0,4},{1,5},{2,6},{3,7},{4,0},{5,1},{6,2},{7,3},{8,12},{9,13},{10,... | collective-permute-start | bytes 196616 | tf_op jit(solution)/shard_map/ppermute | solution.py:28
  117.9 5.0 %collective-permute-start.21 = (bf16[128,256]{1,0:T(8,128)(2,1)S(1)}, bf16[128,256]{1,0:T(8,128)(2,1)S(1)}, u32[]{:S(2)}, u32[]{:S(2)}) collective-permute-start(bf16[128,256]{1,0:T(8,128)(2,1)S(1)} %get-tuple-element.45.refs_0_), channel_id=1, source_target_pairs={{0,2},{1,3},{2,0},{3,1},{4,6},{5,7},{6,4},{7,5},{8,10},{9,11},{10,... | collective-permute-start | bytes 196616 | tf_op jit(solution)/shard_map/ppermute | solution.py:28
  122.9 9.5 %collective-permute-start.26 = (bf16[576,256]{1,0:T(8,128)(2,1)S(1)}, bf16[576,256]{1,0:T(8,128)(2,1)S(1)}, u32[]{:S(2)}, u32[]{:S(2)}) collective-permute-start(bf16[576,256]{1,0:T(8,128)(2,1)S(1)} %join.5.refs_0_), channel_id=1, source_target_pairs={{0,24},{8,16},{16,8},{24,0},{1,25},{9,17},{17,9},{25,1},{2,26},{10... | collective-permute-start | bytes 884744 | tf_op jit(solution)/shard_map/ppermute | solution.py:28
  124.5 10.9 %collective-permute-start.25 = (bf16[576,256]{1,0:T(8,128)(2,1)S(1)}, bf16[576,256]{1,0:T(8,128)(2,1)S(1)}, u32[]{:S(2)}, u32[]{:S(2)}) collective-permute-start(bf16[576,256]{1,0:T(8,128)(2,1)S(1)} %join.5.refs_0_), channel_id=1, source_target_pairs={{0,16},{8,24},{16,0},{24,8},{1,17},{9,25},{17,1},{25,9},{2,18},{10... | collective-permute-start | bytes 884744 | tf_op jit(solution)/shard_map/ppermute | solution.py:28
  125.2 10.2 %collective-permute-start.24 = (bf16[576,256]{1,0:T(8,128)(2,1)S(1)}, bf16[576,256]{1,0:T(8,128)(2,1)S(1)}, u32[]{:S(2)}, u32[]{:S(2)}) collective-permute-start(bf16[576,256]{1,0:T(8,128)(2,1)S(1)} %join.5.refs_0_), channel_id=1, source_target_pairs={{0,8},{8,0},{16,24},{24,16},{1,9},{9,1},{17,25},{25,17},{2,10},{10... | collective-permute-start | bytes 884744 | tf_op jit(solution)/shard_map/ppermute | solution.py:28
  126.4 9.4 %collective-permute-start.27 = (bf16[576,256]{1,0:T(8,128)(2,1)S(1)}, bf16[576,256]{1,0:T(8,128)(2,1)S(1)}, u32[]{:S(2)}, u32[]{:S(2)}) collective-permute-start(bf16[576,256]{1,0:T(8,128)(2,1)S(1)} %join.5.refs_0_), channel_id=1, source_target_pairs={{0,1},{1,0},{2,3},{3,2},{4,5},{5,4},{6,7},{7,6},{8,9},{9,8},{10,11... | collective-permute-start | bytes 884744 | tf_op jit(solution)/shard_map/ppermute | solution.py:28
  132.3 3.5 %collective-permute-start.30 = (bf16[576,256]{1,0:T(8,128)(2,1)S(1)}, bf16[576,256]{1,0:T(8,128)(2,1)S(1)}, u32[]{:S(2)}, u32[]{:S(2)}) collective-permute-start(bf16[576,256]{1,0:T(8,128)(2,1)S(1)} %collective-permute-done.26.refs_3_), channel_id=1, source_target_pairs={{0,1},{1,0},{2,3},{3,2},{4,5},{5,4},{6,7},{7,6},{8,9},{9,8},{10,11... | collective-permute-start | bytes 884744 | tf_op jit(solution)/shard_map/ppermute | solution.py:28
  135.3 1.6 %collective-permute-start.29 = (bf16[576,256]{1,0:T(8,128)(2,1)S(1)}, bf16[576,256]{1,0:T(8,128)(2,1)S(1)}, u32[]{:S(2)}, u32[]{:S(2)}) collective-permute-start(bf16[576,256]{1,0:T(8,128)(2,1)S(1)} %collective-permute-done.25.refs_2_), channel_id=1, source_target_pairs={{0,1},{1,0},{2,3},{3,2},{4,5},{5,4},{6,7},{7,6},{8,9},{9,8},{10,11... | collective-permute-start | bytes 884744 | tf_op jit(solution)/shard_map/ppermute | solution.py:28
  135.3 2.0 %collective-permute-start.28 = (bf16[576,256]{1,0:T(8,128)(2,1)S(1)}, bf16[576,256]{1,0:T(8,128)(2,1)S(1)}, u32[]{:S(2)}, u32[]{:S(2)}) collective-permute-start(bf16[576,256]{1,0:T(8,128)(2,1)S(1)} %collective-permute-done.24.refs_1_), channel_id=1, source_target_pairs={{0,1},{1,0},{2,3},{3,2},{4,5},{5,4},{6,7},{7,6},{8,9},{9,8},{10,11... | collective-permute-start | bytes 884744 | tf_op jit(solution)/shard_map/ppermute | solution.py:28
  (3 other events, 6.6 us)

commit v4 on v3

--- a/solution.py
+++ b/solution.py
@@ -11,8 +11,11 @@
 BF16 = jnp.bfloat16
 SIDE = 64
 RING = 8
+OUT_RING = 4
 PITCH = 72
 GRANT = 36 << 20
+SRC_GRANT = 44 << 20
+SLOW = 10**11
 
 VMEM = pl.BlockSpec(memory_space=pltpu.VMEM)
 SMEM = pl.BlockSpec(memory_space=pltpu.SMEM)
@@ -28,9 +31,9 @@
     return lax.ppermute(x, axis, [(i, i ^ mask) for i in range(size)])
 
 
-def block_terms(count, a, b, c, cube, even, odd):
+def block_terms(count, a, b, c, resid_out, cube, even, odd):
     rank = a.shape[1]
-    resids, pairs_bc, turned, pairs_ab = [], [], [], []
+    turned, pairs_ab = [], []
     for g in range(SIDE // 4):
         b4 = b[g * 4 : g * 4 + 4]
         bc = (b4[:, None, :] * c[None, :, :]).reshape(4 * SIDE, rank)
@@ -42,14 +45,8 @@
         resid = wide.astype(BF16)
         flip = resid.T
         turned += [flip[q * SIDE : (q + 1) * SIDE] for q in range(4)]
-        resids.append(resid)
-        pairs_bc.append(bc)
+        resid_out[:, g * 256 : (g + 1) * 256] = resid
         pairs_ab.append(ab)
-    term_a = jnp.dot(
-        jnp.concatenate(resids, axis=1),
-        jnp.concatenate(pairs_bc, axis=0),
-        preferred_element_type=F32,
-    )
     term_c = jnp.dot(
         jnp.concatenate(turned, axis=1),
         jnp.concatenate(pairs_ab, axis=0),
@@ -75,7 +72,7 @@
         even[pl.ds(u, half, stride=2), :] = mixed[u * half : (u + 1) * half, :128]
         odd[pl.ds(u, half, stride=2), :] = mixed[u * half : (u + 1) * half, 128:]
     term_b = jnp.concatenate([even[...], odd[...]], axis=1)
-    return term_a, term_b, term_c
+    return term_b, term_c
 
 
 def run_pick(blocks, ids, hours, own):
@@ -110,32 +107,36 @@
     )(ids, hours, own)
 
 
-def main_kernel(shape, ids, counts, hours, *refs):
+def main_kernel(shape, ids, counts, hours, near, far, *refs):
     grps, devs, local, hour_rows = shape
     depth = devs // 2
-    pieces, refs = refs[:-11], refs[-11:]
-    hd_acc, s_acc, hd_send, s_send, ring, table, cube, even, odd, ring_sem, in_sem = refs
+    hd_acc, hd_send, b_rows, resids, *refs = refs
+    ring, resid_ring, table, cube, even, odd, ring_sem, resid_sem, in_sem = refs
     blocks = counts.shape[0]
     hour_part = hour_rows // (2 * grps)
     hour_blocks = hour_part // SIDE
     dst_part = local // grps
     part = hour_part + depth * dst_part
+    half = depth * local
     base = 8
 
     def fetch(t):
         slot = lax.rem(t, RING)
         return pltpu.make_async_copy(counts.at[t], ring.at[slot], ring_sem.at[slot])
 
+    def put(t):
+        slot = lax.rem(t, OUT_RING)
+        return pltpu.make_async_copy(resid_ring.at[slot], resids.at[t], resid_sem.at[slot])
+
     for t in range(min(RING, blocks)):
         fetch(t).start()
-    loads, at = [], 0
-    for m, piece in enumerate(pieces):
-        rows = piece.shape[0]
-        loads.append(pltpu.make_async_copy(piece, table.at[pl.ds(at, rows)], in_sem.at[m]))
-        loads[-1].start()
-        at += rows
+    loads = [
+        pltpu.make_async_copy(x, table.at[pl.ds(m * 2 * half, 2 * half)], in_sem.at[m])
+        for m, x in enumerate((near, far))
+    ]
+    for load in loads:
+        load.start()
     hd_acc[...] = jnp.zeros_like(hd_acc)
-    s_acc[...] = jnp.zeros_like(s_acc)
     for load in loads:
         load.wait()
     me, grp = ids[0], ids[1]
@@ -147,33 +148,39 @@
         dst_from = ids[base + 2 * blocks + t] ^ me
         dst_slot = ids[base + 3 * blocks + t]
         hour = ids[base + 4 * blocks + t]
-        fetch(t).wait()
-        slot = lax.rem(t, RING)
         row = dst_slot * SIDE
         turn = (row // dst_part) ^ grp
         inner = (dst_from >> 1) * dst_part + row % dst_part
-        outer = (src_from >> 1) * local + src_slot * SIDE
-        half = depth * local
-        a_at = pl.multiple_of((src_from & 1) * (2 * half) + outer, SIDE)
+        a_at = (src_from & 1) * (2 * half) + (src_from >> 1) * local + src_slot * SIDE
+        a_at = pl.multiple_of(a_at, SIDE)
         b_at = (dst_from & 1) * (2 * half) + half + turn * (depth * dst_part) + inner
         b_at = pl.multiple_of(b_at, SIDE)
-        term_a, term_b, term_c = block_terms(
-            ring.at[slot],
+        here = pl.ds(pl.multiple_of(t * SIDE, SIDE), SIDE)
+        b = table[pl.ds(b_at, SIDE), :]
+        b_rows[here, :] = b
+        fetch(t).wait()
+
+        @pl.when(t >= OUT_RING)
+        def _():
+            put(t - OUT_RING).wait()
+
+        term_b, term_c = block_terms(
+            ring.at[lax.rem(t, RING)],
             table[pl.ds(a_at, SIDE), :],
-            table[pl.ds(b_at, SIDE), :],
-            hours[pl.ds(pl.multiple_of(t * SIDE, SIDE), SIDE), :],
+            b,
+            hours[here, :],
+            resid_ring.at[lax.rem(t, OUT_RING)],
             cube,
             even,
             odd,
         )
-        s_at = pl.multiple_of((src_from & 1) * half + outer, SIDE)
         d_at = ((dst_from & 1) * grps + turn) * part + hour_part + inner
         home = hour // hour_blocks
         h_at = (((home // grps) ^ core) * grps + ((home % grps) ^ grp)) * part
         h_at = h_at + (hour % hour_blocks) * SIDE
-        s_acc[pl.ds(s_at, SIDE), :] += term_a
         hd_acc[pl.ds(pl.multiple_of(d_at, SIDE), SIDE), :] += term_b
         hd_acc[pl.ds(pl.multiple_of(h_at, SIDE), SIDE), :] += term_c
+        put(t).start()
 
         @pl.when(t + RING < blocks)
         def _():
@@ -182,27 +189,80 @@
         return carry
 
     lax.fori_loop(0, blocks, visit, 0)
-    hd_half, s_half = grps * part, depth * local
+    hd_half = grps * part
     hd_send[...] = hd_acc[pl.ds(hd_half, hd_half), :].astype(BF16)
-    s_send[...] = s_acc[pl.ds(s_half, s_half), :].astype(BF16)
+    for t in range(max(0, blocks - OUT_RING), blocks):
+        put(t).wait()
+
+
+def src_kernel(shape, first, last, ids, resids, b_rows, hours, after, *refs):
+    devs, local = shape
+    depth = devs // 2
+    fresh = first == 0
+    blocks = resids.shape[0]
+    refs = refs if fresh else refs[1:]
+    s_acc, *sends, ring, sem = refs
+    me, base = ids[0], 8
+
+    def fetch(t):
+        slot = lax.rem(t - first, RING)
+        return pltpu.make_async_copy(resids.at[t], ring.at[slot], sem.at[slot])
+
+    for t in range(first, min(first + RING, last)):
+        fetch(t).start()
+    if fresh:
+        s_acc[...] = jnp.zeros_like(s_acc)
+
+    def visit(t, carry):
+        src_from = ids[base + t] ^ me
+        src_slot = ids[base + blocks + t]
+        z, order, steps = src_from >> 1, 0, depth // 2
+        while steps:
+            order = order + (z & 1) * steps
+            z, steps = z >> 1, steps // 2
+        s_at = ((src_from & 1) * depth + order) * local + src_slot * SIDE
+        s_at = pl.multiple_of(s_at, SIDE)
+        here = pl.ds(pl.multiple_of(t * SIDE, SIDE), SIDE)
+        b, c = b_rows[here, :], hours[here, :]
+        fetch(t).wait()
+        resid = ring[lax.rem(t - first, RING)]
+        pairs = [
+            (b[g * 4 : g * 4 + 4][:, None, :] * c[None, :, :]).reshape(4 * SIDE, b.shape[1])
+            for g in range(SIDE // 4)
+        ]
+        terms = []
+        for at in range(0, b.shape[1], 128):
+            columns = jnp.concatenate([p[:, at : at + 128] for p in pairs], axis=0)
+            terms.append(jnp.dot(resid, columns, preferred_element_type=F32))
+        s_acc[pl.ds(s_at, SIDE), :] += jnp.concatenate(terms, axis=1)
+
+        @pl.when(t + RING < last)
+        def _():
+            fetch(t + RING).start()
+
+        return carry
+
+    lax.fori_loop(first, last, visit, 0)
+    for send in sends:
+        send[...] = s_acc[pl.ds(depth * local, depth * local), :].astype(BF16)
 
 
 def size_of(shapes):
     return sum(jnp.dtype(t).itemsize * functools.reduce(lambda x, y: x * y, s) for s, t in shapes)
 
 
-def run_main(shape, ids, counts, hours, pieces):
+def run_main(shape, ids, counts, hours, near, far):
     grps, devs, local, hour_rows = shape
     rank = hours.shape[1]
     hd_rows = hour_rows + devs * local
     outs = [
         ((hd_rows, rank), F32),
-        ((devs * local, rank), F32),
         ((hd_rows // 2, rank), BF16),
-        ((devs * local // 2, rank), BF16),
+        (hours.shape, BF16),
     ]
     scratch = [
         ((RING,) + counts.shape[1:], BF16),
+        ((OUT_RING,) + counts.shape[1:], BF16),
         ((devs * 2 * local, rank), BF16),
         ((SIDE // 2 * PITCH, 128), F32),
         ((SIDE, 128), F32),
@@ -211,22 +271,57 @@
     need = max(size_of(outs) + size_of(scratch) + (8 << 20), GRANT)
     return pl.pallas_call(
         functools.partial(main_kernel, shape),
-        in_specs=[SMEM, HBM, VMEM] + [ANY] * len(pieces),
-        out_specs=[VMEM] * 4,
-        out_shape=[jax.ShapeDtypeStruct(s, t) for s, t in outs],
+        in_specs=[SMEM, HBM, VMEM, ANY, ANY],
+        out_specs=[VMEM] * 3 + [HBM],
+        out_shape=[jax.ShapeDtypeStruct(s, t) for s, t in outs]
+        + [jax.ShapeDtypeStruct(counts.shape, BF16)],
         scratch_shapes=[pltpu.VMEM(s, t) for s, t in scratch]
-        + [pltpu.SemaphoreType.DMA((RING,)), pltpu.SemaphoreType.DMA((len(pieces),))],
+        + [
+            pltpu.SemaphoreType.DMA((RING,)),
+            pltpu.SemaphoreType.DMA((OUT_RING,)),
+            pltpu.SemaphoreType.DMA((2,)),
+        ],
         compiler_params=pltpu.CompilerParams(vmem_limit_bytes=need),
         cost_estimate=pl.CostEstimate(
-            flops=8 * counts.size * rank,
-            bytes_accessed=counts.size * 2,
+            flops=6 * counts.size * rank,
+            bytes_accessed=counts.size * 4,
             transcendentals=counts.size,
         ),
-        name="terms",
-    )(ids, counts, hours, *pieces)
-
-
-def call(kernel, name, ins, outs, specs=None, scratch=()):
+        name="hour_dst_terms",
+    )(ids, counts, hours, near, far)
+
+
+def run_src(shape, first, last, ids, resids, b_rows, hours, after, s_acc=None):
+    devs, local = shape
+    rank = hours.shape[1]
+    blocks, rows, columns = resids.shape
+    more = [] if s_acc is None else [s_acc]
+    outs = [((devs * local, rank), F32)]
+    if last == blocks:
+        outs.append(((devs * local // 2, rank), BF16))
+    need = size_of(outs) + size_of([((RING, rows, columns), BF16)]) + (8 << 20)
+    each = rows * columns
+    return pl.pallas_call(
+        functools.partial(src_kernel, shape, first, last),
+        in_specs=[SMEM, HBM, VMEM, VMEM, ANY] + [VMEM] * len(more),
+        out_specs=[VMEM] * len(outs),
+        out_shape=[jax.ShapeDtypeStruct(s, t) for s, t in outs],
+        scratch_shapes=[
+            pltpu.VMEM((RING, rows, columns), BF16),
+            pltpu.SemaphoreType.DMA((RING,)),
+        ],
+        input_output_aliases={5: 0} if more else {},
+        compiler_params=pltpu.CompilerParams(vmem_limit_bytes=max(need, SRC_GRANT)),
+        cost_estimate=pl.CostEstimate(
+            flops=8 * (last - first) * each * rank,
+            bytes_accessed=(last - first) * each * 2,
+            transcendentals=0,
+        ),
+        name="src_terms",
+    )(ids, resids, b_rows, hours, after, *more)
+
+
+def call(kernel, name, ins, outs, specs=None, scratch=(), weight=0):
     shapes = [(x.shape, x.dtype) for x in ins] + list(outs) + list(scratch)
     return pl.pallas_call(
         kernel,
@@ -235,6 +330,9 @@
         out_shape=[jax.ShapeDtypeStruct(s, t) for s, t in outs],
         scratch_shapes=[pltpu.VMEM(s, t) for s, t in scratch],
         compiler_params=pltpu.CompilerParams(vmem_limit_bytes=size_of(shapes) + (4 << 20)),
+        cost_estimate=pl.CostEstimate(
+            flops=weight, bytes_accessed=size_of(shapes), transcendentals=0
+        ),
         name=name,
     )(*ins)
 
@@ -243,15 +341,34 @@
     return [((rows, rank), F32)] + [((rows, rank), BF16)] * (ways - 1)
 
 
-def run_cut(ways, acc, got, name):
+def run_cut(ways, acc, got, after):
     rows, rank = got.shape[0] // ways, got.shape[1]
 
-    def kernel(acc, got, *outs):
+    def kernel(acc, got, after, *outs):
         for m in range(ways):
             at = pl.ds(m * rows, rows)
             outs[m][...] = (acc[at, :] + got[at, :].astype(F32)).astype(outs[m].dtype)
-
-    return call(kernel, name, (acc, got), shares(rows, rank, ways))
+        outs[ways][...] = jnp.zeros_like(outs[ways])
+
+    outs = shares(rows, rank, ways) + [((8, 128), F32)]
+    return call(kernel, "core_hours_dst", (acc, got, after), outs, specs=[VMEM, VMEM, ANY])
+
+
+def halve(keep, got, stay, send):
+    rows = got.shape[0]
+    half = rows // 2
+    stay[...] = keep[pl.ds(0, half), :] + got[pl.ds(0, half), :].astype(F32)
+    at = pl.ds(half, half)
+    send[...] = (keep[at, :] + got[at, :].astype(F32)).astype(BF16)
+
+
+def halves(got):
+    rows, rank = got.shape
+    return [((rows // 2, rank), F32), ((rows // 2, rank), BF16)]
+
+
+def run_halve(keep, got):
+    return call(halve, "src_half", (keep, got), halves(got))
 
 
 def total(refs):
@@ -284,34 +401,53 @@
         shares(each + dst_rows, rank, depth),
         specs=[SMEM] + [VMEM] * ways,
         scratch=[((rows, rank), F32)],
+        weight=SLOW,
     )
 
 
-def run_z(hd_parts, s_parts, hour_rows):
+def run_z(hd_parts, hour_rows, s_acc, s_got):
     n = len(hd_parts)
     rows, rank = hd_parts[0].shape
 
     def kernel(*refs):
-        hour, dst, src = refs[2 * n :]
+        keep, got, hour, dst, stay, send = refs[n:]
+        halve(keep, got, stay, send)
         acc = total(refs[:n]) * (1.0 / SIDE)
         hour[...] = acc[:hour_rows].astype(BF16)
         dst[...] = acc[hour_rows:].astype(BF16)
-        src[...] = total(refs[n : 2 * n]) * (1.0 / SIDE)
-
-    outs = [((hour_rows, rank), BF16), ((rows - hour_rows, rank), BF16), (s_parts[0].shape, F32)]
-    return call(kernel, "z_sum", (*hd_parts, *s_parts), outs)
-
-
-def run_join(parts):
+
+    outs = [((hour_rows, rank), BF16), ((rows - hour_rows, rank), BF16)] + halves(s_got)
+    return call(kernel, "z_sum", (*hd_parts, s_acc, s_got), outs)
+
+
+def run_join(parts, keep=None, got=None):
     rows = [p.shape[0] for p in parts]
+    n = len(parts)
+    outs = [((sum(rows), parts[0].shape[1]), BF16)]
+    if got is None:
+        ins = tuple(parts)
+    else:
+        ins = (*parts, keep, got)
+        outs += halves(got)
 
     def kernel(*refs):
-        at = 0
-        for ref, n in zip(refs[:-1], rows):
-            refs[-1][at : at + n, :] = ref[...]
-            at += n
-
-    return call(kernel, "join", parts, [((sum(rows), parts[0].shape[1]), BF16)])[0]
+        if got is not None:
+            halve(refs[n], refs[n + 1], refs[-2], refs[-1])
+        out, at = refs[len(ins)], 0
+        for ref, n_rows in zip(refs, rows):
+            out[at : at + n_rows, :] = ref[...]
+            at += n_rows
+
+    return call(kernel, "join", ins, outs)
+
+
+def run_src_sum(keep, got, joined):
+    def kernel(keep, got, joined, out, same):
+        out[...] = (keep[...] + got[...].astype(F32)) * (1.0 / SIDE)
+        same[...] = joined[...]
+
+    outs = [(keep.shape, F32), (joined.shape, BF16)]
+    return call(kernel, "src_sum", (keep, got, joined), outs)
 
 
 def run_place(sizes, hour_rows, ids, parts, so_far, dst_rows=0, passed=()):
@@ -392,32 +528,44 @@
     dst_own = lax.dynamic_slice_in_dim(dst_factor, grp * dst_part, dst_part, 0)
     dst_z = [dst_own] + [swap(dst_own, "dev", devs, 2 * m) for m in range(1, depth)]
     src_z = [swap(src_factor, "dev", devs, 2 * m) for m in range(2, depth)]
-    picked, src_same = run_pick(counts.shape[0], ids, hour_factor, src_factor)
+    blocks = counts.shape[0]
+    picked, src_same = run_pick(blocks, ids, hour_factor, src_factor)
     src_z = [src_factor, swap(src_same, "dev", devs, 2)] + src_z
-    dst_here = run_join(dst_z)
+    dst_here = run_join(dst_z)[0]
     dsts = [dst_here] + [swap(dst_here, "grp", grps, m) for m in range(1, grps)]
-    near = run_join(src_z + dsts)
+    near = run_join(src_z + dsts)[0]
     far = swap(near, "dev", devs, 1)
     shape = (grps, devs, local, hour_rows)
-    hd_acc, s_acc, hd_send, s_send = run_main(shape, ids, counts, picked, [near, far])
+    hd_acc, hd_send, b_rows, resids = run_main(shape, ids, counts, picked, near, far)
 
     def exchange(parts, axis, size, step):
         return [parts[0]] + [swap(x, axis, size, step * m) for m, x in enumerate(parts) if m]
 
     hd_got = swap(hd_send, "dev", devs, 1)
+    src = functools.partial(run_src, (devs, local))
+    early = blocks // 4
+    s_acc = src(0, early, ids, resids, b_rows, picked, hd_send)[0]
+    *hd, cut_done = run_cut(grps, hd_acc, hd_got, s_acc)
+    cut_done = swap(cut_done, "dev", devs, 1)
+    s_acc, s_send = src(early, blocks, ids, resids, b_rows, picked, cut_done, s_acc)
     s_got = swap(s_send, "dev", devs, 1)
-    hd = run_cut(grps, hd_acc, hd_got, "core_hours_dst")
-    srcs = run_cut(depth, s_acc, s_got, "core_src")
     hour_part = hour_rows // (2 * grps)
     hd = run_grp(hour_part, depth, ids, exchange(hd, "grp", grps, 1))
-    srcs = exchange(srcs, "dev", devs, 2)
     hour_each = hour_part // depth
-    hour, dst, grad_src = run_z(exchange(hd, "dev", devs, 2), srcs, hour_each)
+    hour, dst, s_keep, s_send = run_z(exchange(hd, "dev", devs, 2), hour_each, s_acc, s_got)
+    s_got = swap(s_send, "dev", devs, 2)
     back = [hour] + [swap(hour, "dev", devs, 2 * m) for m in range(1, depth)]
-    joined = run_join(back + [dst])
+    joined, s_keep, s_send = run_join(back + [dst], s_keep, s_got)
+    step = 4
+    s_got = swap(s_send, "dev", devs, step)
+    while 2 * step < devs:
+        s_keep, s_send = run_halve(s_keep, s_got)
+        step *= 2
+        s_got = swap(s_send, "dev", devs, step)
+    grad_src, same = run_src_sum(s_keep, s_got, joined)
     near = [joined] + [swap(joined, "grp", grps, m) for m in range(1, grps)]
     parts = [(x, 0, m) for m, x in enumerate(near)]
-    parts += [(swap(x, "dev", devs, 1), 1, m) for m, x in enumerate(near)]
+    parts += [(swap(x, "dev", devs, 1), 1, m) for m, x in enumerate([same] + near[1:])]
     grad_hour, grad_dst = run_place(sizes, hour_rows, ids, parts, None, dst_part)
     return grad_src, grad_dst, grad_hour
 

time: 141 us -> 139 us (0.986)
  Pallas kernels: 55.5 us -> 62.9 us
  waiting for transfers between devices: 40.9 us -> 34.8 us
  starting transfers between devices: 40.2 us -> 36.6 us
    pallas_call x0 -> x2, Pallas kernels: none -> 14.1 us  [run_src(): pl.pallas_call(functools.partial(src_kernel, shape, first, last), in_spec...]
    pallas_call x1, Pallas kernels: 48.1 us -> 41.5 us  [run_main(): pl.pallas_call(functools.partial(main_kernel, shape), in_specs=[SMEM, HBM...]
    ppermute x31, waiting for transfers between devices: 40.9 us -> 34.8 us  [swap(): return lax.ppermute(x, axis, [(i, i ^ mask) for i in range(size)])]
    ppermute x31, starting transfers between devices: 40.2 us -> 36.6 us  [swap(): return lax.ppermute(x, axis, [(i, i ^ mask) for i in range(size)])]
  transfers between devices with their start and end apart: 31 -> 31, of which waited for: 17 -> 14; matrix products, arithmetic and copies ran while one was open for 1% -> 1% of each run, Pallas kernels for 2% -> 13%
where the time goes in v4:
time: 139 us; the launch traced here: 138 us
  Pallas kernels  62.9 us (45%)
  starting transfers between devices  36.6 us (26%)
  waiting for transfers between devices  34.8 us (25%)
  local copies, waits for them, and re-layouts  3.31 us (2%)
    pallas_call x1, Pallas kernels, run_main(): pl.pallas_call(functools.partial(main_kernel, shape), in_specs=[SMEM, HBM...  41.5 us
    ppermute x31, starting transfers between devices, swap(): return lax.ppermute(x, axis, [(i, i ^ mask) for i in range(size)])  36.6 us
    ppermute x31, waiting for transfers between devices, swap(): return lax.ppermute(x, axis, [(i, i ^ mask) for i in range(size)])  34.8 us
    pallas_call x2, Pallas kernels, run_src(): pl.pallas_call(functools.partial(src_kernel, shape, first, last), in_spec...  14.1 us
    pallas_call x1, Pallas kernels, run_place(): pl.pallas_call(kernel, in_specs=[SMEM] + [VMEM] * n + [HBM] * len(more),...  3.35 us
  transfers between devices with their start and end apart: 31, of which 14 were waited for; matrix products, arithmetic and copies ran while one was open for 1% of the time, Pallas kernels for 13%

profile of v4, /device:TPU:0, one launch (start us, length us, event | category | flops | bytes accessed | tf_op | source)
XLA Modules:
  0.0 138.4 jit_solution(10165991338077508873)
XLA Ops:
  0.6 4.1 %collective-permute-start.1 = (bf16[256,256]{1,0:T(8,128)(2,1)}, bf16[256,256]{1,0:T(8,128)(2,1)S(1)}, u32[]{:S(2)}, u32[]{:S(2)}) collective-permute-start(bf16[256,256]{1,0:T(8,128)(2,1)} %refs_0_.1), channel_id=1, source_target_pairs={{0,4},{1,5},{2,6},{3,7},{4,0},{5,1},{6,2},{7,3},{8,12},{9,13},{10,... | collective-permute-start | bytes 393224 | tf_op jit(solution)/shard_map/ppermute | solution.py:31
  4.8 1.8 %collective-permute-start.5 = (bf16[64,256]{1,0:T(8,128)(2,1)S(1)}, bf16[64,256]{1,0:T(8,128)(2,1)S(1)}, u32[]{:S(2)}, u32[]{:S(2)}) collective-permute-start(bf16[64,256]{1,0:T(8,128)(2,1)S(1)} %constant_dynamic-slice_fusion.refs_0_), channel_id=1, source_target_pairs={{0,6},{1,7},{2,4},{3,5},{4,2},{5,3},{6,0},{7,1},{8,14},{9,15},{10,... | collective-permute-start | bytes 98312 | tf_op jit(solution)/shard_map/ppermute | solution.py:31
  6.6 1.2 collective-permute-start.4
  7.8 1.3 collective-permute-start.3
  9.1 1.8 %collective-permute-start.2 = (bf16[256,256]{1,0:T(8,128)(2,1)}, bf16[256,256]{1,0:T(8,128)(2,1)S(1)}, u32[]{:S(2)}, u32[]{:S(2)}) collective-permute-start(bf16[256,256]{1,0:T(8,128)(2,1)} %refs_0_.1), channel_id=1, source_target_pairs={{0,6},{1,7},{2,4},{3,5},{4,2},{5,3},{6,0},{7,1},{8,14},{9,15},{10,... | collective-permute-start | bytes 393224 | tf_op jit(solution)/shard_map/ppermute | solution.py:31
  11.8 1.6 %copy-done.1 = bf16[4096,256]{1,0:T(8,128)(2,1)S(1)} copy-done((bf16[4096,256]{1,0:T(8,128)(2,1)S(1)}, bf16[4096,256]{1,0:T(8,128)(2,1)}, u32[]{:S(2)}) %copy-start.1) | copy-done | bytes 2097176
  13.4 0.9 copy-done.2
  14.3 1.9 %pick_hours.1 = (bf16[1536,256]{1,0:T(8,128)(2,1)S(1)}, bf16[256,256]{1,0:T(8,128)(2,1)S(1)}) custom-call(s32[128]{0:T(128)S(1)} %concatenate.3.ids, bf16[4096,256]{1,0:T(8,128)(2,1)S(1)} %copy-done.1, bf16[256,256]{1,0:T(8,128)(2,1)S(1)} %copy-done.2), custom_call_target="tpu_custom_call" | custom-call | tf_op jit(solution)/shard_map/pick_hours/pallas_call | solution.py:96
  16.2 1.4 collective-permute-start
  17.7 2.9 %collective-permute-start.8 = (bf16[256,256]{1,0:T(8,128)(2,1)S(1)}, bf16[256,256]{1,0:T(8,128)(2,1)S(1)}, u32[]{:S(2)}, u32[]{:S(2)}) collective-permute-start(bf16[256,256]{1,0:T(8,128)(2,1)S(1)} %join.3.refs_4_), channel_id=1, source_target_pairs={{0,24},{8,16},{16,8},{24,0},{1,25},{9,17},{17,9},{25,1},{2,26},{10... | collective-permute-start | bytes 393224 | tf_op jit(solution)/shard_map/ppermute | solution.py:31
  21.3 3.4 %collective-permute-done.8.refs_7_ = bf16[256,256]{1,0:T(8,128)(2,1)S(1)} collective-permute-done((bf16[256,256]{1,0:T(8,128)(2,1)S(1)}, bf16[256,256]{1,0:T(8,128)(2,1)S(1)}, u32[]{:S(2)}, u32[]{:S(2)}) %collective-permute-start.8) | collective-permute-done | bytes 131104 | tf_op jit(solution)/shard_map/ppermute | solution.py:31
  24.7 1.1 collective-permute-done.7.refs_6_
  26.2 2.6 %collective-permute-done.9.far = bf16[2048,256]{1,0:T(8,128)(2,1)S(1)} collective-permute-done((bf16[2048,256]{1,0:T(8,128)(2,1)S(1)}, bf16[2048,256]{1,0:T(8,128)(2,1)S(1)}, u32[]{:S(2)}, u32[]{:S(2)}) %collective-permute-start.9) | collective-permute-done | bytes 1048608 | tf_op jit(solution)/shard_map/ppermute | solution.py:31
  28.9 41.5 %hour_dst_terms.1 = (f32[6144,256]{1,0:T(8,128)S(1)}, bf16[3072,256]{1,0:T(8,128)(2,1)S(1)}, bf16[1536,256]{1,0:T(8,128)(2,1)S(1)}, bf16[24,64,4096]{2,1,0:T(8,128)(2,1)}) custom-call(s32[128]{0:T(128)S(1)} %concatenate.3.ids, bf16[24,64,4096]{2,1,0:T(8,128)(2,1)} %counts.1, bf16[1536,256]{1,0:T(8,128)(2,1)S(1)} %get-tuple-element.31.hours, ...), custom_call_target="tpu_custom_call" | custom-call | flops 9663676416 | bytes 25165824 | tf_op jit(solution)/shard_map/hour_dst_terms/pallas_call | solution.py:272
  70.6 4.3 %src_terms.2.after.refs_0_ = f32[2048,256]{1,0:T(8,128)S(1)} custom-call(s32[128]{0:T(128)S(1)} %concatenate.3.ids, bf16[24,64,4096]{2,1,0:T(8,128)(2,1)} %get-tuple-element.35.resids, bf16[1536,256]{1,0:T(8,128)(2,1)S(1)} %get-tuple-element.36.b_rows, bf16[1536,256]{1,0:T(8,128)(2,1)S(1)} %get-tuple-element.31.hours, ...), custom_call_target="tpu_custom_call" | custom-call | flops 3221225472 | bytes 3145728 | tf_op jit(solution)/shard_map/src_terms/pallas_call | solution.py:304
  75.6 1.4 %collective-permute-start.11 = (bf16[768,256]{1,0:T(8,128)(2,1)S(1)}, bf16[768,256]{1,0:T(8,128)(2,1)S(1)}, u32[]{:S(2)}, u32[]{:S(2)}) collective-permute-start(bf16[768,256]{1,0:T(8,128)(2,1)S(1)} %get-tuple-element.38), channel_id=1, source_target_pairs={{0,8},{8,0},{16,24},{24,16},{1,9},{9,1},{17,25},{25,17},{2,10},{10... | collective-permute-start | bytes 1179656 | tf_op jit(solution)/shard_map/ppermute | solution.py:31
  77.7 1.4 %collective-permute-start.13 = (bf16[768,256]{1,0:T(8,128)(2,1)S(1)}, bf16[768,256]{1,0:T(8,128)(2,1)S(1)}, u32[]{:S(2)}, u32[]{:S(2)}) collective-permute-start(bf16[768,256]{1,0:T(8,128)(2,1)S(1)} %get-tuple-element.40), channel_id=1, source_target_pairs={{0,24},{8,16},{16,8},{24,0},{1,25},{9,17},{17,9},{25,1},{2,26},{10... | collective-permute-start | bytes 1179656 | tf_op jit(solution)/shard_map/ppermute | solution.py:31
  79.1 9.7 %src_terms.3 = (f32[2048,256]{1,0:T(8,128)S(1)}, bf16[1024,256]{1,0:T(8,128)(2,1)S(1)}) custom-call(s32[128]{0:T(128)S(1)} %concatenate.3.ids, bf16[24,64,4096]{2,1,0:T(8,128)(2,1)} %get-tuple-element.35.resids, bf16[1536,256]{1,0:T(8,128)(2,1)S(1)} %get-tuple-element.36.b_rows, ...), custom_call_target="tpu_custom_call", output_to_operand_aliasing={{0}: (5, {})} | custom-call | flops 9663676416 | bytes 9437184 | tf_op jit(solution)/shard_map/src_terms/pallas_call | solution.py:304
  89.0 7.4 %collective-permute-done.12.refs_2_ = bf16[768,256]{1,0:T(8,128)(2,1)S(1)} collective-permute-done((bf16[768,256]{1,0:T(8,128)(2,1)S(1)}, bf16[768,256]{1,0:T(8,128)(2,1)S(1)}, u32[]{:S(2)}, u32[]{:S(2)}) %collective-permute-start.12) | collective-permute-done | bytes 393248 | tf_op jit(solution)/shard_map/ppermute | solution.py:31
  97.2 1.0 collective-permute-start.14
  98.2 3.4 %collective-permute-start.15 = (bf16[192,256]{1,0:T(8,128)(2,1)S(1)}, bf16[192,256]{1,0:T(8,128)(2,1)S(1)}, u32[]{:S(2)}, u32[]{:S(2)}) collective-permute-start(bf16[192,256]{1,0:T(8,128)(2,1)S(1)} %get-tuple-element.43), channel_id=1, source_target_pairs={{0,4},{1,5},{2,6},{3,7},{4,0},{5,1},{6,2},{7,3},{8,12},{9,13},{10,... | collective-permute-start | bytes 294920 | tf_op jit(solution)/shard_map/ppermute | solution.py:31
  101.6 1.1 collective-permute-done.14.refs_1_
  102.7 5.8 %collective-permute-done.15.refs_2_ = bf16[192,256]{1,0:T(8,128)(2,1)S(1)} collective-permute-done((bf16[192,256]{1,0:T(8,128)(2,1)S(1)}, bf16[192,256]{1,0:T(8,128)(2,1)S(1)}, u32[]{:S(2)}, u32[]{:S(2)}) %collective-permute-start.15) | collective-permute-done | bytes 98336 | tf_op jit(solution)/shard_map/ppermute | solution.py:31
  108.7 1.7 %collective-permute-start.22 = (bf16[512,256]{1,0:T(8,128)(2,1)S(1)}, bf16[512,256]{1,0:T(8,128)(2,1)S(1)}, u32[]{:S(2)}, u32[]{:S(2)}) collective-permute-start(bf16[512,256]{1,0:T(8,128)(2,1)S(1)} %get-tuple-element.51), channel_id=1, source_target_pairs={{0,2},{1,3},{2,0},{3,1},{4,6},{5,7},{6,4},{7,5},{8,10},{9,11},{10,... | collective-permute-start | bytes 786440 | tf_op jit(solution)/shard_map/ppermute | solution.py:31
  110.3 2.5 %collective-permute-start.21 = (bf16[128,256]{1,0:T(8,128)(2,1)S(1)}, bf16[128,256]{1,0:T(8,128)(2,1)S(1)}, u32[]{:S(2)}, u32[]{:S(2)}) collective-permute-start(bf16[128,256]{1,0:T(8,128)(2,1)S(1)} %get-tuple-element.48.refs_0_), channel_id=1, source_target_pairs={{0,6},{1,7},{2,4},{3,5},{4,2},{5,3},{6,0},{7,1},{8,14},{9,15},{10,... | collective-permute-start | bytes 196616 | tf_op jit(solution)/shard_map/ppermute | solution.py:31
  112.8 1.9 %collective-permute-start.19 = (bf16[128,256]{1,0:T(8,128)(2,1)S(1)}, bf16[128,256]{1,0:T(8,128)(2,1)S(1)}, u32[]{:S(2)}, u32[]{:S(2)}) collective-permute-start(bf16[128,256]{1,0:T(8,128)(2,1)S(1)} %get-tuple-element.48.refs_0_), channel_id=1, source_target_pairs={{0,2},{1,3},{2,0},{3,1},{4,6},{5,7},{6,4},{7,5},{8,10},{9,11},{10,... | collective-permute-start | bytes 196616 | tf_op jit(solution)/shard_map/ppermute | solution.py:31
  114.7 5.6 %collective-permute-done.21.refs_3_ = bf16[128,256]{1,0:T(8,128)(2,1)S(1)} collective-permute-done((bf16[128,256]{1,0:T(8,128)(2,1)S(1)}, bf16[128,256]{1,0:T(8,128)(2,1)S(1)}, u32[]{:S(2)}, u32[]{:S(2)}) %collective-permute-start.21) | collective-permute-done | bytes 65568 | tf_op jit(solution)/shard_map/ppermute | solution.py:31
  120.4 1.6 %collective-permute-start.26 = (bf16[576,256]{1,0:T(8,128)(2,1)S(1)}, bf16[576,256]{1,0:T(8,128)(2,1)S(1)}, u32[]{:S(2)}, u32[]{:S(2)}) collective-permute-start(bf16[576,256]{1,0:T(8,128)(2,1)S(1)} %get-tuple-element.54.joined.refs_0_), channel_id=1, source_target_pairs={{0,24},{8,16},{16,8},{24,0},{1,25},{9,17},{17,9},{25,1},{2,26},{10... | collective-permute-start | bytes 884744 | tf_op jit(solution)/shard_map/ppermute | solution.py:31
  122.7 1.3 collective-permute-start.24
  124.0 2.0 %collective-permute-start.23 = (bf16[256,256]{1,0:T(8,128)(2,1)S(1)}, bf16[256,256]{1,0:T(8,128)(2,1)S(1)}, u32[]{:S(2)}, u32[]{:S(2)}) collective-permute-start(bf16[256,256]{1,0:T(8,128)(2,1)S(1)} %get-tuple-element.53), channel_id=1, source_target_pairs={{0,4},{1,5},{2,6},{3,7},{4,0},{5,1},{6,2},{7,3},{8,12},{9,13},{10,... | collective-permute-start | bytes 393224 | tf_op jit(solution)/shard_map/ppermute | solution.py:31
  125.9 5.3 %collective-permute-done.23.got = bf16[256,256]{1,0:T(8,128)(2,1)S(1)} collective-permute-done((bf16[256,256]{1,0:T(8,128)(2,1)S(1)}, bf16[256,256]{1,0:T(8,128)(2,1)S(1)}, u32[]{:S(2)}, u32[]{:S(2)}) %collective-permute-start.23) | collective-permute-done | bytes 131104 | tf_op jit(solution)/shard_map/ppermute | solution.py:31
  135.1 3.3 %place.1 = (f32[4096,256]{1,0:T(8,128)}, f32[256,256]{1,0:T(8,128)}) custom-call(s32[128]{0:T(128)S(1)} %concatenate.3.ids, bf16[576,256]{1,0:T(8,128)(2,1)S(1)} %get-tuple-element.54.joined.refs_0_, bf16[576,256]{1,0:T(8,128)(2,1)S(1)} %collective-permute-done.24.refs_1_, bf16[576,256]{1,0:T(8,128)(2,1)S(1)} %collective-permute-done.25.refs_2_, ...), custom_call_target="tpu_custom_call" | custom-call | tf_op jit(solution)/shard_map/place/pallas_call | solution.py:493
  (54 shorter events, 9.3 us)
Async XLA Ops:
  0.6 20.5 %collective-permute-start.1 = (bf16[256,256]{1,0:T(8,128)(2,1)}, bf16[256,256]{1,0:T(8,128)(2,1)S(1)}, u32[]{:S(2)}, u32[]{:S(2)}) collective-permute-start(bf16[256,256]{1,0:T(8,128)(2,1)} %refs_0_.1), channel_id=1, source_target_pairs={{0,4},{1,5},{2,6},{3,7},{4,0},{5,1},{6,2},{7,3},{8,12},{9,13},{10,... | collective-permute-start | bytes 393224 | tf_op jit(solution)/shard_map/ppermute | solution.py:31
  4.8 11.4 %collective-permute-start.5 = (bf16[64,256]{1,0:T(8,128)(2,1)S(1)}, bf16[64,256]{1,0:T(8,128)(2,1)S(1)}, u32[]{:S(2)}, u32[]{:S(2)}) collective-permute-start(bf16[64,256]{1,0:T(8,128)(2,1)S(1)} %constant_dynamic-slice_fusion.refs_0_), channel_id=1, source_target_pairs={{0,6},{1,7},{2,4},{3,5},{4,2},{5,3},{6,0},{7,1},{8,14},{9,15},{10,... | collective-permute-start | bytes 98312 | tf_op jit(solution)/shard_map/ppermute | solution.py:31
  6.6 11.1 %collective-permute-start.4 = (bf16[64,256]{1,0:T(8,128)(2,1)S(1)}, bf16[64,256]{1,0:T(8,128)(2,1)S(1)}, u32[]{:S(2)}, u32[]{:S(2)}) collective-permute-start(bf16[64,256]{1,0:T(8,128)(2,1)S(1)} %constant_dynamic-slice_fusion.refs_0_), channel_id=1, source_target_pairs={{0,4},{1,5},{2,6},{3,7},{4,0},{5,1},{6,2},{7,3},{8,12},{9,13},{10,... | collective-permute-start | bytes 98312 | tf_op jit(solution)/shard_map/ppermute | solution.py:31
  7.8 9.9 %collective-permute-start.3 = (bf16[64,256]{1,0:T(8,128)(2,1)S(1)}, bf16[64,256]{1,0:T(8,128)(2,1)S(1)}, u32[]{:S(2)}, u32[]{:S(2)}) collective-permute-start(bf16[64,256]{1,0:T(8,128)(2,1)S(1)} %constant_dynamic-slice_fusion.refs_0_), channel_id=1, source_target_pairs={{0,2},{1,3},{2,0},{3,1},{4,6},{5,7},{6,4},{7,5},{8,10},{9,11},{10,... | collective-permute-start | bytes 98312 | tf_op jit(solution)/shard_map/ppermute | solution.py:31
  9.1 12.1 %collective-permute-start.2 = (bf16[256,256]{1,0:T(8,128)(2,1)}, bf16[256,256]{1,0:T(8,128)(2,1)S(1)}, u32[]{:S(2)}, u32[]{:S(2)}) collective-permute-start(bf16[256,256]{1,0:T(8,128)(2,1)} %refs_0_.1), channel_id=1, source_target_pairs={{0,6},{1,7},{2,4},{3,5},{4,2},{5,3},{6,0},{7,1},{8,14},{9,15},{10,... | collective-permute-start | bytes 393224 | tf_op jit(solution)/shard_map/ppermute | solution.py:31
  14.3 11.8 %copy-start.3 = (bf16[256,256]{1,0:T(8,128)(2,1)S(1)}, bf16[256,256]{1,0:T(8,128)(2,1)}, u32[]{:S(2)}) copy-start(bf16[256,256]{1,0:T(8,128)(2,1)} %refs_0_.1) | copy-start | bytes 393220
  16.2 5.1 %collective-permute-start = (bf16[256,256]{1,0:T(8,128)(2,1)S(1)}, bf16[256,256]{1,0:T(8,128)(2,1)S(1)}, u32[]{:S(2)}, u32[]{:S(2)}) collective-permute-start(bf16[256,256]{1,0:T(8,128)(2,1)S(1)} %get-tuple-element.32), channel_id=1, source_target_pairs={{0,2},{1,3},{2,0},{3,1},{4,6},{5,7},{6,4},{7,5},{8,10},{9,11},{10,... | collective-permute-start | bytes 393224 | tf_op jit(solution)/shard_map/ppermute | solution.py:31
  17.7 7.0 %collective-permute-start.8 = (bf16[256,256]{1,0:T(8,128)(2,1)S(1)}, bf16[256,256]{1,0:T(8,128)(2,1)S(1)}, u32[]{:S(2)}, u32[]{:S(2)}) collective-permute-start(bf16[256,256]{1,0:T(8,128)(2,1)S(1)} %join.3.refs_4_), channel_id=1, source_target_pairs={{0,24},{8,16},{16,8},{24,0},{1,25},{9,17},{17,9},{25,1},{2,26},{10... | collective-permute-start | bytes 393224 | tf_op jit(solution)/shard_map/ppermute | solution.py:31
  20.6 5.3 %collective-permute-start.7 = (bf16[256,256]{1,0:T(8,128)(2,1)S(1)}, bf16[256,256]{1,0:T(8,128)(2,1)S(1)}, u32[]{:S(2)}, u32[]{:S(2)}) collective-permute-start(bf16[256,256]{1,0:T(8,128)(2,1)S(1)} %join.3.refs_4_), channel_id=1, source_target_pairs={{0,16},{8,24},{16,0},{24,8},{1,17},{9,25},{17,1},{25,9},{2,18},{10... | collective-permute-start | bytes 393224 | tf_op jit(solution)/shard_map/ppermute | solution.py:31
  21.1 5.0 %collective-permute-start.6 = (bf16[256,256]{1,0:T(8,128)(2,1)S(1)}, bf16[256,256]{1,0:T(8,128)(2,1)S(1)}, u32[]{:S(2)}, u32[]{:S(2)}) collective-permute-start(bf16[256,256]{1,0:T(8,128)(2,1)S(1)} %join.3.refs_4_), channel_id=1, source_target_pairs={{0,8},{8,0},{16,24},{24,16},{1,9},{9,1},{17,25},{25,17},{2,10},{10... | collective-permute-start | bytes 393224 | tf_op jit(solution)/shard_map/ppermute | solution.py:31
  26.1 2.7 %collective-permute-start.9 = (bf16[2048,256]{1,0:T(8,128)(2,1)S(1)}, bf16[2048,256]{1,0:T(8,128)(2,1)S(1)}, u32[]{:S(2)}, u32[]{:S(2)}) collective-permute-start(bf16[2048,256]{1,0:T(8,128)(2,1)S(1)} %join.4.near), channel_id=1, source_target_pairs={{0,1},{1,0},{2,3},{3,2},{4,5},{5,4},{6,7},{7,6},{8,9},{9,8},{10,11... | collective-permute-start | bytes 3145736 | tf_op jit(solution)/shard_map/ppermute | solution.py:31
  70.4 4.5 %collective-permute-start.10 = (bf16[3072,256]{1,0:T(8,128)(2,1)S(1)}, bf16[3072,256]{1,0:T(8,128)(2,1)S(1)}, u32[]{:S(2)}, u32[]{:S(2)}) collective-permute-start(bf16[3072,256]{1,0:T(8,128)(2,1)S(1)} %get-tuple-element.34.after), channel_id=1, source_target_pairs={{0,1},{1,0},{2,3},{3,2},{4,5},{5,4},{6,7},{7,6},{8,9},{9,8},{10,11... | collective-permute-start | bytes 4718600 | tf_op jit(solution)/shard_map/ppermute | solution.py:31
  75.2 3.9 %collective-permute-start.17 = (f32[8,128]{1,0:T(8,128)S(1)}, f32[8,128]{1,0:T(8,128)S(1)}, u32[]{:S(2)}, u32[]{:S(2)}) collective-permute-start(f32[8,128]{1,0:T(8,128)S(1)} %get-tuple-element.45), channel_id=1, source_target_pairs={{0,1},{1,0},{2,3},{3,2},{4,5},{5,4},{6,7},{7,6},{8,9},{9,8},{10,11... | collective-permute-start | bytes 12296 | tf_op jit(solution)/shard_map/ppermute | solution.py:31
  75.6 13.3 %collective-permute-start.11 = (bf16[768,256]{1,0:T(8,128)(2,1)S(1)}, bf16[768,256]{1,0:T(8,128)(2,1)S(1)}, u32[]{:S(2)}, u32[]{:S(2)}) collective-permute-start(bf16[768,256]{1,0:T(8,128)(2,1)S(1)} %get-tuple-element.38), channel_id=1, source_target_pairs={{0,8},{8,0},{16,24},{24,16},{1,9},{9,1},{17,25},{25,17},{2,10},{10... | collective-permute-start | bytes 1179656 | tf_op jit(solution)/shard_map/ppermute | solution.py:31
  77.0 19.3 %collective-permute-start.12 = (bf16[768,256]{1,0:T(8,128)(2,1)S(1)}, bf16[768,256]{1,0:T(8,128)(2,1)S(1)}, u32[]{:S(2)}, u32[]{:S(2)}) collective-permute-start(bf16[768,256]{1,0:T(8,128)(2,1)S(1)} %get-tuple-element.39), channel_id=1, source_target_pairs={{0,16},{8,24},{16,0},{24,8},{1,17},{9,25},{17,1},{25,9},{2,18},{10... | collective-permute-start | bytes 1179656 | tf_op jit(solution)/shard_map/ppermute | solution.py:31
  77.7 18.6 %collective-permute-start.13 = (bf16[768,256]{1,0:T(8,128)(2,1)S(1)}, bf16[768,256]{1,0:T(8,128)(2,1)S(1)}, u32[]{:S(2)}, u32[]{:S(2)}) collective-permute-start(bf16[768,256]{1,0:T(8,128)(2,1)S(1)} %get-tuple-element.40), channel_id=1, source_target_pairs={{0,24},{8,16},{16,8},{24,0},{1,25},{9,17},{17,9},{25,1},{2,26},{10... | collective-permute-start | bytes 1179656 | tf_op jit(solution)/shard_map/ppermute | solution.py:31
  88.9 19.6 %collective-permute-start.18 = (bf16[1024,256]{1,0:T(8,128)(2,1)S(1)}, bf16[1024,256]{1,0:T(8,128)(2,1)S(1)}, u32[]{:S(2)}, u32[]{:S(2)}) collective-permute-start(bf16[1024,256]{1,0:T(8,128)(2,1)S(1)} %get-tuple-element.47), channel_id=1, source_target_pairs={{0,1},{1,0},{2,3},{3,2},{4,5},{5,4},{6,7},{7,6},{8,9},{9,8},{10,11... | collective-permute-start | bytes 1572872 | tf_op jit(solution)/shard_map/ppermute | solution.py:31
  97.2 5.6 %collective-permute-start.14 = (bf16[192,256]{1,0:T(8,128)(2,1)S(1)}, bf16[192,256]{1,0:T(8,128)(2,1)S(1)}, u32[]{:S(2)}, u32[]{:S(2)}) collective-permute-start(bf16[192,256]{1,0:T(8,128)(2,1)S(1)} %get-tuple-element.42), channel_id=1, source_target_pairs={{0,2},{1,3},{2,0},{3,1},{4,6},{5,7},{6,4},{7,5},{8,10},{9,11},{10,... | collective-permute-start | bytes 294920 | tf_op jit(solution)/shard_map/ppermute | solution.py:31
  98.2 10.3 %collective-permute-start.15 = (bf16[192,256]{1,0:T(8,128)(2,1)S(1)}, bf16[192,256]{1,0:T(8,128)(2,1)S(1)}, u32[]{:S(2)}, u32[]{:S(2)}) collective-permute-start(bf16[192,256]{1,0:T(8,128)(2,1)S(1)} %get-tuple-element.43), channel_id=1, source_target_pairs={{0,4},{1,5},{2,6},{3,7},{4,0},{5,1},{6,2},{7,3},{8,12},{9,13},{10,... | collective-permute-start | bytes 294920 | tf_op jit(solution)/shard_map/ppermute | solution.py:31
  101.6 6.9 %collective-permute-start.16 = (bf16[192,256]{1,0:T(8,128)(2,1)S(1)}, bf16[192,256]{1,0:T(8,128)(2,1)S(1)}, u32[]{:S(2)}, u32[]{:S(2)}) collective-permute-start(bf16[192,256]{1,0:T(8,128)(2,1)S(1)} %get-tuple-element.44), channel_id=1, source_target_pairs={{0,6},{1,7},{2,4},{3,5},{4,2},{5,3},{6,0},{7,1},{8,14},{9,15},{10,... | collective-permute-start | bytes 294920 | tf_op jit(solution)/shard_map/ppermute | solution.py:31
  108.7 11.7 %collective-permute-start.22 = (bf16[512,256]{1,0:T(8,128)(2,1)S(1)}, bf16[512,256]{1,0:T(8,128)(2,1)S(1)}, u32[]{:S(2)}, u32[]{:S(2)}) collective-permute-start(bf16[512,256]{1,0:T(8,128)(2,1)S(1)} %get-tuple-element.51), channel_id=1, source_target_pairs={{0,2},{1,3},{2,0},{3,1},{4,6},{5,7},{6,4},{7,5},{8,10},{9,11},{10,... | collective-permute-start | bytes 786440 | tf_op jit(solution)/shard_map/ppermute | solution.py:31
  110.3 10.0 %collective-permute-start.21 = (bf16[128,256]{1,0:T(8,128)(2,1)S(1)}, bf16[128,256]{1,0:T(8,128)(2,1)S(1)}, u32[]{:S(2)}, u32[]{:S(2)}) collective-permute-start(bf16[128,256]{1,0:T(8,128)(2,1)S(1)} %get-tuple-element.48.refs_0_), channel_id=1, source_target_pairs={{0,6},{1,7},{2,4},{3,5},{4,2},{5,3},{6,0},{7,1},{8,14},{9,15},{10,... | collective-permute-start | bytes 196616 | tf_op jit(solution)/shard_map/ppermute | solution.py:31
  112.8 7.6 %collective-permute-start.20 = (bf16[128,256]{1,0:T(8,128)(2,1)S(1)}, bf16[128,256]{1,0:T(8,128)(2,1)S(1)}, u32[]{:S(2)}, u32[]{:S(2)}) collective-permute-start(bf16[128,256]{1,0:T(8,128)(2,1)S(1)} %get-tuple-element.48.refs_0_), channel_id=1, source_target_pairs={{0,4},{1,5},{2,6},{3,7},{4,0},{5,1},{6,2},{7,3},{8,12},{9,13},{10,... | collective-permute-start | bytes 196616 | tf_op jit(solution)/shard_map/ppermute | solution.py:31
  112.8 7.6 %collective-permute-start.19 = (bf16[128,256]{1,0:T(8,128)(2,1)S(1)}, bf16[128,256]{1,0:T(8,128)(2,1)S(1)}, u32[]{:S(2)}, u32[]{:S(2)}) collective-permute-start(bf16[128,256]{1,0:T(8,128)(2,1)S(1)} %get-tuple-element.48.refs_0_), channel_id=1, source_target_pairs={{0,2},{1,3},{2,0},{3,1},{4,6},{5,7},{6,4},{7,5},{8,10},{9,11},{10,... | collective-permute-start | bytes 196616 | tf_op jit(solution)/shard_map/ppermute | solution.py:31
  120.4 11.6 %collective-permute-start.26 = (bf16[576,256]{1,0:T(8,128)(2,1)S(1)}, bf16[576,256]{1,0:T(8,128)(2,1)S(1)}, u32[]{:S(2)}, u32[]{:S(2)}) collective-permute-start(bf16[576,256]{1,0:T(8,128)(2,1)S(1)} %get-tuple-element.54.joined.refs_0_), channel_id=1, source_target_pairs={{0,24},{8,16},{16,8},{24,0},{1,25},{9,17},{17,9},{25,1},{2,26},{10... | collective-permute-start | bytes 884744 | tf_op jit(solution)/shard_map/ppermute | solution.py:31
  122.0 11.1 %collective-permute-start.25 = (bf16[576,256]{1,0:T(8,128)(2,1)S(1)}, bf16[576,256]{1,0:T(8,128)(2,1)S(1)}, u32[]{:S(2)}, u32[]{:S(2)}) collective-permute-start(bf16[576,256]{1,0:T(8,128)(2,1)S(1)} %get-tuple-element.54.joined.refs_0_), channel_id=1, source_target_pairs={{0,16},{8,24},{16,0},{24,8},{1,17},{9,25},{17,1},{25,9},{2,18},{10... | collective-permute-start | bytes 884744 | tf_op jit(solution)/shard_map/ppermute | solution.py:31
  122.7 10.4 %collective-permute-start.24 = (bf16[576,256]{1,0:T(8,128)(2,1)S(1)}, bf16[576,256]{1,0:T(8,128)(2,1)S(1)}, u32[]{:S(2)}, u32[]{:S(2)}) collective-permute-start(bf16[576,256]{1,0:T(8,128)(2,1)S(1)} %get-tuple-element.54.joined.refs_0_), channel_id=1, source_target_pairs={{0,8},{8,0},{16,24},{24,16},{1,9},{9,1},{17,25},{25,17},{2,10},{10... | collective-permute-start | bytes 884744 | tf_op jit(solution)/shard_map/ppermute | solution.py:31
  124.0 7.3 %collective-permute-start.23 = (bf16[256,256]{1,0:T(8,128)(2,1)S(1)}, bf16[256,256]{1,0:T(8,128)(2,1)S(1)}, u32[]{:S(2)}, u32[]{:S(2)}) collective-permute-start(bf16[256,256]{1,0:T(8,128)(2,1)S(1)} %get-tuple-element.53), channel_id=1, source_target_pairs={{0,4},{1,5},{2,6},{3,7},{4,0},{5,1},{6,2},{7,3},{8,12},{9,13},{10,... | collective-permute-start | bytes 393224 | tf_op jit(solution)/shard_map/ppermute | solution.py:31
  132.0 1.6 %collective-permute-start.27 = (bf16[576,256]{1,0:T(8,128)(2,1)S(1)}, bf16[576,256]{1,0:T(8,128)(2,1)S(1)}, u32[]{:S(2)}, u32[]{:S(2)}) collective-permute-start(bf16[576,256]{1,0:T(8,128)(2,1)S(1)} %get-tuple-element.56), channel_id=1, source_target_pairs={{0,1},{1,0},{2,3},{3,2},{4,5},{5,4},{6,7},{7,6},{8,9},{9,8},{10,11... | collective-permute-start | bytes 884744 | tf_op jit(solution)/shard_map/ppermute | solution.py:31
  132.0 2.0 %collective-permute-start.30 = (bf16[576,256]{1,0:T(8,128)(2,1)S(1)}, bf16[576,256]{1,0:T(8,128)(2,1)S(1)}, u32[]{:S(2)}, u32[]{:S(2)}) collective-permute-start(bf16[576,256]{1,0:T(8,128)(2,1)S(1)} %collective-permute-done.26.refs_3_), channel_id=1, source_target_pairs={{0,1},{1,0},{2,3},{3,2},{4,5},{5,4},{6,7},{7,6},{8,9},{9,8},{10,11... | collective-permute-start | bytes 884744 | tf_op jit(solution)/shard_map/ppermute | solution.py:31
  133.1 1.6 %collective-permute-start.29 = (bf16[576,256]{1,0:T(8,128)(2,1)S(1)}, bf16[576,256]{1,0:T(8,128)(2,1)S(1)}, u32[]{:S(2)}, u32[]{:S(2)}) collective-permute-start(bf16[576,256]{1,0:T(8,128)(2,1)S(1)} %collective-permute-done.25.refs_2_), channel_id=1, source_target_pairs={{0,1},{1,0},{2,3},{3,2},{4,5},{5,4},{6,7},{7,6},{8,9},{9,8},{10,11... | collective-permute-start | bytes 884744 | tf_op jit(solution)/shard_map/ppermute | solution.py:31
  133.1 2.0 %collective-permute-start.28 = (bf16[576,256]{1,0:T(8,128)(2,1)S(1)}, bf16[576,256]{1,0:T(8,128)(2,1)S(1)}, u32[]{:S(2)}, u32[]{:S(2)}) collective-permute-start(bf16[576,256]{1,0:T(8,128)(2,1)S(1)} %collective-permute-done.24.refs_1_), channel_id=1, source_target_pairs={{0,1},{1,0},{2,3},{3,2},{4,5},{5,4},{6,7},{7,6},{8,9},{9,8},{10,11... | collective-permute-start | bytes 884744 | tf_op jit(solution)/shard_map/ppermute | solution.py:31
  (3 other events, 6.6 us)

commit v5 on v4

--- a/solution.py
+++ b/solution.py
@@ -75,11 +75,10 @@
     return term_b, term_c
 
 
-def run_pick(blocks, ids, hours, own):
-    grant = 4 * blocks * SIDE * hours.shape[1] + 4 * own.size + (2 << 20)
+def run_pick(blocks, ids, hours):
     rank = hours.shape[1]
 
-    def kernel(ids, hours, own, out, same, sem):
+    def kernel(ids, hours, out, sem):
         copies = []
         for t in range(blocks):
             at = pl.multiple_of(ids[8 + 4 * blocks + t] * SIDE, SIDE)
@@ -89,22 +88,20 @@
                 )
             )
             copies[-1].start()
-        same[...] = own[...]
         for copy in copies:
             copy.wait()
 
+    grant = 4 * blocks * SIDE * rank + (2 << 20)
     return pl.pallas_call(
         kernel,
-        in_specs=[SMEM, HBM, VMEM],
-        out_specs=[VMEM, VMEM],
-        out_shape=[
-            jax.ShapeDtypeStruct((blocks * SIDE, rank), BF16),
-            jax.ShapeDtypeStruct(own.shape, BF16),
-        ],
+        in_specs=[SMEM, HBM],
+        out_specs=VMEM,
+        out_shape=jax.ShapeDtypeStruct((blocks * SIDE, rank), BF16),
         scratch_shapes=[pltpu.SemaphoreType.DMA((blocks,))],
         compiler_params=pltpu.CompilerParams(vmem_limit_bytes=grant),
+        cost_estimate=pl.CostEstimate(flops=SLOW // 10, bytes_accessed=0, transcendentals=0),
         name="pick_hours",
-    )(ids, hours, own)
+    )(ids, hours)
 
 
 def main_kernel(shape, ids, counts, hours, near, far, *refs):
@@ -420,19 +417,22 @@
     return call(kernel, "z_sum", (*hd_parts, s_acc, s_got), outs)
 
 
-def run_join(parts, keep=None, got=None):
+def run_join(parts, keep=None, got=None, passed=None):
     rows = [p.shape[0] for p in parts]
-    n = len(parts)
     outs = [((sum(rows), parts[0].shape[1]), BF16)]
-    if got is None:
-        ins = tuple(parts)
-    else:
-        ins = (*parts, keep, got)
+    ins = tuple(parts)
+    if got is not None:
+        ins += (keep, got)
         outs += halves(got)
+    if passed is not None:
+        ins += (passed,)
+        outs += [(passed.shape, BF16)]
 
     def kernel(*refs):
         if got is not None:
-            halve(refs[n], refs[n + 1], refs[-2], refs[-1])
+            halve(refs[len(parts)], refs[len(parts) + 1], refs[-2], refs[-1])
+        if passed is not None:
+            refs[-1][...] = refs[len(parts)][...]
         out, at = refs[len(ins)], 0
         for ref, n_rows in zip(refs, rows):
             out[at : at + n_rows, :] = ref[...]
@@ -450,7 +450,7 @@
     return call(kernel, "src_sum", (keep, got, joined), outs)
 
 
-def run_place(sizes, hour_rows, ids, parts, so_far, dst_rows=0, passed=()):
+def run_place(sizes, hour_rows, ids, parts, so_far, dst_rows=0):
     grps, devs = sizes
     depth = devs // 2
     arrays = [p for p, _, _ in parts]
@@ -462,8 +462,6 @@
 
     def kernel(ids, *refs):
         outs = refs[n + len(more) : -2]
-        for i in passed:
-            outs[-1][...] = refs[i][...]
         stage, sem = refs[-2:]
         core, z, grp = ids[0] & 1, ids[0] >> 1, ids[1]
         copies = []
@@ -487,7 +485,6 @@
     outs = [jax.ShapeDtypeStruct((hour_rows, rank), F32)]
     if dst_rows:
         outs.append(jax.ShapeDtypeStruct((grps * dst_rows, rank), F32))
-    outs += [jax.ShapeDtypeStruct(arrays[i].shape, BF16) for i in passed]
     scratch = [((n, part, rank), F32)]
     need = size_of([(p.shape, p.dtype) for p in arrays + outs[1:]] + scratch) + (4 << 20)
     return pl.pallas_call(
@@ -498,6 +495,9 @@
         scratch_shapes=[pltpu.VMEM(s, t) for s, t in scratch] + [pltpu.SemaphoreType.DMA((n,))],
         input_output_aliases={n + 1: 0} if more else {},
         compiler_params=pltpu.CompilerParams(vmem_limit_bytes=need),
+        cost_estimate=pl.CostEstimate(
+            flops=0 if more else SLOW // 10, bytes_accessed=0, transcendentals=0
+        ),
         name="place",
     )(ids, *arrays, *more)
 
@@ -527,11 +527,10 @@
     dst_part = local // grps
     dst_own = lax.dynamic_slice_in_dim(dst_factor, grp * dst_part, dst_part, 0)
     dst_z = [dst_own] + [swap(dst_own, "dev", devs, 2 * m) for m in range(1, depth)]
-    src_z = [swap(src_factor, "dev", devs, 2 * m) for m in range(2, depth)]
+    src_z = [src_factor] + [swap(src_factor, "dev", devs, 2 * m) for m in range(1, depth)]
     blocks = counts.shape[0]
-    picked, src_same = run_pick(blocks, ids, hour_factor, src_factor)
-    src_z = [src_factor, swap(src_same, "dev", devs, 2)] + src_z
-    dst_here = run_join(dst_z)[0]
+    picked = run_pick(blocks, ids, hour_factor)
+    dst_here, src_z[1] = run_join(dst_z, passed=src_z[1])
     dsts = [dst_here] + [swap(dst_here, "grp", grps, m) for m in range(1, grps)]
     near = run_join(src_z + dsts)[0]
     far = swap(near, "dev", devs, 1)
@@ -543,7 +542,7 @@
 
     hd_got = swap(hd_send, "dev", devs, 1)
     src = functools.partial(run_src, (devs, local))
-    early = blocks // 4
+    early = blocks // 6
     s_acc = src(0, early, ids, resids, b_rows, picked, hd_send)[0]
     *hd, cut_done = run_cut(grps, hd_acc, hd_got, s_acc)
     cut_done = swap(cut_done, "dev", devs, 1)
@@ -564,9 +563,13 @@
         s_got = swap(s_send, "dev", devs, step)
     grad_src, same = run_src_sum(s_keep, s_got, joined)
     near = [joined] + [swap(joined, "grp", grps, m) for m in range(1, grps)]
-    parts = [(x, 0, m) for m, x in enumerate(near)]
-    parts += [(swap(x, "dev", devs, 1), 1, m) for m, x in enumerate([same] + near[1:])]
-    grad_hour, grad_dst = run_place(sizes, hour_rows, ids, parts, None, dst_part)
+    far = [swap(x, "dev", devs, 1) for x in [same] + near[1:]]
+    put = functools.partial(run_place, sizes, hour_rows, ids)
+    sooner = [0] + list(range(2, grps))
+    grad_hour = put([(near[m], 0, m) for m in sooner], None)[0]
+    parts = [(near[1], 0, 1)] + [(far[m], 1, m) for m in range(grps)]
+    parts += [(near[m], None, m) for m in sooner]
+    grad_hour, grad_dst = put(parts, grad_hour, dst_part)
     return grad_src, grad_dst, grad_hour
 
 

time: 139 us -> 137 us (0.986)
  waiting for transfers between devices: 34.8 us -> 32.7 us
    ppermute x31, waiting for transfers between devices: 34.8 us -> 32.7 us  [swap(): return lax.ppermute(x, axis, [(i, i ^ mask) for i in range(size)])]
    pallas_call x1 -> x2, Pallas kernels: 3.35 us -> 4.58 us  [run_place(): pl.pallas_call(kernel, in_specs=[SMEM] + [VMEM] * n + [HBM] * len(more),...]
  transfers between devices with their start and end apart: 31 -> 31, of which waited for: 14 -> 14; matrix products, arithmetic and copies ran while one was open for 1% -> 1% of each run, Pallas kernels for 13% -> 14%
where the time goes in v5:
time: 137 us
  Pallas kernels  64.2 us (47%)
  starting transfers between devices  35.7 us (26%)
  waiting for transfers between devices  32.7 us (24%)
  local copies, waits for them, and re-layouts  3.32 us (2%)
    pallas_call x1, Pallas kernels, run_main(): pl.pallas_call(functools.partial(main_kernel, shape), in_specs=[SMEM, HBM...  41.5 us
    ppermute x31, starting transfers between devices, swap(): return lax.ppermute(x, axis, [(i, i ^ mask) for i in range(size)])  35.7 us
    ppermute x31, waiting for transfers between devices, swap(): return lax.ppermute(x, axis, [(i, i ^ mask) for i in range(size)])  32.7 us
    pallas_call x2, Pallas kernels, run_src(): pl.pallas_call(functools.partial(src_kernel, shape, first, last), in_spec...  14.1 us
    pallas_call x2, Pallas kernels, run_place(): pl.pallas_call(kernel, in_specs=[SMEM] + [VMEM] * n + [HBM] * len(more),...  4.58 us
  transfers between devices with their start and end apart: 31, of which 14 were waited for; matrix products, arithmetic and copies ran while one was open for 1% of the time, Pallas kernels for 14%

profile of v5, /device:TPU:0, one launch (start us, length us, event | category | flops | bytes accessed | tf_op | source)
XLA Modules:
  0.0 136.8 jit_solution(8367716393924216700)
XLA Ops:
  0.6 3.1 %collective-permute-start.3 = (bf16[256,256]{1,0:T(8,128)(2,1)}, bf16[256,256]{1,0:T(8,128)(2,1)S(1)}, u32[]{:S(2)}, u32[]{:S(2)}) collective-permute-start(bf16[256,256]{1,0:T(8,128)(2,1)} %refs_0_.1), channel_id=1, source_target_pairs={{0,2},{1,3},{2,0},{3,1},{4,6},{5,7},{6,4},{7,5},{8,10},{9,11},{10,... | collective-permute-start | bytes 393224 | tf_op jit(solution)/shard_map/ppermute | solution.py:31
  3.7 2.9 %collective-permute-start.2 = (bf16[64,256]{1,0:T(8,128)(2,1)S(1)}, bf16[64,256]{1,0:T(8,128)(2,1)S(1)}, u32[]{:S(2)}, u32[]{:S(2)}) collective-permute-start(bf16[64,256]{1,0:T(8,128)(2,1)S(1)} %constant_dynamic-slice_fusion.refs_0_), channel_id=1, source_target_pairs={{0,6},{1,7},{2,4},{3,5},{4,2},{5,3},{6,0},{7,1},{8,14},{9,15},{10,... | collective-permute-start | bytes 98312 | tf_op jit(solution)/shard_map/ppermute | solution.py:31
  6.6 1.5 %collective-permute-start = (bf16[64,256]{1,0:T(8,128)(2,1)S(1)}, bf16[64,256]{1,0:T(8,128)(2,1)S(1)}, u32[]{:S(2)}, u32[]{:S(2)}) collective-permute-start(bf16[64,256]{1,0:T(8,128)(2,1)S(1)} %constant_dynamic-slice_fusion.refs_0_), channel_id=1, source_target_pairs={{0,2},{1,3},{2,0},{3,1},{4,6},{5,7},{6,4},{7,5},{8,10},{9,11},{10,... | collective-permute-start | bytes 98312 | tf_op jit(solution)/shard_map/ppermute | solution.py:31
  8.1 1.7 %collective-permute-start.4 = (bf16[256,256]{1,0:T(8,128)(2,1)}, bf16[256,256]{1,0:T(8,128)(2,1)S(1)}, u32[]{:S(2)}, u32[]{:S(2)}) collective-permute-start(bf16[256,256]{1,0:T(8,128)(2,1)} %refs_0_.1), channel_id=1, source_target_pairs={{0,4},{1,5},{2,6},{3,7},{4,0},{5,1},{6,2},{7,3},{8,12},{9,13},{10,... | collective-permute-start | bytes 393224 | tf_op jit(solution)/shard_map/ppermute | solution.py:31
  9.8 1.0 collective-permute-done.2.refs_3_
  10.8 1.7 %collective-permute-start.5 = (bf16[256,256]{1,0:T(8,128)(2,1)}, bf16[256,256]{1,0:T(8,128)(2,1)S(1)}, u32[]{:S(2)}, u32[]{:S(2)}) collective-permute-start(bf16[256,256]{1,0:T(8,128)(2,1)} %refs_0_.1), channel_id=1, source_target_pairs={{0,6},{1,7},{2,4},{3,5},{4,2},{5,3},{6,0},{7,1},{8,14},{9,15},{10,... | collective-permute-start | bytes 393224 | tf_op jit(solution)/shard_map/ppermute | solution.py:31
  12.5 3.7 %collective-permute-done.1.refs_2_ = bf16[64,256]{1,0:T(8,128)(2,1)S(1)} collective-permute-done((bf16[64,256]{1,0:T(8,128)(2,1)S(1)}, bf16[64,256]{1,0:T(8,128)(2,1)S(1)}, u32[]{:S(2)}, u32[]{:S(2)}) %collective-permute-start.1) | collective-permute-done | bytes 32800 | tf_op jit(solution)/shard_map/ppermute | solution.py:31
  16.2 2.5 %collective-permute-start.8 = (bf16[256,256]{1,0:T(8,128)(2,1)S(1)}, bf16[256,256]{1,0:T(8,128)(2,1)S(1)}, u32[]{:S(2)}, u32[]{:S(2)}) collective-permute-start(bf16[256,256]{1,0:T(8,128)(2,1)S(1)} %get-tuple-element.32.refs_4_), channel_id=1, source_target_pairs={{0,24},{8,16},{16,8},{24,0},{1,25},{9,17},{17,9},{25,1},{2,26},{10... | collective-permute-start | bytes 393224 | tf_op jit(solution)/shard_map/ppermute | solution.py:31
  20.4 1.7 %collective-permute-done.8.refs_7_ = bf16[256,256]{1,0:T(8,128)(2,1)S(1)} collective-permute-done((bf16[256,256]{1,0:T(8,128)(2,1)S(1)}, bf16[256,256]{1,0:T(8,128)(2,1)S(1)}, u32[]{:S(2)}, u32[]{:S(2)}) %collective-permute-start.8) | collective-permute-done | bytes 131104 | tf_op jit(solution)/shard_map/ppermute | solution.py:31
  22.1 1.5 %collective-permute-done.7.refs_6_ = bf16[256,256]{1,0:T(8,128)(2,1)S(1)} collective-permute-done((bf16[256,256]{1,0:T(8,128)(2,1)S(1)}, bf16[256,256]{1,0:T(8,128)(2,1)S(1)}, u32[]{:S(2)}, u32[]{:S(2)}) %collective-permute-start.7) | collective-permute-done | bytes 131104 | tf_op jit(solution)/shard_map/ppermute | solution.py:31
  26.1 1.6 %copy-done.2 = bf16[4096,256]{1,0:T(8,128)(2,1)S(1)} copy-done((bf16[4096,256]{1,0:T(8,128)(2,1)S(1)}, bf16[4096,256]{1,0:T(8,128)(2,1)}, u32[]{:S(2)}) %copy-start.2) | copy-done | bytes 2097176
  27.7 1.9 %pick_hours.1.hours = bf16[1536,256]{1,0:T(8,128)(2,1)S(1)} custom-call(s32[128]{0:T(128)S(1)} %concatenate.3.ids, bf16[4096,256]{1,0:T(8,128)(2,1)S(1)} %copy-done.2), custom_call_target="tpu_custom_call" | custom-call | flops 10000000000 | tf_op jit(solution)/shard_map/pick_hours/pallas_call | solution.py:95
  29.6 41.5 %hour_dst_terms.1 = (f32[6144,256]{1,0:T(8,128)S(1)}, bf16[3072,256]{1,0:T(8,128)(2,1)S(1)}, bf16[1536,256]{1,0:T(8,128)(2,1)S(1)}, bf16[24,64,4096]{2,1,0:T(8,128)(2,1)}) custom-call(s32[128]{0:T(128)S(1)} %concatenate.3.ids, bf16[24,64,4096]{2,1,0:T(8,128)(2,1)} %counts.1, bf16[1536,256]{1,0:T(8,128)(2,1)S(1)} %pick_hours.1.hours, ...), custom_call_target="tpu_custom_call" | custom-call | flops 9663676416 | bytes 25165824 | tf_op jit(solution)/shard_map/hour_dst_terms/pallas_call | solution.py:269
  71.6 3.4 %src_terms.2.after.refs_0_ = f32[2048,256]{1,0:T(8,128)S(1)} custom-call(s32[128]{0:T(128)S(1)} %concatenate.3.ids, bf16[24,64,4096]{2,1,0:T(8,128)(2,1)} %get-tuple-element.35.resids, bf16[1536,256]{1,0:T(8,128)(2,1)S(1)} %get-tuple-element.36.b_rows, bf16[1536,256]{1,0:T(8,128)(2,1)S(1)} %pick_hours.1.hours, bf16[3072,256]{1,0:T(8,128)(2,1)S(1)} %get-tuple-element.34.after), custom_call_target="tpu_custom_call" | custom-call | flops 2147483648 | bytes 2097152 | tf_op jit(solution)/shard_map/src_terms/pallas_call | solution.py:301
  75.4 1.0 collective-permute-start.11
  76.4 1.1 collective-permute-start.12
  77.5 1.4 %collective-permute-start.13 = (bf16[768,256]{1,0:T(8,128)(2,1)S(1)}, bf16[768,256]{1,0:T(8,128)(2,1)S(1)}, u32[]{:S(2)}, u32[]{:S(2)}) collective-permute-start(bf16[768,256]{1,0:T(8,128)(2,1)S(1)} %get-tuple-element.40), channel_id=1, source_target_pairs={{0,24},{8,16},{16,8},{24,0},{1,25},{9,17},{17,9},{25,1},{2,26},{10... | collective-permute-start | bytes 1179656 | tf_op jit(solution)/shard_map/ppermute | solution.py:31
  79.0 10.6 %src_terms.3 = (f32[2048,256]{1,0:T(8,128)S(1)}, bf16[1024,256]{1,0:T(8,128)(2,1)S(1)}) custom-call(s32[128]{0:T(128)S(1)} %concatenate.3.ids, bf16[24,64,4096]{2,1,0:T(8,128)(2,1)} %get-tuple-element.35.resids, bf16[1536,256]{1,0:T(8,128)(2,1)S(1)} %get-tuple-element.36.b_rows, ...), custom_call_target="tpu_custom_call", output_to_operand_aliasing={{0}: (5, {})} | custom-call | flops 10737418240 | bytes 10485760 | tf_op jit(solution)/shard_map/src_terms/pallas_call | solution.py:301
  89.7 5.0 %collective-permute-done.12.refs_2_ = bf16[768,256]{1,0:T(8,128)(2,1)S(1)} collective-permute-done((bf16[768,256]{1,0:T(8,128)(2,1)S(1)}, bf16[768,256]{1,0:T(8,128)(2,1)S(1)}, u32[]{:S(2)}, u32[]{:S(2)}) %collective-permute-start.12) | collective-permute-done | bytes 393248 | tf_op jit(solution)/shard_map/ppermute | solution.py:31
  94.7 1.6 %collective-permute-done.13.refs_3_ = bf16[768,256]{1,0:T(8,128)(2,1)S(1)} collective-permute-done((bf16[768,256]{1,0:T(8,128)(2,1)S(1)}, bf16[768,256]{1,0:T(8,128)(2,1)S(1)}, u32[]{:S(2)}, u32[]{:S(2)}) %collective-permute-start.13) | collective-permute-done | bytes 393248 | tf_op jit(solution)/shard_map/ppermute | solution.py:31
  97.3 4.3 %collective-permute-start.16 = (bf16[192,256]{1,0:T(8,128)(2,1)S(1)}, bf16[192,256]{1,0:T(8,128)(2,1)S(1)}, u32[]{:S(2)}, u32[]{:S(2)}) collective-permute-start(bf16[192,256]{1,0:T(8,128)(2,1)S(1)} %get-tuple-element.44), channel_id=1, source_target_pairs={{0,6},{1,7},{2,4},{3,5},{4,2},{5,3},{6,0},{7,1},{8,14},{9,15},{10,... | collective-permute-start | bytes 294920 | tf_op jit(solution)/shard_map/ppermute | solution.py:31
  101.6 1.0 collective-permute-done.14.refs_1_
  102.7 5.2 %collective-permute-done.15.refs_2_ = bf16[192,256]{1,0:T(8,128)(2,1)S(1)} collective-permute-done((bf16[192,256]{1,0:T(8,128)(2,1)S(1)}, bf16[192,256]{1,0:T(8,128)(2,1)S(1)}, u32[]{:S(2)}, u32[]{:S(2)}) %collective-permute-start.15) | collective-permute-done | bytes 98336 | tf_op jit(solution)/shard_map/ppermute | solution.py:31
  108.0 1.7 %collective-permute-start.22 = (bf16[512,256]{1,0:T(8,128)(2,1)S(1)}, bf16[512,256]{1,0:T(8,128)(2,1)S(1)}, u32[]{:S(2)}, u32[]{:S(2)}) collective-permute-start(bf16[512,256]{1,0:T(8,128)(2,1)S(1)} %get-tuple-element.51), channel_id=1, source_target_pairs={{0,2},{1,3},{2,0},{3,1},{4,6},{5,7},{6,4},{7,5},{8,10},{9,11},{10,... | collective-permute-start | bytes 786440 | tf_op jit(solution)/shard_map/ppermute | solution.py:31
  109.7 1.4 collective-permute-start.21
  111.6 2.5 %collective-permute-start.19 = (bf16[128,256]{1,0:T(8,128)(2,1)S(1)}, bf16[128,256]{1,0:T(8,128)(2,1)S(1)}, u32[]{:S(2)}, u32[]{:S(2)}) collective-permute-start(bf16[128,256]{1,0:T(8,128)(2,1)S(1)} %get-tuple-element.48.refs_0_), channel_id=1, source_target_pairs={{0,2},{1,3},{2,0},{3,1},{4,6},{5,7},{6,4},{7,5},{8,10},{9,11},{10,... | collective-permute-start | bytes 196616 | tf_op jit(solution)/shard_map/ppermute | solution.py:31
  114.1 4.8 %collective-permute-done.21.refs_3_ = bf16[128,256]{1,0:T(8,128)(2,1)S(1)} collective-permute-done((bf16[128,256]{1,0:T(8,128)(2,1)S(1)}, bf16[128,256]{1,0:T(8,128)(2,1)S(1)}, u32[]{:S(2)}, u32[]{:S(2)}) %collective-permute-start.21) | collective-permute-done | bytes 65568 | tf_op jit(solution)/shard_map/ppermute | solution.py:31
  119.9 1.8 %collective-permute-start.27 = (bf16[576,256]{1,0:T(8,128)(2,1)S(1)}, bf16[576,256]{1,0:T(8,128)(2,1)S(1)}, u32[]{:S(2)}, u32[]{:S(2)}) collective-permute-start(bf16[576,256]{1,0:T(8,128)(2,1)S(1)} %get-tuple-element.54.joined.refs_0_.refs_5_), channel_id=1, source_target_pairs={{0,16},{8,24},{16,0},{24,8},{1,17},{9,25},{17,1},{25,9},{2,18},{10... | collective-permute-start | bytes 884744 | tf_op jit(solution)/shard_map/ppermute | solution.py:31
  122.6 1.9 %collective-permute-start.23 = (bf16[256,256]{1,0:T(8,128)(2,1)S(1)}, bf16[256,256]{1,0:T(8,128)(2,1)S(1)}, u32[]{:S(2)}, u32[]{:S(2)}) collective-permute-start(bf16[256,256]{1,0:T(8,128)(2,1)S(1)} %get-tuple-element.53), channel_id=1, source_target_pairs={{0,4},{1,5},{2,6},{3,7},{4,0},{5,1},{6,2},{7,3},{8,12},{9,13},{10,... | collective-permute-start | bytes 393224 | tf_op jit(solution)/shard_map/ppermute | solution.py:31
  124.5 5.3 %collective-permute-done.23.got = bf16[256,256]{1,0:T(8,128)(2,1)S(1)} collective-permute-done((bf16[256,256]{1,0:T(8,128)(2,1)S(1)}, bf16[256,256]{1,0:T(8,128)(2,1)S(1)}, u32[]{:S(2)}, u32[]{:S(2)}) %collective-permute-start.23) | collective-permute-done | bytes 131104 | tf_op jit(solution)/shard_map/ppermute | solution.py:31
  132.1 1.7 %place.2.refs_8_ = f32[4096,256]{1,0:T(8,128)} custom-call(s32[128]{0:T(128)S(1)} %concatenate.3.ids, bf16[576,256]{1,0:T(8,128)(2,1)S(1)} %get-tuple-element.54.joined.refs_0_.refs_5_, bf16[576,256]{1,0:T(8,128)(2,1)S(1)} %collective-permute-done.27.refs_1_.refs_6_, bf16[576,256]{1,0:T(8,128)(2,1)S(1)} %collective-permute-done.29.refs_2_.refs_7_), custom_call_target="tpu_custom_call" | custom-call | flops 10000000000 | tf_op jit(solution)/shard_map/place/pallas_call | solution.py:490
  133.9 2.8 %place.3 = (f32[4096,256]{1,0:T(8,128)}, f32[256,256]{1,0:T(8,128)}) custom-call(s32[128]{0:T(128)S(1)} %concatenate.3.ids, bf16[576,256]{1,0:T(8,128)(2,1)S(1)} %collective-permute-done.24.refs_0_, bf16[576,256]{1,0:T(8,128)(2,1)S(1)} %collective-permute-done.25.refs_1_, ...), custom_call_target="tpu_custom_call", output_to_operand_aliasing={{0}: (9, {})} | custom-call | tf_op jit(solution)/shard_map/place/pallas_call | solution.py:490
  (53 shorter events, 10.9 us)
Async XLA Ops:
  0.6 3.1 %copy-start = (bf16[256,256]{1,0:T(8,128)(2,1)S(1)}, bf16[256,256]{1,0:T(8,128)(2,1)}, u32[]{:S(2)}) copy-start(bf16[256,256]{1,0:T(8,128)(2,1)} %param.11) | copy-start | bytes 393220
  0.6 15.5 %collective-permute-start.3 = (bf16[256,256]{1,0:T(8,128)(2,1)}, bf16[256,256]{1,0:T(8,128)(2,1)S(1)}, u32[]{:S(2)}, u32[]{:S(2)}) collective-permute-start(bf16[256,256]{1,0:T(8,128)(2,1)} %refs_0_.1), channel_id=1, source_target_pairs={{0,2},{1,3},{2,0},{3,1},{4,6},{5,7},{6,4},{7,5},{8,10},{9,11},{10,... | collective-permute-start | bytes 393224 | tf_op jit(solution)/shard_map/ppermute | solution.py:31
  3.7 7.1 %collective-permute-start.2 = (bf16[64,256]{1,0:T(8,128)(2,1)S(1)}, bf16[64,256]{1,0:T(8,128)(2,1)S(1)}, u32[]{:S(2)}, u32[]{:S(2)}) collective-permute-start(bf16[64,256]{1,0:T(8,128)(2,1)S(1)} %constant_dynamic-slice_fusion.refs_0_), channel_id=1, source_target_pairs={{0,6},{1,7},{2,4},{3,5},{4,2},{5,3},{6,0},{7,1},{8,14},{9,15},{10,... | collective-permute-start | bytes 98312 | tf_op jit(solution)/shard_map/ppermute | solution.py:31
  6.6 9.6 %collective-permute-start.1 = (bf16[64,256]{1,0:T(8,128)(2,1)S(1)}, bf16[64,256]{1,0:T(8,128)(2,1)S(1)}, u32[]{:S(2)}, u32[]{:S(2)}) collective-permute-start(bf16[64,256]{1,0:T(8,128)(2,1)S(1)} %constant_dynamic-slice_fusion.refs_0_), channel_id=1, source_target_pairs={{0,4},{1,5},{2,6},{3,7},{4,0},{5,1},{6,2},{7,3},{8,12},{9,13},{10,... | collective-permute-start | bytes 98312 | tf_op jit(solution)/shard_map/ppermute | solution.py:31
  6.6 9.6 %collective-permute-start = (bf16[64,256]{1,0:T(8,128)(2,1)S(1)}, bf16[64,256]{1,0:T(8,128)(2,1)S(1)}, u32[]{:S(2)}, u32[]{:S(2)}) collective-permute-start(bf16[64,256]{1,0:T(8,128)(2,1)S(1)} %constant_dynamic-slice_fusion.refs_0_), channel_id=1, source_target_pairs={{0,2},{1,3},{2,0},{3,1},{4,6},{5,7},{6,4},{7,5},{8,10},{9,11},{10,... | collective-permute-start | bytes 98312 | tf_op jit(solution)/shard_map/ppermute | solution.py:31
  8.1 12.3 %collective-permute-start.4 = (bf16[256,256]{1,0:T(8,128)(2,1)}, bf16[256,256]{1,0:T(8,128)(2,1)S(1)}, u32[]{:S(2)}, u32[]{:S(2)}) collective-permute-start(bf16[256,256]{1,0:T(8,128)(2,1)} %refs_0_.1), channel_id=1, source_target_pairs={{0,4},{1,5},{2,6},{3,7},{4,0},{5,1},{6,2},{7,3},{8,12},{9,13},{10,... | collective-permute-start | bytes 393224 | tf_op jit(solution)/shard_map/ppermute | solution.py:31
  10.8 9.6 %collective-permute-start.5 = (bf16[256,256]{1,0:T(8,128)(2,1)}, bf16[256,256]{1,0:T(8,128)(2,1)S(1)}, u32[]{:S(2)}, u32[]{:S(2)}) collective-permute-start(bf16[256,256]{1,0:T(8,128)(2,1)} %refs_0_.1), channel_id=1, source_target_pairs={{0,6},{1,7},{2,4},{3,5},{4,2},{5,3},{6,0},{7,1},{8,14},{9,15},{10,... | collective-permute-start | bytes 393224 | tf_op jit(solution)/shard_map/ppermute | solution.py:31
  16.2 5.9 %collective-permute-start.8 = (bf16[256,256]{1,0:T(8,128)(2,1)S(1)}, bf16[256,256]{1,0:T(8,128)(2,1)S(1)}, u32[]{:S(2)}, u32[]{:S(2)}) collective-permute-start(bf16[256,256]{1,0:T(8,128)(2,1)S(1)} %get-tuple-element.32.refs_4_), channel_id=1, source_target_pairs={{0,24},{8,16},{16,8},{24,0},{1,25},{9,17},{17,9},{25,1},{2,26},{10... | collective-permute-start | bytes 393224 | tf_op jit(solution)/shard_map/ppermute | solution.py:31
  18.7 5.0 %collective-permute-start.7 = (bf16[256,256]{1,0:T(8,128)(2,1)S(1)}, bf16[256,256]{1,0:T(8,128)(2,1)S(1)}, u32[]{:S(2)}, u32[]{:S(2)}) collective-permute-start(bf16[256,256]{1,0:T(8,128)(2,1)S(1)} %get-tuple-element.32.refs_4_), channel_id=1, source_target_pairs={{0,16},{8,24},{16,0},{24,8},{1,17},{9,25},{17,1},{25,9},{2,18},{10... | collective-permute-start | bytes 393224 | tf_op jit(solution)/shard_map/ppermute | solution.py:31
  19.2 5.0 %collective-permute-start.6 = (bf16[256,256]{1,0:T(8,128)(2,1)S(1)}, bf16[256,256]{1,0:T(8,128)(2,1)S(1)}, u32[]{:S(2)}, u32[]{:S(2)}) collective-permute-start(bf16[256,256]{1,0:T(8,128)(2,1)S(1)} %get-tuple-element.32.refs_4_), channel_id=1, source_target_pairs={{0,8},{8,0},{16,24},{24,16},{1,9},{9,1},{17,25},{25,17},{2,10},{10... | collective-permute-start | bytes 393224 | tf_op jit(solution)/shard_map/ppermute | solution.py:31
  25.2 4.4 %collective-permute-start.9 = (bf16[2048,256]{1,0:T(8,128)(2,1)S(1)}, bf16[2048,256]{1,0:T(8,128)(2,1)S(1)}, u32[]{:S(2)}, u32[]{:S(2)}) collective-permute-start(bf16[2048,256]{1,0:T(8,128)(2,1)S(1)} %join.4.near), channel_id=1, source_target_pairs={{0,1},{1,0},{2,3},{3,2},{4,5},{5,4},{6,7},{7,6},{8,9},{9,8},{10,11... | collective-permute-start | bytes 3145736 | tf_op jit(solution)/shard_map/ppermute | solution.py:31
  71.1 4.0 %collective-permute-start.10 = (bf16[3072,256]{1,0:T(8,128)(2,1)S(1)}, bf16[3072,256]{1,0:T(8,128)(2,1)S(1)}, u32[]{:S(2)}, u32[]{:S(2)}) collective-permute-start(bf16[3072,256]{1,0:T(8,128)(2,1)S(1)} %get-tuple-element.34.after), channel_id=1, source_target_pairs={{0,1},{1,0},{2,3},{3,2},{4,5},{5,4},{6,7},{7,6},{8,9},{9,8},{10,11... | collective-permute-start | bytes 4718600 | tf_op jit(solution)/shard_map/ppermute | solution.py:31
  75.3 3.6 %collective-permute-start.17 = (f32[8,128]{1,0:T(8,128)S(1)}, f32[8,128]{1,0:T(8,128)S(1)}, u32[]{:S(2)}, u32[]{:S(2)}) collective-permute-start(f32[8,128]{1,0:T(8,128)S(1)} %get-tuple-element.45), channel_id=1, source_target_pairs={{0,1},{1,0},{2,3},{3,2},{4,5},{5,4},{6,7},{7,6},{8,9},{9,8},{10,11... | collective-permute-start | bytes 12296 | tf_op jit(solution)/shard_map/ppermute | solution.py:31
  75.4 14.3 %collective-permute-start.11 = (bf16[768,256]{1,0:T(8,128)(2,1)S(1)}, bf16[768,256]{1,0:T(8,128)(2,1)S(1)}, u32[]{:S(2)}, u32[]{:S(2)}) collective-permute-start(bf16[768,256]{1,0:T(8,128)(2,1)S(1)} %get-tuple-element.38), channel_id=1, source_target_pairs={{0,8},{8,0},{16,24},{24,16},{1,9},{9,1},{17,25},{25,17},{2,10},{10... | collective-permute-start | bytes 1179656 | tf_op jit(solution)/shard_map/ppermute | solution.py:31
  76.4 18.3 %collective-permute-start.12 = (bf16[768,256]{1,0:T(8,128)(2,1)S(1)}, bf16[768,256]{1,0:T(8,128)(2,1)S(1)}, u32[]{:S(2)}, u32[]{:S(2)}) collective-permute-start(bf16[768,256]{1,0:T(8,128)(2,1)S(1)} %get-tuple-element.39), channel_id=1, source_target_pairs={{0,16},{8,24},{16,0},{24,8},{1,17},{9,25},{17,1},{25,9},{2,18},{10... | collective-permute-start | bytes 1179656 | tf_op jit(solution)/shard_map/ppermute | solution.py:31
  77.5 18.8 %collective-permute-start.13 = (bf16[768,256]{1,0:T(8,128)(2,1)S(1)}, bf16[768,256]{1,0:T(8,128)(2,1)S(1)}, u32[]{:S(2)}, u32[]{:S(2)}) collective-permute-start(bf16[768,256]{1,0:T(8,128)(2,1)S(1)} %get-tuple-element.40), channel_id=1, source_target_pairs={{0,24},{8,16},{16,8},{24,0},{1,25},{9,17},{17,9},{25,1},{2,26},{10... | collective-permute-start | bytes 1179656 | tf_op jit(solution)/shard_map/ppermute | solution.py:31
  89.6 18.3 %collective-permute-start.18 = (bf16[1024,256]{1,0:T(8,128)(2,1)S(1)}, bf16[1024,256]{1,0:T(8,128)(2,1)S(1)}, u32[]{:S(2)}, u32[]{:S(2)}) collective-permute-start(bf16[1024,256]{1,0:T(8,128)(2,1)S(1)} %get-tuple-element.47), channel_id=1, source_target_pairs={{0,1},{1,0},{2,3},{3,2},{4,5},{5,4},{6,7},{7,6},{8,9},{9,8},{10,11... | collective-permute-start | bytes 1572872 | tf_op jit(solution)/shard_map/ppermute | solution.py:31
  97.2 5.5 %collective-permute-start.14 = (bf16[192,256]{1,0:T(8,128)(2,1)S(1)}, bf16[192,256]{1,0:T(8,128)(2,1)S(1)}, u32[]{:S(2)}, u32[]{:S(2)}) collective-permute-start(bf16[192,256]{1,0:T(8,128)(2,1)S(1)} %get-tuple-element.42), channel_id=1, source_target_pairs={{0,2},{1,3},{2,0},{3,1},{4,6},{5,7},{6,4},{7,5},{8,10},{9,11},{10,... | collective-permute-start | bytes 294920 | tf_op jit(solution)/shard_map/ppermute | solution.py:31
  97.3 10.6 %collective-permute-start.15 = (bf16[192,256]{1,0:T(8,128)(2,1)S(1)}, bf16[192,256]{1,0:T(8,128)(2,1)S(1)}, u32[]{:S(2)}, u32[]{:S(2)}) collective-permute-start(bf16[192,256]{1,0:T(8,128)(2,1)S(1)} %get-tuple-element.43), channel_id=1, source_target_pairs={{0,4},{1,5},{2,6},{3,7},{4,0},{5,1},{6,2},{7,3},{8,12},{9,13},{10,... | collective-permute-start | bytes 294920 | tf_op jit(solution)/shard_map/ppermute | solution.py:31
  97.3 10.5 %collective-permute-start.16 = (bf16[192,256]{1,0:T(8,128)(2,1)S(1)}, bf16[192,256]{1,0:T(8,128)(2,1)S(1)}, u32[]{:S(2)}, u32[]{:S(2)}) collective-permute-start(bf16[192,256]{1,0:T(8,128)(2,1)S(1)} %get-tuple-element.44), channel_id=1, source_target_pairs={{0,6},{1,7},{2,4},{3,5},{4,2},{5,3},{6,0},{7,1},{8,14},{9,15},{10,... | collective-permute-start | bytes 294920 | tf_op jit(solution)/shard_map/ppermute | solution.py:31
  108.0 11.0 %collective-permute-start.22 = (bf16[512,256]{1,0:T(8,128)(2,1)S(1)}, bf16[512,256]{1,0:T(8,128)(2,1)S(1)}, u32[]{:S(2)}, u32[]{:S(2)}) collective-permute-start(bf16[512,256]{1,0:T(8,128)(2,1)S(1)} %get-tuple-element.51), channel_id=1, source_target_pairs={{0,2},{1,3},{2,0},{3,1},{4,6},{5,7},{6,4},{7,5},{8,10},{9,11},{10,... | collective-permute-start | bytes 786440 | tf_op jit(solution)/shard_map/ppermute | solution.py:31
  109.7 9.2 %collective-permute-start.21 = (bf16[128,256]{1,0:T(8,128)(2,1)S(1)}, bf16[128,256]{1,0:T(8,128)(2,1)S(1)}, u32[]{:S(2)}, u32[]{:S(2)}) collective-permute-start(bf16[128,256]{1,0:T(8,128)(2,1)S(1)} %get-tuple-element.48.refs_0_), channel_id=1, source_target_pairs={{0,6},{1,7},{2,4},{3,5},{4,2},{5,3},{6,0},{7,1},{8,14},{9,15},{10,... | collective-permute-start | bytes 196616 | tf_op jit(solution)/shard_map/ppermute | solution.py:31
  111.1 7.8 %collective-permute-start.20 = (bf16[128,256]{1,0:T(8,128)(2,1)S(1)}, bf16[128,256]{1,0:T(8,128)(2,1)S(1)}, u32[]{:S(2)}, u32[]{:S(2)}) collective-permute-start(bf16[128,256]{1,0:T(8,128)(2,1)S(1)} %get-tuple-element.48.refs_0_), channel_id=1, source_target_pairs={{0,4},{1,5},{2,6},{3,7},{4,0},{5,1},{6,2},{7,3},{8,12},{9,13},{10,... | collective-permute-start | bytes 196616 | tf_op jit(solution)/shard_map/ppermute | solution.py:31
  111.6 7.4 %collective-permute-start.19 = (bf16[128,256]{1,0:T(8,128)(2,1)S(1)}, bf16[128,256]{1,0:T(8,128)(2,1)S(1)}, u32[]{:S(2)}, u32[]{:S(2)}) collective-permute-start(bf16[128,256]{1,0:T(8,128)(2,1)S(1)} %get-tuple-element.48.refs_0_), channel_id=1, source_target_pairs={{0,2},{1,3},{2,0},{3,1},{4,6},{5,7},{6,4},{7,5},{8,10},{9,11},{10,... | collective-permute-start | bytes 196616 | tf_op jit(solution)/shard_map/ppermute | solution.py:31
  119.0 11.6 %collective-permute-start.29 = (bf16[576,256]{1,0:T(8,128)(2,1)S(1)}, bf16[576,256]{1,0:T(8,128)(2,1)S(1)}, u32[]{:S(2)}, u32[]{:S(2)}) collective-permute-start(bf16[576,256]{1,0:T(8,128)(2,1)S(1)} %get-tuple-element.54.joined.refs_0_.refs_5_), channel_id=1, source_target_pairs={{0,24},{8,16},{16,8},{24,0},{1,25},{9,17},{17,9},{25,1},{2,26},{10... | collective-permute-start | bytes 884744 | tf_op jit(solution)/shard_map/ppermute | solution.py:31
  119.9 11.7 %collective-permute-start.27 = (bf16[576,256]{1,0:T(8,128)(2,1)S(1)}, bf16[576,256]{1,0:T(8,128)(2,1)S(1)}, u32[]{:S(2)}, u32[]{:S(2)}) collective-permute-start(bf16[576,256]{1,0:T(8,128)(2,1)S(1)} %get-tuple-element.54.joined.refs_0_.refs_5_), channel_id=1, source_target_pairs={{0,16},{8,24},{16,0},{24,8},{1,17},{9,25},{17,1},{25,9},{2,18},{10... | collective-permute-start | bytes 884744 | tf_op jit(solution)/shard_map/ppermute | solution.py:31
  121.7 10.0 %collective-permute-start.24 = (bf16[576,256]{1,0:T(8,128)(2,1)S(1)}, bf16[576,256]{1,0:T(8,128)(2,1)S(1)}, u32[]{:S(2)}, u32[]{:S(2)}) collective-permute-start(bf16[576,256]{1,0:T(8,128)(2,1)S(1)} %get-tuple-element.54.joined.refs_0_.refs_5_), channel_id=1, source_target_pairs={{0,8},{8,0},{16,24},{24,16},{1,9},{9,1},{17,25},{25,17},{2,10},{10... | collective-permute-start | bytes 884744 | tf_op jit(solution)/shard_map/ppermute | solution.py:31
  122.6 7.3 %collective-permute-start.23 = (bf16[256,256]{1,0:T(8,128)(2,1)S(1)}, bf16[256,256]{1,0:T(8,128)(2,1)S(1)}, u32[]{:S(2)}, u32[]{:S(2)}) collective-permute-start(bf16[256,256]{1,0:T(8,128)(2,1)S(1)} %get-tuple-element.53), channel_id=1, source_target_pairs={{0,4},{1,5},{2,6},{3,7},{4,0},{5,1},{6,2},{7,3},{8,12},{9,13},{10,... | collective-permute-start | bytes 393224 | tf_op jit(solution)/shard_map/ppermute | solution.py:31
  130.6 3.2 %collective-permute-start.25 = (bf16[576,256]{1,0:T(8,128)(2,1)S(1)}, bf16[576,256]{1,0:T(8,128)(2,1)S(1)}, u32[]{:S(2)}, u32[]{:S(2)}) collective-permute-start(bf16[576,256]{1,0:T(8,128)(2,1)S(1)} %get-tuple-element.56), channel_id=1, source_target_pairs={{0,1},{1,0},{2,3},{3,2},{4,5},{5,4},{6,7},{7,6},{8,9},{9,8},{10,11... | collective-permute-start | bytes 884744 | tf_op jit(solution)/shard_map/ppermute | solution.py:31
  130.6 3.3 %collective-permute-start.30 = (bf16[576,256]{1,0:T(8,128)(2,1)S(1)}, bf16[576,256]{1,0:T(8,128)(2,1)S(1)}, u32[]{:S(2)}, u32[]{:S(2)}) collective-permute-start(bf16[576,256]{1,0:T(8,128)(2,1)S(1)} %collective-permute-done.29.refs_2_.refs_7_), channel_id=1, source_target_pairs={{0,1},{1,0},{2,3},{3,2},{4,5},{5,4},{6,7},{7,6},{8,9},{9,8},{10,11... | collective-permute-start | bytes 884744 | tf_op jit(solution)/shard_map/ppermute | solution.py:31
  131.6 2.3 %collective-permute-start.28 = (bf16[576,256]{1,0:T(8,128)(2,1)S(1)}, bf16[576,256]{1,0:T(8,128)(2,1)S(1)}, u32[]{:S(2)}, u32[]{:S(2)}) collective-permute-start(bf16[576,256]{1,0:T(8,128)(2,1)S(1)} %collective-permute-done.27.refs_1_.refs_6_), channel_id=1, source_target_pairs={{0,1},{1,0},{2,3},{3,2},{4,5},{5,4},{6,7},{7,6},{8,9},{9,8},{10,11... | collective-permute-start | bytes 884744 | tf_op jit(solution)/shard_map/ppermute | solution.py:31
  131.6 2.3 %collective-permute-start.26 = (bf16[576,256]{1,0:T(8,128)(2,1)S(1)}, bf16[576,256]{1,0:T(8,128)(2,1)S(1)}, u32[]{:S(2)}, u32[]{:S(2)}) collective-permute-start(bf16[576,256]{1,0:T(8,128)(2,1)S(1)} %collective-permute-done.24.refs_0_), channel_id=1, source_target_pairs={{0,1},{1,0},{2,3},{3,2},{4,5},{5,4},{6,7},{7,6},{8,9},{9,8},{10,11... | collective-permute-start | bytes 884744 | tf_op jit(solution)/shard_map/ppermute | solution.py:31
  (2 other events, 2.5 us)

commit v6 on v5

--- a/solution.py
+++ b/solution.py
@@ -11,7 +11,6 @@
 BF16 = jnp.bfloat16
 SIDE = 64
 RING = 8
-OUT_RING = 4
 PITCH = 72
 GRANT = 36 << 20
 SRC_GRANT = 44 << 20
@@ -31,22 +30,26 @@
     return lax.ppermute(x, axis, [(i, i ^ mask) for i in range(size)])
 
 
-def block_terms(count, a, b, c, resid_out, cube, even, odd):
+def block_resid(count, a, b, c, resid_out, cube):
+    rank = a.shape[1]
+    for g in range(SIDE // 4):
+        b4 = b[g * 4 : g * 4 + 4]
+        bc = (b4[:, None, :] * c[None, :, :]).reshape(4 * SIDE, rank)
+        theta = lax.dot_general(a, bc, (((1,), (1,)), ((), ())), preferred_element_type=F32)
+        wide = jnp.exp(theta) - count[:, g * 256 : (g + 1) * 256].astype(F32)
+        for p in range(2):
+            cube[pl.ds((g * 2 + p) * PITCH, SIDE), :] = wide[:, p * 128 : (p + 1) * 128]
+        resid_out[:, g * 256 : (g + 1) * 256] = wide.astype(BF16)
+
+
+def block_terms(resid, a, b, c, cube, even, odd):
     rank = a.shape[1]
     turned, pairs_ab = [], []
     for g in range(SIDE // 4):
         b4 = b[g * 4 : g * 4 + 4]
-        bc = (b4[:, None, :] * c[None, :, :]).reshape(4 * SIDE, rank)
-        ab = (b4[:, None, :] * a[None, :, :]).reshape(4 * SIDE, rank)
-        theta = lax.dot_general(a, bc, (((1,), (1,)), ((), ())), preferred_element_type=F32)
-        wide = jnp.exp(theta) - count[:, g * 256 : (g + 1) * 256].astype(F32)
-        for p in range(2):
-            cube[pl.ds((g * 2 + p) * PITCH, SIDE), :] = wide[:, p * 128 : (p + 1) * 128]
-        resid = wide.astype(BF16)
-        flip = resid.T
+        pairs_ab.append((b4[:, None, :] * a[None, :, :]).reshape(4 * SIDE, rank))
+        flip = resid[:, g * 256 : (g + 1) * 256].T
         turned += [flip[q * SIDE : (q + 1) * SIDE] for q in range(4)]
-        resid_out[:, g * 256 : (g + 1) * 256] = resid
-        pairs_ab.append(ab)
     term_c = jnp.dot(
         jnp.concatenate(turned, axis=1),
         jnp.concatenate(pairs_ab, axis=0),
@@ -75,11 +78,12 @@
     return term_b, term_c
 
 
-def run_pick(blocks, ids, hours):
+def run_pick(blocks, ids, hours, own):
     rank = hours.shape[1]
 
-    def kernel(ids, hours, out, sem):
-        copies = []
+    def kernel(ids, hours, own, out, same, sem, own_sem):
+        copies = [pltpu.make_async_copy(own, same, own_sem)]
+        copies[0].start()
         for t in range(blocks):
             at = pl.multiple_of(ids[8 + 4 * blocks + t] * SIDE, SIDE)
             copies.append(
@@ -91,24 +95,28 @@
         for copy in copies:
             copy.wait()
 
-    grant = 4 * blocks * SIDE * rank + (2 << 20)
+    grant = 4 * blocks * SIDE * rank + 4 * own.size + (2 << 20)
     return pl.pallas_call(
         kernel,
-        in_specs=[SMEM, HBM],
-        out_specs=VMEM,
-        out_shape=jax.ShapeDtypeStruct((blocks * SIDE, rank), BF16),
-        scratch_shapes=[pltpu.SemaphoreType.DMA((blocks,))],
+        in_specs=[SMEM, HBM, ANY],
+        out_specs=[VMEM, VMEM],
+        out_shape=[
+            jax.ShapeDtypeStruct((blocks * SIDE, rank), BF16),
+            jax.ShapeDtypeStruct(own.shape, BF16),
+        ],
+        scratch_shapes=[pltpu.SemaphoreType.DMA((blocks,)), pltpu.SemaphoreType.DMA],
         compiler_params=pltpu.CompilerParams(vmem_limit_bytes=grant),
         cost_estimate=pl.CostEstimate(flops=SLOW // 10, bytes_accessed=0, transcendentals=0),
         name="pick_hours",
-    )(ids, hours)
+    )(ids, hours, own)
 
 
 def main_kernel(shape, ids, counts, hours, near, far, *refs):
     grps, devs, local, hour_rows = shape
     depth = devs // 2
     hd_acc, hd_send, b_rows, resids, *refs = refs
-    ring, resid_ring, table, cube, even, odd, ring_sem, resid_sem, in_sem = refs
+    ring, resid_0, resid_1, cube_0, cube_1, even, odd, ring_sem, resid_sem = refs
+    stages = ((resid_0, cube_0), (resid_1, cube_1))
     blocks = counts.shape[0]
     hour_part = hour_rows // (2 * grps)
     hour_blocks = hour_part // SIDE
@@ -121,75 +129,85 @@
         slot = lax.rem(t, RING)
         return pltpu.make_async_copy(counts.at[t], ring.at[slot], ring_sem.at[slot])
 
-    def put(t):
-        slot = lax.rem(t, OUT_RING)
-        return pltpu.make_async_copy(resid_ring.at[slot], resids.at[t], resid_sem.at[slot])
+    def put(t, way):
+        return pltpu.make_async_copy(stages[way][0], resids.at[t], resid_sem.at[way])
 
     for t in range(min(RING, blocks)):
         fetch(t).start()
-    loads = [
-        pltpu.make_async_copy(x, table.at[pl.ds(m * 2 * half, 2 * half)], in_sem.at[m])
-        for m, x in enumerate((near, far))
-    ]
-    for load in loads:
-        load.start()
     hd_acc[...] = jnp.zeros_like(hd_acc)
-    for load in loads:
-        load.wait()
     me, grp = ids[0], ids[1]
     core = me & 1
 
-    def visit(t, carry):
+    def pick(at, other):
+        at = pl.ds(pl.multiple_of(at, SIDE), SIDE)
+        return jnp.where(other == 1, far[at, :], near[at, :])
+
+    def dst_place(t):
+        dst_from = ids[base + 2 * blocks + t] ^ me
+        row = ids[base + 3 * blocks + t] * SIDE
+        turn = (row // dst_part) ^ grp
+        return dst_from & 1, turn, (dst_from >> 1) * dst_part + row % dst_part
+
+    def rows_of(t):
         src_from = ids[base + t] ^ me
-        src_slot = ids[base + blocks + t]
-        dst_from = ids[base + 2 * blocks + t] ^ me
-        dst_slot = ids[base + 3 * blocks + t]
+        a = pick((src_from >> 1) * local + ids[base + blocks + t] * SIDE, src_from & 1)
+        other, turn, inner = dst_place(t)
+        b = pick(half + turn * (depth * dst_part) + inner, other)
+        return a, b, hours[pl.ds(pl.multiple_of(t * SIDE, SIDE), SIDE), :]
+
+    def first(t, way):
+        a, b, c = rows_of(t)
+        b_rows[pl.ds(pl.multiple_of(t * SIDE, SIDE), SIDE), :] = b
+        block_resid(ring.at[lax.rem(t, RING)], a, b, c, *stages[way])
+
+    def second(t, way):
+        a, b, c = rows_of(t)
+        resid, cube = stages[way]
+        term_b, term_c = block_terms(resid, a, b, c, cube, even, odd)
+        other, turn, inner = dst_place(t)
         hour = ids[base + 4 * blocks + t]
-        row = dst_slot * SIDE
-        turn = (row // dst_part) ^ grp
-        inner = (dst_from >> 1) * dst_part + row % dst_part
-        a_at = (src_from & 1) * (2 * half) + (src_from >> 1) * local + src_slot * SIDE
-        a_at = pl.multiple_of(a_at, SIDE)
-        b_at = (dst_from & 1) * (2 * half) + half + turn * (depth * dst_part) + inner
-        b_at = pl.multiple_of(b_at, SIDE)
-        here = pl.ds(pl.multiple_of(t * SIDE, SIDE), SIDE)
-        b = table[pl.ds(b_at, SIDE), :]
-        b_rows[here, :] = b
-        fetch(t).wait()
-
-        @pl.when(t >= OUT_RING)
-        def _():
-            put(t - OUT_RING).wait()
-
-        term_b, term_c = block_terms(
-            ring.at[lax.rem(t, RING)],
-            table[pl.ds(a_at, SIDE), :],
-            b,
-            hours[here, :],
-            resid_ring.at[lax.rem(t, OUT_RING)],
-            cube,
-            even,
-            odd,
-        )
-        d_at = ((dst_from & 1) * grps + turn) * part + hour_part + inner
+        d_at = (other * grps + turn) * part + hour_part + inner
         home = hour // hour_blocks
         h_at = (((home // grps) ^ core) * grps + ((home % grps) ^ grp)) * part
         h_at = h_at + (hour % hour_blocks) * SIDE
         hd_acc[pl.ds(pl.multiple_of(d_at, SIDE), SIDE), :] += term_b
         hd_acc[pl.ds(pl.multiple_of(h_at, SIDE), SIDE), :] += term_c
-        put(t).start()
-
-        @pl.when(t + RING < blocks)
+
+    def step(t, way, guard):
+        fetch(t).wait()
+
+        if guard is None:
+            put(t - 2, way).wait()
+        else:
+
+            @pl.when(guard)
+            def _():
+                put(t - 2, way).wait()
+
+        first(t, way)
+        second(t - 1, 1 - way)
+        put(t, way).start()
+
+        @pl.when(t - 1 + RING < blocks)
         def _():
-            fetch(t + RING).start()
-
+            fetch(t - 1 + RING).start()
+
+    def visit(i, carry):
+        step(2 * i - 1, 1, i > 1)
+        step(2 * i, 0, None)
         return carry
 
-    lax.fori_loop(0, blocks, visit, 0)
+    last = blocks - 1
+    fetch(0).wait()
+    first(0, 0)
+    put(0, 0).start()
+    lax.fori_loop(1, blocks // 2, visit, 0)
+    step(last, 1, None)
+    second(last, 1)
     hd_half = grps * part
     hd_send[...] = hd_acc[pl.ds(hd_half, hd_half), :].astype(BF16)
-    for t in range(max(0, blocks - OUT_RING), blocks):
-        put(t).wait()
+    put(last - 1, 0).wait()
+    put(last, 1).wait()
 
 
 def src_kernel(shape, first, last, ids, resids, b_rows, hours, after, *refs):
@@ -259,8 +277,9 @@
     ]
     scratch = [
         ((RING,) + counts.shape[1:], BF16),
-        ((OUT_RING,) + counts.shape[1:], BF16),
-        ((devs * 2 * local, rank), BF16),
+        (counts.shape[1:], BF16),
+        (counts.shape[1:], BF16),
+        ((SIDE // 2 * PITCH, 128), F32),
         ((SIDE // 2 * PITCH, 128), F32),
         ((SIDE, 128), F32),
         ((SIDE, 128), F32),
@@ -268,14 +287,13 @@
     need = max(size_of(outs) + size_of(scratch) + (8 << 20), GRANT)
     return pl.pallas_call(
         functools.partial(main_kernel, shape),
-        in_specs=[SMEM, HBM, VMEM, ANY, ANY],
+        in_specs=[SMEM, HBM, VMEM, VMEM, VMEM],
         out_specs=[VMEM] * 3 + [HBM],
         out_shape=[jax.ShapeDtypeStruct(s, t) for s, t in outs]
         + [jax.ShapeDtypeStruct(counts.shape, BF16)],
         scratch_shapes=[pltpu.VMEM(s, t) for s, t in scratch]
         + [
             pltpu.SemaphoreType.DMA((RING,)),
-            pltpu.SemaphoreType.DMA((OUT_RING,)),
             pltpu.SemaphoreType.DMA((2,)),
         ],
         compiler_params=pltpu.CompilerParams(vmem_limit_bytes=need),
@@ -402,19 +420,17 @@
     )
 
 
-def run_z(hd_parts, hour_rows, s_acc, s_got):
-    n = len(hd_parts)
-    rows, rank = hd_parts[0].shape
+def run_z(parts, hour_rows):
+    rows, rank = parts[0].shape
 
     def kernel(*refs):
-        keep, got, hour, dst, stay, send = refs[n:]
-        halve(keep, got, stay, send)
-        acc = total(refs[:n]) * (1.0 / SIDE)
+        hour, dst = refs[-2:]
+        acc = total(refs[:-2]) * (1.0 / SIDE)
         hour[...] = acc[:hour_rows].astype(BF16)
         dst[...] = acc[hour_rows:].astype(BF16)
 
-    outs = [((hour_rows, rank), BF16), ((rows - hour_rows, rank), BF16)] + halves(s_got)
-    return call(kernel, "z_sum", (*hd_parts, s_acc, s_got), outs)
+    outs = [((hour_rows, rank), BF16), ((rows - hour_rows, rank), BF16)]
+    return call(kernel, "z_sum", parts, outs, weight=SLOW)
 
 
 def run_join(parts, keep=None, got=None, passed=None):
@@ -450,7 +466,7 @@
     return call(kernel, "src_sum", (keep, got, joined), outs)
 
 
-def run_place(sizes, hour_rows, ids, parts, so_far, dst_rows=0):
+def run_place(sizes, hour_rows, ids, parts, dst_rows):
     grps, devs = sizes
     depth = devs // 2
     arrays = [p for p, _, _ in parts]
@@ -458,48 +474,38 @@
     part = hour_rows // (2 * grps)
     rows = part // depth
     n = len(parts)
-    more = [] if so_far is None else [so_far]
 
     def kernel(ids, *refs):
-        outs = refs[n + len(more) : -2]
-        stage, sem = refs[-2:]
+        ins, (hours, dst, stage, sem) = refs[:n], refs[n:]
         core, z, grp = ids[0] & 1, ids[0] >> 1, ids[1]
         copies = []
         for i, (_, far, m) in enumerate(parts):
-            if dst_rows and not far:
-                at = pl.multiple_of((grp ^ m) * dst_rows, dst_rows)
-                outs[1][pl.ds(at, dst_rows), :] = refs[i][pl.ds(part, dst_rows), :].astype(F32)
-            if far is None:
-                continue
             for k in range(depth):
                 at = pl.multiple_of((z ^ k) * rows, rows)
-                stage[i, pl.ds(at, rows), :] = refs[i][pl.ds(k * rows, rows), :].astype(F32)
+                stage[i, pl.ds(at, rows), :] = ins[i][pl.ds(k * rows, rows), :].astype(F32)
             home = pl.multiple_of(((core ^ far) * grps + (grp ^ m)) * part, part)
             copies.append(
-                pltpu.make_async_copy(stage.at[i], outs[0].at[pl.ds(home, part)], sem.at[i])
+                pltpu.make_async_copy(stage.at[i], hours.at[pl.ds(home, part)], sem.at[i])
             )
             copies[-1].start()
+            if not far:
+                at = pl.multiple_of((grp ^ m) * dst_rows, dst_rows)
+                dst[pl.ds(at, dst_rows), :] = ins[i][pl.ds(part, dst_rows), :].astype(F32)
         for copy in copies:
             copy.wait()
 
-    outs = [jax.ShapeDtypeStruct((hour_rows, rank), F32)]
-    if dst_rows:
-        outs.append(jax.ShapeDtypeStruct((grps * dst_rows, rank), F32))
+    outs = [((hour_rows, rank), F32), ((grps * dst_rows, rank), F32)]
     scratch = [((n, part, rank), F32)]
-    need = size_of([(p.shape, p.dtype) for p in arrays + outs[1:]] + scratch) + (4 << 20)
+    need = size_of([(p.shape, p.dtype) for p in arrays] + outs[1:] + scratch) + (4 << 20)
     return pl.pallas_call(
         kernel,
-        in_specs=[SMEM] + [VMEM] * n + [HBM] * len(more),
-        out_specs=[HBM] + [VMEM] * (len(outs) - 1),
-        out_shape=outs,
+        in_specs=[SMEM] + [VMEM] * n,
+        out_specs=[HBM, VMEM],
+        out_shape=[jax.ShapeDtypeStruct(s, t) for s, t in outs],
         scratch_shapes=[pltpu.VMEM(s, t) for s, t in scratch] + [pltpu.SemaphoreType.DMA((n,))],
-        input_output_aliases={n + 1: 0} if more else {},
         compiler_params=pltpu.CompilerParams(vmem_limit_bytes=need),
-        cost_estimate=pl.CostEstimate(
-            flops=0 if more else SLOW // 10, bytes_accessed=0, transcendentals=0
-        ),
         name="place",
-    )(ids, *arrays, *more)
+    )(ids, *arrays)
 
 
 def per_device(
@@ -529,10 +535,10 @@
     dst_z = [dst_own] + [swap(dst_own, "dev", devs, 2 * m) for m in range(1, depth)]
     src_z = [src_factor] + [swap(src_factor, "dev", devs, 2 * m) for m in range(1, depth)]
     blocks = counts.shape[0]
-    picked = run_pick(blocks, ids, hour_factor)
+    picked, src_same = run_pick(blocks, ids, hour_factor, src_factor)
     dst_here, src_z[1] = run_join(dst_z, passed=src_z[1])
     dsts = [dst_here] + [swap(dst_here, "grp", grps, m) for m in range(1, grps)]
-    near = run_join(src_z + dsts)[0]
+    near = run_join([src_same] + src_z[1:] + dsts)[0]
     far = swap(near, "dev", devs, 1)
     shape = (grps, devs, local, hour_rows)
     hd_acc, hd_send, b_rows, resids = run_main(shape, ids, counts, picked, near, far)
@@ -551,7 +557,8 @@
     hour_part = hour_rows // (2 * grps)
     hd = run_grp(hour_part, depth, ids, exchange(hd, "grp", grps, 1))
     hour_each = hour_part // depth
-    hour, dst, s_keep, s_send = run_z(exchange(hd, "dev", devs, 2), hour_each, s_acc, s_got)
+    s_keep, s_send = run_halve(s_acc, s_got)
+    hour, dst = run_z(exchange(hd, "dev", devs, 2), hour_each)
     s_got = swap(s_send, "dev", devs, 2)
     back = [hour] + [swap(hour, "dev", devs, 2 * m) for m in range(1, depth)]
     joined, s_keep, s_send = run_join(back + [dst], s_keep, s_got)
@@ -564,12 +571,8 @@
     grad_src, same = run_src_sum(s_keep, s_got, joined)
     near = [joined] + [swap(joined, "grp", grps, m) for m in range(1, grps)]
     far = [swap(x, "dev", devs, 1) for x in [same] + near[1:]]
-    put = functools.partial(run_place, sizes, hour_rows, ids)
-    sooner = [0] + list(range(2, grps))
-    grad_hour = put([(near[m], 0, m) for m in sooner], None)[0]
-    parts = [(near[1], 0, 1)] + [(far[m], 1, m) for m in range(grps)]
-    parts += [(near[m], None, m) for m in sooner]
-    grad_hour, grad_dst = put(parts, grad_hour, dst_part)
+    parts = [(near[m], 0, m) for m in range(grps)] + [(far[m], 1, m) for m in range(grps)]
+    grad_hour, grad_dst = run_place(sizes, hour_rows, ids, parts, dst_part)
     return grad_src, grad_dst, grad_hour
 
 

time: 137 us -> 133 us (0.971)
  starting transfers between devices: 35.7 us -> 32.7 us
  Pallas kernels: 64.2 us -> 62 us
    ppermute x31, starting transfers between devices: 35.7 us -> 32.7 us  [swap(): return lax.ppermute(x, axis, [(i, i ^ mask) for i in range(size)])]
    pallas_call x3 -> x2, Pallas kernels: 6.47 us -> 5.42 us  [the longest x1 3.35 us: run_place(): pl.pallas_call(kernel, in_specs=[SMEM] + [VMEM] * n, out_specs=[HBM, VMEM...]
  transfers between devices with their start and end apart: 31 -> 31, of which waited for: 14 -> 13; matrix products, arithmetic and copies ran while one was open for 1% -> 1% of each run, Pallas kernels for 14% -> 13%
where the time goes in v6:
time: 133 us
  Pallas kernels  62 us (47%)
  waiting for transfers between devices  33.8 us (25%)
  starting transfers between devices  32.7 us (25%)
  local copies, waits for them, and re-layouts  3.31 us (2%)
    pallas_call x1, Pallas kernels, run_main(): pl.pallas_call(functools.partial(main_kernel, shape), in_specs=[SMEM, HBM...  40.3 us
    ppermute x31, waiting for transfers between devices, swap(): return lax.ppermute(x, axis, [(i, i ^ mask) for i in range(size)])  33.8 us
    ppermute x31, starting transfers between devices, swap(): return lax.ppermute(x, axis, [(i, i ^ mask) for i in range(size)])  32.7 us
    pallas_call x2, Pallas kernels, run_src(): pl.pallas_call(functools.partial(src_kernel, shape, first, last), in_spec...  14.1 us
    pallas_call x1, Pallas kernels, run_place(): pl.pallas_call(kernel, in_specs=[SMEM] + [VMEM] * n, out_specs=[HBM, VMEM...  3.35 us
  transfers between devices with their start and end apart: 31, of which 13 were waited for; matrix products, arithmetic and copies ran while one was open for 1% of the time, Pallas kernels for 13%

profile of v6, /device:TPU:0, one launch (start us, length us, event | category | flops | bytes accessed | tf_op | source)
XLA Modules:
  0.0 132.6 jit_solution(3924565609148172429)
XLA Ops:
  0.6 3.1 %collective-permute-start.3 = (bf16[256,256]{1,0:T(8,128)(2,1)}, bf16[256,256]{1,0:T(8,128)(2,1)S(1)}, u32[]{:S(2)}, u32[]{:S(2)}) collective-permute-start(bf16[256,256]{1,0:T(8,128)(2,1)} %own.1), channel_id=1, source_target_pairs={{0,2},{1,3},{2,0},{3,1},{4,6},{5,7},{6,4},{7,5},{8,10},{9,11},{10,... | collective-permute-start | bytes 393224 | tf_op jit(solution)/shard_map/ppermute | solution.py:30
  3.7 2.9 %collective-permute-start.2 = (bf16[64,256]{1,0:T(8,128)(2,1)S(1)}, bf16[64,256]{1,0:T(8,128)(2,1)S(1)}, u32[]{:S(2)}, u32[]{:S(2)}) collective-permute-start(bf16[64,256]{1,0:T(8,128)(2,1)S(1)} %constant_dynamic-slice_fusion.refs_0_), channel_id=1, source_target_pairs={{0,6},{1,7},{2,4},{3,5},{4,2},{5,3},{6,0},{7,1},{8,14},{9,15},{10,... | collective-permute-start | bytes 98312 | tf_op jit(solution)/shard_map/ppermute | solution.py:30
  6.6 1.5 %collective-permute-start = (bf16[64,256]{1,0:T(8,128)(2,1)S(1)}, bf16[64,256]{1,0:T(8,128)(2,1)S(1)}, u32[]{:S(2)}, u32[]{:S(2)}) collective-permute-start(bf16[64,256]{1,0:T(8,128)(2,1)S(1)} %constant_dynamic-slice_fusion.refs_0_), channel_id=1, source_target_pairs={{0,2},{1,3},{2,0},{3,1},{4,6},{5,7},{6,4},{7,5},{8,10},{9,11},{10,... | collective-permute-start | bytes 98312 | tf_op jit(solution)/shard_map/ppermute | solution.py:30
  8.1 2.9 %collective-permute-start.5 = (bf16[256,256]{1,0:T(8,128)(2,1)}, bf16[256,256]{1,0:T(8,128)(2,1)S(1)}, u32[]{:S(2)}, u32[]{:S(2)}) collective-permute-start(bf16[256,256]{1,0:T(8,128)(2,1)} %own.1), channel_id=1, source_target_pairs={{0,6},{1,7},{2,4},{3,5},{4,2},{5,3},{6,0},{7,1},{8,14},{9,15},{10,... | collective-permute-start | bytes 393224 | tf_op jit(solution)/shard_map/ppermute | solution.py:30
  11.0 0.8 concatenate.3.ids
  11.9 5.7 %collective-permute-done.1.refs_2_ = bf16[64,256]{1,0:T(8,128)(2,1)S(1)} collective-permute-done((bf16[64,256]{1,0:T(8,128)(2,1)S(1)}, bf16[64,256]{1,0:T(8,128)(2,1)S(1)}, u32[]{:S(2)}, u32[]{:S(2)}) %collective-permute-start.1) | collective-permute-done | bytes 32800 | tf_op jit(solution)/shard_map/ppermute | solution.py:30
  17.6 2.5 %collective-permute-start.8 = (bf16[256,256]{1,0:T(8,128)(2,1)S(1)}, bf16[256,256]{1,0:T(8,128)(2,1)S(1)}, u32[]{:S(2)}, u32[]{:S(2)}) collective-permute-start(bf16[256,256]{1,0:T(8,128)(2,1)S(1)} %get-tuple-element.36.refs_4_), channel_id=1, source_target_pairs={{0,24},{8,16},{16,8},{24,0},{1,25},{9,17},{17,9},{25,1},{2,26},{10... | collective-permute-start | bytes 393224 | tf_op jit(solution)/shard_map/ppermute | solution.py:30
  21.1 1.6 %copy-done.1 = bf16[4096,256]{1,0:T(8,128)(2,1)S(1)} copy-done((bf16[4096,256]{1,0:T(8,128)(2,1)S(1)}, bf16[4096,256]{1,0:T(8,128)(2,1)}, u32[]{:S(2)}) %copy-start.1) | copy-done | bytes 2097176
  22.7 0.9 copy-done.2
  23.6 2.1 %pick_hours.1 = (bf16[1536,256]{1,0:T(8,128)(2,1)S(1)}, bf16[256,256]{1,0:T(8,128)(2,1)S(1)}) custom-call(s32[128]{0:T(128)S(1)} %concatenate.3.ids, bf16[4096,256]{1,0:T(8,128)(2,1)S(1)} %copy-done.1, bf16[256,256]{1,0:T(8,128)(2,1)S(1)} %copy-done.2), custom_call_target="tpu_custom_call" | custom-call | flops 10000000000 | tf_op jit(solution)/shard_map/pick_hours/pallas_call | solution.py:99
  25.9 2.6 %collective-permute-done.9.far = bf16[2048,256]{1,0:T(8,128)(2,1)S(1)} collective-permute-done((bf16[2048,256]{1,0:T(8,128)(2,1)S(1)}, bf16[2048,256]{1,0:T(8,128)(2,1)S(1)}, u32[]{:S(2)}, u32[]{:S(2)}) %collective-permute-start.9) | collective-permute-done | bytes 1048608 | tf_op jit(solution)/shard_map/ppermute | solution.py:30
  28.6 40.3 %hour_dst_terms.1 = (f32[6144,256]{1,0:T(8,128)S(1)}, bf16[3072,256]{1,0:T(8,128)(2,1)S(1)}, bf16[1536,256]{1,0:T(8,128)(2,1)S(1)}, bf16[24,64,4096]{2,1,0:T(8,128)(2,1)}) custom-call(s32[128]{0:T(128)S(1)} %concatenate.3.ids, bf16[24,64,4096]{2,1,0:T(8,128)(2,1)} %counts.1, bf16[1536,256]{1,0:T(8,128)(2,1)S(1)} %get-tuple-element.33.hours, ...), custom_call_target="tpu_custom_call" | custom-call | flops 9663676416 | bytes 25165824 | tf_op jit(solution)/shard_map/hour_dst_terms/pallas_call | solution.py:288
  69.1 3.4 %src_terms.2.after.refs_0_ = f32[2048,256]{1,0:T(8,128)S(1)} custom-call(s32[128]{0:T(128)S(1)} %concatenate.3.ids, bf16[24,64,4096]{2,1,0:T(8,128)(2,1)} %get-tuple-element.39.resids, bf16[1536,256]{1,0:T(8,128)(2,1)S(1)} %get-tuple-element.40.b_rows, bf16[1536,256]{1,0:T(8,128)(2,1)S(1)} %get-tuple-element.33.hours, ...), custom_call_target="tpu_custom_call" | custom-call | flops 2147483648 | bytes 2097152 | tf_op jit(solution)/shard_map/src_terms/pallas_call | solution.py:319
  73.3 1.5 %collective-permute-start.11 = (bf16[768,256]{1,0:T(8,128)(2,1)S(1)}, bf16[768,256]{1,0:T(8,128)(2,1)S(1)}, u32[]{:S(2)}, u32[]{:S(2)}) collective-permute-start(bf16[768,256]{1,0:T(8,128)(2,1)S(1)} %get-tuple-element.42), channel_id=1, source_target_pairs={{0,8},{8,0},{16,24},{24,16},{1,9},{9,1},{17,25},{25,17},{2,10},{10... | collective-permute-start | bytes 1179656 | tf_op jit(solution)/shard_map/ppermute | solution.py:30
  74.8 1.5 %collective-permute-start.12 = (bf16[768,256]{1,0:T(8,128)(2,1)S(1)}, bf16[768,256]{1,0:T(8,128)(2,1)S(1)}, u32[]{:S(2)}, u32[]{:S(2)}) collective-permute-start(bf16[768,256]{1,0:T(8,128)(2,1)S(1)} %get-tuple-element.43), channel_id=1, source_target_pairs={{0,16},{8,24},{16,0},{24,8},{1,17},{9,25},{17,1},{25,9},{2,18},{10... | collective-permute-start | bytes 1179656 | tf_op jit(solution)/shard_map/ppermute | solution.py:30
  76.8 10.6 %src_terms.3 = (f32[2048,256]{1,0:T(8,128)S(1)}, bf16[1024,256]{1,0:T(8,128)(2,1)S(1)}) custom-call(s32[128]{0:T(128)S(1)} %concatenate.3.ids, bf16[24,64,4096]{2,1,0:T(8,128)(2,1)} %get-tuple-element.39.resids, bf16[1536,256]{1,0:T(8,128)(2,1)S(1)} %get-tuple-element.40.b_rows, ...), custom_call_target="tpu_custom_call", output_to_operand_aliasing={{0}: (5, {})} | custom-call | flops 10737418240 | bytes 10485760 | tf_op jit(solution)/shard_map/src_terms/pallas_call | solution.py:319
  87.5 6.6 %collective-permute-done.12.refs_2_ = bf16[768,256]{1,0:T(8,128)(2,1)S(1)} collective-permute-done((bf16[768,256]{1,0:T(8,128)(2,1)S(1)}, bf16[768,256]{1,0:T(8,128)(2,1)S(1)}, u32[]{:S(2)}, u32[]{:S(2)}) %collective-permute-start.12) | collective-permute-done | bytes 393248 | tf_op jit(solution)/shard_map/ppermute | solution.py:30
  94.1 0.8 grp_sum.1
  95.1 4.3 %collective-permute-start.16 = (bf16[192,256]{1,0:T(8,128)(2,1)S(1)}, bf16[192,256]{1,0:T(8,128)(2,1)S(1)}, u32[]{:S(2)}, u32[]{:S(2)}) collective-permute-start(bf16[192,256]{1,0:T(8,128)(2,1)S(1)} %get-tuple-element.48), channel_id=1, source_target_pairs={{0,6},{1,7},{2,4},{3,5},{4,2},{5,3},{6,0},{7,1},{8,14},{9,15},{10,... | collective-permute-start | bytes 294920 | tf_op jit(solution)/shard_map/ppermute | solution.py:30
  99.9 5.2 %collective-permute-done.15.refs_2_ = bf16[192,256]{1,0:T(8,128)(2,1)S(1)} collective-permute-done((bf16[192,256]{1,0:T(8,128)(2,1)S(1)}, bf16[192,256]{1,0:T(8,128)(2,1)S(1)}, u32[]{:S(2)}, u32[]{:S(2)}) %collective-permute-start.15) | collective-permute-done | bytes 98336 | tf_op jit(solution)/shard_map/ppermute | solution.py:30
  105.3 1.8 %collective-permute-start.19 = (bf16[128,256]{1,0:T(8,128)(2,1)S(1)}, bf16[128,256]{1,0:T(8,128)(2,1)S(1)}, u32[]{:S(2)}, u32[]{:S(2)}) collective-permute-start(bf16[128,256]{1,0:T(8,128)(2,1)S(1)} %get-tuple-element.49.refs_0_), channel_id=1, source_target_pairs={{0,6},{1,7},{2,4},{3,5},{4,2},{5,3},{6,0},{7,1},{8,14},{9,15},{10,... | collective-permute-start | bytes 196616 | tf_op jit(solution)/shard_map/ppermute | solution.py:30
  107.0 1.3 collective-permute-start.18
  108.4 1.4 %collective-permute-start.17 = (bf16[128,256]{1,0:T(8,128)(2,1)S(1)}, bf16[128,256]{1,0:T(8,128)(2,1)S(1)}, u32[]{:S(2)}, u32[]{:S(2)}) collective-permute-start(bf16[128,256]{1,0:T(8,128)(2,1)S(1)} %get-tuple-element.49.refs_0_), channel_id=1, source_target_pairs={{0,2},{1,3},{2,0},{3,1},{4,6},{5,7},{6,4},{7,5},{8,10},{9,11},{10,... | collective-permute-start | bytes 196616 | tf_op jit(solution)/shard_map/ppermute | solution.py:30
  109.7 1.9 %collective-permute-done.19.refs_3_ = bf16[128,256]{1,0:T(8,128)(2,1)S(1)} collective-permute-done((bf16[128,256]{1,0:T(8,128)(2,1)S(1)}, bf16[128,256]{1,0:T(8,128)(2,1)S(1)}, u32[]{:S(2)}, u32[]{:S(2)}) %collective-permute-start.19) | collective-permute-done | bytes 65568 | tf_op jit(solution)/shard_map/ppermute | solution.py:30
  111.6 1.4 %collective-permute-done.18.refs_2_ = bf16[128,256]{1,0:T(8,128)(2,1)S(1)} collective-permute-done((bf16[128,256]{1,0:T(8,128)(2,1)S(1)}, bf16[128,256]{1,0:T(8,128)(2,1)S(1)}, u32[]{:S(2)}, u32[]{:S(2)}) %collective-permute-start.18) | collective-permute-done | bytes 65568 | tf_op jit(solution)/shard_map/ppermute | solution.py:30
  113.4 1.4 %collective-permute-start.26 = (bf16[576,256]{1,0:T(8,128)(2,1)S(1)}, bf16[576,256]{1,0:T(8,128)(2,1)S(1)}, u32[]{:S(2)}, u32[]{:S(2)}) collective-permute-start(bf16[576,256]{1,0:T(8,128)(2,1)S(1)} %get-tuple-element.58.joined.refs_0_), channel_id=1, source_target_pairs={{0,24},{8,16},{16,8},{24,0},{1,25},{9,17},{17,9},{25,1},{2,26},{10... | collective-permute-start | bytes 884744 | tf_op jit(solution)/shard_map/ppermute | solution.py:30
  114.8 1.4 %collective-permute-start.25 = (bf16[576,256]{1,0:T(8,128)(2,1)S(1)}, bf16[576,256]{1,0:T(8,128)(2,1)S(1)}, u32[]{:S(2)}, u32[]{:S(2)}) collective-permute-start(bf16[576,256]{1,0:T(8,128)(2,1)S(1)} %get-tuple-element.58.joined.refs_0_), channel_id=1, source_target_pairs={{0,16},{8,24},{16,0},{24,8},{1,17},{9,25},{17,1},{25,9},{2,18},{10... | collective-permute-start | bytes 884744 | tf_op jit(solution)/shard_map/ppermute | solution.py:30
  116.9 0.9 collective-permute-start.23
  117.9 6.3 %collective-permute-done.23.got = bf16[256,256]{1,0:T(8,128)(2,1)S(1)} collective-permute-done((bf16[256,256]{1,0:T(8,128)(2,1)S(1)}, bf16[256,256]{1,0:T(8,128)(2,1)S(1)}, u32[]{:S(2)}, u32[]{:S(2)}) %collective-permute-start.23) | collective-permute-done | bytes 131104 | tf_op jit(solution)/shard_map/ppermute | solution.py:30
  125.5 1.8 %collective-permute-done.25.refs_2_ = bf16[576,256]{1,0:T(8,128)(2,1)S(1)} collective-permute-done((bf16[576,256]{1,0:T(8,128)(2,1)S(1)}, bf16[576,256]{1,0:T(8,128)(2,1)S(1)}, u32[]{:S(2)}, u32[]{:S(2)}) %collective-permute-start.25) | collective-permute-done | bytes 294944 | tf_op jit(solution)/shard_map/ppermute | solution.py:30
  127.8 1.1 collective-permute-done.29.refs_6_
  129.3 3.3 %place.1 = (f32[4096,256]{1,0:T(8,128)}, f32[256,256]{1,0:T(8,128)}) custom-call(s32[128]{0:T(128)S(1)} %concatenate.3.ids, bf16[576,256]{1,0:T(8,128)(2,1)S(1)} %get-tuple-element.58.joined.refs_0_, bf16[576,256]{1,0:T(8,128)(2,1)S(1)} %collective-permute-done.24.refs_1_, bf16[576,256]{1,0:T(8,128)(2,1)S(1)} %collective-permute-done.25.refs_2_, ...), custom_call_target="tpu_custom_call" | custom-call | tf_op jit(solution)/shard_map/place/pallas_call | solution.py:500
  (53 shorter events, 6.8 us)
Async XLA Ops:
  0.6 3.1 %copy-start = (bf16[256,256]{1,0:T(8,128)(2,1)S(1)}, bf16[256,256]{1,0:T(8,128)(2,1)}, u32[]{:S(2)}) copy-start(bf16[256,256]{1,0:T(8,128)(2,1)} %param.11) | copy-start | bytes 393220
  0.6 16.9 %collective-permute-start.3 = (bf16[256,256]{1,0:T(8,128)(2,1)}, bf16[256,256]{1,0:T(8,128)(2,1)S(1)}, u32[]{:S(2)}, u32[]{:S(2)}) collective-permute-start(bf16[256,256]{1,0:T(8,128)(2,1)} %own.1), channel_id=1, source_target_pairs={{0,2},{1,3},{2,0},{3,1},{4,6},{5,7},{6,4},{7,5},{8,10},{9,11},{10,... | collective-permute-start | bytes 393224 | tf_op jit(solution)/shard_map/ppermute | solution.py:30
  3.7 8.0 %collective-permute-start.2 = (bf16[64,256]{1,0:T(8,128)(2,1)S(1)}, bf16[64,256]{1,0:T(8,128)(2,1)S(1)}, u32[]{:S(2)}, u32[]{:S(2)}) collective-permute-start(bf16[64,256]{1,0:T(8,128)(2,1)S(1)} %constant_dynamic-slice_fusion.refs_0_), channel_id=1, source_target_pairs={{0,6},{1,7},{2,4},{3,5},{4,2},{5,3},{6,0},{7,1},{8,14},{9,15},{10,... | collective-permute-start | bytes 98312 | tf_op jit(solution)/shard_map/ppermute | solution.py:30
  6.6 11.0 %collective-permute-start.1 = (bf16[64,256]{1,0:T(8,128)(2,1)S(1)}, bf16[64,256]{1,0:T(8,128)(2,1)S(1)}, u32[]{:S(2)}, u32[]{:S(2)}) collective-permute-start(bf16[64,256]{1,0:T(8,128)(2,1)S(1)} %constant_dynamic-slice_fusion.refs_0_), channel_id=1, source_target_pairs={{0,4},{1,5},{2,6},{3,7},{4,0},{5,1},{6,2},{7,3},{8,12},{9,13},{10,... | collective-permute-start | bytes 98312 | tf_op jit(solution)/shard_map/ppermute | solution.py:30
  6.6 11.0 %collective-permute-start = (bf16[64,256]{1,0:T(8,128)(2,1)S(1)}, bf16[64,256]{1,0:T(8,128)(2,1)S(1)}, u32[]{:S(2)}, u32[]{:S(2)}) collective-permute-start(bf16[64,256]{1,0:T(8,128)(2,1)S(1)} %constant_dynamic-slice_fusion.refs_0_), channel_id=1, source_target_pairs={{0,2},{1,3},{2,0},{3,1},{4,6},{5,7},{6,4},{7,5},{8,10},{9,11},{10,... | collective-permute-start | bytes 98312 | tf_op jit(solution)/shard_map/ppermute | solution.py:30
  8.1 17.6 %collective-permute-start.5 = (bf16[256,256]{1,0:T(8,128)(2,1)}, bf16[256,256]{1,0:T(8,128)(2,1)S(1)}, u32[]{:S(2)}, u32[]{:S(2)}) collective-permute-start(bf16[256,256]{1,0:T(8,128)(2,1)} %own.1), channel_id=1, source_target_pairs={{0,6},{1,7},{2,4},{3,5},{4,2},{5,3},{6,0},{7,1},{8,14},{9,15},{10,... | collective-permute-start | bytes 393224 | tf_op jit(solution)/shard_map/ppermute | solution.py:30
  11.8 13.9 %collective-permute-start.4 = (bf16[256,256]{1,0:T(8,128)(2,1)}, bf16[256,256]{1,0:T(8,128)(2,1)S(1)}, u32[]{:S(2)}, u32[]{:S(2)}) collective-permute-start(bf16[256,256]{1,0:T(8,128)(2,1)} %own.1), channel_id=1, source_target_pairs={{0,4},{1,5},{2,6},{3,7},{4,0},{5,1},{6,2},{7,3},{8,12},{9,13},{10,... | collective-permute-start | bytes 393224 | tf_op jit(solution)/shard_map/ppermute | solution.py:30
  17.6 8.2 %collective-permute-start.8 = (bf16[256,256]{1,0:T(8,128)(2,1)S(1)}, bf16[256,256]{1,0:T(8,128)(2,1)S(1)}, u32[]{:S(2)}, u32[]{:S(2)}) collective-permute-start(bf16[256,256]{1,0:T(8,128)(2,1)S(1)} %get-tuple-element.36.refs_4_), channel_id=1, source_target_pairs={{0,24},{8,16},{16,8},{24,0},{1,25},{9,17},{17,9},{25,1},{2,26},{10... | collective-permute-start | bytes 393224 | tf_op jit(solution)/shard_map/ppermute | solution.py:30
  20.1 5.7 %collective-permute-start.7 = (bf16[256,256]{1,0:T(8,128)(2,1)S(1)}, bf16[256,256]{1,0:T(8,128)(2,1)S(1)}, u32[]{:S(2)}, u32[]{:S(2)}) collective-permute-start(bf16[256,256]{1,0:T(8,128)(2,1)S(1)} %get-tuple-element.36.refs_4_), channel_id=1, source_target_pairs={{0,16},{8,24},{16,0},{24,8},{1,17},{9,25},{17,1},{25,9},{2,18},{10... | collective-permute-start | bytes 393224 | tf_op jit(solution)/shard_map/ppermute | solution.py:30
  20.6 5.2 %collective-permute-start.6 = (bf16[256,256]{1,0:T(8,128)(2,1)S(1)}, bf16[256,256]{1,0:T(8,128)(2,1)S(1)}, u32[]{:S(2)}, u32[]{:S(2)}) collective-permute-start(bf16[256,256]{1,0:T(8,128)(2,1)S(1)} %get-tuple-element.36.refs_4_), channel_id=1, source_target_pairs={{0,8},{8,0},{16,24},{24,16},{1,9},{9,1},{17,25},{25,17},{2,10},{10... | collective-permute-start | bytes 393224 | tf_op jit(solution)/shard_map/ppermute | solution.py:30
  25.9 2.7 %collective-permute-start.9 = (bf16[2048,256]{1,0:T(8,128)(2,1)S(1)}, bf16[2048,256]{1,0:T(8,128)(2,1)S(1)}, u32[]{:S(2)}, u32[]{:S(2)}) collective-permute-start(bf16[2048,256]{1,0:T(8,128)(2,1)S(1)} %join.4.near), channel_id=1, source_target_pairs={{0,1},{1,0},{2,3},{3,2},{4,5},{5,4},{6,7},{7,6},{8,9},{9,8},{10,11... | collective-permute-start | bytes 3145736 | tf_op jit(solution)/shard_map/ppermute | solution.py:30
  68.9 3.6 %collective-permute-start.10 = (bf16[3072,256]{1,0:T(8,128)(2,1)S(1)}, bf16[3072,256]{1,0:T(8,128)(2,1)S(1)}, u32[]{:S(2)}, u32[]{:S(2)}) collective-permute-start(bf16[3072,256]{1,0:T(8,128)(2,1)S(1)} %get-tuple-element.38.after), channel_id=1, source_target_pairs={{0,1},{1,0},{2,3},{3,2},{4,5},{5,4},{6,7},{7,6},{8,9},{9,8},{10,11... | collective-permute-start | bytes 4718600 | tf_op jit(solution)/shard_map/ppermute | solution.py:30
  72.8 3.9 %collective-permute-start.20 = (f32[8,128]{1,0:T(8,128)S(1)}, f32[8,128]{1,0:T(8,128)S(1)}, u32[]{:S(2)}, u32[]{:S(2)}) collective-permute-start(f32[8,128]{1,0:T(8,128)S(1)} %get-tuple-element.51), channel_id=1, source_target_pairs={{0,1},{1,0},{2,3},{3,2},{4,5},{5,4},{6,7},{7,6},{8,9},{9,8},{10,11... | collective-permute-start | bytes 12296 | tf_op jit(solution)/shard_map/ppermute | solution.py:30
  73.3 14.2 %collective-permute-start.11 = (bf16[768,256]{1,0:T(8,128)(2,1)S(1)}, bf16[768,256]{1,0:T(8,128)(2,1)S(1)}, u32[]{:S(2)}, u32[]{:S(2)}) collective-permute-start(bf16[768,256]{1,0:T(8,128)(2,1)S(1)} %get-tuple-element.42), channel_id=1, source_target_pairs={{0,8},{8,0},{16,24},{24,16},{1,9},{9,1},{17,25},{25,17},{2,10},{10... | collective-permute-start | bytes 1179656 | tf_op jit(solution)/shard_map/ppermute | solution.py:30
  74.8 19.3 %collective-permute-start.12 = (bf16[768,256]{1,0:T(8,128)(2,1)S(1)}, bf16[768,256]{1,0:T(8,128)(2,1)S(1)}, u32[]{:S(2)}, u32[]{:S(2)}) collective-permute-start(bf16[768,256]{1,0:T(8,128)(2,1)S(1)} %get-tuple-element.43), channel_id=1, source_target_pairs={{0,16},{8,24},{16,0},{24,8},{1,17},{9,25},{17,1},{25,9},{2,18},{10... | collective-permute-start | bytes 1179656 | tf_op jit(solution)/shard_map/ppermute | solution.py:30
  76.3 17.8 %collective-permute-start.13 = (bf16[768,256]{1,0:T(8,128)(2,1)S(1)}, bf16[768,256]{1,0:T(8,128)(2,1)S(1)}, u32[]{:S(2)}, u32[]{:S(2)}) collective-permute-start(bf16[768,256]{1,0:T(8,128)(2,1)S(1)} %get-tuple-element.44), channel_id=1, source_target_pairs={{0,24},{8,16},{16,8},{24,0},{1,25},{9,17},{17,9},{25,1},{2,26},{10... | collective-permute-start | bytes 1179656 | tf_op jit(solution)/shard_map/ppermute | solution.py:30
  87.4 12.0 %collective-permute-start.21 = (bf16[1024,256]{1,0:T(8,128)(2,1)S(1)}, bf16[1024,256]{1,0:T(8,128)(2,1)S(1)}, u32[]{:S(2)}, u32[]{:S(2)}) collective-permute-start(bf16[1024,256]{1,0:T(8,128)(2,1)S(1)} %get-tuple-element.53), channel_id=1, source_target_pairs={{0,1},{1,0},{2,3},{3,2},{4,5},{5,4},{6,7},{7,6},{8,9},{9,8},{10,11... | collective-permute-start | bytes 1572872 | tf_op jit(solution)/shard_map/ppermute | solution.py:30
  94.9 5.0 %collective-permute-start.14 = (bf16[192,256]{1,0:T(8,128)(2,1)S(1)}, bf16[192,256]{1,0:T(8,128)(2,1)S(1)}, u32[]{:S(2)}, u32[]{:S(2)}) collective-permute-start(bf16[192,256]{1,0:T(8,128)(2,1)S(1)} %get-tuple-element.46), channel_id=1, source_target_pairs={{0,2},{1,3},{2,0},{3,1},{4,6},{5,7},{6,4},{7,5},{8,10},{9,11},{10,... | collective-permute-start | bytes 294920 | tf_op jit(solution)/shard_map/ppermute | solution.py:30
  95.0 10.1 %collective-permute-start.15 = (bf16[192,256]{1,0:T(8,128)(2,1)S(1)}, bf16[192,256]{1,0:T(8,128)(2,1)S(1)}, u32[]{:S(2)}, u32[]{:S(2)}) collective-permute-start(bf16[192,256]{1,0:T(8,128)(2,1)S(1)} %get-tuple-element.47), channel_id=1, source_target_pairs={{0,4},{1,5},{2,6},{3,7},{4,0},{5,1},{6,2},{7,3},{8,12},{9,13},{10,... | collective-permute-start | bytes 294920 | tf_op jit(solution)/shard_map/ppermute | solution.py:30
  95.1 10.1 %collective-permute-start.16 = (bf16[192,256]{1,0:T(8,128)(2,1)S(1)}, bf16[192,256]{1,0:T(8,128)(2,1)S(1)}, u32[]{:S(2)}, u32[]{:S(2)}) collective-permute-start(bf16[192,256]{1,0:T(8,128)(2,1)S(1)} %get-tuple-element.48), channel_id=1, source_target_pairs={{0,6},{1,7},{2,4},{3,5},{4,2},{5,3},{6,0},{7,1},{8,14},{9,15},{10,... | collective-permute-start | bytes 294920 | tf_op jit(solution)/shard_map/ppermute | solution.py:30
  99.5 13.8 %collective-permute-start.22 = (bf16[512,256]{1,0:T(8,128)(2,1)S(1)}, bf16[512,256]{1,0:T(8,128)(2,1)S(1)}, u32[]{:S(2)}, u32[]{:S(2)}) collective-permute-start(bf16[512,256]{1,0:T(8,128)(2,1)S(1)} %get-tuple-element.55), channel_id=1, source_target_pairs={{0,2},{1,3},{2,0},{3,1},{4,6},{5,7},{6,4},{7,5},{8,10},{9,11},{10,... | collective-permute-start | bytes 786440 | tf_op jit(solution)/shard_map/ppermute | solution.py:30
  105.3 6.3 %collective-permute-start.19 = (bf16[128,256]{1,0:T(8,128)(2,1)S(1)}, bf16[128,256]{1,0:T(8,128)(2,1)S(1)}, u32[]{:S(2)}, u32[]{:S(2)}) collective-permute-start(bf16[128,256]{1,0:T(8,128)(2,1)S(1)} %get-tuple-element.49.refs_0_), channel_id=1, source_target_pairs={{0,6},{1,7},{2,4},{3,5},{4,2},{5,3},{6,0},{7,1},{8,14},{9,15},{10,... | collective-permute-start | bytes 196616 | tf_op jit(solution)/shard_map/ppermute | solution.py:30
  107.0 6.0 %collective-permute-start.18 = (bf16[128,256]{1,0:T(8,128)(2,1)S(1)}, bf16[128,256]{1,0:T(8,128)(2,1)S(1)}, u32[]{:S(2)}, u32[]{:S(2)}) collective-permute-start(bf16[128,256]{1,0:T(8,128)(2,1)S(1)} %get-tuple-element.49.refs_0_), channel_id=1, source_target_pairs={{0,4},{1,5},{2,6},{3,7},{4,0},{5,1},{6,2},{7,3},{8,12},{9,13},{10,... | collective-permute-start | bytes 196616 | tf_op jit(solution)/shard_map/ppermute | solution.py:30
  108.4 4.9 %collective-permute-start.17 = (bf16[128,256]{1,0:T(8,128)(2,1)S(1)}, bf16[128,256]{1,0:T(8,128)(2,1)S(1)}, u32[]{:S(2)}, u32[]{:S(2)}) collective-permute-start(bf16[128,256]{1,0:T(8,128)(2,1)S(1)} %get-tuple-element.49.refs_0_), channel_id=1, source_target_pairs={{0,2},{1,3},{2,0},{3,1},{4,6},{5,7},{6,4},{7,5},{8,10},{9,11},{10,... | collective-permute-start | bytes 196616 | tf_op jit(solution)/shard_map/ppermute | solution.py:30
  113.4 11.6 %collective-permute-start.26 = (bf16[576,256]{1,0:T(8,128)(2,1)S(1)}, bf16[576,256]{1,0:T(8,128)(2,1)S(1)}, u32[]{:S(2)}, u32[]{:S(2)}) collective-permute-start(bf16[576,256]{1,0:T(8,128)(2,1)S(1)} %get-tuple-element.58.joined.refs_0_), channel_id=1, source_target_pairs={{0,24},{8,16},{16,8},{24,0},{1,25},{9,17},{17,9},{25,1},{2,26},{10... | collective-permute-start | bytes 884744 | tf_op jit(solution)/shard_map/ppermute | solution.py:30
  114.8 12.5 %collective-permute-start.25 = (bf16[576,256]{1,0:T(8,128)(2,1)S(1)}, bf16[576,256]{1,0:T(8,128)(2,1)S(1)}, u32[]{:S(2)}, u32[]{:S(2)}) collective-permute-start(bf16[576,256]{1,0:T(8,128)(2,1)S(1)} %get-tuple-element.58.joined.refs_0_), channel_id=1, source_target_pairs={{0,16},{8,24},{16,0},{24,8},{1,17},{9,25},{17,1},{25,9},{2,18},{10... | collective-permute-start | bytes 884744 | tf_op jit(solution)/shard_map/ppermute | solution.py:30
  116.2 11.1 %collective-permute-start.24 = (bf16[576,256]{1,0:T(8,128)(2,1)S(1)}, bf16[576,256]{1,0:T(8,128)(2,1)S(1)}, u32[]{:S(2)}, u32[]{:S(2)}) collective-permute-start(bf16[576,256]{1,0:T(8,128)(2,1)S(1)} %get-tuple-element.58.joined.refs_0_), channel_id=1, source_target_pairs={{0,8},{8,0},{16,24},{24,16},{1,9},{9,1},{17,25},{25,17},{2,10},{10... | collective-permute-start | bytes 884744 | tf_op jit(solution)/shard_map/ppermute | solution.py:30
  116.9 7.3 %collective-permute-start.23 = (bf16[256,256]{1,0:T(8,128)(2,1)S(1)}, bf16[256,256]{1,0:T(8,128)(2,1)S(1)}, u32[]{:S(2)}, u32[]{:S(2)}) collective-permute-start(bf16[256,256]{1,0:T(8,128)(2,1)S(1)} %get-tuple-element.57), channel_id=1, source_target_pairs={{0,4},{1,5},{2,6},{3,7},{4,0},{5,1},{6,2},{7,3},{8,12},{9,13},{10,... | collective-permute-start | bytes 393224 | tf_op jit(solution)/shard_map/ppermute | solution.py:30
  124.9 2.8 %collective-permute-start.27 = (bf16[576,256]{1,0:T(8,128)(2,1)S(1)}, bf16[576,256]{1,0:T(8,128)(2,1)S(1)}, u32[]{:S(2)}, u32[]{:S(2)}) collective-permute-start(bf16[576,256]{1,0:T(8,128)(2,1)S(1)} %get-tuple-element.60), channel_id=1, source_target_pairs={{0,1},{1,0},{2,3},{3,2},{4,5},{5,4},{6,7},{7,6},{8,9},{9,8},{10,11... | collective-permute-start | bytes 884744 | tf_op jit(solution)/shard_map/ppermute | solution.py:30
  125.0 2.8 %collective-permute-start.30 = (bf16[576,256]{1,0:T(8,128)(2,1)S(1)}, bf16[576,256]{1,0:T(8,128)(2,1)S(1)}, u32[]{:S(2)}, u32[]{:S(2)}) collective-permute-start(bf16[576,256]{1,0:T(8,128)(2,1)S(1)} %collective-permute-done.26.refs_3_), channel_id=1, source_target_pairs={{0,1},{1,0},{2,3},{3,2},{4,5},{5,4},{6,7},{7,6},{8,9},{9,8},{10,11... | collective-permute-start | bytes 884744 | tf_op jit(solution)/shard_map/ppermute | solution.py:30
  127.3 1.6 %collective-permute-start.29 = (bf16[576,256]{1,0:T(8,128)(2,1)S(1)}, bf16[576,256]{1,0:T(8,128)(2,1)S(1)}, u32[]{:S(2)}, u32[]{:S(2)}) collective-permute-start(bf16[576,256]{1,0:T(8,128)(2,1)S(1)} %collective-permute-done.25.refs_2_), channel_id=1, source_target_pairs={{0,1},{1,0},{2,3},{3,2},{4,5},{5,4},{6,7},{7,6},{8,9},{9,8},{10,11... | collective-permute-start | bytes 884744 | tf_op jit(solution)/shard_map/ppermute | solution.py:30
  127.3 2.0 %collective-permute-start.28 = (bf16[576,256]{1,0:T(8,128)(2,1)S(1)}, bf16[576,256]{1,0:T(8,128)(2,1)S(1)}, u32[]{:S(2)}, u32[]{:S(2)}) collective-permute-start(bf16[576,256]{1,0:T(8,128)(2,1)S(1)} %collective-permute-done.24.refs_1_), channel_id=1, source_target_pairs={{0,1},{1,0},{2,3},{3,2},{4,5},{5,4},{6,7},{7,6},{8,9},{9,8},{10,11... | collective-permute-start | bytes 884744 | tf_op jit(solution)/shard_map/ppermute | solution.py:30
  (2 other events, 2.5 us)

commit v7 on v6

--- a/solution.py
+++ b/solution.py
@@ -393,14 +393,14 @@
     return acc
 
 
-def run_grp(hour_part, depth, ids, parts):
+def run_grp(hour_part, depth, parts):
     rows, rank = parts[0].shape
     ways = len(parts)
     each, dst_rows = hour_part // depth, (rows - hour_part) // depth
 
-    def kernel(ids, *refs):
+    def kernel(*refs):
         outs, acc = refs[ways:-1], refs[-1]
-        z = ids[0] >> 1
+        z = lax.axis_index("dev") >> 1
         acc[...] = total(refs[:ways])
         for m in range(depth):
             kind = outs[m].dtype
@@ -412,9 +412,8 @@
     return call(
         kernel,
         "grp_sum",
-        (ids, *parts),
+        parts,
         shares(each + dst_rows, rank, depth),
-        specs=[SMEM] + [VMEM] * ways,
         scratch=[((rows, rank), F32)],
         weight=SLOW,
     )
@@ -466,7 +465,7 @@
     return call(kernel, "src_sum", (keep, got, joined), outs)
 
 
-def run_place(sizes, hour_rows, ids, parts, dst_rows):
+def run_place(sizes, hour_rows, parts, dst_rows):
     grps, devs = sizes
     depth = devs // 2
     arrays = [p for p, _, _ in parts]
@@ -475,9 +474,10 @@
     rows = part // depth
     n = len(parts)
 
-    def kernel(ids, *refs):
-        ins, (hours, dst, stage, sem) = refs[:n], refs[n:]
-        core, z, grp = ids[0] & 1, ids[0] >> 1, ids[1]
+    def kernel(*refs):
+        ins, (hours, dst, stage, dst_stage, sem) = refs[:n], refs[n:]
+        dev, grp = lax.axis_index("dev"), lax.axis_index("grp")
+        core, z = dev & 1, dev >> 1
         copies = []
         for i, (_, far, m) in enumerate(parts):
             for k in range(depth):
@@ -490,22 +490,27 @@
             copies[-1].start()
             if not far:
                 at = pl.multiple_of((grp ^ m) * dst_rows, dst_rows)
-                dst[pl.ds(at, dst_rows), :] = ins[i][pl.ds(part, dst_rows), :].astype(F32)
+                new = ins[i][pl.ds(part, dst_rows), :].astype(F32)
+                dst_stage[pl.ds(at, dst_rows), :] = new
+            if i == grps - 1:
+                copies.append(pltpu.make_async_copy(dst_stage, dst, sem.at[n]))
+                copies[-1].start()
         for copy in copies:
             copy.wait()
 
     outs = [((hour_rows, rank), F32), ((grps * dst_rows, rank), F32)]
-    scratch = [((n, part, rank), F32)]
-    need = size_of([(p.shape, p.dtype) for p in arrays] + outs[1:] + scratch) + (4 << 20)
+    scratch = [((n, part, rank), F32), outs[1]]
+    need = size_of([(p.shape, p.dtype) for p in arrays] + scratch) + (4 << 20)
     return pl.pallas_call(
         kernel,
-        in_specs=[SMEM] + [VMEM] * n,
-        out_specs=[HBM, VMEM],
+        in_specs=[VMEM] * n,
+        out_specs=[HBM, HBM],
         out_shape=[jax.ShapeDtypeStruct(s, t) for s, t in outs],
-        scratch_shapes=[pltpu.VMEM(s, t) for s, t in scratch] + [pltpu.SemaphoreType.DMA((n,))],
+        scratch_shapes=[pltpu.VMEM(s, t) for s, t in scratch]
+        + [pltpu.SemaphoreType.DMA((n + 1,))],
         compiler_params=pltpu.CompilerParams(vmem_limit_bytes=need),
         name="place",
-    )(ids, *arrays)
+    )(*arrays)
 
 
 def per_device(
@@ -548,14 +553,14 @@
 
     hd_got = swap(hd_send, "dev", devs, 1)
     src = functools.partial(run_src, (devs, local))
-    early = blocks // 6
+    early = blocks // 8
     s_acc = src(0, early, ids, resids, b_rows, picked, hd_send)[0]
     *hd, cut_done = run_cut(grps, hd_acc, hd_got, s_acc)
     cut_done = swap(cut_done, "dev", devs, 1)
     s_acc, s_send = src(early, blocks, ids, resids, b_rows, picked, cut_done, s_acc)
     s_got = swap(s_send, "dev", devs, 1)
     hour_part = hour_rows // (2 * grps)
-    hd = run_grp(hour_part, depth, ids, exchange(hd, "grp", grps, 1))
+    hd = run_grp(hour_part, depth, exchange(hd, "grp", grps, 1))
     hour_each = hour_part // depth
     s_keep, s_send = run_halve(s_acc, s_got)
     hour, dst = run_z(exchange(hd, "dev", devs, 2), hour_each)
@@ -572,7 +577,7 @@
     near = [joined] + [swap(joined, "grp", grps, m) for m in range(1, grps)]
     far = [swap(x, "dev", devs, 1) for x in [same] + near[1:]]
     parts = [(near[m], 0, m) for m in range(grps)] + [(far[m], 1, m) for m in range(grps)]
-    grad_hour, grad_dst = run_place(sizes, hour_rows, ids, parts, dst_part)
+    grad_hour, grad_dst = run_place(sizes, hour_rows, parts, dst_part)
     return grad_src, grad_dst, grad_hour
 
 

time: 133 us -> 131 us (0.985)
  Pallas kernels: 62 us -> 60.3 us
  transfers between devices with their start and end apart: 31 -> 31, of which waited for: 13 -> 15; matrix products, arithmetic and copies ran while one was open for 1% -> 1% of each run, Pallas kernels for 13% -> 13%
where the time goes in v7:
time: 131 us
  Pallas kernels  60.3 us (46%)
  waiting for transfers between devices  34.1 us (26%)
  starting transfers between devices  32.3 us (25%)
  local copies, waits for them, and re-layouts  3.31 us (3%)
    pallas_call x1, Pallas kernels, run_main(): pl.pallas_call(functools.partial(main_kernel, shape), in_specs=[SMEM, HBM...  40.3 us
    ppermute x31, waiting for transfers between devices, swap(): return lax.ppermute(x, axis, [(i, i ^ mask) for i in range(size)])  34.1 us
    ppermute x31, starting transfers between devices, swap(): return lax.ppermute(x, axis, [(i, i ^ mask) for i in range(size)])  32.3 us
    pallas_call x2, Pallas kernels, run_src(): pl.pallas_call(functools.partial(src_kernel, shape, first, last), in_spec...  14.1 us
  transfers between devices with their start and end apart: 31, of which 15 were waited for; matrix products, arithmetic and copies ran while one was open for 1% of the time, Pallas kernels for 13%

profile of v7, /device:TPU:0, one launch (start us, length us, event | category | flops | bytes accessed | tf_op | source)
XLA Modules:
  0.0 130.9 jit_solution(17004503032190687500)
XLA Ops:
  0.6 3.1 %collective-permute-start.3 = (bf16[256,256]{1,0:T(8,128)(2,1)}, bf16[256,256]{1,0:T(8,128)(2,1)S(1)}, u32[]{:S(2)}, u32[]{:S(2)}) collective-permute-start(bf16[256,256]{1,0:T(8,128)(2,1)} %own.1), channel_id=1, source_target_pairs={{0,2},{1,3},{2,0},{3,1},{4,6},{5,7},{6,4},{7,5},{8,10},{9,11},{10,... | collective-permute-start | bytes 393224 | tf_op jit(solution)/shard_map/ppermute | solution.py:30
  3.7 2.9 %collective-permute-start.2 = (bf16[64,256]{1,0:T(8,128)(2,1)S(1)}, bf16[64,256]{1,0:T(8,128)(2,1)S(1)}, u32[]{:S(2)}, u32[]{:S(2)}) collective-permute-start(bf16[64,256]{1,0:T(8,128)(2,1)S(1)} %constant_dynamic-slice_fusion.refs_0_), channel_id=1, source_target_pairs={{0,6},{1,7},{2,4},{3,5},{4,2},{5,3},{6,0},{7,1},{8,14},{9,15},{10,... | collective-permute-start | bytes 98312 | tf_op jit(solution)/shard_map/ppermute | solution.py:30
  6.6 1.5 %collective-permute-start = (bf16[64,256]{1,0:T(8,128)(2,1)S(1)}, bf16[64,256]{1,0:T(8,128)(2,1)S(1)}, u32[]{:S(2)}, u32[]{:S(2)}) collective-permute-start(bf16[64,256]{1,0:T(8,128)(2,1)S(1)} %constant_dynamic-slice_fusion.refs_0_), channel_id=1, source_target_pairs={{0,2},{1,3},{2,0},{3,1},{4,6},{5,7},{6,4},{7,5},{8,10},{9,11},{10,... | collective-permute-start | bytes 98312 | tf_op jit(solution)/shard_map/ppermute | solution.py:30
  8.1 2.9 %collective-permute-start.5 = (bf16[256,256]{1,0:T(8,128)(2,1)}, bf16[256,256]{1,0:T(8,128)(2,1)S(1)}, u32[]{:S(2)}, u32[]{:S(2)}) collective-permute-start(bf16[256,256]{1,0:T(8,128)(2,1)} %own.1), channel_id=1, source_target_pairs={{0,6},{1,7},{2,4},{3,5},{4,2},{5,3},{6,0},{7,1},{8,14},{9,15},{10,... | collective-permute-start | bytes 393224 | tf_op jit(solution)/shard_map/ppermute | solution.py:30
  11.0 0.8 concatenate.3.ids
  11.9 5.7 %collective-permute-done.1.refs_2_ = bf16[64,256]{1,0:T(8,128)(2,1)S(1)} collective-permute-done((bf16[64,256]{1,0:T(8,128)(2,1)S(1)}, bf16[64,256]{1,0:T(8,128)(2,1)S(1)}, u32[]{:S(2)}, u32[]{:S(2)}) %collective-permute-start.1) | collective-permute-done | bytes 32800 | tf_op jit(solution)/shard_map/ppermute | solution.py:30
  17.6 2.5 %collective-permute-start.8 = (bf16[256,256]{1,0:T(8,128)(2,1)S(1)}, bf16[256,256]{1,0:T(8,128)(2,1)S(1)}, u32[]{:S(2)}, u32[]{:S(2)}) collective-permute-start(bf16[256,256]{1,0:T(8,128)(2,1)S(1)} %get-tuple-element.36.refs_4_), channel_id=1, source_target_pairs={{0,24},{8,16},{16,8},{24,0},{1,25},{9,17},{17,9},{25,1},{2,26},{10... | collective-permute-start | bytes 393224 | tf_op jit(solution)/shard_map/ppermute | solution.py:30
  21.1 1.6 %copy-done.1 = bf16[4096,256]{1,0:T(8,128)(2,1)S(1)} copy-done((bf16[4096,256]{1,0:T(8,128)(2,1)S(1)}, bf16[4096,256]{1,0:T(8,128)(2,1)}, u32[]{:S(2)}) %copy-start.1) | copy-done | bytes 2097176
  22.7 0.9 copy-done.2
  23.6 2.1 %pick_hours.1 = (bf16[1536,256]{1,0:T(8,128)(2,1)S(1)}, bf16[256,256]{1,0:T(8,128)(2,1)S(1)}) custom-call(s32[128]{0:T(128)S(1)} %concatenate.3.ids, bf16[4096,256]{1,0:T(8,128)(2,1)S(1)} %copy-done.1, bf16[256,256]{1,0:T(8,128)(2,1)S(1)} %copy-done.2), custom_call_target="tpu_custom_call" | custom-call | flops 10000000000 | tf_op jit(solution)/shard_map/pick_hours/pallas_call | solution.py:99
  25.9 2.6 %collective-permute-done.9.far = bf16[2048,256]{1,0:T(8,128)(2,1)S(1)} collective-permute-done((bf16[2048,256]{1,0:T(8,128)(2,1)S(1)}, bf16[2048,256]{1,0:T(8,128)(2,1)S(1)}, u32[]{:S(2)}, u32[]{:S(2)}) %collective-permute-start.9) | collective-permute-done | bytes 1048608 | tf_op jit(solution)/shard_map/ppermute | solution.py:30
  28.6 40.3 %hour_dst_terms.1 = (f32[6144,256]{1,0:T(8,128)S(1)}, bf16[3072,256]{1,0:T(8,128)(2,1)S(1)}, bf16[1536,256]{1,0:T(8,128)(2,1)S(1)}, bf16[24,64,4096]{2,1,0:T(8,128)(2,1)}) custom-call(s32[128]{0:T(128)S(1)} %concatenate.3.ids, bf16[24,64,4096]{2,1,0:T(8,128)(2,1)} %counts.1, bf16[1536,256]{1,0:T(8,128)(2,1)S(1)} %get-tuple-element.33.hours, ...), custom_call_target="tpu_custom_call" | custom-call | flops 9663676416 | bytes 25165824 | tf_op jit(solution)/shard_map/hour_dst_terms/pallas_call | solution.py:288
  69.1 3.0 %src_terms.2.after.refs_0_ = f32[2048,256]{1,0:T(8,128)S(1)} custom-call(s32[128]{0:T(128)S(1)} %concatenate.3.ids, bf16[24,64,4096]{2,1,0:T(8,128)(2,1)} %get-tuple-element.39.resids, bf16[1536,256]{1,0:T(8,128)(2,1)S(1)} %get-tuple-element.40.b_rows, bf16[1536,256]{1,0:T(8,128)(2,1)S(1)} %get-tuple-element.33.hours, ...), custom_call_target="tpu_custom_call" | custom-call | flops 1610612736 | bytes 1572864 | tf_op jit(solution)/shard_map/src_terms/pallas_call | solution.py:319
  72.9 1.5 %collective-permute-start.11 = (bf16[768,256]{1,0:T(8,128)(2,1)S(1)}, bf16[768,256]{1,0:T(8,128)(2,1)S(1)}, u32[]{:S(2)}, u32[]{:S(2)}) collective-permute-start(bf16[768,256]{1,0:T(8,128)(2,1)S(1)} %get-tuple-element.42), channel_id=1, source_target_pairs={{0,8},{8,0},{16,24},{24,16},{1,9},{9,1},{17,25},{25,17},{2,10},{10... | collective-permute-start | bytes 1179656 | tf_op jit(solution)/shard_map/ppermute | solution.py:30
  74.4 1.5 %collective-permute-start.12 = (bf16[768,256]{1,0:T(8,128)(2,1)S(1)}, bf16[768,256]{1,0:T(8,128)(2,1)S(1)}, u32[]{:S(2)}, u32[]{:S(2)}) collective-permute-start(bf16[768,256]{1,0:T(8,128)(2,1)S(1)} %get-tuple-element.43), channel_id=1, source_target_pairs={{0,16},{8,24},{16,0},{24,8},{1,17},{9,25},{17,1},{25,9},{2,18},{10... | collective-permute-start | bytes 1179656 | tf_op jit(solution)/shard_map/ppermute | solution.py:30
  76.4 11.1 %src_terms.3 = (f32[2048,256]{1,0:T(8,128)S(1)}, bf16[1024,256]{1,0:T(8,128)(2,1)S(1)}) custom-call(s32[128]{0:T(128)S(1)} %concatenate.3.ids, bf16[24,64,4096]{2,1,0:T(8,128)(2,1)} %get-tuple-element.39.resids, bf16[1536,256]{1,0:T(8,128)(2,1)S(1)} %get-tuple-element.40.b_rows, ...), custom_call_target="tpu_custom_call", output_to_operand_aliasing={{0}: (5, {})} | custom-call | flops 11274289152 | bytes 11010048 | tf_op jit(solution)/shard_map/src_terms/pallas_call | solution.py:319
  87.5 6.4 %collective-permute-done.12.refs_2_ = bf16[768,256]{1,0:T(8,128)(2,1)S(1)} collective-permute-done((bf16[768,256]{1,0:T(8,128)(2,1)S(1)}, bf16[768,256]{1,0:T(8,128)(2,1)S(1)}, u32[]{:S(2)}, u32[]{:S(2)}) %collective-permute-start.12) | collective-permute-done | bytes 393248 | tf_op jit(solution)/shard_map/ppermute | solution.py:30
  94.4 4.3 %collective-permute-start.16 = (bf16[192,256]{1,0:T(8,128)(2,1)S(1)}, bf16[192,256]{1,0:T(8,128)(2,1)S(1)}, u32[]{:S(2)}, u32[]{:S(2)}) collective-permute-start(bf16[192,256]{1,0:T(8,128)(2,1)S(1)} %get-tuple-element.48), channel_id=1, source_target_pairs={{0,6},{1,7},{2,4},{3,5},{4,2},{5,3},{6,0},{7,1},{8,14},{9,15},{10,... | collective-permute-start | bytes 294920 | tf_op jit(solution)/shard_map/ppermute | solution.py:30
  99.3 5.2 %collective-permute-done.15.refs_2_ = bf16[192,256]{1,0:T(8,128)(2,1)S(1)} collective-permute-done((bf16[192,256]{1,0:T(8,128)(2,1)S(1)}, bf16[192,256]{1,0:T(8,128)(2,1)S(1)}, u32[]{:S(2)}, u32[]{:S(2)}) %collective-permute-start.15) | collective-permute-done | bytes 98336 | tf_op jit(solution)/shard_map/ppermute | solution.py:30
  104.6 1.8 %collective-permute-start.19 = (bf16[128,256]{1,0:T(8,128)(2,1)S(1)}, bf16[128,256]{1,0:T(8,128)(2,1)S(1)}, u32[]{:S(2)}, u32[]{:S(2)}) collective-permute-start(bf16[128,256]{1,0:T(8,128)(2,1)S(1)} %get-tuple-element.49.refs_0_), channel_id=1, source_target_pairs={{0,6},{1,7},{2,4},{3,5},{4,2},{5,3},{6,0},{7,1},{8,14},{9,15},{10,... | collective-permute-start | bytes 196616 | tf_op jit(solution)/shard_map/ppermute | solution.py:30
  106.4 1.3 collective-permute-start.18
  107.7 1.4 %collective-permute-start.17 = (bf16[128,256]{1,0:T(8,128)(2,1)S(1)}, bf16[128,256]{1,0:T(8,128)(2,1)S(1)}, u32[]{:S(2)}, u32[]{:S(2)}) collective-permute-start(bf16[128,256]{1,0:T(8,128)(2,1)S(1)} %get-tuple-element.49.refs_0_), channel_id=1, source_target_pairs={{0,2},{1,3},{2,0},{3,1},{4,6},{5,7},{6,4},{7,5},{8,10},{9,11},{10,... | collective-permute-start | bytes 196616 | tf_op jit(solution)/shard_map/ppermute | solution.py:30
  109.0 1.9 %collective-permute-done.19.refs_3_ = bf16[128,256]{1,0:T(8,128)(2,1)S(1)} collective-permute-done((bf16[128,256]{1,0:T(8,128)(2,1)S(1)}, bf16[128,256]{1,0:T(8,128)(2,1)S(1)}, u32[]{:S(2)}, u32[]{:S(2)}) %collective-permute-start.19) | collective-permute-done | bytes 65568 | tf_op jit(solution)/shard_map/ppermute | solution.py:30
  110.9 1.4 %collective-permute-done.18.refs_2_ = bf16[128,256]{1,0:T(8,128)(2,1)S(1)} collective-permute-done((bf16[128,256]{1,0:T(8,128)(2,1)S(1)}, bf16[128,256]{1,0:T(8,128)(2,1)S(1)}, u32[]{:S(2)}, u32[]{:S(2)}) %collective-permute-start.18) | collective-permute-done | bytes 65568 | tf_op jit(solution)/shard_map/ppermute | solution.py:30
  112.7 1.6 %collective-permute-start.26 = (bf16[576,256]{1,0:T(8,128)(2,1)S(1)}, bf16[576,256]{1,0:T(8,128)(2,1)S(1)}, u32[]{:S(2)}, u32[]{:S(2)}) collective-permute-start(bf16[576,256]{1,0:T(8,128)(2,1)S(1)} %get-tuple-element.58.joined.refs_0_), channel_id=1, source_target_pairs={{0,24},{8,16},{16,8},{24,0},{1,25},{9,17},{17,9},{25,1},{2,26},{10... | collective-permute-start | bytes 884744 | tf_op jit(solution)/shard_map/ppermute | solution.py:30
  114.3 1.5 %collective-permute-start.25 = (bf16[576,256]{1,0:T(8,128)(2,1)S(1)}, bf16[576,256]{1,0:T(8,128)(2,1)S(1)}, u32[]{:S(2)}, u32[]{:S(2)}) collective-permute-start(bf16[576,256]{1,0:T(8,128)(2,1)S(1)} %get-tuple-element.58.joined.refs_0_), channel_id=1, source_target_pairs={{0,16},{8,24},{16,0},{24,8},{1,17},{9,25},{17,1},{25,9},{2,18},{10... | collective-permute-start | bytes 884744 | tf_op jit(solution)/shard_map/ppermute | solution.py:30
  116.2 1.0 collective-permute-start.23
  117.2 6.3 %collective-permute-done.23.got = bf16[256,256]{1,0:T(8,128)(2,1)S(1)} collective-permute-done((bf16[256,256]{1,0:T(8,128)(2,1)S(1)}, bf16[256,256]{1,0:T(8,128)(2,1)S(1)}, u32[]{:S(2)}, u32[]{:S(2)}) %collective-permute-start.23) | collective-permute-done | bytes 131104 | tf_op jit(solution)/shard_map/ppermute | solution.py:30
  123.5 0.7 src_sum.1
  124.8 1.9 %collective-permute-done.25.refs_2_ = bf16[576,256]{1,0:T(8,128)(2,1)S(1)} collective-permute-done((bf16[576,256]{1,0:T(8,128)(2,1)S(1)}, bf16[576,256]{1,0:T(8,128)(2,1)S(1)}, u32[]{:S(2)}, u32[]{:S(2)}) %collective-permute-start.25) | collective-permute-done | bytes 294944 | tf_op jit(solution)/shard_map/ppermute | solution.py:30
  127.2 1.1 collective-permute-done.29.refs_6_
  128.7 2.2 %place.1 = (f32[4096,256]{1,0:T(8,128)}, f32[256,256]{1,0:T(8,128)}) custom-call(bf16[576,256]{1,0:T(8,128)(2,1)S(1)} %get-tuple-element.58.joined.refs_0_, bf16[576,256]{1,0:T(8,128)(2,1)S(1)} %collective-permute-done.24.refs_1_, bf16[576,256]{1,0:T(8,128)(2,1)S(1)} %collective-permute-done.25.refs_2_, ...), custom_call_target="tpu_custom_call" | custom-call | tf_op jit(solution)/shard_map/place/pallas_call | solution.py:504
  (53 shorter events, 6.1 us)
Async XLA Ops:
  0.6 3.1 %copy-start = (bf16[256,256]{1,0:T(8,128)(2,1)S(1)}, bf16[256,256]{1,0:T(8,128)(2,1)}, u32[]{:S(2)}) copy-start(bf16[256,256]{1,0:T(8,128)(2,1)} %param.11) | copy-start | bytes 393220
  0.6 16.9 %collective-permute-start.3 = (bf16[256,256]{1,0:T(8,128)(2,1)}, bf16[256,256]{1,0:T(8,128)(2,1)S(1)}, u32[]{:S(2)}, u32[]{:S(2)}) collective-permute-start(bf16[256,256]{1,0:T(8,128)(2,1)} %own.1), channel_id=1, source_target_pairs={{0,2},{1,3},{2,0},{3,1},{4,6},{5,7},{6,4},{7,5},{8,10},{9,11},{10,... | collective-permute-start | bytes 393224 | tf_op jit(solution)/shard_map/ppermute | solution.py:30
  3.7 8.0 %collective-permute-start.2 = (bf16[64,256]{1,0:T(8,128)(2,1)S(1)}, bf16[64,256]{1,0:T(8,128)(2,1)S(1)}, u32[]{:S(2)}, u32[]{:S(2)}) collective-permute-start(bf16[64,256]{1,0:T(8,128)(2,1)S(1)} %constant_dynamic-slice_fusion.refs_0_), channel_id=1, source_target_pairs={{0,6},{1,7},{2,4},{3,5},{4,2},{5,3},{6,0},{7,1},{8,14},{9,15},{10,... | collective-permute-start | bytes 98312 | tf_op jit(solution)/shard_map/ppermute | solution.py:30
  6.6 11.0 %collective-permute-start.1 = (bf16[64,256]{1,0:T(8,128)(2,1)S(1)}, bf16[64,256]{1,0:T(8,128)(2,1)S(1)}, u32[]{:S(2)}, u32[]{:S(2)}) collective-permute-start(bf16[64,256]{1,0:T(8,128)(2,1)S(1)} %constant_dynamic-slice_fusion.refs_0_), channel_id=1, source_target_pairs={{0,4},{1,5},{2,6},{3,7},{4,0},{5,1},{6,2},{7,3},{8,12},{9,13},{10,... | collective-permute-start | bytes 98312 | tf_op jit(solution)/shard_map/ppermute | solution.py:30
  6.6 11.0 %collective-permute-start = (bf16[64,256]{1,0:T(8,128)(2,1)S(1)}, bf16[64,256]{1,0:T(8,128)(2,1)S(1)}, u32[]{:S(2)}, u32[]{:S(2)}) collective-permute-start(bf16[64,256]{1,0:T(8,128)(2,1)S(1)} %constant_dynamic-slice_fusion.refs_0_), channel_id=1, source_target_pairs={{0,2},{1,3},{2,0},{3,1},{4,6},{5,7},{6,4},{7,5},{8,10},{9,11},{10,... | collective-permute-start | bytes 98312 | tf_op jit(solution)/shard_map/ppermute | solution.py:30
  8.1 17.6 %collective-permute-start.5 = (bf16[256,256]{1,0:T(8,128)(2,1)}, bf16[256,256]{1,0:T(8,128)(2,1)S(1)}, u32[]{:S(2)}, u32[]{:S(2)}) collective-permute-start(bf16[256,256]{1,0:T(8,128)(2,1)} %own.1), channel_id=1, source_target_pairs={{0,6},{1,7},{2,4},{3,5},{4,2},{5,3},{6,0},{7,1},{8,14},{9,15},{10,... | collective-permute-start | bytes 393224 | tf_op jit(solution)/shard_map/ppermute | solution.py:30
  11.8 13.9 %collective-permute-start.4 = (bf16[256,256]{1,0:T(8,128)(2,1)}, bf16[256,256]{1,0:T(8,128)(2,1)S(1)}, u32[]{:S(2)}, u32[]{:S(2)}) collective-permute-start(bf16[256,256]{1,0:T(8,128)(2,1)} %own.1), channel_id=1, source_target_pairs={{0,4},{1,5},{2,6},{3,7},{4,0},{5,1},{6,2},{7,3},{8,12},{9,13},{10,... | collective-permute-start | bytes 393224 | tf_op jit(solution)/shard_map/ppermute | solution.py:30
  17.6 8.2 %collective-permute-start.8 = (bf16[256,256]{1,0:T(8,128)(2,1)S(1)}, bf16[256,256]{1,0:T(8,128)(2,1)S(1)}, u32[]{:S(2)}, u32[]{:S(2)}) collective-permute-start(bf16[256,256]{1,0:T(8,128)(2,1)S(1)} %get-tuple-element.36.refs_4_), channel_id=1, source_target_pairs={{0,24},{8,16},{16,8},{24,0},{1,25},{9,17},{17,9},{25,1},{2,26},{10... | collective-permute-start | bytes 393224 | tf_op jit(solution)/shard_map/ppermute | solution.py:30
  20.1 5.7 %collective-permute-start.7 = (bf16[256,256]{1,0:T(8,128)(2,1)S(1)}, bf16[256,256]{1,0:T(8,128)(2,1)S(1)}, u32[]{:S(2)}, u32[]{:S(2)}) collective-permute-start(bf16[256,256]{1,0:T(8,128)(2,1)S(1)} %get-tuple-element.36.refs_4_), channel_id=1, source_target_pairs={{0,16},{8,24},{16,0},{24,8},{1,17},{9,25},{17,1},{25,9},{2,18},{10... | collective-permute-start | bytes 393224 | tf_op jit(solution)/shard_map/ppermute | solution.py:30
  20.6 5.2 %collective-permute-start.6 = (bf16[256,256]{1,0:T(8,128)(2,1)S(1)}, bf16[256,256]{1,0:T(8,128)(2,1)S(1)}, u32[]{:S(2)}, u32[]{:S(2)}) collective-permute-start(bf16[256,256]{1,0:T(8,128)(2,1)S(1)} %get-tuple-element.36.refs_4_), channel_id=1, source_target_pairs={{0,8},{8,0},{16,24},{24,16},{1,9},{9,1},{17,25},{25,17},{2,10},{10... | collective-permute-start | bytes 393224 | tf_op jit(solution)/shard_map/ppermute | solution.py:30
  25.9 2.7 %collective-permute-start.9 = (bf16[2048,256]{1,0:T(8,128)(2,1)S(1)}, bf16[2048,256]{1,0:T(8,128)(2,1)S(1)}, u32[]{:S(2)}, u32[]{:S(2)}) collective-permute-start(bf16[2048,256]{1,0:T(8,128)(2,1)S(1)} %join.4.near), channel_id=1, source_target_pairs={{0,1},{1,0},{2,3},{3,2},{4,5},{5,4},{6,7},{7,6},{8,9},{9,8},{10,11... | collective-permute-start | bytes 3145736 | tf_op jit(solution)/shard_map/ppermute | solution.py:30
  68.9 3.5 %collective-permute-start.10 = (bf16[3072,256]{1,0:T(8,128)(2,1)S(1)}, bf16[3072,256]{1,0:T(8,128)(2,1)S(1)}, u32[]{:S(2)}, u32[]{:S(2)}) collective-permute-start(bf16[3072,256]{1,0:T(8,128)(2,1)S(1)} %get-tuple-element.38.after), channel_id=1, source_target_pairs={{0,1},{1,0},{2,3},{3,2},{4,5},{5,4},{6,7},{7,6},{8,9},{9,8},{10,11... | collective-permute-start | bytes 4718600 | tf_op jit(solution)/shard_map/ppermute | solution.py:30
  72.7 3.7 %collective-permute-start.20 = (f32[8,128]{1,0:T(8,128)S(1)}, f32[8,128]{1,0:T(8,128)S(1)}, u32[]{:S(2)}, u32[]{:S(2)}) collective-permute-start(f32[8,128]{1,0:T(8,128)S(1)} %get-tuple-element.51), channel_id=1, source_target_pairs={{0,1},{1,0},{2,3},{3,2},{4,5},{5,4},{6,7},{7,6},{8,9},{9,8},{10,11... | collective-permute-start | bytes 12296 | tf_op jit(solution)/shard_map/ppermute | solution.py:30
  72.9 14.7 %collective-permute-start.11 = (bf16[768,256]{1,0:T(8,128)(2,1)S(1)}, bf16[768,256]{1,0:T(8,128)(2,1)S(1)}, u32[]{:S(2)}, u32[]{:S(2)}) collective-permute-start(bf16[768,256]{1,0:T(8,128)(2,1)S(1)} %get-tuple-element.42), channel_id=1, source_target_pairs={{0,8},{8,0},{16,24},{24,16},{1,9},{9,1},{17,25},{25,17},{2,10},{10... | collective-permute-start | bytes 1179656 | tf_op jit(solution)/shard_map/ppermute | solution.py:30
  74.4 19.5 %collective-permute-start.12 = (bf16[768,256]{1,0:T(8,128)(2,1)S(1)}, bf16[768,256]{1,0:T(8,128)(2,1)S(1)}, u32[]{:S(2)}, u32[]{:S(2)}) collective-permute-start(bf16[768,256]{1,0:T(8,128)(2,1)S(1)} %get-tuple-element.43), channel_id=1, source_target_pairs={{0,16},{8,24},{16,0},{24,8},{1,17},{9,25},{17,1},{25,9},{2,18},{10... | collective-permute-start | bytes 1179656 | tf_op jit(solution)/shard_map/ppermute | solution.py:30
  75.9 18.0 %collective-permute-start.13 = (bf16[768,256]{1,0:T(8,128)(2,1)S(1)}, bf16[768,256]{1,0:T(8,128)(2,1)S(1)}, u32[]{:S(2)}, u32[]{:S(2)}) collective-permute-start(bf16[768,256]{1,0:T(8,128)(2,1)S(1)} %get-tuple-element.44), channel_id=1, source_target_pairs={{0,24},{8,16},{16,8},{24,0},{1,25},{9,17},{17,9},{25,1},{2,26},{10... | collective-permute-start | bytes 1179656 | tf_op jit(solution)/shard_map/ppermute | solution.py:30
  87.5 11.3 %collective-permute-start.21 = (bf16[1024,256]{1,0:T(8,128)(2,1)S(1)}, bf16[1024,256]{1,0:T(8,128)(2,1)S(1)}, u32[]{:S(2)}, u32[]{:S(2)}) collective-permute-start(bf16[1024,256]{1,0:T(8,128)(2,1)S(1)} %get-tuple-element.53), channel_id=1, source_target_pairs={{0,1},{1,0},{2,3},{3,2},{4,5},{5,4},{6,7},{7,6},{8,9},{9,8},{10,11... | collective-permute-start | bytes 1572872 | tf_op jit(solution)/shard_map/ppermute | solution.py:30
  94.2 5.0 %collective-permute-start.14 = (bf16[192,256]{1,0:T(8,128)(2,1)S(1)}, bf16[192,256]{1,0:T(8,128)(2,1)S(1)}, u32[]{:S(2)}, u32[]{:S(2)}) collective-permute-start(bf16[192,256]{1,0:T(8,128)(2,1)S(1)} %get-tuple-element.46), channel_id=1, source_target_pairs={{0,2},{1,3},{2,0},{3,1},{4,6},{5,7},{6,4},{7,5},{8,10},{9,11},{10,... | collective-permute-start | bytes 294920 | tf_op jit(solution)/shard_map/ppermute | solution.py:30
  94.3 10.1 %collective-permute-start.15 = (bf16[192,256]{1,0:T(8,128)(2,1)S(1)}, bf16[192,256]{1,0:T(8,128)(2,1)S(1)}, u32[]{:S(2)}, u32[]{:S(2)}) collective-permute-start(bf16[192,256]{1,0:T(8,128)(2,1)S(1)} %get-tuple-element.47), channel_id=1, source_target_pairs={{0,4},{1,5},{2,6},{3,7},{4,0},{5,1},{6,2},{7,3},{8,12},{9,13},{10,... | collective-permute-start | bytes 294920 | tf_op jit(solution)/shard_map/ppermute | solution.py:30
  94.4 10.1 %collective-permute-start.16 = (bf16[192,256]{1,0:T(8,128)(2,1)S(1)}, bf16[192,256]{1,0:T(8,128)(2,1)S(1)}, u32[]{:S(2)}, u32[]{:S(2)}) collective-permute-start(bf16[192,256]{1,0:T(8,128)(2,1)S(1)} %get-tuple-element.48), channel_id=1, source_target_pairs={{0,6},{1,7},{2,4},{3,5},{4,2},{5,3},{6,0},{7,1},{8,14},{9,15},{10,... | collective-permute-start | bytes 294920 | tf_op jit(solution)/shard_map/ppermute | solution.py:30
  98.8 13.8 %collective-permute-start.22 = (bf16[512,256]{1,0:T(8,128)(2,1)S(1)}, bf16[512,256]{1,0:T(8,128)(2,1)S(1)}, u32[]{:S(2)}, u32[]{:S(2)}) collective-permute-start(bf16[512,256]{1,0:T(8,128)(2,1)S(1)} %get-tuple-element.55), channel_id=1, source_target_pairs={{0,2},{1,3},{2,0},{3,1},{4,6},{5,7},{6,4},{7,5},{8,10},{9,11},{10,... | collective-permute-start | bytes 786440 | tf_op jit(solution)/shard_map/ppermute | solution.py:30
  104.6 6.3 %collective-permute-start.19 = (bf16[128,256]{1,0:T(8,128)(2,1)S(1)}, bf16[128,256]{1,0:T(8,128)(2,1)S(1)}, u32[]{:S(2)}, u32[]{:S(2)}) collective-permute-start(bf16[128,256]{1,0:T(8,128)(2,1)S(1)} %get-tuple-element.49.refs_0_), channel_id=1, source_target_pairs={{0,6},{1,7},{2,4},{3,5},{4,2},{5,3},{6,0},{7,1},{8,14},{9,15},{10,... | collective-permute-start | bytes 196616 | tf_op jit(solution)/shard_map/ppermute | solution.py:30
  106.4 6.0 %collective-permute-start.18 = (bf16[128,256]{1,0:T(8,128)(2,1)S(1)}, bf16[128,256]{1,0:T(8,128)(2,1)S(1)}, u32[]{:S(2)}, u32[]{:S(2)}) collective-permute-start(bf16[128,256]{1,0:T(8,128)(2,1)S(1)} %get-tuple-element.49.refs_0_), channel_id=1, source_target_pairs={{0,4},{1,5},{2,6},{3,7},{4,0},{5,1},{6,2},{7,3},{8,12},{9,13},{10,... | collective-permute-start | bytes 196616 | tf_op jit(solution)/shard_map/ppermute | solution.py:30
  107.7 4.9 %collective-permute-start.17 = (bf16[128,256]{1,0:T(8,128)(2,1)S(1)}, bf16[128,256]{1,0:T(8,128)(2,1)S(1)}, u32[]{:S(2)}, u32[]{:S(2)}) collective-permute-start(bf16[128,256]{1,0:T(8,128)(2,1)S(1)} %get-tuple-element.49.refs_0_), channel_id=1, source_target_pairs={{0,2},{1,3},{2,0},{3,1},{4,6},{5,7},{6,4},{7,5},{8,10},{9,11},{10,... | collective-permute-start | bytes 196616 | tf_op jit(solution)/shard_map/ppermute | solution.py:30
  112.7 11.6 %collective-permute-start.26 = (bf16[576,256]{1,0:T(8,128)(2,1)S(1)}, bf16[576,256]{1,0:T(8,128)(2,1)S(1)}, u32[]{:S(2)}, u32[]{:S(2)}) collective-permute-start(bf16[576,256]{1,0:T(8,128)(2,1)S(1)} %get-tuple-element.58.joined.refs_0_), channel_id=1, source_target_pairs={{0,24},{8,16},{16,8},{24,0},{1,25},{9,17},{17,9},{25,1},{2,26},{10... | collective-permute-start | bytes 884744 | tf_op jit(solution)/shard_map/ppermute | solution.py:30
  114.3 12.4 %collective-permute-start.25 = (bf16[576,256]{1,0:T(8,128)(2,1)S(1)}, bf16[576,256]{1,0:T(8,128)(2,1)S(1)}, u32[]{:S(2)}, u32[]{:S(2)}) collective-permute-start(bf16[576,256]{1,0:T(8,128)(2,1)S(1)} %get-tuple-element.58.joined.refs_0_), channel_id=1, source_target_pairs={{0,16},{8,24},{16,0},{24,8},{1,17},{9,25},{17,1},{25,9},{2,18},{10... | collective-permute-start | bytes 884744 | tf_op jit(solution)/shard_map/ppermute | solution.py:30
  115.8 11.0 %collective-permute-start.24 = (bf16[576,256]{1,0:T(8,128)(2,1)S(1)}, bf16[576,256]{1,0:T(8,128)(2,1)S(1)}, u32[]{:S(2)}, u32[]{:S(2)}) collective-permute-start(bf16[576,256]{1,0:T(8,128)(2,1)S(1)} %get-tuple-element.58.joined.refs_0_), channel_id=1, source_target_pairs={{0,8},{8,0},{16,24},{24,16},{1,9},{9,1},{17,25},{25,17},{2,10},{10... | collective-permute-start | bytes 884744 | tf_op jit(solution)/shard_map/ppermute | solution.py:30
  116.2 7.3 %collective-permute-start.23 = (bf16[256,256]{1,0:T(8,128)(2,1)S(1)}, bf16[256,256]{1,0:T(8,128)(2,1)S(1)}, u32[]{:S(2)}, u32[]{:S(2)}) collective-permute-start(bf16[256,256]{1,0:T(8,128)(2,1)S(1)} %get-tuple-element.57), channel_id=1, source_target_pairs={{0,4},{1,5},{2,6},{3,7},{4,0},{5,1},{6,2},{7,3},{8,12},{9,13},{10,... | collective-permute-start | bytes 393224 | tf_op jit(solution)/shard_map/ppermute | solution.py:30
  124.2 2.9 %collective-permute-start.27 = (bf16[576,256]{1,0:T(8,128)(2,1)S(1)}, bf16[576,256]{1,0:T(8,128)(2,1)S(1)}, u32[]{:S(2)}, u32[]{:S(2)}) collective-permute-start(bf16[576,256]{1,0:T(8,128)(2,1)S(1)} %get-tuple-element.60), channel_id=1, source_target_pairs={{0,1},{1,0},{2,3},{3,2},{4,5},{5,4},{6,7},{7,6},{8,9},{9,8},{10,11... | collective-permute-start | bytes 884744 | tf_op jit(solution)/shard_map/ppermute | solution.py:30
  124.2 2.9 %collective-permute-start.30 = (bf16[576,256]{1,0:T(8,128)(2,1)S(1)}, bf16[576,256]{1,0:T(8,128)(2,1)S(1)}, u32[]{:S(2)}, u32[]{:S(2)}) collective-permute-start(bf16[576,256]{1,0:T(8,128)(2,1)S(1)} %collective-permute-done.26.refs_3_), channel_id=1, source_target_pairs={{0,1},{1,0},{2,3},{3,2},{4,5},{5,4},{6,7},{7,6},{8,9},{9,8},{10,11... | collective-permute-start | bytes 884744 | tf_op jit(solution)/shard_map/ppermute | solution.py:30
  126.7 1.6 %collective-permute-start.29 = (bf16[576,256]{1,0:T(8,128)(2,1)S(1)}, bf16[576,256]{1,0:T(8,128)(2,1)S(1)}, u32[]{:S(2)}, u32[]{:S(2)}) collective-permute-start(bf16[576,256]{1,0:T(8,128)(2,1)S(1)} %collective-permute-done.25.refs_2_), channel_id=1, source_target_pairs={{0,1},{1,0},{2,3},{3,2},{4,5},{5,4},{6,7},{7,6},{8,9},{9,8},{10,11... | collective-permute-start | bytes 884744 | tf_op jit(solution)/shard_map/ppermute | solution.py:30
  126.9 1.8 %collective-permute-start.28 = (bf16[576,256]{1,0:T(8,128)(2,1)S(1)}, bf16[576,256]{1,0:T(8,128)(2,1)S(1)}, u32[]{:S(2)}, u32[]{:S(2)}) collective-permute-start(bf16[576,256]{1,0:T(8,128)(2,1)S(1)} %collective-permute-done.24.refs_1_), channel_id=1, source_target_pairs={{0,1},{1,0},{2,3},{3,2},{4,5},{5,4},{6,7},{7,6},{8,9},{9,8},{10,11... | collective-permute-start | bytes 884744 | tf_op jit(solution)/shard_map/ppermute | solution.py:30
  (2 other events, 2.5 us)

commit v8 on v7

--- a/solution.py
+++ b/solution.py
@@ -132,9 +132,12 @@
     def put(t, way):
         return pltpu.make_async_copy(stages[way][0], resids.at[t], resid_sem.at[way])
 
-    for t in range(min(RING, blocks)):
+    ahead = 2
+    for t in range(ahead):
         fetch(t).start()
     hd_acc[...] = jnp.zeros_like(hd_acc)
+    for t in range(ahead, min(RING, blocks)):
+        fetch(t).start()
     me, grp = ids[0], ids[1]
     core = me & 1
 
@@ -465,52 +468,61 @@
     return call(kernel, "src_sum", (keep, got, joined), outs)
 
 
-def run_place(sizes, hour_rows, parts, dst_rows):
+def run_place(sizes, hour_rows, parts, other, dst_rows, so_far=None):
     grps, devs = sizes
     depth = devs // 2
-    arrays = [p for p, _, _ in parts]
-    rank = arrays[0].shape[1]
+    rank = parts[0].shape[1]
     part = hour_rows // (2 * grps)
     rows = part // depth
-    n = len(parts)
+    near = so_far is None
 
     def kernel(*refs):
-        ins, (hours, dst, stage, dst_stage, sem) = refs[:n], refs[n:]
+        ins = refs[:grps]
+        if near:
+            hours, dst, stage, sem, dst_stage = refs[grps:]
+        else:
+            hours, stage, sem = refs[grps + 1 :]
         dev, grp = lax.axis_index("dev"), lax.axis_index("grp")
         core, z = dev & 1, dev >> 1
         copies = []
-        for i, (_, far, m) in enumerate(parts):
+        if near:
+            for m in range(grps):
+                at = pl.multiple_of((grp ^ m) * dst_rows, dst_rows)
+                new = ins[m][pl.ds(part, dst_rows), :].astype(F32)
+                dst_stage[pl.ds(at, dst_rows), :] = new
+            copies.append(pltpu.make_async_copy(dst_stage, dst, sem.at[grps]))
+            copies[-1].start()
+        for m in range(grps):
             for k in range(depth):
                 at = pl.multiple_of((z ^ k) * rows, rows)
-                stage[i, pl.ds(at, rows), :] = ins[i][pl.ds(k * rows, rows), :].astype(F32)
-            home = pl.multiple_of(((core ^ far) * grps + (grp ^ m)) * part, part)
+                stage[m, pl.ds(at, rows), :] = ins[m][pl.ds(k * rows, rows), :].astype(F32)
+            home = pl.multiple_of(((core ^ other) * grps + (grp ^ m)) * part, part)
             copies.append(
-                pltpu.make_async_copy(stage.at[i], hours.at[pl.ds(home, part)], sem.at[i])
+                pltpu.make_async_copy(stage.at[m], hours.at[pl.ds(home, part)], sem.at[m])
             )
             copies[-1].start()
-            if not far:
-                at = pl.multiple_of((grp ^ m) * dst_rows, dst_rows)
-                new = ins[i][pl.ds(part, dst_rows), :].astype(F32)
-                dst_stage[pl.ds(at, dst_rows), :] = new
-            if i == grps - 1:
-                copies.append(pltpu.make_async_copy(dst_stage, dst, sem.at[n]))
-                copies[-1].start()
         for copy in copies:
             copy.wait()
 
-    outs = [((hour_rows, rank), F32), ((grps * dst_rows, rank), F32)]
-    scratch = [((n, part, rank), F32), outs[1]]
-    need = size_of([(p.shape, p.dtype) for p in arrays] + scratch) + (4 << 20)
+    outs = [((hour_rows, rank), F32)]
+    scratch = [((grps, part, rank), F32)]
+    extra = [((grps * dst_rows, rank), F32)] if near else []
+    need = size_of([(p.shape, p.dtype) for p in parts] + scratch + extra) + (4 << 20)
     return pl.pallas_call(
         kernel,
-        in_specs=[VMEM] * n,
-        out_specs=[HBM, HBM],
-        out_shape=[jax.ShapeDtypeStruct(s, t) for s, t in outs],
+        in_specs=[VMEM] * grps + [HBM] * (not near),
+        out_specs=[HBM] * len(outs + extra),
+        out_shape=[jax.ShapeDtypeStruct(s, t) for s, t in outs + extra],
         scratch_shapes=[pltpu.VMEM(s, t) for s, t in scratch]
-        + [pltpu.SemaphoreType.DMA((n + 1,))],
+        + [pltpu.SemaphoreType.DMA((grps + 1,))]
+        + [pltpu.VMEM(s, t) for s, t in extra],
+        input_output_aliases={} if near else {grps: 0},
         compiler_params=pltpu.CompilerParams(vmem_limit_bytes=need),
+        cost_estimate=pl.CostEstimate(
+            flops=SLOW // 10 if near else 0, bytes_accessed=0, transcendentals=0
+        ),
         name="place",
-    )(*arrays)
+    )(*parts, *([] if near else [so_far]))
 
 
 def per_device(
@@ -576,8 +588,8 @@
     grad_src, same = run_src_sum(s_keep, s_got, joined)
     near = [joined] + [swap(joined, "grp", grps, m) for m in range(1, grps)]
     far = [swap(x, "dev", devs, 1) for x in [same] + near[1:]]
-    parts = [(near[m], 0, m) for m in range(grps)] + [(far[m], 1, m) for m in range(grps)]
-    grad_hour, grad_dst = run_place(sizes, hour_rows, parts, dst_part)
+    grad_hour, grad_dst = run_place(sizes, hour_rows, near, 0, dst_part)
+    grad_hour = run_place(sizes, hour_rows, far, 1, dst_part, grad_hour)[0]
     return grad_src, grad_dst, grad_hour
 
 

time: 131 us -> 130 us (level)
  waiting for transfers between devices: 34.1 us -> 32.7 us
    ppermute x31, waiting for transfers between devices: 34.1 us -> 32.7 us  [swap(): return lax.ppermute(x, axis, [(i, i ^ mask) for i in range(size)])]
    pallas_call x1 -> x2, Pallas kernels: 2.2 us -> 2.89 us  [run_place(): pl.pallas_call(kernel, in_specs=[VMEM] * grps + [HBM] * (not near), out_s...]
  transfers between devices with their start and end apart: 31 -> 31, of which waited for: 15 -> 13; matrix products, arithmetic and copies ran while one was open for 1% -> 1% of each run, Pallas kernels for 13% -> 14%
where the time goes in v8:
time: 130 us
  Pallas kernels  61 us (47%)
  waiting for transfers between devices  32.7 us (25%)
  starting transfers between devices  32.3 us (25%)
  local copies, waits for them, and re-layouts  3.31 us (3%)
    pallas_call x1, Pallas kernels, run_main(): pl.pallas_call(functools.partial(main_kernel, shape), in_specs=[SMEM, HBM...  40.3 us
    ppermute x31, waiting for transfers between devices, swap(): return lax.ppermute(x, axis, [(i, i ^ mask) for i in range(size)])  32.7 us
    ppermute x31, starting transfers between devices, swap(): return lax.ppermute(x, axis, [(i, i ^ mask) for i in range(size)])  32.3 us
    pallas_call x2, Pallas kernels, run_src(): pl.pallas_call(functools.partial(src_kernel, shape, first, last), in_spec...  14.1 us
    pallas_call x2, Pallas kernels, run_place(): pl.pallas_call(kernel, in_specs=[VMEM] * grps + [HBM] * (not near), out_s...  2.89 us
  transfers between devices with their start and end apart: 31, of which 13 were waited for; matrix products, arithmetic and copies ran while one was open for 1% of the time, Pallas kernels for 14%

profile of v8, /device:TPU:0, one launch (start us, length us, event | category | flops | bytes accessed | tf_op | source)
XLA Modules:
  0.0 130.1 jit_solution(1259293957922944102)
XLA Ops:
  0.6 3.1 %collective-permute-start.3 = (bf16[256,256]{1,0:T(8,128)(2,1)}, bf16[256,256]{1,0:T(8,128)(2,1)S(1)}, u32[]{:S(2)}, u32[]{:S(2)}) collective-permute-start(bf16[256,256]{1,0:T(8,128)(2,1)} %own.1), channel_id=1, source_target_pairs={{0,2},{1,3},{2,0},{3,1},{4,6},{5,7},{6,4},{7,5},{8,10},{9,11},{10,... | collective-permute-start | bytes 393224 | tf_op jit(solution)/shard_map/ppermute | solution.py:30
  3.7 2.9 %collective-permute-start.2 = (bf16[64,256]{1,0:T(8,128)(2,1)S(1)}, bf16[64,256]{1,0:T(8,128)(2,1)S(1)}, u32[]{:S(2)}, u32[]{:S(2)}) collective-permute-start(bf16[64,256]{1,0:T(8,128)(2,1)S(1)} %constant_dynamic-slice_fusion.refs_0_), channel_id=1, source_target_pairs={{0,6},{1,7},{2,4},{3,5},{4,2},{5,3},{6,0},{7,1},{8,14},{9,15},{10,... | collective-permute-start | bytes 98312 | tf_op jit(solution)/shard_map/ppermute | solution.py:30
  6.6 1.5 %collective-permute-start = (bf16[64,256]{1,0:T(8,128)(2,1)S(1)}, bf16[64,256]{1,0:T(8,128)(2,1)S(1)}, u32[]{:S(2)}, u32[]{:S(2)}) collective-permute-start(bf16[64,256]{1,0:T(8,128)(2,1)S(1)} %constant_dynamic-slice_fusion.refs_0_), channel_id=1, source_target_pairs={{0,2},{1,3},{2,0},{3,1},{4,6},{5,7},{6,4},{7,5},{8,10},{9,11},{10,... | collective-permute-start | bytes 98312 | tf_op jit(solution)/shard_map/ppermute | solution.py:30
  8.1 2.9 %collective-permute-start.5 = (bf16[256,256]{1,0:T(8,128)(2,1)}, bf16[256,256]{1,0:T(8,128)(2,1)S(1)}, u32[]{:S(2)}, u32[]{:S(2)}) collective-permute-start(bf16[256,256]{1,0:T(8,128)(2,1)} %own.1), channel_id=1, source_target_pairs={{0,6},{1,7},{2,4},{3,5},{4,2},{5,3},{6,0},{7,1},{8,14},{9,15},{10,... | collective-permute-start | bytes 393224 | tf_op jit(solution)/shard_map/ppermute | solution.py:30
  11.0 0.8 concatenate.3.ids
  11.9 5.7 %collective-permute-done.1.refs_2_ = bf16[64,256]{1,0:T(8,128)(2,1)S(1)} collective-permute-done((bf16[64,256]{1,0:T(8,128)(2,1)S(1)}, bf16[64,256]{1,0:T(8,128)(2,1)S(1)}, u32[]{:S(2)}, u32[]{:S(2)}) %collective-permute-start.1) | collective-permute-done | bytes 32800 | tf_op jit(solution)/shard_map/ppermute | solution.py:30
  17.6 2.5 %collective-permute-start.8 = (bf16[256,256]{1,0:T(8,128)(2,1)S(1)}, bf16[256,256]{1,0:T(8,128)(2,1)S(1)}, u32[]{:S(2)}, u32[]{:S(2)}) collective-permute-start(bf16[256,256]{1,0:T(8,128)(2,1)S(1)} %get-tuple-element.36.refs_4_), channel_id=1, source_target_pairs={{0,24},{8,16},{16,8},{24,0},{1,25},{9,17},{17,9},{25,1},{2,26},{10... | collective-permute-start | bytes 393224 | tf_op jit(solution)/shard_map/ppermute | solution.py:30
  21.1 1.6 %copy-done.1 = bf16[4096,256]{1,0:T(8,128)(2,1)S(1)} copy-done((bf16[4096,256]{1,0:T(8,128)(2,1)S(1)}, bf16[4096,256]{1,0:T(8,128)(2,1)}, u32[]{:S(2)}) %copy-start.1) | copy-done | bytes 2097176
  22.7 0.9 copy-done.2
  23.6 2.1 %pick_hours.1 = (bf16[1536,256]{1,0:T(8,128)(2,1)S(1)}, bf16[256,256]{1,0:T(8,128)(2,1)S(1)}) custom-call(s32[128]{0:T(128)S(1)} %concatenate.3.ids, bf16[4096,256]{1,0:T(8,128)(2,1)S(1)} %copy-done.1, bf16[256,256]{1,0:T(8,128)(2,1)S(1)} %copy-done.2), custom_call_target="tpu_custom_call" | custom-call | flops 10000000000 | tf_op jit(solution)/shard_map/pick_hours/pallas_call | solution.py:99
  25.9 2.6 %collective-permute-done.9.far = bf16[2048,256]{1,0:T(8,128)(2,1)S(1)} collective-permute-done((bf16[2048,256]{1,0:T(8,128)(2,1)S(1)}, bf16[2048,256]{1,0:T(8,128)(2,1)S(1)}, u32[]{:S(2)}, u32[]{:S(2)}) %collective-permute-start.9) | collective-permute-done | bytes 1048608 | tf_op jit(solution)/shard_map/ppermute | solution.py:30
  28.6 40.3 %hour_dst_terms.1 = (f32[6144,256]{1,0:T(8,128)S(1)}, bf16[3072,256]{1,0:T(8,128)(2,1)S(1)}, bf16[1536,256]{1,0:T(8,128)(2,1)S(1)}, bf16[24,64,4096]{2,1,0:T(8,128)(2,1)}) custom-call(s32[128]{0:T(128)S(1)} %concatenate.3.ids, bf16[24,64,4096]{2,1,0:T(8,128)(2,1)} %counts.1, bf16[1536,256]{1,0:T(8,128)(2,1)S(1)} %get-tuple-element.33.hours, ...), custom_call_target="tpu_custom_call" | custom-call | flops 9663676416 | bytes 25165824 | tf_op jit(solution)/shard_map/hour_dst_terms/pallas_call | solution.py:291
  69.1 3.0 %src_terms.2.after.refs_0_ = f32[2048,256]{1,0:T(8,128)S(1)} custom-call(s32[128]{0:T(128)S(1)} %concatenate.3.ids, bf16[24,64,4096]{2,1,0:T(8,128)(2,1)} %get-tuple-element.39.resids, bf16[1536,256]{1,0:T(8,128)(2,1)S(1)} %get-tuple-element.40.b_rows, bf16[1536,256]{1,0:T(8,128)(2,1)S(1)} %get-tuple-element.33.hours, ...), custom_call_target="tpu_custom_call" | custom-call | flops 1610612736 | bytes 1572864 | tf_op jit(solution)/shard_map/src_terms/pallas_call | solution.py:322
  72.9 1.5 %collective-permute-start.11 = (bf16[768,256]{1,0:T(8,128)(2,1)S(1)}, bf16[768,256]{1,0:T(8,128)(2,1)S(1)}, u32[]{:S(2)}, u32[]{:S(2)}) collective-permute-start(bf16[768,256]{1,0:T(8,128)(2,1)S(1)} %get-tuple-element.42), channel_id=1, source_target_pairs={{0,8},{8,0},{16,24},{24,16},{1,9},{9,1},{17,25},{25,17},{2,10},{10... | collective-permute-start | bytes 1179656 | tf_op jit(solution)/shard_map/ppermute | solution.py:30
  74.4 1.5 %collective-permute-start.12 = (bf16[768,256]{1,0:T(8,128)(2,1)S(1)}, bf16[768,256]{1,0:T(8,128)(2,1)S(1)}, u32[]{:S(2)}, u32[]{:S(2)}) collective-permute-start(bf16[768,256]{1,0:T(8,128)(2,1)S(1)} %get-tuple-element.43), channel_id=1, source_target_pairs={{0,16},{8,24},{16,0},{24,8},{1,17},{9,25},{17,1},{25,9},{2,18},{10... | collective-permute-start | bytes 1179656 | tf_op jit(solution)/shard_map/ppermute | solution.py:30
  76.4 11.1 %src_terms.3 = (f32[2048,256]{1,0:T(8,128)S(1)}, bf16[1024,256]{1,0:T(8,128)(2,1)S(1)}) custom-call(s32[128]{0:T(128)S(1)} %concatenate.3.ids, bf16[24,64,4096]{2,1,0:T(8,128)(2,1)} %get-tuple-element.39.resids, bf16[1536,256]{1,0:T(8,128)(2,1)S(1)} %get-tuple-element.40.b_rows, ...), custom_call_target="tpu_custom_call", output_to_operand_aliasing={{0}: (5, {})} | custom-call | flops 11274289152 | bytes 11010048 | tf_op jit(solution)/shard_map/src_terms/pallas_call | solution.py:322
  87.5 6.4 %collective-permute-done.12.refs_2_ = bf16[768,256]{1,0:T(8,128)(2,1)S(1)} collective-permute-done((bf16[768,256]{1,0:T(8,128)(2,1)S(1)}, bf16[768,256]{1,0:T(8,128)(2,1)S(1)}, u32[]{:S(2)}, u32[]{:S(2)}) %collective-permute-start.12) | collective-permute-done | bytes 393248 | tf_op jit(solution)/shard_map/ppermute | solution.py:30
  94.4 4.3 %collective-permute-start.16 = (bf16[192,256]{1,0:T(8,128)(2,1)S(1)}, bf16[192,256]{1,0:T(8,128)(2,1)S(1)}, u32[]{:S(2)}, u32[]{:S(2)}) collective-permute-start(bf16[192,256]{1,0:T(8,128)(2,1)S(1)} %get-tuple-element.48), channel_id=1, source_target_pairs={{0,6},{1,7},{2,4},{3,5},{4,2},{5,3},{6,0},{7,1},{8,14},{9,15},{10,... | collective-permute-start | bytes 294920 | tf_op jit(solution)/shard_map/ppermute | solution.py:30
  99.3 5.2 %collective-permute-done.15.refs_2_ = bf16[192,256]{1,0:T(8,128)(2,1)S(1)} collective-permute-done((bf16[192,256]{1,0:T(8,128)(2,1)S(1)}, bf16[192,256]{1,0:T(8,128)(2,1)S(1)}, u32[]{:S(2)}, u32[]{:S(2)}) %collective-permute-start.15) | collective-permute-done | bytes 98336 | tf_op jit(solution)/shard_map/ppermute | solution.py:30
  104.6 1.8 %collective-permute-start.19 = (bf16[128,256]{1,0:T(8,128)(2,1)S(1)}, bf16[128,256]{1,0:T(8,128)(2,1)S(1)}, u32[]{:S(2)}, u32[]{:S(2)}) collective-permute-start(bf16[128,256]{1,0:T(8,128)(2,1)S(1)} %get-tuple-element.49.refs_0_), channel_id=1, source_target_pairs={{0,6},{1,7},{2,4},{3,5},{4,2},{5,3},{6,0},{7,1},{8,14},{9,15},{10,... | collective-permute-start | bytes 196616 | tf_op jit(solution)/shard_map/ppermute | solution.py:30
  106.4 1.3 %collective-permute-start.18 = (bf16[128,256]{1,0:T(8,128)(2,1)S(1)}, bf16[128,256]{1,0:T(8,128)(2,1)S(1)}, u32[]{:S(2)}, u32[]{:S(2)}) collective-permute-start(bf16[128,256]{1,0:T(8,128)(2,1)S(1)} %get-tuple-element.49.refs_0_), channel_id=1, source_target_pairs={{0,4},{1,5},{2,6},{3,7},{4,0},{5,1},{6,2},{7,3},{8,12},{9,13},{10,... | collective-permute-start | bytes 196616 | tf_op jit(solution)/shard_map/ppermute | solution.py:30
  107.7 1.4 %collective-permute-start.17 = (bf16[128,256]{1,0:T(8,128)(2,1)S(1)}, bf16[128,256]{1,0:T(8,128)(2,1)S(1)}, u32[]{:S(2)}, u32[]{:S(2)}) collective-permute-start(bf16[128,256]{1,0:T(8,128)(2,1)S(1)} %get-tuple-element.49.refs_0_), channel_id=1, source_target_pairs={{0,2},{1,3},{2,0},{3,1},{4,6},{5,7},{6,4},{7,5},{8,10},{9,11},{10,... | collective-permute-start | bytes 196616 | tf_op jit(solution)/shard_map/ppermute | solution.py:30
  109.0 1.9 %collective-permute-done.19.refs_3_ = bf16[128,256]{1,0:T(8,128)(2,1)S(1)} collective-permute-done((bf16[128,256]{1,0:T(8,128)(2,1)S(1)}, bf16[128,256]{1,0:T(8,128)(2,1)S(1)}, u32[]{:S(2)}, u32[]{:S(2)}) %collective-permute-start.19) | collective-permute-done | bytes 65568 | tf_op jit(solution)/shard_map/ppermute | solution.py:30
  110.9 1.4 %collective-permute-done.18.refs_2_ = bf16[128,256]{1,0:T(8,128)(2,1)S(1)} collective-permute-done((bf16[128,256]{1,0:T(8,128)(2,1)S(1)}, bf16[128,256]{1,0:T(8,128)(2,1)S(1)}, u32[]{:S(2)}, u32[]{:S(2)}) %collective-permute-start.18) | collective-permute-done | bytes 65568 | tf_op jit(solution)/shard_map/ppermute | solution.py:30
  112.7 1.6 %collective-permute-start.26 = (bf16[576,256]{1,0:T(8,128)(2,1)S(1)}, bf16[576,256]{1,0:T(8,128)(2,1)S(1)}, u32[]{:S(2)}, u32[]{:S(2)}) collective-permute-start(bf16[576,256]{1,0:T(8,128)(2,1)S(1)} %get-tuple-element.58.joined.refs_0_), channel_id=1, source_target_pairs={{0,24},{8,16},{16,8},{24,0},{1,25},{9,17},{17,9},{25,1},{2,26},{10... | collective-permute-start | bytes 884744 | tf_op jit(solution)/shard_map/ppermute | solution.py:30
  114.3 1.5 %collective-permute-start.25 = (bf16[576,256]{1,0:T(8,128)(2,1)S(1)}, bf16[576,256]{1,0:T(8,128)(2,1)S(1)}, u32[]{:S(2)}, u32[]{:S(2)}) collective-permute-start(bf16[576,256]{1,0:T(8,128)(2,1)S(1)} %get-tuple-element.58.joined.refs_0_), channel_id=1, source_target_pairs={{0,16},{8,24},{16,0},{24,8},{1,17},{9,25},{17,1},{25,9},{2,18},{10... | collective-permute-start | bytes 884744 | tf_op jit(solution)/shard_map/ppermute | solution.py:30
  116.2 1.0 collective-permute-start.23
  117.2 6.3 %collective-permute-done.23.got = bf16[256,256]{1,0:T(8,128)(2,1)S(1)} collective-permute-done((bf16[256,256]{1,0:T(8,128)(2,1)S(1)}, bf16[256,256]{1,0:T(8,128)(2,1)S(1)}, u32[]{:S(2)}, u32[]{:S(2)}) %collective-permute-start.23) | collective-permute-done | bytes 131104 | tf_op jit(solution)/shard_map/ppermute | solution.py:30
  123.5 0.7 src_sum.1
  124.8 1.9 %collective-permute-done.25.refs_2_ = bf16[576,256]{1,0:T(8,128)(2,1)S(1)} collective-permute-done((bf16[576,256]{1,0:T(8,128)(2,1)S(1)}, bf16[576,256]{1,0:T(8,128)(2,1)S(1)}, u32[]{:S(2)}, u32[]{:S(2)}) %collective-permute-start.25) | collective-permute-done | bytes 294944 | tf_op jit(solution)/shard_map/ppermute | solution.py:30
  127.2 1.5 %place.2 = (f32[4096,256]{1,0:T(8,128)}, f32[256,256]{1,0:T(8,128)}) custom-call(bf16[576,256]{1,0:T(8,128)(2,1)S(1)} %get-tuple-element.58.joined.refs_0_, bf16[576,256]{1,0:T(8,128)(2,1)S(1)} %collective-permute-done.24.refs_1_, bf16[576,256]{1,0:T(8,128)(2,1)S(1)} %collective-permute-done.25.refs_2_, bf16[576,256]{1,0:T(8,128)(2,1)S(1)} %collective-permute-done.26.refs_3_), custom_call_target="tpu_custom_call" | custom-call | flops 10000000000 | tf_op jit(solution)/shard_map/place/pallas_call | solution.py:511
  128.7 1.4 %place.3 = f32[4096,256]{1,0:T(8,128)} custom-call(bf16[576,256]{1,0:T(8,128)(2,1)S(1)} %collective-permute-done.27.refs_0_, bf16[576,256]{1,0:T(8,128)(2,1)S(1)} %collective-permute-done.28.refs_1_, bf16[576,256]{1,0:T(8,128)(2,1)S(1)} %collective-permute-done.29.refs_2_, ...), custom_call_target="tpu_custom_call", output_to_operand_aliasing={{}: (4, {})} | custom-call | tf_op jit(solution)/shard_map/place/pallas_call | solution.py:511
  (54 shorter events, 5.7 us)
Async XLA Ops:
  0.6 3.1 %copy-start = (bf16[256,256]{1,0:T(8,128)(2,1)S(1)}, bf16[256,256]{1,0:T(8,128)(2,1)}, u32[]{:S(2)}) copy-start(bf16[256,256]{1,0:T(8,128)(2,1)} %param.11) | copy-start | bytes 393220
  0.6 16.9 %collective-permute-start.3 = (bf16[256,256]{1,0:T(8,128)(2,1)}, bf16[256,256]{1,0:T(8,128)(2,1)S(1)}, u32[]{:S(2)}, u32[]{:S(2)}) collective-permute-start(bf16[256,256]{1,0:T(8,128)(2,1)} %own.1), channel_id=1, source_target_pairs={{0,2},{1,3},{2,0},{3,1},{4,6},{5,7},{6,4},{7,5},{8,10},{9,11},{10,... | collective-permute-start | bytes 393224 | tf_op jit(solution)/shard_map/ppermute | solution.py:30
  3.7 8.0 %collective-permute-start.2 = (bf16[64,256]{1,0:T(8,128)(2,1)S(1)}, bf16[64,256]{1,0:T(8,128)(2,1)S(1)}, u32[]{:S(2)}, u32[]{:S(2)}) collective-permute-start(bf16[64,256]{1,0:T(8,128)(2,1)S(1)} %constant_dynamic-slice_fusion.refs_0_), channel_id=1, source_target_pairs={{0,6},{1,7},{2,4},{3,5},{4,2},{5,3},{6,0},{7,1},{8,14},{9,15},{10,... | collective-permute-start | bytes 98312 | tf_op jit(solution)/shard_map/ppermute | solution.py:30
  6.6 11.0 %collective-permute-start.1 = (bf16[64,256]{1,0:T(8,128)(2,1)S(1)}, bf16[64,256]{1,0:T(8,128)(2,1)S(1)}, u32[]{:S(2)}, u32[]{:S(2)}) collective-permute-start(bf16[64,256]{1,0:T(8,128)(2,1)S(1)} %constant_dynamic-slice_fusion.refs_0_), channel_id=1, source_target_pairs={{0,4},{1,5},{2,6},{3,7},{4,0},{5,1},{6,2},{7,3},{8,12},{9,13},{10,... | collective-permute-start | bytes 98312 | tf_op jit(solution)/shard_map/ppermute | solution.py:30
  6.6 11.0 %collective-permute-start = (bf16[64,256]{1,0:T(8,128)(2,1)S(1)}, bf16[64,256]{1,0:T(8,128)(2,1)S(1)}, u32[]{:S(2)}, u32[]{:S(2)}) collective-permute-start(bf16[64,256]{1,0:T(8,128)(2,1)S(1)} %constant_dynamic-slice_fusion.refs_0_), channel_id=1, source_target_pairs={{0,2},{1,3},{2,0},{3,1},{4,6},{5,7},{6,4},{7,5},{8,10},{9,11},{10,... | collective-permute-start | bytes 98312 | tf_op jit(solution)/shard_map/ppermute | solution.py:30
  8.1 17.6 %collective-permute-start.5 = (bf16[256,256]{1,0:T(8,128)(2,1)}, bf16[256,256]{1,0:T(8,128)(2,1)S(1)}, u32[]{:S(2)}, u32[]{:S(2)}) collective-permute-start(bf16[256,256]{1,0:T(8,128)(2,1)} %own.1), channel_id=1, source_target_pairs={{0,6},{1,7},{2,4},{3,5},{4,2},{5,3},{6,0},{7,1},{8,14},{9,15},{10,... | collective-permute-start | bytes 393224 | tf_op jit(solution)/shard_map/ppermute | solution.py:30
  11.8 13.9 %collective-permute-start.4 = (bf16[256,256]{1,0:T(8,128)(2,1)}, bf16[256,256]{1,0:T(8,128)(2,1)S(1)}, u32[]{:S(2)}, u32[]{:S(2)}) collective-permute-start(bf16[256,256]{1,0:T(8,128)(2,1)} %own.1), channel_id=1, source_target_pairs={{0,4},{1,5},{2,6},{3,7},{4,0},{5,1},{6,2},{7,3},{8,12},{9,13},{10,... | collective-permute-start | bytes 393224 | tf_op jit(solution)/shard_map/ppermute | solution.py:30
  17.6 8.2 %collective-permute-start.8 = (bf16[256,256]{1,0:T(8,128)(2,1)S(1)}, bf16[256,256]{1,0:T(8,128)(2,1)S(1)}, u32[]{:S(2)}, u32[]{:S(2)}) collective-permute-start(bf16[256,256]{1,0:T(8,128)(2,1)S(1)} %get-tuple-element.36.refs_4_), channel_id=1, source_target_pairs={{0,24},{8,16},{16,8},{24,0},{1,25},{9,17},{17,9},{25,1},{2,26},{10... | collective-permute-start | bytes 393224 | tf_op jit(solution)/shard_map/ppermute | solution.py:30
  20.1 5.7 %collective-permute-start.7 = (bf16[256,256]{1,0:T(8,128)(2,1)S(1)}, bf16[256,256]{1,0:T(8,128)(2,1)S(1)}, u32[]{:S(2)}, u32[]{:S(2)}) collective-permute-start(bf16[256,256]{1,0:T(8,128)(2,1)S(1)} %get-tuple-element.36.refs_4_), channel_id=1, source_target_pairs={{0,16},{8,24},{16,0},{24,8},{1,17},{9,25},{17,1},{25,9},{2,18},{10... | collective-permute-start | bytes 393224 | tf_op jit(solution)/shard_map/ppermute | solution.py:30
  20.6 5.2 %collective-permute-start.6 = (bf16[256,256]{1,0:T(8,128)(2,1)S(1)}, bf16[256,256]{1,0:T(8,128)(2,1)S(1)}, u32[]{:S(2)}, u32[]{:S(2)}) collective-permute-start(bf16[256,256]{1,0:T(8,128)(2,1)S(1)} %get-tuple-element.36.refs_4_), channel_id=1, source_target_pairs={{0,8},{8,0},{16,24},{24,16},{1,9},{9,1},{17,25},{25,17},{2,10},{10... | collective-permute-start | bytes 393224 | tf_op jit(solution)/shard_map/ppermute | solution.py:30
  25.9 2.7 %collective-permute-start.9 = (bf16[2048,256]{1,0:T(8,128)(2,1)S(1)}, bf16[2048,256]{1,0:T(8,128)(2,1)S(1)}, u32[]{:S(2)}, u32[]{:S(2)}) collective-permute-start(bf16[2048,256]{1,0:T(8,128)(2,1)S(1)} %join.4.near), channel_id=1, source_target_pairs={{0,1},{1,0},{2,3},{3,2},{4,5},{5,4},{6,7},{7,6},{8,9},{9,8},{10,11... | collective-permute-start | bytes 3145736 | tf_op jit(solution)/shard_map/ppermute | solution.py:30
  68.9 3.5 %collective-permute-start.10 = (bf16[3072,256]{1,0:T(8,128)(2,1)S(1)}, bf16[3072,256]{1,0:T(8,128)(2,1)S(1)}, u32[]{:S(2)}, u32[]{:S(2)}) collective-permute-start(bf16[3072,256]{1,0:T(8,128)(2,1)S(1)} %get-tuple-element.38.after), channel_id=1, source_target_pairs={{0,1},{1,0},{2,3},{3,2},{4,5},{5,4},{6,7},{7,6},{8,9},{9,8},{10,11... | collective-permute-start | bytes 4718600 | tf_op jit(solution)/shard_map/ppermute | solution.py:30
  72.7 3.7 %collective-permute-start.20 = (f32[8,128]{1,0:T(8,128)S(1)}, f32[8,128]{1,0:T(8,128)S(1)}, u32[]{:S(2)}, u32[]{:S(2)}) collective-permute-start(f32[8,128]{1,0:T(8,128)S(1)} %get-tuple-element.51), channel_id=1, source_target_pairs={{0,1},{1,0},{2,3},{3,2},{4,5},{5,4},{6,7},{7,6},{8,9},{9,8},{10,11... | collective-permute-start | bytes 12296 | tf_op jit(solution)/shard_map/ppermute | solution.py:30
  72.9 14.7 %collective-permute-start.11 = (bf16[768,256]{1,0:T(8,128)(2,1)S(1)}, bf16[768,256]{1,0:T(8,128)(2,1)S(1)}, u32[]{:S(2)}, u32[]{:S(2)}) collective-permute-start(bf16[768,256]{1,0:T(8,128)(2,1)S(1)} %get-tuple-element.42), channel_id=1, source_target_pairs={{0,8},{8,0},{16,24},{24,16},{1,9},{9,1},{17,25},{25,17},{2,10},{10... | collective-permute-start | bytes 1179656 | tf_op jit(solution)/shard_map/ppermute | solution.py:30
  74.4 19.5 %collective-permute-start.12 = (bf16[768,256]{1,0:T(8,128)(2,1)S(1)}, bf16[768,256]{1,0:T(8,128)(2,1)S(1)}, u32[]{:S(2)}, u32[]{:S(2)}) collective-permute-start(bf16[768,256]{1,0:T(8,128)(2,1)S(1)} %get-tuple-element.43), channel_id=1, source_target_pairs={{0,16},{8,24},{16,0},{24,8},{1,17},{9,25},{17,1},{25,9},{2,18},{10... | collective-permute-start | bytes 1179656 | tf_op jit(solution)/shard_map/ppermute | solution.py:30
  75.9 18.0 %collective-permute-start.13 = (bf16[768,256]{1,0:T(8,128)(2,1)S(1)}, bf16[768,256]{1,0:T(8,128)(2,1)S(1)}, u32[]{:S(2)}, u32[]{:S(2)}) collective-permute-start(bf16[768,256]{1,0:T(8,128)(2,1)S(1)} %get-tuple-element.44), channel_id=1, source_target_pairs={{0,24},{8,16},{16,8},{24,0},{1,25},{9,17},{17,9},{25,1},{2,26},{10... | collective-permute-start | bytes 1179656 | tf_op jit(solution)/shard_map/ppermute | solution.py:30
  87.5 11.3 %collective-permute-start.21 = (bf16[1024,256]{1,0:T(8,128)(2,1)S(1)}, bf16[1024,256]{1,0:T(8,128)(2,1)S(1)}, u32[]{:S(2)}, u32[]{:S(2)}) collective-permute-start(bf16[1024,256]{1,0:T(8,128)(2,1)S(1)} %get-tuple-element.53), channel_id=1, source_target_pairs={{0,1},{1,0},{2,3},{3,2},{4,5},{5,4},{6,7},{7,6},{8,9},{9,8},{10,11... | collective-permute-start | bytes 1572872 | tf_op jit(solution)/shard_map/ppermute | solution.py:30
  94.2 5.0 %collective-permute-start.14 = (bf16[192,256]{1,0:T(8,128)(2,1)S(1)}, bf16[192,256]{1,0:T(8,128)(2,1)S(1)}, u32[]{:S(2)}, u32[]{:S(2)}) collective-permute-start(bf16[192,256]{1,0:T(8,128)(2,1)S(1)} %get-tuple-element.46), channel_id=1, source_target_pairs={{0,2},{1,3},{2,0},{3,1},{4,6},{5,7},{6,4},{7,5},{8,10},{9,11},{10,... | collective-permute-start | bytes 294920 | tf_op jit(solution)/shard_map/ppermute | solution.py:30
  94.3 10.1 %collective-permute-start.15 = (bf16[192,256]{1,0:T(8,128)(2,1)S(1)}, bf16[192,256]{1,0:T(8,128)(2,1)S(1)}, u32[]{:S(2)}, u32[]{:S(2)}) collective-permute-start(bf16[192,256]{1,0:T(8,128)(2,1)S(1)} %get-tuple-element.47), channel_id=1, source_target_pairs={{0,4},{1,5},{2,6},{3,7},{4,0},{5,1},{6,2},{7,3},{8,12},{9,13},{10,... | collective-permute-start | bytes 294920 | tf_op jit(solution)/shard_map/ppermute | solution.py:30
  94.4 10.1 %collective-permute-start.16 = (bf16[192,256]{1,0:T(8,128)(2,1)S(1)}, bf16[192,256]{1,0:T(8,128)(2,1)S(1)}, u32[]{:S(2)}, u32[]{:S(2)}) collective-permute-start(bf16[192,256]{1,0:T(8,128)(2,1)S(1)} %get-tuple-element.48), channel_id=1, source_target_pairs={{0,6},{1,7},{2,4},{3,5},{4,2},{5,3},{6,0},{7,1},{8,14},{9,15},{10,... | collective-permute-start | bytes 294920 | tf_op jit(solution)/shard_map/ppermute | solution.py:30
  98.8 13.8 %collective-permute-start.22 = (bf16[512,256]{1,0:T(8,128)(2,1)S(1)}, bf16[512,256]{1,0:T(8,128)(2,1)S(1)}, u32[]{:S(2)}, u32[]{:S(2)}) collective-permute-start(bf16[512,256]{1,0:T(8,128)(2,1)S(1)} %get-tuple-element.55), channel_id=1, source_target_pairs={{0,2},{1,3},{2,0},{3,1},{4,6},{5,7},{6,4},{7,5},{8,10},{9,11},{10,... | collective-permute-start | bytes 786440 | tf_op jit(solution)/shard_map/ppermute | solution.py:30
  104.6 6.3 %collective-permute-start.19 = (bf16[128,256]{1,0:T(8,128)(2,1)S(1)}, bf16[128,256]{1,0:T(8,128)(2,1)S(1)}, u32[]{:S(2)}, u32[]{:S(2)}) collective-permute-start(bf16[128,256]{1,0:T(8,128)(2,1)S(1)} %get-tuple-element.49.refs_0_), channel_id=1, source_target_pairs={{0,6},{1,7},{2,4},{3,5},{4,2},{5,3},{6,0},{7,1},{8,14},{9,15},{10,... | collective-permute-start | bytes 196616 | tf_op jit(solution)/shard_map/ppermute | solution.py:30
  106.4 6.0 %collective-permute-start.18 = (bf16[128,256]{1,0:T(8,128)(2,1)S(1)}, bf16[128,256]{1,0:T(8,128)(2,1)S(1)}, u32[]{:S(2)}, u32[]{:S(2)}) collective-permute-start(bf16[128,256]{1,0:T(8,128)(2,1)S(1)} %get-tuple-element.49.refs_0_), channel_id=1, source_target_pairs={{0,4},{1,5},{2,6},{3,7},{4,0},{5,1},{6,2},{7,3},{8,12},{9,13},{10,... | collective-permute-start | bytes 196616 | tf_op jit(solution)/shard_map/ppermute | solution.py:30
  107.7 4.9 %collective-permute-start.17 = (bf16[128,256]{1,0:T(8,128)(2,1)S(1)}, bf16[128,256]{1,0:T(8,128)(2,1)S(1)}, u32[]{:S(2)}, u32[]{:S(2)}) collective-permute-start(bf16[128,256]{1,0:T(8,128)(2,1)S(1)} %get-tuple-element.49.refs_0_), channel_id=1, source_target_pairs={{0,2},{1,3},{2,0},{3,1},{4,6},{5,7},{6,4},{7,5},{8,10},{9,11},{10,... | collective-permute-start | bytes 196616 | tf_op jit(solution)/shard_map/ppermute | solution.py:30
  112.7 11.6 %collective-permute-start.26 = (bf16[576,256]{1,0:T(8,128)(2,1)S(1)}, bf16[576,256]{1,0:T(8,128)(2,1)S(1)}, u32[]{:S(2)}, u32[]{:S(2)}) collective-permute-start(bf16[576,256]{1,0:T(8,128)(2,1)S(1)} %get-tuple-element.58.joined.refs_0_), channel_id=1, source_target_pairs={{0,24},{8,16},{16,8},{24,0},{1,25},{9,17},{17,9},{25,1},{2,26},{10... | collective-permute-start | bytes 884744 | tf_op jit(solution)/shard_map/ppermute | solution.py:30
  114.3 12.4 %collective-permute-start.25 = (bf16[576,256]{1,0:T(8,128)(2,1)S(1)}, bf16[576,256]{1,0:T(8,128)(2,1)S(1)}, u32[]{:S(2)}, u32[]{:S(2)}) collective-permute-start(bf16[576,256]{1,0:T(8,128)(2,1)S(1)} %get-tuple-element.58.joined.refs_0_), channel_id=1, source_target_pairs={{0,16},{8,24},{16,0},{24,8},{1,17},{9,25},{17,1},{25,9},{2,18},{10... | collective-permute-start | bytes 884744 | tf_op jit(solution)/shard_map/ppermute | solution.py:30
  115.8 11.0 %collective-permute-start.24 = (bf16[576,256]{1,0:T(8,128)(2,1)S(1)}, bf16[576,256]{1,0:T(8,128)(2,1)S(1)}, u32[]{:S(2)}, u32[]{:S(2)}) collective-permute-start(bf16[576,256]{1,0:T(8,128)(2,1)S(1)} %get-tuple-element.58.joined.refs_0_), channel_id=1, source_target_pairs={{0,8},{8,0},{16,24},{24,16},{1,9},{9,1},{17,25},{25,17},{2,10},{10... | collective-permute-start | bytes 884744 | tf_op jit(solution)/shard_map/ppermute | solution.py:30
  116.2 7.3 %collective-permute-start.23 = (bf16[256,256]{1,0:T(8,128)(2,1)S(1)}, bf16[256,256]{1,0:T(8,128)(2,1)S(1)}, u32[]{:S(2)}, u32[]{:S(2)}) collective-permute-start(bf16[256,256]{1,0:T(8,128)(2,1)S(1)} %get-tuple-element.57), channel_id=1, source_target_pairs={{0,4},{1,5},{2,6},{3,7},{4,0},{5,1},{6,2},{7,3},{8,12},{9,13},{10,... | collective-permute-start | bytes 393224 | tf_op jit(solution)/shard_map/ppermute | solution.py:30
  124.2 4.4 %collective-permute-start.27 = (bf16[576,256]{1,0:T(8,128)(2,1)S(1)}, bf16[576,256]{1,0:T(8,128)(2,1)S(1)}, u32[]{:S(2)}, u32[]{:S(2)}) collective-permute-start(bf16[576,256]{1,0:T(8,128)(2,1)S(1)} %get-tuple-element.61), channel_id=1, source_target_pairs={{0,1},{1,0},{2,3},{3,2},{4,5},{5,4},{6,7},{7,6},{8,9},{9,8},{10,11... | collective-permute-start | bytes 884744 | tf_op jit(solution)/shard_map/ppermute | solution.py:30
  124.2 4.4 %collective-permute-start.30 = (bf16[576,256]{1,0:T(8,128)(2,1)S(1)}, bf16[576,256]{1,0:T(8,128)(2,1)S(1)}, u32[]{:S(2)}, u32[]{:S(2)}) collective-permute-start(bf16[576,256]{1,0:T(8,128)(2,1)S(1)} %collective-permute-done.26.refs_3_), channel_id=1, source_target_pairs={{0,1},{1,0},{2,3},{3,2},{4,5},{5,4},{6,7},{7,6},{8,9},{9,8},{10,11... | collective-permute-start | bytes 884744 | tf_op jit(solution)/shard_map/ppermute | solution.py:30
  126.7 2.0 %collective-permute-start.29 = (bf16[576,256]{1,0:T(8,128)(2,1)S(1)}, bf16[576,256]{1,0:T(8,128)(2,1)S(1)}, u32[]{:S(2)}, u32[]{:S(2)}) collective-permute-start(bf16[576,256]{1,0:T(8,128)(2,1)S(1)} %collective-permute-done.25.refs_2_), channel_id=1, source_target_pairs={{0,1},{1,0},{2,3},{3,2},{4,5},{5,4},{6,7},{7,6},{8,9},{9,8},{10,11... | collective-permute-start | bytes 884744 | tf_op jit(solution)/shard_map/ppermute | solution.py:30
  126.9 1.9 %collective-permute-start.28 = (bf16[576,256]{1,0:T(8,128)(2,1)S(1)}, bf16[576,256]{1,0:T(8,128)(2,1)S(1)}, u32[]{:S(2)}, u32[]{:S(2)}) collective-permute-start(bf16[576,256]{1,0:T(8,128)(2,1)S(1)} %collective-permute-done.24.refs_1_), channel_id=1, source_target_pairs={{0,1},{1,0},{2,3},{3,2},{4,5},{5,4},{6,7},{7,6},{8,9},{9,8},{10,11... | collective-permute-start | bytes 884744 | tf_op jit(solution)/shard_map/ppermute | solution.py:30
  (2 other events, 2.5 us)

commit v9 on v8

--- a/solution.py
+++ b/solution.py
@@ -261,8 +261,11 @@
         return carry
 
     lax.fori_loop(first, last, visit, 0)
+    at = depth * local
     for send in sends:
-        send[...] = s_acc[pl.ds(depth * local, depth * local), :].astype(BF16)
+        rows = send.shape[0]
+        send[...] = s_acc[pl.ds(at, rows), :].astype(BF16)
+        at += rows
 
 
 def size_of(shapes):
@@ -316,7 +319,7 @@
     more = [] if s_acc is None else [s_acc]
     outs = [((devs * local, rank), F32)]
     if last == blocks:
-        outs.append(((devs * local // 2, rank), BF16))
+        outs += [((devs * local // 4, rank), BF16)] * 2
     need = size_of(outs) + size_of([((RING, rows, columns), BF16)]) + (8 << 20)
     each = rows * columns
     return pl.pallas_call(
@@ -385,6 +388,21 @@
     return [((rows // 2, rank), F32), ((rows // 2, rank), BF16)]
 
 
+def run_first_halve(keep, low, high):
+    half, rank = low.shape
+
+    def kernel(keep, low, high, stay, send):
+        stay[...] = keep[pl.ds(0, half), :] + low[...].astype(F32)
+        send[...] = (keep[pl.ds(half, half), :] + high[...].astype(F32)).astype(BF16)
+
+    return call(
+        kernel,
+        "src_half",
+        (keep, low, high),
+        [((half, rank), F32), ((half, rank), BF16)],
+    )
+
+
 def run_halve(keep, got):
     return call(halve, "src_half", (keep, got), halves(got))
 
@@ -396,13 +414,13 @@
     return acc
 
 
-def run_grp(hour_part, depth, parts):
+def run_grp(hour_part, depth, parts, after):
     rows, rank = parts[0].shape
     ways = len(parts)
     each, dst_rows = hour_part // depth, (rows - hour_part) // depth
 
     def kernel(*refs):
-        outs, acc = refs[ways:-1], refs[-1]
+        outs, acc = refs[ways + 1 : -1], refs[-1]
         z = lax.axis_index("dev") >> 1
         acc[...] = total(refs[:ways])
         for m in range(depth):
@@ -415,40 +433,38 @@
     return call(
         kernel,
         "grp_sum",
-        parts,
+        (*parts, after),
         shares(each + dst_rows, rank, depth),
+        specs=[VMEM] * ways + [ANY],
         scratch=[((rows, rank), F32)],
         weight=SLOW,
     )
 
 
-def run_z(parts, hour_rows):
+def run_z(parts, hour_rows, keep, got):
+    n = len(parts)
     rows, rank = parts[0].shape
 
     def kernel(*refs):
-        hour, dst = refs[-2:]
-        acc = total(refs[:-2]) * (1.0 / SIDE)
+        keep, got, hour, dst, stay, send = refs[n:]
+        halve(keep, got, stay, send)
+        acc = total(refs[:n]) * (1.0 / SIDE)
         hour[...] = acc[:hour_rows].astype(BF16)
         dst[...] = acc[hour_rows:].astype(BF16)
 
-    outs = [((hour_rows, rank), BF16), ((rows - hour_rows, rank), BF16)]
-    return call(kernel, "z_sum", parts, outs, weight=SLOW)
-
-
-def run_join(parts, keep=None, got=None, passed=None):
+    outs = [((hour_rows, rank), BF16), ((rows - hour_rows, rank), BF16)] + halves(got)
+    return call(kernel, "z_sum", (*parts, keep, got), outs, weight=SLOW)
+
+
+def run_join(parts, passed=None):
     rows = [p.shape[0] for p in parts]
     outs = [((sum(rows), parts[0].shape[1]), BF16)]
     ins = tuple(parts)
-    if got is not None:
-        ins += (keep, got)
-        outs += halves(got)
     if passed is not None:
         ins += (passed,)
         outs += [(passed.shape, BF16)]
 
     def kernel(*refs):
-        if got is not None:
-            halve(refs[len(parts)], refs[len(parts) + 1], refs[-2], refs[-1])
         if passed is not None:
             refs[-1][...] = refs[len(parts)][...]
         out, at = refs[len(ins)], 0
@@ -569,16 +585,17 @@
     s_acc = src(0, early, ids, resids, b_rows, picked, hd_send)[0]
     *hd, cut_done = run_cut(grps, hd_acc, hd_got, s_acc)
     cut_done = swap(cut_done, "dev", devs, 1)
-    s_acc, s_send = src(early, blocks, ids, resids, b_rows, picked, cut_done, s_acc)
-    s_got = swap(s_send, "dev", devs, 1)
+    s_acc, *s_sends = src(early, blocks, ids, resids, b_rows, picked, cut_done, s_acc)
+    s_got = [swap(x, "dev", devs, 1) for x in s_sends]
     hour_part = hour_rows // (2 * grps)
-    hd = run_grp(hour_part, depth, exchange(hd, "grp", grps, 1))
+    s_keep, s_send = run_first_halve(s_acc, *s_got)
+    hd = run_grp(hour_part, depth, exchange(hd, "grp", grps, 1), s_keep)
     hour_each = hour_part // depth
-    s_keep, s_send = run_halve(s_acc, s_got)
-    hour, dst = run_z(exchange(hd, "dev", devs, 2), hour_each)
     s_got = swap(s_send, "dev", devs, 2)
+    hd = exchange(hd, "dev", devs, 2)
+    hour, dst, s_keep, s_send = run_z(hd, hour_each, s_keep, s_got)
     back = [hour] + [swap(hour, "dev", devs, 2 * m) for m in range(1, depth)]
-    joined, s_keep, s_send = run_join(back + [dst], s_keep, s_got)
+    joined = run_join(back + [dst])[0]
     step = 4
     s_got = swap(s_send, "dev", devs, step)
     while 2 * step < devs:

time: 130 us -> 132 us (1.015)
    ppermute x31 -> x32, waiting for transfers between devices: 32.7 us -> 34 us  [swap(): return lax.ppermute(x, axis, [(i, i ^ mask) for i in range(size)])]
    ppermute x31 -> x32, starting transfers between devices: 32.3 us -> 32.9 us  [swap(): return lax.ppermute(x, axis, [(i, i ^ mask) for i in range(size)])]
  transfers between devices with their start and end apart: 31 -> 32, of which waited for: 13 -> 13; matrix products, arithmetic and copies ran while one was open for 1% -> 1% of each run, Pallas kernels for 14% -> 14%
where the time goes in v9:
time: 132 us
  Pallas kernels  61 us (46%)
  waiting for transfers between devices  34 us (26%)
  starting transfers between devices  32.9 us (25%)
  local copies, waits for them, and re-layouts  3.31 us (3%)
    pallas_call x1, Pallas kernels, run_main(): pl.pallas_call(functools.partial(main_kernel, shape), in_specs=[SMEM, HBM...  40.3 us
    ppermute x32, waiting for transfers between devices, swap(): return lax.ppermute(x, axis, [(i, i ^ mask) for i in range(size)])  34 us
    ppermute x32, starting transfers between devices, swap(): return lax.ppermute(x, axis, [(i, i ^ mask) for i in range(size)])  32.9 us
    pallas_call x2, Pallas kernels, run_src(): pl.pallas_call(functools.partial(src_kernel, shape, first, last), in_spec...  14.1 us
    pallas_call x2, Pallas kernels, run_place(): pl.pallas_call(kernel, in_specs=[VMEM] * grps + [HBM] * (not near), out_s...  2.89 us
  transfers between devices with their start and end apart: 32, of which 13 were waited for; matrix products, arithmetic and copies ran while one was open for 1% of the time, Pallas kernels for 14%

profile of v9, /device:TPU:0, one launch (start us, length us, event | category | flops | bytes accessed | tf_op | source)
XLA Modules:
  0.0 132.0 jit_solution(18185089016534034782)
XLA Ops:
  0.6 3.1 %collective-permute-start.3 = (bf16[256,256]{1,0:T(8,128)(2,1)}, bf16[256,256]{1,0:T(8,128)(2,1)S(1)}, u32[]{:S(2)}, u32[]{:S(2)}) collective-permute-start(bf16[256,256]{1,0:T(8,128)(2,1)} %own.1), channel_id=1, source_target_pairs={{0,2},{1,3},{2,0},{3,1},{4,6},{5,7},{6,4},{7,5},{8,10},{9,11},{10,... | collective-permute-start | bytes 393224 | tf_op jit(solution)/shard_map/ppermute | solution.py:30
  3.7 2.9 %collective-permute-start.2 = (bf16[64,256]{1,0:T(8,128)(2,1)S(1)}, bf16[64,256]{1,0:T(8,128)(2,1)S(1)}, u32[]{:S(2)}, u32[]{:S(2)}) collective-permute-start(bf16[64,256]{1,0:T(8,128)(2,1)S(1)} %constant_dynamic-slice_fusion.refs_0_), channel_id=1, source_target_pairs={{0,6},{1,7},{2,4},{3,5},{4,2},{5,3},{6,0},{7,1},{8,14},{9,15},{10,... | collective-permute-start | bytes 98312 | tf_op jit(solution)/shard_map/ppermute | solution.py:30
  6.6 1.5 %collective-permute-start = (bf16[64,256]{1,0:T(8,128)(2,1)S(1)}, bf16[64,256]{1,0:T(8,128)(2,1)S(1)}, u32[]{:S(2)}, u32[]{:S(2)}) collective-permute-start(bf16[64,256]{1,0:T(8,128)(2,1)S(1)} %constant_dynamic-slice_fusion.refs_0_), channel_id=1, source_target_pairs={{0,2},{1,3},{2,0},{3,1},{4,6},{5,7},{6,4},{7,5},{8,10},{9,11},{10,... | collective-permute-start | bytes 98312 | tf_op jit(solution)/shard_map/ppermute | solution.py:30
  8.1 2.9 %collective-permute-start.5 = (bf16[256,256]{1,0:T(8,128)(2,1)}, bf16[256,256]{1,0:T(8,128)(2,1)S(1)}, u32[]{:S(2)}, u32[]{:S(2)}) collective-permute-start(bf16[256,256]{1,0:T(8,128)(2,1)} %own.1), channel_id=1, source_target_pairs={{0,6},{1,7},{2,4},{3,5},{4,2},{5,3},{6,0},{7,1},{8,14},{9,15},{10,... | collective-permute-start | bytes 393224 | tf_op jit(solution)/shard_map/ppermute | solution.py:30
  11.0 0.8 concatenate.3.ids
  11.9 5.7 %collective-permute-done.1.refs_2_ = bf16[64,256]{1,0:T(8,128)(2,1)S(1)} collective-permute-done((bf16[64,256]{1,0:T(8,128)(2,1)S(1)}, bf16[64,256]{1,0:T(8,128)(2,1)S(1)}, u32[]{:S(2)}, u32[]{:S(2)}) %collective-permute-start.1) | collective-permute-done | bytes 32800 | tf_op jit(solution)/shard_map/ppermute | solution.py:30
  17.6 2.5 %collective-permute-start.8 = (bf16[256,256]{1,0:T(8,128)(2,1)S(1)}, bf16[256,256]{1,0:T(8,128)(2,1)S(1)}, u32[]{:S(2)}, u32[]{:S(2)}) collective-permute-start(bf16[256,256]{1,0:T(8,128)(2,1)S(1)} %get-tuple-element.36.refs_4_), channel_id=1, source_target_pairs={{0,24},{8,16},{16,8},{24,0},{1,25},{9,17},{17,9},{25,1},{2,26},{10... | collective-permute-start | bytes 393224 | tf_op jit(solution)/shard_map/ppermute | solution.py:30
  21.1 1.6 %copy-done.1 = bf16[4096,256]{1,0:T(8,128)(2,1)S(1)} copy-done((bf16[4096,256]{1,0:T(8,128)(2,1)S(1)}, bf16[4096,256]{1,0:T(8,128)(2,1)}, u32[]{:S(2)}) %copy-start.1) | copy-done | bytes 2097176
  22.7 0.9 copy-done.2
  23.6 2.1 %pick_hours.1 = (bf16[1536,256]{1,0:T(8,128)(2,1)S(1)}, bf16[256,256]{1,0:T(8,128)(2,1)S(1)}) custom-call(s32[128]{0:T(128)S(1)} %concatenate.3.ids, bf16[4096,256]{1,0:T(8,128)(2,1)S(1)} %copy-done.1, bf16[256,256]{1,0:T(8,128)(2,1)S(1)} %copy-done.2), custom_call_target="tpu_custom_call" | custom-call | flops 10000000000 | tf_op jit(solution)/shard_map/pick_hours/pallas_call | solution.py:99
  25.9 2.6 %collective-permute-done.9.far = bf16[2048,256]{1,0:T(8,128)(2,1)S(1)} collective-permute-done((bf16[2048,256]{1,0:T(8,128)(2,1)S(1)}, bf16[2048,256]{1,0:T(8,128)(2,1)S(1)}, u32[]{:S(2)}, u32[]{:S(2)}) %collective-permute-start.9) | collective-permute-done | bytes 1048608 | tf_op jit(solution)/shard_map/ppermute | solution.py:30
  28.6 40.3 %hour_dst_terms.1 = (f32[6144,256]{1,0:T(8,128)S(1)}, bf16[3072,256]{1,0:T(8,128)(2,1)S(1)}, bf16[1536,256]{1,0:T(8,128)(2,1)S(1)}, bf16[24,64,4096]{2,1,0:T(8,128)(2,1)}) custom-call(s32[128]{0:T(128)S(1)} %concatenate.3.ids, bf16[24,64,4096]{2,1,0:T(8,128)(2,1)} %counts.1, bf16[1536,256]{1,0:T(8,128)(2,1)S(1)} %get-tuple-element.33.hours, ...), custom_call_target="tpu_custom_call" | custom-call | flops 9663676416 | bytes 25165824 | tf_op jit(solution)/shard_map/hour_dst_terms/pallas_call | solution.py:294
  69.1 3.0 %src_terms.2.after.refs_0_ = f32[2048,256]{1,0:T(8,128)S(1)} custom-call(s32[128]{0:T(128)S(1)} %concatenate.3.ids, bf16[24,64,4096]{2,1,0:T(8,128)(2,1)} %get-tuple-element.39.resids, bf16[1536,256]{1,0:T(8,128)(2,1)S(1)} %get-tuple-element.40.b_rows, bf16[1536,256]{1,0:T(8,128)(2,1)S(1)} %get-tuple-element.33.hours, ...), custom_call_target="tpu_custom_call" | custom-call | flops 1610612736 | bytes 1572864 | tf_op jit(solution)/shard_map/src_terms/pallas_call | solution.py:325
  72.9 1.5 %collective-permute-start.11 = (bf16[768,256]{1,0:T(8,128)(2,1)S(1)}, bf16[768,256]{1,0:T(8,128)(2,1)S(1)}, u32[]{:S(2)}, u32[]{:S(2)}) collective-permute-start(bf16[768,256]{1,0:T(8,128)(2,1)S(1)} %get-tuple-element.42), channel_id=1, source_target_pairs={{0,8},{8,0},{16,24},{24,16},{1,9},{9,1},{17,25},{25,17},{2,10},{10... | collective-permute-start | bytes 1179656 | tf_op jit(solution)/shard_map/ppermute | solution.py:30
  74.4 1.5 %collective-permute-start.12 = (bf16[768,256]{1,0:T(8,128)(2,1)S(1)}, bf16[768,256]{1,0:T(8,128)(2,1)S(1)}, u32[]{:S(2)}, u32[]{:S(2)}) collective-permute-start(bf16[768,256]{1,0:T(8,128)(2,1)S(1)} %get-tuple-element.43), channel_id=1, source_target_pairs={{0,16},{8,24},{16,0},{24,8},{1,17},{9,25},{17,1},{25,9},{2,18},{10... | collective-permute-start | bytes 1179656 | tf_op jit(solution)/shard_map/ppermute | solution.py:30
  76.4 11.1 %src_terms.3 = (f32[2048,256]{1,0:T(8,128)S(1)}, bf16[512,256]{1,0:T(8,128)(2,1)S(1)}, bf16[512,256]{1,0:T(8,128)(2,1)S(1)}) custom-call(s32[128]{0:T(128)S(1)} %concatenate.3.ids, bf16[24,64,4096]{2,1,0:T(8,128)(2,1)} %get-tuple-element.39.resids, bf16[1536,256]{1,0:T(8,128)(2,1)S(1)} %get-tuple-element.40.b_rows, ...), custom_call_target="tpu_custom_call", output_to_operand_aliasing={{0}: (5, {})} | custom-call | flops 11274289152 | bytes 11010048 | tf_op jit(solution)/shard_map/src_terms/pallas_call | solution.py:325
  88.0 1.0 collective-permute-done.15.low
  89.6 4.3 %collective-permute-done.12.refs_2_ = bf16[768,256]{1,0:T(8,128)(2,1)S(1)} collective-permute-done((bf16[768,256]{1,0:T(8,128)(2,1)S(1)}, bf16[768,256]{1,0:T(8,128)(2,1)S(1)}, u32[]{:S(2)}, u32[]{:S(2)}) %collective-permute-start.12) | collective-permute-done | bytes 393248 | tf_op jit(solution)/shard_map/ppermute | solution.py:30
  94.4 4.3 %collective-permute-start.19 = (bf16[192,256]{1,0:T(8,128)(2,1)S(1)}, bf16[192,256]{1,0:T(8,128)(2,1)S(1)}, u32[]{:S(2)}, u32[]{:S(2)}) collective-permute-start(bf16[192,256]{1,0:T(8,128)(2,1)S(1)} %get-tuple-element.53), channel_id=1, source_target_pairs={{0,6},{1,7},{2,4},{3,5},{4,2},{5,3},{6,0},{7,1},{8,14},{9,15},{10,... | collective-permute-start | bytes 294920 | tf_op jit(solution)/shard_map/ppermute | solution.py:30
  98.7 5.2 %collective-permute-done.17.refs_1_ = bf16[192,256]{1,0:T(8,128)(2,1)S(1)} collective-permute-done((bf16[192,256]{1,0:T(8,128)(2,1)S(1)}, bf16[192,256]{1,0:T(8,128)(2,1)S(1)}, u32[]{:S(2)}, u32[]{:S(2)}) %collective-permute-start.17) | collective-permute-done | bytes 98336 | tf_op jit(solution)/shard_map/ppermute | solution.py:30
  104.6 2.0 %collective-permute-start.24 = (bf16[128,256]{1,0:T(8,128)(2,1)S(1)}, bf16[128,256]{1,0:T(8,128)(2,1)S(1)}, u32[]{:S(2)}, u32[]{:S(2)}) collective-permute-start(bf16[128,256]{1,0:T(8,128)(2,1)S(1)} %get-tuple-element.57.refs_0_), channel_id=1, source_target_pairs={{0,6},{1,7},{2,4},{3,5},{4,2},{5,3},{6,0},{7,1},{8,14},{9,15},{10,... | collective-permute-start | bytes 196616 | tf_op jit(solution)/shard_map/ppermute | solution.py:30
  106.7 1.1 collective-permute-start.23
  107.8 1.3 collective-permute-start.22
  109.1 1.9 %collective-permute-done.24.refs_3_ = bf16[128,256]{1,0:T(8,128)(2,1)S(1)} collective-permute-done((bf16[128,256]{1,0:T(8,128)(2,1)S(1)}, bf16[128,256]{1,0:T(8,128)(2,1)S(1)}, u32[]{:S(2)}, u32[]{:S(2)}) %collective-permute-start.24) | collective-permute-done | bytes 65568 | tf_op jit(solution)/shard_map/ppermute | solution.py:30
  111.0 2.0 %collective-permute-done.23.refs_2_ = bf16[128,256]{1,0:T(8,128)(2,1)S(1)} collective-permute-done((bf16[128,256]{1,0:T(8,128)(2,1)S(1)}, bf16[128,256]{1,0:T(8,128)(2,1)S(1)}, u32[]{:S(2)}, u32[]{:S(2)}) %collective-permute-start.23) | collective-permute-done | bytes 65568 | tf_op jit(solution)/shard_map/ppermute | solution.py:30
  113.0 2.4 %collective-permute-start.27 = (bf16[576,256]{1,0:T(8,128)(2,1)S(1)}, bf16[576,256]{1,0:T(8,128)(2,1)S(1)}, u32[]{:S(2)}, u32[]{:S(2)}) collective-permute-start(bf16[576,256]{1,0:T(8,128)(2,1)S(1)} %join.5.joined.refs_0_), channel_id=1, source_target_pairs={{0,24},{8,16},{16,8},{24,0},{1,25},{9,17},{17,9},{25,1},{2,26},{10... | collective-permute-start | bytes 884744 | tf_op jit(solution)/shard_map/ppermute | solution.py:30
  116.5 0.9 collective-permute-start.21
  117.4 6.2 %collective-permute-done.21.got = bf16[256,256]{1,0:T(8,128)(2,1)S(1)} collective-permute-done((bf16[256,256]{1,0:T(8,128)(2,1)S(1)}, bf16[256,256]{1,0:T(8,128)(2,1)S(1)}, u32[]{:S(2)}, u32[]{:S(2)}) %collective-permute-start.21) | collective-permute-done | bytes 131104 | tf_op jit(solution)/shard_map/ppermute | solution.py:30
  123.6 0.7 src_sum.1
  124.9 3.7 %collective-permute-done.26.refs_2_ = bf16[576,256]{1,0:T(8,128)(2,1)S(1)} collective-permute-done((bf16[576,256]{1,0:T(8,128)(2,1)S(1)}, bf16[576,256]{1,0:T(8,128)(2,1)S(1)}, u32[]{:S(2)}, u32[]{:S(2)}) %collective-permute-start.26) | collective-permute-done | bytes 294944 | tf_op jit(solution)/shard_map/ppermute | solution.py:30
  129.1 1.5 %place.2 = (f32[4096,256]{1,0:T(8,128)}, f32[256,256]{1,0:T(8,128)}) custom-call(bf16[576,256]{1,0:T(8,128)(2,1)S(1)} %join.5.joined.refs_0_, bf16[576,256]{1,0:T(8,128)(2,1)S(1)} %collective-permute-done.25.refs_1_, bf16[576,256]{1,0:T(8,128)(2,1)S(1)} %collective-permute-done.26.refs_2_, bf16[576,256]{1,0:T(8,128)(2,1)S(1)} %collective-permute-done.27.refs_3_), custom_call_target="tpu_custom_call" | custom-call | flops 10000000000 | tf_op jit(solution)/shard_map/place/pallas_call | solution.py:527
  130.6 1.4 %place.3 = f32[4096,256]{1,0:T(8,128)} custom-call(bf16[576,256]{1,0:T(8,128)(2,1)S(1)} %collective-permute-done.28.refs_0_, bf16[576,256]{1,0:T(8,128)(2,1)S(1)} %collective-permute-done.29.refs_1_, bf16[576,256]{1,0:T(8,128)(2,1)S(1)} %collective-permute-done.30.refs_2_, ...), custom_call_target="tpu_custom_call", output_to_operand_aliasing={{}: (4, {})} | custom-call | tf_op jit(solution)/shard_map/place/pallas_call | solution.py:527
  (56 shorter events, 7.3 us)
Async XLA Ops:
  0.6 16.9 %collective-permute-start.3 = (bf16[256,256]{1,0:T(8,128)(2,1)}, bf16[256,256]{1,0:T(8,128)(2,1)S(1)}, u32[]{:S(2)}, u32[]{:S(2)}) collective-permute-start(bf16[256,256]{1,0:T(8,128)(2,1)} %own.1), channel_id=1, source_target_pairs={{0,2},{1,3},{2,0},{3,1},{4,6},{5,7},{6,4},{7,5},{8,10},{9,11},{10,... | collective-permute-start | bytes 393224 | tf_op jit(solution)/shard_map/ppermute | solution.py:30
  3.7 8.0 %collective-permute-start.2 = (bf16[64,256]{1,0:T(8,128)(2,1)S(1)}, bf16[64,256]{1,0:T(8,128)(2,1)S(1)}, u32[]{:S(2)}, u32[]{:S(2)}) collective-permute-start(bf16[64,256]{1,0:T(8,128)(2,1)S(1)} %constant_dynamic-slice_fusion.refs_0_), channel_id=1, source_target_pairs={{0,6},{1,7},{2,4},{3,5},{4,2},{5,3},{6,0},{7,1},{8,14},{9,15},{10,... | collective-permute-start | bytes 98312 | tf_op jit(solution)/shard_map/ppermute | solution.py:30
  6.6 11.0 %collective-permute-start.1 = (bf16[64,256]{1,0:T(8,128)(2,1)S(1)}, bf16[64,256]{1,0:T(8,128)(2,1)S(1)}, u32[]{:S(2)}, u32[]{:S(2)}) collective-permute-start(bf16[64,256]{1,0:T(8,128)(2,1)S(1)} %constant_dynamic-slice_fusion.refs_0_), channel_id=1, source_target_pairs={{0,4},{1,5},{2,6},{3,7},{4,0},{5,1},{6,2},{7,3},{8,12},{9,13},{10,... | collective-permute-start | bytes 98312 | tf_op jit(solution)/shard_map/ppermute | solution.py:30
  6.6 11.0 %collective-permute-start = (bf16[64,256]{1,0:T(8,128)(2,1)S(1)}, bf16[64,256]{1,0:T(8,128)(2,1)S(1)}, u32[]{:S(2)}, u32[]{:S(2)}) collective-permute-start(bf16[64,256]{1,0:T(8,128)(2,1)S(1)} %constant_dynamic-slice_fusion.refs_0_), channel_id=1, source_target_pairs={{0,2},{1,3},{2,0},{3,1},{4,6},{5,7},{6,4},{7,5},{8,10},{9,11},{10,... | collective-permute-start | bytes 98312 | tf_op jit(solution)/shard_map/ppermute | solution.py:30
  8.1 17.6 %collective-permute-start.5 = (bf16[256,256]{1,0:T(8,128)(2,1)}, bf16[256,256]{1,0:T(8,128)(2,1)S(1)}, u32[]{:S(2)}, u32[]{:S(2)}) collective-permute-start(bf16[256,256]{1,0:T(8,128)(2,1)} %own.1), channel_id=1, source_target_pairs={{0,6},{1,7},{2,4},{3,5},{4,2},{5,3},{6,0},{7,1},{8,14},{9,15},{10,... | collective-permute-start | bytes 393224 | tf_op jit(solution)/shard_map/ppermute | solution.py:30
  11.8 13.9 %collective-permute-start.4 = (bf16[256,256]{1,0:T(8,128)(2,1)}, bf16[256,256]{1,0:T(8,128)(2,1)S(1)}, u32[]{:S(2)}, u32[]{:S(2)}) collective-permute-start(bf16[256,256]{1,0:T(8,128)(2,1)} %own.1), channel_id=1, source_target_pairs={{0,4},{1,5},{2,6},{3,7},{4,0},{5,1},{6,2},{7,3},{8,12},{9,13},{10,... | collective-permute-start | bytes 393224 | tf_op jit(solution)/shard_map/ppermute | solution.py:30
  17.6 8.2 %collective-permute-start.8 = (bf16[256,256]{1,0:T(8,128)(2,1)S(1)}, bf16[256,256]{1,0:T(8,128)(2,1)S(1)}, u32[]{:S(2)}, u32[]{:S(2)}) collective-permute-start(bf16[256,256]{1,0:T(8,128)(2,1)S(1)} %get-tuple-element.36.refs_4_), channel_id=1, source_target_pairs={{0,24},{8,16},{16,8},{24,0},{1,25},{9,17},{17,9},{25,1},{2,26},{10... | collective-permute-start | bytes 393224 | tf_op jit(solution)/shard_map/ppermute | solution.py:30
  20.1 5.7 %collective-permute-start.7 = (bf16[256,256]{1,0:T(8,128)(2,1)S(1)}, bf16[256,256]{1,0:T(8,128)(2,1)S(1)}, u32[]{:S(2)}, u32[]{:S(2)}) collective-permute-start(bf16[256,256]{1,0:T(8,128)(2,1)S(1)} %get-tuple-element.36.refs_4_), channel_id=1, source_target_pairs={{0,16},{8,24},{16,0},{24,8},{1,17},{9,25},{17,1},{25,9},{2,18},{10... | collective-permute-start | bytes 393224 | tf_op jit(solution)/shard_map/ppermute | solution.py:30
  20.6 5.2 %collective-permute-start.6 = (bf16[256,256]{1,0:T(8,128)(2,1)S(1)}, bf16[256,256]{1,0:T(8,128)(2,1)S(1)}, u32[]{:S(2)}, u32[]{:S(2)}) collective-permute-start(bf16[256,256]{1,0:T(8,128)(2,1)S(1)} %get-tuple-element.36.refs_4_), channel_id=1, source_target_pairs={{0,8},{8,0},{16,24},{24,16},{1,9},{9,1},{17,25},{25,17},{2,10},{10... | collective-permute-start | bytes 393224 | tf_op jit(solution)/shard_map/ppermute | solution.py:30
  25.9 2.7 %collective-permute-start.9 = (bf16[2048,256]{1,0:T(8,128)(2,1)S(1)}, bf16[2048,256]{1,0:T(8,128)(2,1)S(1)}, u32[]{:S(2)}, u32[]{:S(2)}) collective-permute-start(bf16[2048,256]{1,0:T(8,128)(2,1)S(1)} %join.4.near), channel_id=1, source_target_pairs={{0,1},{1,0},{2,3},{3,2},{4,5},{5,4},{6,7},{7,6},{8,9},{9,8},{10,11... | collective-permute-start | bytes 3145736 | tf_op jit(solution)/shard_map/ppermute | solution.py:30
  68.9 3.5 %collective-permute-start.10 = (bf16[3072,256]{1,0:T(8,128)(2,1)S(1)}, bf16[3072,256]{1,0:T(8,128)(2,1)S(1)}, u32[]{:S(2)}, u32[]{:S(2)}) collective-permute-start(bf16[3072,256]{1,0:T(8,128)(2,1)S(1)} %get-tuple-element.38.after), channel_id=1, source_target_pairs={{0,1},{1,0},{2,3},{3,2},{4,5},{5,4},{6,7},{7,6},{8,9},{9,8},{10,11... | collective-permute-start | bytes 4718600 | tf_op jit(solution)/shard_map/ppermute | solution.py:30
  72.7 3.7 %collective-permute-start.14 = (f32[8,128]{1,0:T(8,128)S(1)}, f32[8,128]{1,0:T(8,128)S(1)}, u32[]{:S(2)}, u32[]{:S(2)}) collective-permute-start(f32[8,128]{1,0:T(8,128)S(1)} %get-tuple-element.45), channel_id=1, source_target_pairs={{0,1},{1,0},{2,3},{3,2},{4,5},{5,4},{6,7},{7,6},{8,9},{9,8},{10,11... | collective-permute-start | bytes 12296 | tf_op jit(solution)/shard_map/ppermute | solution.py:30
  72.9 16.8 %collective-permute-start.11 = (bf16[768,256]{1,0:T(8,128)(2,1)S(1)}, bf16[768,256]{1,0:T(8,128)(2,1)S(1)}, u32[]{:S(2)}, u32[]{:S(2)}) collective-permute-start(bf16[768,256]{1,0:T(8,128)(2,1)S(1)} %get-tuple-element.42), channel_id=1, source_target_pairs={{0,8},{8,0},{16,24},{24,16},{1,9},{9,1},{17,25},{25,17},{2,10},{10... | collective-permute-start | bytes 1179656 | tf_op jit(solution)/shard_map/ppermute | solution.py:30
  74.4 19.5 %collective-permute-start.12 = (bf16[768,256]{1,0:T(8,128)(2,1)S(1)}, bf16[768,256]{1,0:T(8,128)(2,1)S(1)}, u32[]{:S(2)}, u32[]{:S(2)}) collective-permute-start(bf16[768,256]{1,0:T(8,128)(2,1)S(1)} %get-tuple-element.43), channel_id=1, source_target_pairs={{0,16},{8,24},{16,0},{24,8},{1,17},{9,25},{17,1},{25,9},{2,18},{10... | collective-permute-start | bytes 1179656 | tf_op jit(solution)/shard_map/ppermute | solution.py:30
  75.9 18.0 %collective-permute-start.13 = (bf16[768,256]{1,0:T(8,128)(2,1)S(1)}, bf16[768,256]{1,0:T(8,128)(2,1)S(1)}, u32[]{:S(2)}, u32[]{:S(2)}) collective-permute-start(bf16[768,256]{1,0:T(8,128)(2,1)S(1)} %get-tuple-element.44), channel_id=1, source_target_pairs={{0,24},{8,16},{16,8},{24,0},{1,25},{9,17},{17,9},{25,1},{2,26},{10... | collective-permute-start | bytes 1179656 | tf_op jit(solution)/shard_map/ppermute | solution.py:30
  87.5 1.6 %collective-permute-start.15 = (bf16[512,256]{1,0:T(8,128)(2,1)S(1)}, bf16[512,256]{1,0:T(8,128)(2,1)S(1)}, u32[]{:S(2)}, u32[]{:S(2)}) collective-permute-start(bf16[512,256]{1,0:T(8,128)(2,1)S(1)} %get-tuple-element.47), channel_id=1, source_target_pairs={{0,1},{1,0},{2,3},{3,2},{4,5},{5,4},{6,7},{7,6},{8,9},{9,8},{10,11... | collective-permute-start | bytes 786440 | tf_op jit(solution)/shard_map/ppermute | solution.py:30
  87.5 1.9 %collective-permute-start.16 = (bf16[512,256]{1,0:T(8,128)(2,1)S(1)}, bf16[512,256]{1,0:T(8,128)(2,1)S(1)}, u32[]{:S(2)}, u32[]{:S(2)}) collective-permute-start(bf16[512,256]{1,0:T(8,128)(2,1)S(1)} %get-tuple-element.48), channel_id=1, source_target_pairs={{0,1},{1,0},{2,3},{3,2},{4,5},{5,4},{6,7},{7,6},{8,9},{9,8},{10,11... | collective-permute-start | bytes 786440 | tf_op jit(solution)/shard_map/ppermute | solution.py:30
  89.6 15.0 %collective-permute-start.20 = (bf16[512,256]{1,0:T(8,128)(2,1)S(1)}, bf16[512,256]{1,0:T(8,128)(2,1)S(1)}, u32[]{:S(2)}, u32[]{:S(2)}) collective-permute-start(bf16[512,256]{1,0:T(8,128)(2,1)S(1)} %get-tuple-element.54), channel_id=1, source_target_pairs={{0,2},{1,3},{2,0},{3,1},{4,6},{5,7},{6,4},{7,5},{8,10},{9,11},{10,... | collective-permute-start | bytes 786440 | tf_op jit(solution)/shard_map/ppermute | solution.py:30
  94.2 9.7 %collective-permute-start.17 = (bf16[192,256]{1,0:T(8,128)(2,1)S(1)}, bf16[192,256]{1,0:T(8,128)(2,1)S(1)}, u32[]{:S(2)}, u32[]{:S(2)}) collective-permute-start(bf16[192,256]{1,0:T(8,128)(2,1)S(1)} %get-tuple-element.51), channel_id=1, source_target_pairs={{0,2},{1,3},{2,0},{3,1},{4,6},{5,7},{6,4},{7,5},{8,10},{9,11},{10,... | collective-permute-start | bytes 294920 | tf_op jit(solution)/shard_map/ppermute | solution.py:30
  94.3 10.2 %collective-permute-start.18 = (bf16[192,256]{1,0:T(8,128)(2,1)S(1)}, bf16[192,256]{1,0:T(8,128)(2,1)S(1)}, u32[]{:S(2)}, u32[]{:S(2)}) collective-permute-start(bf16[192,256]{1,0:T(8,128)(2,1)S(1)} %get-tuple-element.52), channel_id=1, source_target_pairs={{0,4},{1,5},{2,6},{3,7},{4,0},{5,1},{6,2},{7,3},{8,12},{9,13},{10,... | collective-permute-start | bytes 294920 | tf_op jit(solution)/shard_map/ppermute | solution.py:30
  94.4 10.1 %collective-permute-start.19 = (bf16[192,256]{1,0:T(8,128)(2,1)S(1)}, bf16[192,256]{1,0:T(8,128)(2,1)S(1)}, u32[]{:S(2)}, u32[]{:S(2)}) collective-permute-start(bf16[192,256]{1,0:T(8,128)(2,1)S(1)} %get-tuple-element.53), channel_id=1, source_target_pairs={{0,6},{1,7},{2,4},{3,5},{4,2},{5,3},{6,0},{7,1},{8,14},{9,15},{10,... | collective-permute-start | bytes 294920 | tf_op jit(solution)/shard_map/ppermute | solution.py:30
  104.6 6.3 %collective-permute-start.24 = (bf16[128,256]{1,0:T(8,128)(2,1)S(1)}, bf16[128,256]{1,0:T(8,128)(2,1)S(1)}, u32[]{:S(2)}, u32[]{:S(2)}) collective-permute-start(bf16[128,256]{1,0:T(8,128)(2,1)S(1)} %get-tuple-element.57.refs_0_), channel_id=1, source_target_pairs={{0,6},{1,7},{2,4},{3,5},{4,2},{5,3},{6,0},{7,1},{8,14},{9,15},{10,... | collective-permute-start | bytes 196616 | tf_op jit(solution)/shard_map/ppermute | solution.py:30
  106.7 6.3 %collective-permute-start.23 = (bf16[128,256]{1,0:T(8,128)(2,1)S(1)}, bf16[128,256]{1,0:T(8,128)(2,1)S(1)}, u32[]{:S(2)}, u32[]{:S(2)}) collective-permute-start(bf16[128,256]{1,0:T(8,128)(2,1)S(1)} %get-tuple-element.57.refs_0_), channel_id=1, source_target_pairs={{0,4},{1,5},{2,6},{3,7},{4,0},{5,1},{6,2},{7,3},{8,12},{9,13},{10,... | collective-permute-start | bytes 196616 | tf_op jit(solution)/shard_map/ppermute | solution.py:30
  107.8 5.2 %collective-permute-start.22 = (bf16[128,256]{1,0:T(8,128)(2,1)S(1)}, bf16[128,256]{1,0:T(8,128)(2,1)S(1)}, u32[]{:S(2)}, u32[]{:S(2)}) collective-permute-start(bf16[128,256]{1,0:T(8,128)(2,1)S(1)} %get-tuple-element.57.refs_0_), channel_id=1, source_target_pairs={{0,2},{1,3},{2,0},{3,1},{4,6},{5,7},{6,4},{7,5},{8,10},{9,11},{10,... | collective-permute-start | bytes 196616 | tf_op jit(solution)/shard_map/ppermute | solution.py:30
  113.0 11.4 %collective-permute-start.27 = (bf16[576,256]{1,0:T(8,128)(2,1)S(1)}, bf16[576,256]{1,0:T(8,128)(2,1)S(1)}, u32[]{:S(2)}, u32[]{:S(2)}) collective-permute-start(bf16[576,256]{1,0:T(8,128)(2,1)S(1)} %join.5.joined.refs_0_), channel_id=1, source_target_pairs={{0,24},{8,16},{16,8},{24,0},{1,25},{9,17},{17,9},{25,1},{2,26},{10... | collective-permute-start | bytes 884744 | tf_op jit(solution)/shard_map/ppermute | solution.py:30
  115.4 13.2 %collective-permute-start.26 = (bf16[576,256]{1,0:T(8,128)(2,1)S(1)}, bf16[576,256]{1,0:T(8,128)(2,1)S(1)}, u32[]{:S(2)}, u32[]{:S(2)}) collective-permute-start(bf16[576,256]{1,0:T(8,128)(2,1)S(1)} %join.5.joined.refs_0_), channel_id=1, source_target_pairs={{0,16},{8,24},{16,0},{24,8},{1,17},{9,25},{17,1},{25,9},{2,18},{10... | collective-permute-start | bytes 884744 | tf_op jit(solution)/shard_map/ppermute | solution.py:30
  116.0 12.7 %collective-permute-start.25 = (bf16[576,256]{1,0:T(8,128)(2,1)S(1)}, bf16[576,256]{1,0:T(8,128)(2,1)S(1)}, u32[]{:S(2)}, u32[]{:S(2)}) collective-permute-start(bf16[576,256]{1,0:T(8,128)(2,1)S(1)} %join.5.joined.refs_0_), channel_id=1, source_target_pairs={{0,8},{8,0},{16,24},{24,16},{1,9},{9,1},{17,25},{25,17},{2,10},{10... | collective-permute-start | bytes 884744 | tf_op jit(solution)/shard_map/ppermute | solution.py:30
  116.5 7.1 %collective-permute-start.21 = (bf16[256,256]{1,0:T(8,128)(2,1)S(1)}, bf16[256,256]{1,0:T(8,128)(2,1)S(1)}, u32[]{:S(2)}, u32[]{:S(2)}) collective-permute-start(bf16[256,256]{1,0:T(8,128)(2,1)S(1)} %get-tuple-element.56), channel_id=1, source_target_pairs={{0,4},{1,5},{2,6},{3,7},{4,0},{5,1},{6,2},{7,3},{8,12},{9,13},{10,... | collective-permute-start | bytes 393224 | tf_op jit(solution)/shard_map/ppermute | solution.py:30
  124.4 6.2 %collective-permute-start.28 = (bf16[576,256]{1,0:T(8,128)(2,1)S(1)}, bf16[576,256]{1,0:T(8,128)(2,1)S(1)}, u32[]{:S(2)}, u32[]{:S(2)}) collective-permute-start(bf16[576,256]{1,0:T(8,128)(2,1)S(1)} %get-tuple-element.61), channel_id=1, source_target_pairs={{0,1},{1,0},{2,3},{3,2},{4,5},{5,4},{6,7},{7,6},{8,9},{9,8},{10,11... | collective-permute-start | bytes 884744 | tf_op jit(solution)/shard_map/ppermute | solution.py:30
  124.4 6.2 %collective-permute-start.31 = (bf16[576,256]{1,0:T(8,128)(2,1)S(1)}, bf16[576,256]{1,0:T(8,128)(2,1)S(1)}, u32[]{:S(2)}, u32[]{:S(2)}) collective-permute-start(bf16[576,256]{1,0:T(8,128)(2,1)S(1)} %collective-permute-done.27.refs_3_), channel_id=1, source_target_pairs={{0,1},{1,0},{2,3},{3,2},{4,5},{5,4},{6,7},{7,6},{8,9},{9,8},{10,11... | collective-permute-start | bytes 884744 | tf_op jit(solution)/shard_map/ppermute | solution.py:30
  128.6 2.0 %collective-permute-start.30 = (bf16[576,256]{1,0:T(8,128)(2,1)S(1)}, bf16[576,256]{1,0:T(8,128)(2,1)S(1)}, u32[]{:S(2)}, u32[]{:S(2)}) collective-permute-start(bf16[576,256]{1,0:T(8,128)(2,1)S(1)} %collective-permute-done.26.refs_2_), channel_id=1, source_target_pairs={{0,1},{1,0},{2,3},{3,2},{4,5},{5,4},{6,7},{7,6},{8,9},{9,8},{10,11... | collective-permute-start | bytes 884744 | tf_op jit(solution)/shard_map/ppermute | solution.py:30
  128.7 1.9 %collective-permute-start.29 = (bf16[576,256]{1,0:T(8,128)(2,1)S(1)}, bf16[576,256]{1,0:T(8,128)(2,1)S(1)}, u32[]{:S(2)}, u32[]{:S(2)}) collective-permute-start(bf16[576,256]{1,0:T(8,128)(2,1)S(1)} %collective-permute-done.25.refs_1_), channel_id=1, source_target_pairs={{0,1},{1,0},{2,3},{3,2},{4,5},{5,4},{6,7},{7,6},{8,9},{9,8},{10,11... | collective-permute-start | bytes 884744 | tf_op jit(solution)/shard_map/ppermute | solution.py:30
  (3 other events, 5.6 us)
